TPU v7x, 256 devices: a whole 4x4x8 slice. The times are simulated.
256 devices in a mesh: row: 32 (over z, x), col: 8 (over y, core).
Axes of the slice: x: 4, y: 4, z: 8, core: 2. Of those that a mesh axis runs over, the one named last changes fastest.
Arguments:
- rhs: bfloat16 [4, 8192, 256], P(None, 'row'), may hold values from -6 to 6
- dinv: bfloat16 [4, 8192, 256], P(None, 'row'), may hold values from -0.125 to 1.1875, as said below
- factor: bfloat16 [6, 8192, 24, 256], P(None, 'row', 'col'), may hold values from -0.046875 to 0.046875
- cols: int32 [6, 32, 24], P(None, 'row', 'col'), may hold values from 0 to 31, as said below
- live: int32 [6, 32], P(None, 'row'), may hold values from 1 to 24, as said below
Outputs:
- solved: float32 [4, 8192, 256], P(None, 'row', 'col')
Inputs may be any that keep to these rules, and one draw needn't show every extreme that they name: Each 256 x 256 block of dinv is lower triangular with diagonal entries from about 0.6 to 1.1875. `cols`: the 24 slots of one tile row and level pair name distinct tile columns. Every level pair has a tile row with all 24 slots live and one with a single live slot.
All inputs are finite; a program needn't handle non-finite values.
Results may differ from a plain program's by a relative error of at most 0.003.
Values may be sent and summed in bfloat16 or wider, within the bound.
No kernel may reach another device: no remote copies, remote signals or barrier semaphores. Data moves between devices by JAX's collectives and lax.ppermute only.
A program may use at most 64 MiB of HBM per device.

v0:
```python
import jax
import jax.numpy as jnp
from jax import lax
from jax.sharding import PartitionSpec as P


def local(rhs, dinv, factor, cols, live):
    level_count = rhs.shape[0]
    tile_size = dinv.shape[2]
    row_count = dinv.shape[1]
    tiles_here = row_count // tile_size
    probe_count = rhs.shape[2]
    slots_here = factor.shape[2]
    col_count = lax.axis_size("col")
    col_place = lax.axis_index("col")
    probe_block = probe_count // col_count
    slot_global = col_place * slots_here + jnp.arange(slots_here, dtype=jnp.int32)
    finished = []
    outputs = []
    for target in range(level_count):
        partial_value = jnp.zeros((tiles_here, tile_size, probe_count), jnp.float32)
        for anchor in range(target):
            pair_slot = target * (target - 1) // 2 + anchor
            factor_tiles = factor[pair_slot].reshape(tiles_here, tile_size, slots_here, tile_size)
            live_mask = (slot_global[None, :] < live[pair_slot][:, None]).astype(jnp.bfloat16)
            column_ids = cols[pair_slot]
            known_rows = finished[anchor]
            owner_row = column_ids // tiles_here
            local_tile = column_ids % tiles_here
            lane_index = (
                owner_row[:, :, None] * col_count
                + jnp.arange(col_count, dtype=jnp.int32)[None, None, :]
            )
            chosen = (
                known_rows[lane_index, local_tile[:, :, None]] * live_mask[:, :, None, None, None]
            )
            contrib = jnp.einsum(
                "takb,tkcbq->tacq", factor_tiles, chosen, preferred_element_type=jnp.float32
            )
            contrib = contrib.reshape(tiles_here, tile_size, probe_count)
            partial_value = partial_value + contrib
        rhs_tiles = rhs[target].reshape(tiles_here, tile_size, probe_count)
        dinv_tiles = dinv[target].reshape(tiles_here, tile_size, tile_size)
        if target > 0:
            shares = lax.psum_scatter(partial_value, "col", scatter_dimension=2, tiled=True)
        else:
            shares = jnp.zeros((tiles_here, tile_size, probe_block), jnp.float32)
        rhs_block = lax.dynamic_slice_in_dim(rhs_tiles, col_place * probe_block, probe_block, 2)
        residual = (rhs_block.astype(jnp.float32) - shares).astype(jnp.bfloat16)
        answer = jnp.einsum(
            "tab,tbq->taq", dinv_tiles, residual, preferred_element_type=jnp.float32
        )
        outputs.append(answer.reshape(row_count, probe_block))
        if target + 1 < level_count:
            finished.append(
                lax.all_gather(
                    answer.astype(jnp.bfloat16)[None], ("row", "col"), axis=0, tiled=True
                )
            )
    return jnp.stack(outputs)


def solution(mesh):
    in_specs = (
        P(None, "row", None),
        P(None, "row", None),
        P(None, "row", "col", None),
        P(None, "row", "col"),
        P(None, "row"),
    )
    out_specs = P(None, "row", "col")
    return jax.shard_map(local, mesh=mesh, in_specs=in_specs, out_specs=out_specs, check_vma=False)
```

profile of v0, /device:TPU:2, one launch (start us, length us, event | category | flops | bytes accessed | tf_op | source)
XLA Modules:
  0.0 486.6 jit_solution(322274683269350538)
XLA Ops:
  6.5 1.1 fusion.61
  7.7 1.8 bitcast_convert_fusion.2
  9.4 0.0 all-gather.7.cloned.1.call-update
  9.5 0.0 reduce-scatter.4.cloned.1.call-start
  9.5 1.4 multiply_reduce_fusion.2
  10.9 0.1 compare_select_fusion.4
  11.0 0.1 reshape.924
  11.1 1.5 fusion.62
  12.7 1.2 compare_convert_fusion.4
  13.9 108.8 %all-gather.7.cloned.1.call-done = bf16[65536,32]{0,1:T(8,128)(2,1)} async-done(((bf16[256,32]{0,1:T(8,128)(2,1)}), bf16[65536,32]{0,1:T(8,128)(2,1)}) %all-gather.7.cloned.1.call-update) | async-done | bytes 4194320 | tf_op jit(solution)/shard_map/all_gather | solution.py:56
  122.7 3.2 copy.30
  125.9 4.3 copy.16
  130.3 2.9 gather_fusion
  133.2 0.1 broadcast_multiply_fusion.5
  133.3 1.0 convolution_bitcast_fusion.5
  134.3 0.0 reduce-scatter.4.cloned.1.call-update
  134.3 0.0 all-gather.9.cloned.1.call-start
  134.4 0.1 constant_dynamic-slice_fusion.2
  134.5 0.1 copy.25
  134.6 32.1 %reduce-scatter.4.cloned.1.call-done = f32[1,256,32]{1,2,0:T(8,128)} async-done(((f32[1,256,256]{1,2,0:T(8,128)}), f32[1,256,32]{1,2,0:T(8,128)}) %reduce-scatter.4.cloned.1.call-update) | async-done | bytes 32784 | tf_op jit(solution)/shard_map/reduce_scatter | solution.py:45
  166.7 1.7 bitcast_convert_fusion.1
  168.4 0.0 reduce-scatter.6.cloned.1.call-start
  168.5 0.1 compare_select_fusion.2
  168.6 0.1 reshape.940
  168.7 0.1 reshape.932
  168.8 1.3 compare_convert_fusion.2
  170.1 2.8 gather_fusion.1
  172.9 0.1 broadcast_multiply_fusion.4
  173.0 105.6 %all-gather.9.cloned.1.call-done = bf16[65536,32]{0,1:T(8,128)(2,1)} async-done(((bf16[256,32]{0,1:T(8,128)(2,1)}), bf16[65536,32]{0,1:T(8,128)(2,1)}) %all-gather.9.cloned.1.call-update) | async-done | bytes 4194320 | tf_op jit(solution)/shard_map/all_gather | solution.py:56
  278.6 3.2 copy.31
  281.8 4.4 copy.19
  286.2 2.8 gather_fusion.2
  289.0 0.1 broadcast_multiply_fusion.3
  289.1 0.3 convolution_bitcast_fusion.3
  289.4 1.0 fusion.1
  290.5 0.0 all-gather.11.cloned.1.call-start
  290.5 0.1 constant_dynamic-slice_fusion.1
  290.6 0.1 copy.27
  290.7 32.2 %reduce-scatter.6.cloned.1.call-done = f32[1,256,32]{1,2,0:T(8,128)} async-done(((f32[1,256,256]{1,2,0:T(8,128)}), f32[1,256,32]{1,2,0:T(8,128)}) %reduce-scatter.6.cloned.1.call-update) | async-done | bytes 32784 | tf_op jit(solution)/shard_map/reduce_scatter | solution.py:45
  322.9 1.7 bitcast_convert_fusion
  324.6 0.2 reduce-scatter.8.cloned.1.call-start
  324.9 0.1 reshape.948
  325.0 0.1 compare_select_fusion
  325.1 0.1 reshape.964
  325.2 0.1 reshape.956
  325.3 1.2 compare_convert_fusion
  326.5 2.8 gather_fusion.3
  329.3 0.1 broadcast_multiply_fusion.2
  329.4 2.8 gather_fusion.4
  332.2 0.1 broadcast_multiply_fusion.1
  332.3 0.3 convolution_bitcast_fusion.1
  332.6 101.3 %all-gather.11.cloned.1.call-done = bf16[65536,32]{0,1:T(8,128)(2,1)} async-done(((bf16[256,32]{0,1:T(8,128)(2,1)}), bf16[65536,32]{0,1:T(8,128)(2,1)}) %all-gather.11.cloned.1.call-update) | async-done | bytes 4194320 | tf_op jit(solution)/shard_map/all_gather | solution.py:56
  433.9 3.2 copy.32
  437.1 4.3 copy.23
  441.4 2.8 gather_fusion.5
  444.2 0.1 broadcast_multiply_fusion
  444.4 0.3 convolution_bitcast_fusion
  444.7 1.0 fusion.4
  445.7 0.1 constant_dynamic-slice_fusion
  445.8 0.1 copy.29
  445.9 32.1 %reduce-scatter.8.cloned.1.call-done = f32[1,256,32]{1,2,0:T(8,128)} async-done(((f32[1,256,256]{1,2,0:T(8,128)}), f32[1,256,32]{1,2,0:T(8,128)}) %reduce-scatter.8.cloned.1.call-update) | async-done | bytes 32784 | tf_op jit(solution)/shard_map/reduce_scatter | solution.py:45
  478.0 1.1 convolution_bitcast_fusion.6
  479.1 0.0 copy-done.3
  479.1 0.7 pad_maximum_fusion
  (24 shorter events, 0.3 us)
Async XLA Ops:
  6.5 116.2 %all-gather.7.cloned.1.call-start = ((), (), s32[]{:S(2)}) async-start(), calls=%async_computation.6 | async-start | bytes 4210688 | tf_op jit(solution)/shard_map/all_gather | solution.py:56
  9.5 157.2 %reduce-scatter.4.cloned.1.call-start = ((), (), s32[]{:S(2)}) async-start(), calls=%async_computation.3 | async-start | bytes 294912 | tf_op jit(solution)/shard_map/reduce_scatter | solution.py:45
  130.3 3.0 copy-start
  134.3 144.3 %all-gather.9.cloned.1.call-start = ((), (), s32[]{:S(2)}) async-start(), calls=%async_computation.7 | async-start | bytes 4210688 | tf_op jit(solution)/shard_map/all_gather | solution.py:56
  168.4 154.4 %reduce-scatter.6.cloned.1.call-start = ((), (), s32[]{:S(2)}) async-start(), calls=%async_computation.4 | async-start | bytes 294912 | tf_op jit(solution)/shard_map/reduce_scatter | solution.py:45
  290.5 143.4 %all-gather.11.cloned.1.call-start = ((), (), s32[]{:S(2)}) async-start(), calls=%async_computation.8 | async-start | bytes 4210688 | tf_op jit(solution)/shard_map/all_gather | solution.py:56
  324.6 153.4 %reduce-scatter.8.cloned.1.call-start = ((), (), s32[]{:S(2)}) async-start(), calls=%async_computation.5 | async-start | bytes 294912 | tf_op jit(solution)/shard_map/reduce_scatter | solution.py:45
  444.3 34.8 %copy-start.1 = (f32[32,256]{1,0:T(8,128)S(1)}, f32[32,256]{1,0:T(8,128)}, u32[]{:S(2)}) copy-start(f32[32,256]{1,0:T(8,128)} %get-tuple-element.22) | copy-start | bytes 98308
  444.3 34.7 %copy-start.2 = (f32[32,256]{1,0:T(8,128)S(1)}, f32[32,256]{1,0:T(8,128)}, u32[]{:S(2)}) copy-start(f32[32,256]{1,0:T(8,128)} %get-tuple-element.24) | copy-start | bytes 98308
  444.3 34.8 %copy-start.3 = (f32[32,256]{1,0:T(8,128)S(1)}, f32[32,256]{1,0:T(8,128)}, u32[]{:S(2)}) copy-start(f32[32,256]{1,0:T(8,128)} %get-tuple-element.26) | copy-start | bytes 98308
Sparse Core Ops, SparseCore 0:
  11.1 111.5 all-gather.6
  134.5 32.1 reduce-scatter.3
  171.1 107.4 all-gather.8
  290.6 32.2 reduce-scatter.5
  326.5 107.3 all-gather.10
  445.8 32.1 reduce-scatter.7
where the time goes:
time: 487 us
  waiting for transfers between devices  412 us (85%)
  local copies, waits for them, and re-layouts  43.2 us (9%)
  between operations  13.7 us (3%)
  matrix products  10.2 us (2%)
  other arithmetic  6.75 us (1%)
    all_gather x3, waiting for transfers between devices, local(): lax.all_gather(answer.astype(jnp.bfloat16)[None], ('row', 'col'), axis=0,...  316 us
    reduce_scatter x3, waiting for transfers between devices, local(): lax.psum_scatter(partial_value, 'col', scatter_dimension=2, tiled=True)  96.4 us
    gather x6, local copies, waits for them, and re-layouts, local(): known_rows[lane_index, local_tile[:, :, None]]  16.9 us
    all_gather x3, local copies, waits for them, and re-layouts, local(): lax.all_gather(answer.astype(jnp.bfloat16)[None], ('row', 'col'), axis=0,...  13.1 us
    unnamed x14, local copies, waits for them, and re-layouts  9.81 us
  transfers between devices with their start and end apart: 6, of which 6 were waited for; matrix products, arithmetic and copies ran while one was open for 3% of the time, Pallas kernels for 0%

commit v1 on v0

v1 whole, which is shorter than its diff:
```python
import functools

import jax
import jax.numpy as jnp
from jax import lax
from jax.experimental import pallas as pl
from jax.experimental.pallas import tpu as pltpu
from jax.sharding import PartitionSpec as P

NT_DIMS = (((1,), (1,)), ((), ()))


def dot_nt(a, b):
    return lax.dot_general(a, b, NT_DIMS, preferred_element_type=jnp.float32)


def probe_rows(place, rhs):
    block = 32
    probe = lax.broadcasted_iota(jnp.int32, (block, rhs.shape[1]), 1)
    mine = lax.broadcasted_iota(jnp.int32, (block, rhs.shape[1]), 0) + place * block
    return dot_nt((probe == mine).astype(jnp.bfloat16), rhs)


def level_kernel(level, copies, *refs):
    place, cols, live = refs[:3]
    rhs, dinv = refs[3:5]
    known = refs[5 : 5 + level]
    tiles = refs[5 + level : 5 + 2 * level]
    answer, spread = refs[5 + 2 * level :]
    total = probe_rows(place[0], rhs[0])
    base = level * (level - 1) // 2
    slots = cols.shape[1]
    update = jnp.zeros_like(total)
    for anchor in range(level):
        pair = base + anchor
        for slot in range(slots):
            block = known[anchor][cols[pair, slot]]
            block = jnp.where(slot < live[pair, 0], block, jnp.zeros_like(block))
            update = update + dot_nt(block, tiles[anchor][slot])
    residual = (total - update).astype(jnp.bfloat16)
    result = dot_nt(residual, dinv[0])
    answer[...] = result
    if copies:
        rounded = result.astype(jnp.bfloat16)
        for copy in range(copies):
            spread[copy] = rounded


def level_call(level, copies, place, cols, live, rhs, dinv, known, tiles):
    size = dinv.shape[2]
    smem = pl.BlockSpec(memory_space=pltpu.SMEM)
    vmem = pl.BlockSpec(memory_space=pltpu.VMEM)
    pick = pl.BlockSpec((1, size, size), lambda i: (level, 0, 0))
    count = max(copies, 1)
    whole = lambda a: pl.BlockSpec(a.shape, lambda i, n=a.ndim: (0,) * n)
    return pl.pallas_call(
        functools.partial(level_kernel, level, copies),
        grid=(1,),
        out_shape=(
            jax.ShapeDtypeStruct((32, size), jnp.float32),
            jax.ShapeDtypeStruct((count, 32, size), jnp.bfloat16),
        ),
        in_specs=[smem, smem, smem, pick, pick] + [whole(a) for a in known] + [whole(a) for a in tiles],
        out_specs=(
            pl.BlockSpec((32, size), lambda i: (0, 0)),
            pl.BlockSpec((count, 32, size), lambda i: (0, 0, 0)),
        ),
        compiler_params=pltpu.CompilerParams(vmem_limit_bytes=48 * 1024 * 1024),
        name="level%d" % level,
    )(place, cols, live, rhs, dinv, *known, *tiles)


def local(rhs, dinv, factor, cols, live):
    levels = rhs.shape[0]
    rows = lax.axis_size("row")
    place = lax.axis_index("col").astype(jnp.int32).reshape(1)
    tiles = factor.transpose(0, 2, 1, 3)
    all_cols = lax.all_gather(cols[:, 0, :], "col", axis=1, tiled=True)
    gathered = []
    for level in range(1, levels):
        base = level * (level - 1) // 2
        part = tiles[base : base + level]
        gathered.append(lax.all_gather(part, "col", axis=1, tiled=True))
    known, answers = [], []
    for level in range(levels):
        copies = rows if level + 1 < levels else 0
        use = [gathered[level - 1][a] for a in range(level)] if level else []
        answer, spread = level_call(level, copies, place, all_cols, live, rhs, dinv, known, use)
        answers.append(answer)
        if copies:
            known.append(lax.all_to_all(spread, "row", 0, 0, tiled=True))
    return jnp.stack(answers).transpose(0, 2, 1)


def solution(mesh):
    in_specs = (
        P(None, "row", None),
        P(None, "row", None),
        P(None, "row", "col", None),
        P(None, "row", "col"),
        P(None, "row"),
    )
    out_specs = P(None, "row", "col")
    return jax.shard_map(local, mesh=mesh, in_specs=in_specs, out_specs=out_specs, check_vma=False)
```

time: 487 us -> 171 us (0.35)
  waiting for transfers between devices: 412 us -> 57.8 us
  blocking collectives: 0 us -> 40.7 us
  local copies, waits for them, and re-layouts: 43.2 us -> 26.8 us
  starting transfers between devices: 0.39 us -> 15.7 us
  Pallas kernels: 0 us -> 14.6 us
  matrix products: 10.2 us -> 0 us
  other arithmetic: 6.75 us -> 0.66 us
    all_gather x3, waiting for transfers between devices: 316 us -> 57.7 us  [local(): gathered.append(lax.all_gather(part, 'col', axis=1, tiled=True))]
    reduce_scatter x3 -> x0, waiting for transfers between devices: 96.4 us -> none  [local(): lax.psum_scatter(partial_value, 'col', scatter_dimension=2, tiled=True)]
    all_to_all x0 -> x1, blocking collectives: none -> 28.7 us  [local(): known.append(lax.all_to_all(spread, 'row', 0, 0, tiled=True))]
    gather x6 -> x0, local copies, waits for them, and re-layouts: 16.9 us -> none  [local(): known_rows[lane_index, local_tile[:, :, None]]]
    all_to_all x0 -> x2, starting transfers between devices: none -> 15.6 us  [local(): known.append(lax.all_to_all(spread, 'row', 0, 0, tiled=True))]
    pallas_call x0 -> x4, Pallas kernels: none -> 14.6 us  [level_call(): pl.pallas_call(functools.partial(level_kernel, level, copies), grid=(1,),...]
    all_gather x3 -> x1, local copies, waits for them, and re-layouts: 13.1 us -> 0.08 us  [local(): all_cols = lax.all_gather(cols[:, 0, :], 'col', axis=1, tiled=True)]
    all_gather x0 -> x1, blocking collectives: none -> 12 us  [local(): all_cols = lax.all_gather(cols[:, 0, :], 'col', axis=1, tiled=True)]
  transfers between devices with their start and end apart: 6 -> 5, of which waited for: 6 -> 2; matrix products, arithmetic and copies ran while one was open for 3% -> 9% of each run, Pallas kernels for 0% -> 5%
where the time goes in v1:
time: 171 us; the launch traced here: 169 us
  waiting for transfers between devices  57.8 us (34%)
  blocking collectives  40.7 us (24%)
  local copies, waits for them, and re-layouts  26.8 us (16%)
  starting transfers between devices  15.7 us (9%)
  Pallas kernels  14.6 us (9%)
  between operations  13.2 us (8%)
    all_gather x3, waiting for transfers between devices, local(): gathered.append(lax.all_gather(part, 'col', axis=1, tiled=True))  57.7 us
    all_to_all x1, blocking collectives, local(): known.append(lax.all_to_all(spread, 'row', 0, 0, tiled=True))  28.7 us
    all_to_all x2, starting transfers between devices, local(): known.append(lax.all_to_all(spread, 'row', 0, 0, tiled=True))  15.6 us
    pallas_call x4, Pallas kernels, level_call(): pl.pallas_call(functools.partial(level_kernel, level, copies), grid=(1,),...  14.6 us
    all_gather x1, blocking collectives, local(): all_cols = lax.all_gather(cols[:, 0, :], 'col', axis=1, tiled=True)  12 us
    squeeze x2, local copies, waits for them, and re-layouts, local(): use = [gathered[level - 1][a] for a in range(level)] if level else []  10.9 us
    unnamed x27, local copies, waits for them, and re-layouts  9.47 us
    slice x3, local copies, waits for them, and re-layouts, local(): part = tiles[base:base + level]  6.31 us
  transfers between devices with their start and end apart: 5, of which 2 were waited for; matrix products, arithmetic and copies ran while one was open for 9% of the time, Pallas kernels for 5%

profile of v1, /device:TPU:2, one launch (start us, length us, event | category | flops | bytes accessed | tf_op | source)
XLA Modules:
  0.0 169.3 jit_solution(6564627438512898993)
XLA Ops:
  6.5 0.0 all-gather.5.cloned.1.call-start
  6.5 1.8 %slice_bitcast_fusion.5 = bf16[1,3,256,256]{3,2,0,1:T(8,128)(2,1)} fusion(bf16[6,3,256,256]{3,2,1,0:T(8,128)(2,1)} %bitcast.31), kind=kLoop, calls=%fused_computation.5 | loop fusion | bytes 786432 | tf_op jit(solution)/shard_map/slice | solution.py:82
  8.3 0.0 copy-start.12
  8.3 0.0 copy-start.11
  8.3 0.0 copy-start.3
  8.3 0.0 copy-start.6
  8.3 0.0 all-gather.5.cloned.1.call-update
  8.3 0.0 all-gather.7.cloned.1.call-start
  8.4 2.1 %slice.33 = bf16[2,3,256,256]{3,2,1,0:T(8,128)(2,1)} slice(bf16[6,3,256,256]{3,2,1,0:T(8,128)(2,1)} %bitcast.32), slice={[1:3], [0:3], [0:256], [0:256]} | slice | bytes 1572864 | tf_op jit(solution)/shard_map/slice | solution.py:82
  10.5 0.0 all-gather.7.cloned.1.call-update
  10.6 0.0 all-gather.9.cloned.1.call-start
  10.6 2.4 %slice.36 = bf16[3,3,256,256]{3,2,1,0:T(8,128)(2,1)} slice(bf16[6,3,256,256]{3,2,1,0:T(8,128)(2,1)} %bitcast.33), slice={[3:6], [0:3], [0:256], [0:256]} | slice | bytes 2359296 | tf_op jit(solution)/shard_map/slice | solution.py:82
  13.0 0.0 all-gather.9.cloned.1.call-update
  13.0 0.0 copy-done.12
  13.0 0.1 copy.12.refs_2_
  13.1 0.0 copy-done.11
  13.1 12.0 %all-gather = s32[6,1,24]{0,1,2:T(1,128)S(1)} all-gather(s32[6,1,3]{0,1,2:T(1,128)S(1)} %copy-done.11), channel_id=2, replica_groups=mesh['row'=32,'col'=8] {'col'}, dimensions={2}, use_global_device_ids=true | all-gather | bytes 648 | tf_op jit(solution)/shard_map/all_gather | solution.py:78
  25.1 0.1 copy.11
  25.2 0.0 copy-done.3
  25.2 0.0 copy-done.6
  25.2 1.0 level0.1
  26.2 28.7 %all_to_all.15.refs_5_ = bf16[32,32,256]{2,1,0:T(8,128)(2,1)S(1)} all-to-all(bf16[32,32,256]{2,1,0:T(8,128)(2,1)S(1)} %get-tuple-element.13), channel_id=1, replica_groups=mesh['row'=32,'col'=8] {'row'}, dimensions={0} | all-to-all | bytes 1048576 | tf_op jit(solution)/shard_map/all_to_all | solution.py:91
  54.9 0.0 copy-start
  54.9 0.0 all-gather.5.cloned.1.call-done
  54.9 0.0 copy-start.9
  54.9 2.3 %copy-done.9 = bf16[1,24,256,256]{3,2,0,1:T(8,128)(2,1)S(1)} copy-done((bf16[1,24,256,256]{3,2,0,1:T(8,128)(2,1)S(1)}, bf16[1,24,256,256]{3,2,0,1:T(8,128)(2,1)}, u32[]{:S(2)}) %copy-start.9) | copy-done | bytes 3145752
  57.3 2.7 %level1.1 = (f32[32,256]{1,0:T(8,128)S(1)}, bf16[32,32,256]{2,1,0:T(8,128)(2,1)}) custom-call(s32[1]{0:T(128)} %bitcast.refs_0_, s32[6,24]{1,0:T(8,128)S(1)} %bitcast.24, s32[6,1]{1,0:T(8,128)S(1)} %copy.12.refs_2_, bf16[4,256,256]{2,1,0:T(8,128)(2,1)S(1)} %copy-done.3, bf16[4,256,256]{2,1,0:T(8,128)(2,1)S(1)} %copy-done.6, ...), custom_call_target="tpu_custom_call" | custom-call | tf_op jit(solution)/shard_map/level1/pallas_call | solution.py:56
  60.0 5.4 %all-to-all-start.1 = ((bf16[32,32,256]{2,1,0:T(8,128)(2,1)}), bf16[32,32,256]{2,1,0:T(8,128)(2,1)}, u32[]{:S(2)}, u32[]{:S(2)}) async-start(bf16[32,32,256]{2,1,0:T(8,128)(2,1)} %get-tuple-element.15), calls=%async_computation.1 | async-start | bytes 1048576 | tf_op jit(solution)/shard_map/all_to_all | solution.py:91
  65.4 0.0 copy-done
  65.4 22.5 %all-gather.7.cloned.1.call-done = bf16[2,24,256,256]{3,2,1,0:T(8,128)(2,1)} async-done(((bf16[2,3,256,256]{3,2,1,0:T(8,128)(2,1)}), bf16[2,24,256,256]{3,2,1,0:T(8,128)(2,1)}) %all-gather.7.cloned.1.call-update) | async-done | bytes 6291472 | tf_op jit(solution)/shard_map/all_gather | solution.py:83
  87.9 5.1 %slice_bitcast_fusion.3 = (bf16[24,256,256]{2,1,0:T(8,128)(2,1)}, bf16[24,256,256]{2,1,0:T(8,128)(2,1)S(1)}) fusion(bf16[2,24,256,256]{3,2,1,0:T(8,128)(2,1)} %all-gather.7.cloned.1.call-done), kind=kLoop, calls=%fused_computation.3 | loop fusion | bytes 12582912 | tf_op jit(solution)/shard_map/squeeze | solution.py:87
  93.0 0.0 all-to-all-done.1.refs_6_
  93.0 0.0 copy-start.1
  93.0 1.0 copy-done.1
  94.0 0.0 copy-start.4
  94.0 1.0 copy-done.4
  95.1 0.0 copy-start.7
  95.1 1.0 copy-done.7
  96.1 4.2 %level2.1 = (f32[32,256]{1,0:T(8,128)S(1)}, bf16[32,32,256]{2,1,0:T(8,128)(2,1)S(1)}) custom-call(s32[1]{0:T(128)} %bitcast.refs_0_, s32[6,24]{1,0:T(8,128)S(1)} %bitcast.25, s32[6,1]{1,0:T(8,128)S(1)} %copy.12.refs_2_, bf16[4,256,256]{2,1,0:T(8,128)(2,1)S(1)} %copy-done.4, bf16[4,256,256]{2,1,0:T(8,128)(2,1)S(1)} %copy-done.7, ...), custom_call_target="tpu_custom_call" | custom-call | tf_op jit(solution)/shard_map/level2/pallas_call | solution.py:56
  100.3 0.0 copy-start.10
  100.4 0.8 copy-done.10
  101.2 10.2 %all-to-all-start.2 = ((bf16[32,32,256]{2,1,0:T(8,128)(2,1)}), bf16[32,32,256]{2,1,0:T(8,128)(2,1)}, u32[]{:S(2)}, u32[]{:S(2)}) async-start(bf16[32,32,256]{2,1,0:T(8,128)(2,1)} %copy-done.10), calls=%async_computation.2 | async-start | bytes 1048576 | tf_op jit(solution)/shard_map/all_to_all | solution.py:91
  111.3 35.2 %all-gather.9.cloned.1.call-done = bf16[3,24,256,256]{3,2,1,0:T(8,128)(2,1)} async-done(((bf16[3,3,256,256]{3,2,1,0:T(8,128)(2,1)}), bf16[3,24,256,256]{3,2,1,0:T(8,128)(2,1)}) %all-gather.9.cloned.1.call-update) | async-done | bytes 9437200 | tf_op jit(solution)/shard_map/all_gather | solution.py:83
  146.6 5.9 %slice_bitcast_fusion = (bf16[24,256,256]{2,1,0:T(8,128)(2,1)}, bf16[24,256,256]{2,1,0:T(8,128)(2,1)}, bf16[24,256,256]{2,1,0:T(8,128)(2,1)S(1)}) fusion(bf16[3,24,256,256]{3,2,1,0:T(8,128)(2,1)} %all-gather.9.cloned.1.call-done), kind=kLoop, calls=%fused_computation | loop fusion | bytes 18874368 | tf_op jit(solution)/shard_map/squeeze | solution.py:87
  152.4 0.0 all-to-all-done.2.refs_7_
  152.4 0.0 copy-start.2
  152.4 1.0 copy-done.2
  153.5 0.0 copy-start.5
  153.5 1.0 copy-done.5
  154.5 0.0 copy-start.8
  154.5 1.0 copy-done.8
  155.5 6.6 %level3.1 = (f32[32,256]{1,0:T(8,128)S(1)}, bf16[1,32,256]{2,1,0:T(8,128)(2,1)}) custom-call(s32[1]{0:T(128)} %bitcast.refs_0_, s32[6,24]{1,0:T(8,128)S(1)} %bitcast.26, s32[6,1]{1,0:T(8,128)S(1)} %copy.12.refs_2_, bf16[4,256,256]{2,1,0:T(8,128)(2,1)S(1)} %copy-done.5, bf16[4,256,256]{2,1,0:T(8,128)(2,1)S(1)} %copy-done.8, ...), custom_call_target="tpu_custom_call" | custom-call | tf_op jit(solution)/shard_map/level3/pallas_call | solution.py:56
  162.1 0.7 maximum_bitcast_fusion
Async XLA Ops:
  6.5 48.4 %all-gather.5.cloned.1.call-start = ((), (), s32[]{:S(2)}) async-start(), calls=%async_computation.3 | async-start | bytes 3538944 | tf_op jit(solution)/shard_map/all_gather | solution.py:83
  8.3 4.7 %copy-start.12 = (s32[6,1]{0,1:T(1,128)S(1)}, s32[6,1]{0,1:T(1,128)}, u32[]{:S(2)}) copy-start(s32[6,1]{0,1:T(1,128)} %param.9) | copy-start | bytes 76
  8.3 4.8 %copy-start.11 = (s32[6,1,3]{0,1,2:T(1,128)S(1)}, s32[6,1,3]{0,1,2:T(1,128)}, u32[]{:S(2)}) copy-start(s32[6,1,3]{0,1,2:T(1,128)} %param.8) | copy-start | bytes 220
  8.3 16.9 %copy-start.3 = (bf16[4,256,256]{2,1,0:T(8,128)(2,1)S(1)}, bf16[4,256,256]{2,1,0:T(8,128)(2,1)}, u32[]{:S(2)}) copy-start(bf16[4,256,256]{2,1,0:T(8,128)(2,1)} %refs_3_.7) | copy-start | bytes 1572868
  8.3 16.9 %copy-start.6 = (bf16[4,256,256]{2,1,0:T(8,128)(2,1)S(1)}, bf16[4,256,256]{2,1,0:T(8,128)(2,1)}, u32[]{:S(2)}) copy-start(bf16[4,256,256]{2,1,0:T(8,128)(2,1)} %refs_4_.7) | copy-start | bytes 1572868
  8.3 79.6 %all-gather.7.cloned.1.call-start = ((), (), s32[]{:S(2)}) async-start(), calls=%async_computation.4 | async-start | bytes 7077888 | tf_op jit(solution)/shard_map/all_gather | solution.py:83
  10.6 136.0 %all-gather.9.cloned.1.call-start = ((), (), s32[]{:S(2)}) async-start(), calls=%async_computation.5 | async-start | bytes 10616832 | tf_op jit(solution)/shard_map/all_gather | solution.py:83
  54.9 10.4 %copy-start = (bf16[32,32,256]{2,1,0:T(8,128)(2,1)}, bf16[32,32,256]{2,1,0:T(8,128)(2,1)S(1)}, u32[]{:S(2)}) copy-start(bf16[32,32,256]{2,1,0:T(8,128)(2,1)S(1)} %all_to_all.15.refs_5_) | copy-start | bytes 1572868
  54.9 2.3 %copy-start.9 = (bf16[1,24,256,256]{3,2,0,1:T(8,128)(2,1)S(1)}, bf16[1,24,256,256]{3,2,0,1:T(8,128)(2,1)}, u32[]{:S(2)}) copy-start(bf16[1,24,256,256]{3,2,0,1:T(8,128)(2,1)} %all-gather.5.cloned.1.call-done) | copy-start | bytes 9437188
  60.0 33.0 %all-to-all-start.1 = ((bf16[32,32,256]{2,1,0:T(8,128)(2,1)}), bf16[32,32,256]{2,1,0:T(8,128)(2,1)}, u32[]{:S(2)}, u32[]{:S(2)}) async-start(bf16[32,32,256]{2,1,0:T(8,128)(2,1)} %get-tuple-element.15), calls=%async_computation.1 | async-start | bytes 1048576 | tf_op jit(solution)/shard_map/all_to_all | solution.py:91
  93.0 1.0 copy-start.1
  94.0 1.0 copy-start.4
  95.1 1.0 copy-start.7
  100.3 0.8 copy-start.10
  101.2 51.3 %all-to-all-start.2 = ((bf16[32,32,256]{2,1,0:T(8,128)(2,1)}), bf16[32,32,256]{2,1,0:T(8,128)(2,1)}, u32[]{:S(2)}, u32[]{:S(2)}) async-start(bf16[32,32,256]{2,1,0:T(8,128)(2,1)} %copy-done.10), calls=%async_computation.2 | async-start | bytes 1048576 | tf_op jit(solution)/shard_map/all_to_all | solution.py:91
  152.4 1.0 copy-start.2
  153.5 1.0 copy-start.5
  154.5 1.0 copy-start.8
Sparse Core Ops, SparseCore 0:
  9.2 33.2 all-gather.4
  44.3 43.5 all-gather.6
  89.7 56.7 all-gather.8

commit v2 on v1

v2 whole, which is shorter than its diff:
```python
import functools

import jax
import jax.numpy as jnp
from jax import lax
from jax.experimental import pallas as pl
from jax.experimental.pallas import tpu as pltpu
from jax.sharding import PartitionSpec as P

NT_DIMS = (((1,), (1,)), ((), ()))
BLOCK = 32
SMEM = pl.BlockSpec(memory_space=pltpu.SMEM)
ANY = pl.BlockSpec(memory_space=pl.ANY)
CHIPS = 4
SAME = [(2 * y, 2 * ((y + 1) % CHIPS)) for y in range(CHIPS)] + [
    (2 * y + 1, 2 * ((y - 1) % CHIPS) + 1) for y in range(CHIPS)
]
CROSS = [(2 * y + 1, 2 * ((y + 1) % CHIPS)) for y in range(CHIPS)] + [
    (2 * y, 2 * ((y - 1) % CHIPS) + 1) for y in range(CHIPS)
]
FAR = [(p, (p + 4) % 8) for p in range(8)]
SWAP = [(p, p ^ 1) for p in range(8)]


def dot_nt(a, b):
    return lax.dot_general(a, b, NT_DIMS, preferred_element_type=jnp.float32)


def probe_rows(place, rhs):
    probe = lax.broadcasted_iota(jnp.int32, (BLOCK, rhs.shape[1]), 1)
    mine = lax.broadcasted_iota(jnp.int32, (BLOCK, rhs.shape[1]), 0) + place * BLOCK
    return dot_nt((probe == mine).astype(jnp.bfloat16), rhs)


def owners(place):
    chip, core = lax.div(place, 2), lax.rem(place, 2)
    out = []
    for c in (core, 1 - core):
        near = lax.rem(chip + 3 + 2 * c, CHIPS)
        far = lax.rem(chip + 2, CHIPS)
        out += [chip * 2 + c, near * 2 + c, near * 2 + 1 - c, far * 2 + c]
    return out


def spread_out(result, spread):
    rounded = result.astype(jnp.bfloat16)
    for copy in range(spread.shape[0]):
        spread[copy] = rounded


def first_kernel(cuts, place, rhs, dinv, tiles, answer, spread, *rest):
    parts, sems = rest[: len(cuts)], rest[len(cuts)]
    copies = [
        pltpu.make_async_copy(tiles.at[pl.ds(low, high - low)], part, sems.at[n])
        for n, ((low, high), part) in enumerate(zip(cuts, parts))
    ]
    for copy in copies:
        copy.start()
    residual = probe_rows(place[0], rhs[0]).astype(jnp.bfloat16)
    result = dot_nt(residual, dinv[0])
    answer[...] = result
    spread_out(result, spread)
    for copy in copies:
        copy.wait()


def first_call(rows, cuts, place, rhs, dinv, tiles):
    size = dinv.shape[2]
    pick = pl.BlockSpec((1, size, size), lambda i: (0, 0, 0))
    return pl.pallas_call(
        functools.partial(first_kernel, cuts),
        grid=(1,),
        out_shape=(
            jax.ShapeDtypeStruct((BLOCK, size), jnp.float32),
            jax.ShapeDtypeStruct((rows, BLOCK, size), jnp.bfloat16),
        )
        + tuple(jax.ShapeDtypeStruct((high - low,) + tiles.shape[1:], tiles.dtype) for low, high in cuts),
        in_specs=[SMEM, pick, pick, ANY],
        out_specs=(
            pl.BlockSpec((BLOCK, size), lambda i: (0, 0)),
            pl.BlockSpec((rows, BLOCK, size), lambda i: (0, 0, 0)),
        )
        + (ANY,) * len(cuts),
        scratch_shapes=[pltpu.SemaphoreType.DMA((len(cuts),))],
        name="level0",
    )(place, rhs, dinv, tiles)


def sum_kernel(pairs, flavours, begin, end, place, cols_here, cols_there, live, *refs):
    refs = list(refs)
    start = refs.pop(0)
    dinv = refs.pop(0) if end else None
    known = [refs.pop(0) for _ in pairs]
    tiles = [[refs.pop(0) for _ in range(1 if whole else 8)] for whole in flavours]
    total = probe_rows(place[0], start[0]) if begin else start[...]
    owner = owners(place[0])
    slots = cols_here.shape[2]
    update = jnp.zeros_like(total)
    for n, pair in enumerate(pairs):
        for piece in range(8):
            cols = cols_here if piece < 4 else cols_there
            for slot in range(slots):
                block = known[n][cols[piece % 4, pair, slot]]
                alive = owner[piece] * slots + slot < live[pair, 0]
                block = jnp.where(alive, block, jnp.zeros_like(block))
                if flavours[n]:
                    tile = tiles[n][0][0, owner[piece] * slots + slot]
                else:
                    tile = tiles[n][piece][0, slot]
                update = update + dot_nt(block, tile)
    total = total - update
    if not end:
        refs[0][...] = total
        return
    result = dot_nt(total.astype(jnp.bfloat16), dinv[0])
    refs[0][...] = result
    if len(refs) > 1:
        spread_out(result, refs[1])


def sum_call(name, level, pairs, begin, end, rows, scalars, start, dinv, known, tiles):
    size = dinv.shape[2]
    pick = pl.BlockSpec((1, size, size), lambda i: (level, 0, 0))
    flat = pl.BlockSpec((BLOCK, size), lambda i: (0, 0))
    cube = pl.BlockSpec((32, BLOCK, size), lambda i: (0, 0, 0))
    args = list(scalars) + [start]
    specs = [SMEM] * 4 + [pick if begin else flat]
    if end:
        args.append(dinv)
        specs.append(pick)
    for array in known:
        args.append(array)
        specs.append(cube)
    flavours = tuple(len(group) == 1 for group in tiles)
    for group in tiles:
        for array, index in group:
            args.append(array)
            specs.append(pl.BlockSpec((1,) + array.shape[1:], lambda i, n=index: (n, 0, 0, 0)))
    out_shape = [jax.ShapeDtypeStruct((BLOCK, size), jnp.float32)]
    out_specs = [flat]
    if end and rows:
        out_shape.append(jax.ShapeDtypeStruct((rows, BLOCK, size), jnp.bfloat16))
        out_specs.append(pl.BlockSpec((rows, BLOCK, size), lambda i: (0, 0, 0)))
    count = len(pairs)
    return pl.pallas_call(
        functools.partial(sum_kernel, tuple(pairs), flavours, begin, end),
        grid=(1,),
        out_shape=tuple(out_shape),
        in_specs=specs,
        out_specs=tuple(out_specs),
        cost_estimate=pl.CostEstimate(
            flops=2 * 24 * count * size * size * size, bytes_accessed=count * 24 * size * size * 2, transcendentals=0
        ),
        compiler_params=pltpu.CompilerParams(vmem_limit_bytes=40 * 1024 * 1024),
        name=name,
    )(*args)


def local(rhs, dinv, factor, cols, live):
    rows = lax.axis_size("row")
    place = lax.axis_index("col").astype(jnp.int32).reshape(1)
    tiles = factor.transpose(0, 2, 1, 3)
    move = lambda array, pairs: lax.ppermute(array, "col", pairs)

    answer0, spread0, part1, part2, part3 = first_call(rows, ((0, 1), (1, 3), (3, 6)), place, rhs, dinv, tiles)

    def ring(part, forward):
        same, cross = move(part, SAME), move(part, CROSS)
        far = move(same, SAME) if forward else move(part, FAR)
        return [same, cross, far]

    got1 = ring(part1, False)
    got2 = ring(part2, True)
    own = cols[:, 0, :]
    cols_here = jnp.stack([own, move(own, SAME), move(own, CROSS), move(own, FAR)])
    cols_there = move(cols_here, SWAP)
    swapped = move(tiles, SWAP)
    gathered3 = lax.all_gather(part3, "col", axis=1, tiled=True)

    there1 = [move(a, SWAP) for a in got1]
    there2 = [move(a, SWAP) for a in got2]

    def pieces(pair, index, part, got, there):
        return [(part, index)] + [(a, index) for a in got] + [(swapped, pair)] + [(a, index) for a in there]

    scalars = (place, cols_here, cols_there, live)
    known0 = lax.all_to_all(spread0, "row", 0, 0, tiled=True)
    answer1, spread1 = sum_call(
        "level1", 1, (0,), True, True, rows, scalars, rhs, dinv, [known0], [pieces(0, 0, part1, got1, there1)]
    )
    known1 = lax.all_to_all(spread1, "row", 0, 0, tiled=True)
    (early2,) = sum_call(
        "early2", 2, (1,), True, False, 0, scalars, rhs, dinv, [known0], [pieces(1, 0, part2, got2, there2)]
    )
    answer2, spread2 = sum_call(
        "level2", 2, (2,), False, True, rows, scalars, early2, dinv, [known1], [pieces(2, 1, part2, got2, there2)]
    )
    known2 = lax.all_to_all(spread2, "row", 0, 0, tiled=True)
    (early3,) = sum_call(
        "early3", 3, (3, 4), True, False, 0, scalars, rhs, dinv, [known0, known1], [[(gathered3, 0)], [(gathered3, 1)]]
    )
    (answer3,) = sum_call(
        "level3", 3, (5,), False, True, 0, scalars, early3, dinv, [known2], [[(gathered3, 2)]]
    )
    return jnp.stack([answer0, answer1, answer2, answer3]).transpose(0, 2, 1)


def solution(mesh):
    in_specs = (
        P(None, "row", None),
        P(None, "row", None),
        P(None, "row", "col", None),
        P(None, "row", "col"),
        P(None, "row"),
    )
    out_specs = P(None, "row", "col")
    return jax.shard_map(local, mesh=mesh, in_specs=in_specs, out_specs=out_specs, check_vma=False)
```

time: 171 us -> 237 us (1.39)
  Pallas kernels: 14.6 us -> 87.4 us
  blocking collectives: 40.7 us -> 0 us
  starting transfers between devices: 15.7 us -> 44.7 us
  waiting for transfers between devices: 57.8 us -> 67.2 us
  local copies, waits for them, and re-layouts: 26.8 us -> 22.6 us
    pallas_call x4 -> x6, Pallas kernels: 14.6 us -> 87.4 us  [the longest x1 74.4 us: first_call(): pl.pallas_call(functools.partial(first_kernel, cuts), grid=(1,), out_shap...]
    all_gather x3 -> x1, waiting for transfers between devices: 57.7 us -> 0.02 us  [local(): gathered3 = lax.all_gather(part3, 'col', axis=1, tiled=True)]
    ppermute x0 -> x17, waiting for transfers between devices: none -> 51.2 us  [local(): move = lambda array, pairs: lax.ppermute(array, 'col', pairs)]
    all_to_all x1 -> x0, blocking collectives: 28.7 us -> none  [local(): known.append(lax.all_to_all(spread, 'row', 0, 0, tiled=True))]
    all_to_all x2 -> x3, waiting for transfers between devices: 0.01 us -> 15.9 us  [the longest x1 9.49 us: local(): known2 = lax.all_to_all(spread2, 'row', 0, 0, tiled=True)]
    all_to_all x2 -> x3, starting transfers between devices: 15.6 us -> 31.5 us  [the longest x1 14.3 us: local(): known1 = lax.all_to_all(spread1, 'row', 0, 0, tiled=True)]
    ppermute x0 -> x17, starting transfers between devices: none -> 13.3 us  [local(): move = lambda array, pairs: lax.ppermute(array, 'col', pairs)]
    unnamed x27 -> x46, local copies, waits for them, and re-layouts: 9.47 us -> 22.2 us
  transfers between devices with their start and end apart: 5 -> 21, of which waited for: 2 -> 12; matrix products, arithmetic and copies ran while one was open for 9% -> 0% of each run, Pallas kernels for 5% -> 5%
where the time goes in v2:
time: 237 us; the launch traced here: 236 us
  Pallas kernels  87.4 us (37%)
  waiting for transfers between devices  67.2 us (28%)
  starting transfers between devices  44.7 us (19%)
  local copies, waits for them, and re-layouts  22.6 us (10%)
  between operations  13.6 us (6%)
    pallas_call x1, Pallas kernels, first_call(): pl.pallas_call(functools.partial(first_kernel, cuts), grid=(1,), out_shap...  74.4 us
    ppermute x17, waiting for transfers between devices, local(): move = lambda array, pairs: lax.ppermute(array, 'col', pairs)  51.2 us
    unnamed x46, local copies, waits for them, and re-layouts  22.2 us
    all_to_all x1, starting transfers between devices, local(): known1 = lax.all_to_all(spread1, 'row', 0, 0, tiled=True)  14.3 us
    ppermute x17, starting transfers between devices, local(): move = lambda array, pairs: lax.ppermute(array, 'col', pairs)  13.3 us
    pallas_call x5, Pallas kernels, sum_call(): pl.pallas_call(functools.partial(sum_kernel, tuple(pairs), flavours, begi...  13 us
    all_to_all x1, starting transfers between devices, local(): known0 = lax.all_to_all(spread0, 'row', 0, 0, tiled=True)  11.6 us
    all_to_all x1, waiting for transfers between devices, local(): known2 = lax.all_to_all(spread2, 'row', 0, 0, tiled=True)  9.49 us
  transfers between devices with their start and end apart: 21, of which 12 were waited for; matrix products, arithmetic and copies ran while one was open for 0% of the time, Pallas kernels for 5%

profile of v2, /device:TPU:2, one launch (start us, length us, event | category | flops | bytes accessed | tf_op | source)
XLA Modules:
  0.0 236.2 jit_solution(7667572187631914985)
XLA Ops:
  6.5 74.4 %level0.1 = (f32[32,256]{1,0:T(8,128)}, bf16[32,32,256]{2,1,0:T(8,128)(2,1)}, bf16[1,3,256,256]{3,2,1,0:T(8,128)(2,1)}, bf16[2,3,256,256]{3,2,1,0:T(8,128)(2,1)}, bf16[3,3,256,256]{3,2,1,0:T(8,128)(2,1)}) custom-call(s32[1]{0:T(128)} %bitcast.place, bf16[4,256,256]{2,1,0:T(8,128)(2,1)} %refs_0_.5, bf16[4,256,256]{2,1,0:T(8,128)(2,1)} %refs_1_.5, ...), custom_call_target="tpu_custom_call" | custom-call | tf_op jit(solution)/shard_map/level0/pallas_call | solution.py:70
  81.0 0.0 all-gather.2.cloned.1.call-update
  81.0 0.1 collective-permute-start.7
  81.1 1.7 collective-permute-start.11
  82.8 2.9 %collective-permute-start.6 = (bf16[1,3,256,256]{3,2,1,0:T(8,128)(2,1)}, bf16[1,3,256,256]{3,2,1,0:T(8,128)(2,1)}, u32[]{:S(2)}, u32[]{:S(2)}) collective-permute-start(bf16[1,3,256,256]{3,2,1,0:T(8,128)(2,1)} %get-tuple-element.16.refs_3_), channel_id=1, source_target_pairs={{0,4},{1,5},{2,6},{3,7},{4,0},{5,1},{6,2},{7,3},{8,12},{9,13},{10,... | collective-permute-start | bytes 1179656 | tf_op jit(solution)/shard_map/ppermute | solution.py:163
  85.7 11.6 %all-to-all-start = ((bf16[32,32,256]{2,1,0:T(8,128)(2,1)}), bf16[32,32,256]{2,1,0:T(8,128)(2,1)S(1)}, u32[]{:S(2)}, u32[]{:S(2)}) async-start(bf16[32,32,256]{2,1,0:T(8,128)(2,1)} %get-tuple-element.15), calls=%async_computation | async-start | bytes 1048576 | tf_op jit(solution)/shard_map/all_to_all | solution.py:187
  97.3 0.1 collective-permute-start.4
  97.4 0.6 collective-permute-start
  98.0 0.1 copy.29
  98.1 21.8 %collective-permute-done = s32[6,3]{0,1:T(4,128)S(1)} collective-permute-done((s32[6,3]{0,1:T(4,128)S(1)}, s32[6,3]{0,1:T(4,128)S(1)}, u32[]{:S(2)}, u32[]{:S(2)}) %collective-permute-start) | collective-permute-done | bytes 104 | tf_op jit(solution)/shard_map/ppermute | solution.py:163
  119.9 0.9 collective-permute-start.1
  120.8 0.1 copy.30
  120.9 3.2 %collective-permute-done.1 = s32[6,3]{0,1:T(4,128)S(1)} collective-permute-done((s32[6,3]{0,1:T(4,128)S(1)}, s32[6,3]{0,1:T(4,128)S(1)}, u32[]{:S(2)}, u32[]{:S(2)}) %collective-permute-start.1) | collective-permute-done | bytes 104 | tf_op jit(solution)/shard_map/ppermute | solution.py:163
  124.1 1.3 collective-permute-start.2
  125.4 0.1 copy.31
  125.5 3.7 %collective-permute-done.2 = s32[6,3]{0,1:T(4,128)S(1)} collective-permute-done((s32[6,3]{0,1:T(4,128)S(1)}, s32[6,3]{0,1:T(4,128)S(1)}, u32[]{:S(2)}, u32[]{:S(2)}) %collective-permute-start.2) | collective-permute-done | bytes 104 | tf_op jit(solution)/shard_map/ppermute | solution.py:163
  129.2 0.1 copy.32
  129.3 0.0 collective-permute-start.3
  129.4 1.2 collective-permute-done.3.cols_there
  130.5 2.2 collective-permute-start.5
  132.7 0.0 collective-permute-done.6.refs_6_
  132.8 0.8 collective-permute-start.12
  133.6 0.0 collective-permute-done.11.refs_3_.refs_4_
  133.6 1.3 collective-permute-start.13
  134.9 15.8 %collective-permute-done.5.refs_5_ = bf16[1,3,256,256]{3,2,1,0:T(8,128)(2,1)} collective-permute-done((bf16[1,3,256,256]{3,2,1,0:T(8,128)(2,1)}, bf16[1,3,256,256]{3,2,1,0:T(8,128)(2,1)}, u32[]{:S(2)}, u32[]{:S(2)}) %collective-permute-start.5) | collective-permute-done | bytes 393248 | tf_op jit(solution)/shard_map/ppermute | solution.py:163
  150.7 0.7 copy-done.17
  151.4 0.5 collective-permute-start.9
  151.9 0.1 copy.33.live
  152.0 0.9 collective-permute-done.8.refs_8_
  152.9 0.7 collective-permute-done.9.refs_9_
  153.6 0.0 copy-start.3
  153.6 1.0 copy-done.3
  154.7 1.0 copy-done.16
  155.7 1.0 copy-done.18
  156.7 2.7 %level1.1 = (f32[32,256]{1,0:T(8,128)S(1)}, bf16[32,32,256]{2,1,0:T(8,128)(2,1)S(1)}) custom-call(s32[1]{0:T(128)} %bitcast.place, s32[4,6,3]{2,1,0:T(8,128)S(1)} %pad_add_fusion.cols_here, s32[4,6,3]{2,1,0:T(8,128)S(1)} %collective-permute-done.3.cols_there, s32[6,1]{1,0:T(8,128)S(1)} %copy.33.live, bf16[4,256,256]{2,1,0:T(8,128)(2,1)S(1)} %copy-done.2, ...), custom_call_target="tpu_custom_call" | custom-call | flops 805306368 | bytes 3145728 | tf_op jit(solution)/shard_map/level1/pallas_call | solution.py:145
  159.4 0.8 copy-done.14
  160.2 14.3 %all-to-all-start.1 = ((bf16[32,32,256]{2,1,0:T(8,128)(2,1)}), bf16[32,32,256]{2,1,0:T(8,128)(2,1)}, u32[]{:S(2)}, u32[]{:S(2)}) async-start(bf16[32,32,256]{2,1,0:T(8,128)(2,1)} %copy-done.14), calls=%async_computation.1 | async-start | bytes 1048576 | tf_op jit(solution)/shard_map/all_to_all | solution.py:191
  174.5 0.1 collective-permute-start.14
  174.6 0.5 collective-permute-start.15
  175.1 0.3 collective-permute-start.16
  175.4 1.7 collective-permute-done.14.refs_7_.refs_8_
  177.1 1.1 collective-permute-done.15.refs_8_.refs_9_
  178.2 1.1 collective-permute-done.16.refs_9_.refs_10_
  179.3 1.1 copy-done.6
  180.5 2.3 early2.1.refs_0_
  182.8 0.9 copy-done.8
  183.7 0.9 copy-done.10
  184.6 0.9 copy-done.12
  185.5 6.4 %all-to-all-done.1.refs_2_ = bf16[32,32,256]{2,1,0:T(8,128)(2,1)} async-done(((bf16[32,32,256]{2,1,0:T(8,128)(2,1)}), bf16[32,32,256]{2,1,0:T(8,128)(2,1)}, u32[]{:S(2)}, u32[]{:S(2)}) %all-to-all-start.1) | async-done | bytes 524320 | tf_op jit(solution)/shard_map/all_to_all | solution.py:191
  191.9 1.0 copy-done.4
  193.0 1.1 copy-done.7
  194.1 1.1 copy-done.9
  195.2 1.1 copy-done.11
  196.4 1.1 copy-done.13
  197.5 2.7 %level2.1 = (f32[32,256]{1,0:T(8,128)S(1)}, bf16[32,32,256]{2,1,0:T(8,128)(2,1)S(1)}) custom-call(s32[1]{0:T(128)} %bitcast.place, s32[4,6,3]{2,1,0:T(8,128)S(1)} %pad_add_fusion.cols_here, s32[4,6,3]{2,1,0:T(8,128)S(1)} %collective-permute-done.3.cols_there, s32[6,1]{1,0:T(8,128)S(1)} %copy.33.live, f32[32,256]{1,0:T(8,128)S(1)} %early2.1.refs_0_, ...), custom_call_target="tpu_custom_call" | custom-call | flops 805306368 | bytes 3145728 | tf_op jit(solution)/shard_map/level2/pallas_call | solution.py:145
  200.2 0.8 copy-done.15
  200.9 5.6 %all-to-all-start.2 = ((bf16[32,32,256]{2,1,0:T(8,128)(2,1)}), bf16[32,32,256]{2,1,0:T(8,128)(2,1)S(1)}, u32[]{:S(2)}, u32[]{:S(2)}) async-start(bf16[32,32,256]{2,1,0:T(8,128)(2,1)} %copy-done.15), calls=%async_computation.2 | async-start | bytes 1048576 | tf_op jit(solution)/shard_map/all_to_all | solution.py:198
  206.5 0.0 all-gather.2.cloned.1.call-done.refs_3_.refs_4_
  206.6 3.7 %copy-done = bf16[3,24,256,256]{3,2,1,0:T(8,128)(2,1)S(1)} copy-done((bf16[3,24,256,256]{3,2,1,0:T(8,128)(2,1)S(1)}, bf16[3,24,256,256]{3,2,1,0:T(8,128)(2,1)}, u32[]{:S(2)}) %copy-start) | copy-done | bytes 9437208
  210.2 3.0 %early3.1.refs_0_ = f32[32,256]{1,0:T(8,128)S(1)} custom-call(s32[1]{0:T(128)} %bitcast.place, s32[4,6,3]{2,1,0:T(8,128)S(1)} %pad_add_fusion.cols_here, s32[4,6,3]{2,1,0:T(8,128)S(1)} %collective-permute-done.3.cols_there, s32[6,1]{1,0:T(8,128)S(1)} %copy.33.live, bf16[4,256,256]{2,1,0:T(8,128)(2,1)S(1)} %copy-done.2, ...), custom_call_target="tpu_custom_call" | custom-call | flops 1610612736 | bytes 6291456 | tf_op jit(solution)/shard_map/early3/pallas_call | solution.py:145
  213.2 9.5 %all-to-all-done.2.refs_2_ = bf16[32,32,256]{2,1,0:T(8,128)(2,1)S(1)} async-done(((bf16[32,32,256]{2,1,0:T(8,128)(2,1)}), bf16[32,32,256]{2,1,0:T(8,128)(2,1)S(1)}, u32[]{:S(2)}, u32[]{:S(2)}) %all-to-all-start.2) | async-done | bytes 524320 | tf_op jit(solution)/shard_map/all_to_all | solution.py:198
  222.7 3.7 %copy-done.1 = bf16[3,24,256,256]{3,2,1,0:T(8,128)(2,1)S(1)} copy-done((bf16[3,24,256,256]{3,2,1,0:T(8,128)(2,1)S(1)}, bf16[3,24,256,256]{3,2,1,0:T(8,128)(2,1)}, u32[]{:S(2)}) %copy-start.1) | copy-done | bytes 9437208
  226.4 2.3 level3.1
  228.7 0.7 maximum_bitcast_fusion
  (37 shorter events, 0.1 us)
Async XLA Ops:
  6.5 200.0 %all-gather.2.cloned.1.call-start = ((), (), s32[]{:S(2)}) async-start(), calls=%async_computation.3 | async-start | bytes 10616832 | tf_op jit(solution)/shard_map/all_gather | solution.py:178
  6.5 90.9 %copy-start.20 = (s32[6,1,3]{0,1,2:T(1,128)S(1)}, s32[6,1,3]{0,1,2:T(1,128)}, u32[]{:S(2)}) copy-start(s32[6,1,3]{0,1,2:T(1,128)} %param.8) | copy-start | bytes 220
  6.5 145.4 %copy-start.21 = (s32[6,1]{0,1:T(1,128)S(1)}, s32[6,1]{0,1:T(1,128)}, u32[]{:S(2)}) copy-start(s32[6,1]{0,1:T(1,128)} %param.9) | copy-start | bytes 76
  6.5 147.1 %copy-start.2 = (bf16[4,256,256]{2,1,0:T(8,128)(2,1)S(1)}, bf16[4,256,256]{2,1,0:T(8,128)(2,1)}, u32[]{:S(2)}) copy-start(bf16[4,256,256]{2,1,0:T(8,128)(2,1)} %refs_0_.5) | copy-start | bytes 1572868
  81.0 72.6 %collective-permute-start.7 = (bf16[6,3,256,256]{3,2,1,0:T(8,128)(2,1)}, bf16[6,3,256,256]{3,2,1,0:T(8,128)(2,1)S(1)}, u32[]{:S(2)}, u32[]{:S(2)}) collective-permute-start(bf16[6,3,256,256]{3,2,1,0:T(8,128)(2,1)} %bitcast.19), channel_id=1, source_target_pairs={{0,1},{1,0},{2,3},{3,2},{4,5},{5,4},{6,7},{7,6},{8,9},{9,8},{10,11... | collective-permute-start | bytes 7077896 | tf_op jit(solution)/shard_map/ppermute | solution.py:163
  81.1 52.5 %collective-permute-start.11 = (bf16[2,3,256,256]{3,2,1,0:T(8,128)(2,1)}, bf16[2,3,256,256]{3,2,1,0:T(8,128)(2,1)}, u32[]{:S(2)}, u32[]{:S(2)}) collective-permute-start(bf16[2,3,256,256]{3,2,1,0:T(8,128)(2,1)} %get-tuple-element.18.refs_2_.refs_3_), channel_id=1, source_target_pairs={{0,2},{2,4},{4,6},{6,0},{1,7},{3,1},{5,3},{7,5},{8,10},{10,12},{12... | collective-permute-start | bytes 2359304 | tf_op jit(solution)/shard_map/ppermute | solution.py:163
  82.8 50.0 %collective-permute-start.6 = (bf16[1,3,256,256]{3,2,1,0:T(8,128)(2,1)}, bf16[1,3,256,256]{3,2,1,0:T(8,128)(2,1)}, u32[]{:S(2)}, u32[]{:S(2)}) collective-permute-start(bf16[1,3,256,256]{3,2,1,0:T(8,128)(2,1)} %get-tuple-element.16.refs_3_), channel_id=1, source_target_pairs={{0,4},{1,5},{2,6},{3,7},{4,0},{5,1},{6,2},{7,3},{8,12},{9,13},{10,... | collective-permute-start | bytes 1179656 | tf_op jit(solution)/shard_map/ppermute | solution.py:163
  85.7 67.9 %all-to-all-start = ((bf16[32,32,256]{2,1,0:T(8,128)(2,1)}), bf16[32,32,256]{2,1,0:T(8,128)(2,1)S(1)}, u32[]{:S(2)}, u32[]{:S(2)}) async-start(bf16[32,32,256]{2,1,0:T(8,128)(2,1)} %get-tuple-element.15), calls=%async_computation | async-start | bytes 1048576 | tf_op jit(solution)/shard_map/all_to_all | solution.py:187
  97.3 35.5 %collective-permute-start.4 = (bf16[1,3,256,256]{3,2,1,0:T(8,128)(2,1)}, bf16[1,3,256,256]{3,2,1,0:T(8,128)(2,1)}, u32[]{:S(2)}, u32[]{:S(2)}) collective-permute-start(bf16[1,3,256,256]{3,2,1,0:T(8,128)(2,1)} %get-tuple-element.16.refs_3_), channel_id=1, source_target_pairs={{0,2},{2,4},{4,6},{6,0},{1,7},{3,1},{5,3},{7,5},{8,10},{10,12},{12... | collective-permute-start | bytes 1179656 | tf_op jit(solution)/shard_map/ppermute | solution.py:163
  97.4 22.5 %collective-permute-start = (s32[6,3]{0,1:T(4,128)S(1)}, s32[6,3]{0,1:T(4,128)S(1)}, u32[]{:S(2)}, u32[]{:S(2)}) collective-permute-start(s32[6,3]{0,1:T(4,128)S(1)} %bitcast.25), channel_id=1, source_target_pairs={{0,2},{2,4},{4,6},{6,0},{1,7},{3,1},{5,3},{7,5},{8,10},{10,12},{12... | collective-permute-start | bytes 224 | tf_op jit(solution)/shard_map/ppermute | solution.py:163
  119.9 4.2 %collective-permute-start.1 = (s32[6,3]{0,1:T(4,128)S(1)}, s32[6,3]{0,1:T(4,128)S(1)}, u32[]{:S(2)}, u32[]{:S(2)}) collective-permute-start(s32[6,3]{0,1:T(4,128)S(1)} %bitcast.26), channel_id=1, source_target_pairs={{1,2},{3,4},{5,6},{7,0},{0,7},{2,1},{4,3},{6,5},{9,10},{11,12},{13... | collective-permute-start | bytes 224 | tf_op jit(solution)/shard_map/ppermute | solution.py:163
  124.1 5.1 %collective-permute-start.2 = (s32[6,3]{0,1:T(4,128)S(1)}, s32[6,3]{0,1:T(4,128)S(1)}, u32[]{:S(2)}, u32[]{:S(2)}) collective-permute-start(s32[6,3]{0,1:T(4,128)S(1)} %bitcast.27), channel_id=1, source_target_pairs={{0,4},{1,5},{2,6},{3,7},{4,0},{5,1},{6,2},{7,3},{8,12},{9,13},{10,... | collective-permute-start | bytes 224 | tf_op jit(solution)/shard_map/ppermute | solution.py:163
  129.3 1.2 collective-permute-start.3
  130.5 20.1 %collective-permute-start.5 = (bf16[1,3,256,256]{3,2,1,0:T(8,128)(2,1)}, bf16[1,3,256,256]{3,2,1,0:T(8,128)(2,1)}, u32[]{:S(2)}, u32[]{:S(2)}) collective-permute-start(bf16[1,3,256,256]{3,2,1,0:T(8,128)(2,1)} %get-tuple-element.16.refs_3_), channel_id=1, source_target_pairs={{1,2},{3,4},{5,6},{7,0},{0,7},{2,1},{4,3},{6,5},{9,10},{11,12},{13... | collective-permute-start | bytes 1179656 | tf_op jit(solution)/shard_map/ppermute | solution.py:163
  132.8 17.9 %collective-permute-start.10 = (bf16[1,3,256,256]{3,2,1,0:T(8,128)(2,1)}, bf16[1,3,256,256]{3,2,1,0:T(8,128)(2,1)S(1)}, u32[]{:S(2)}, u32[]{:S(2)}) collective-permute-start(bf16[1,3,256,256]{3,2,1,0:T(8,128)(2,1)} %collective-permute-done.6.refs_6_), channel_id=1, source_target_pairs={{0,1},{1,0},{2,3},{3,2},{4,5},{5,4},{6,7},{7,6},{8,9},{9,8},{10,11... | collective-permute-start | bytes 1179656 | tf_op jit(solution)/shard_map/ppermute | solution.py:163
  132.8 41.8 %collective-permute-start.12 = (bf16[2,3,256,256]{3,2,1,0:T(8,128)(2,1)}, bf16[2,3,256,256]{3,2,1,0:T(8,128)(2,1)}, u32[]{:S(2)}, u32[]{:S(2)}) collective-permute-start(bf16[2,3,256,256]{3,2,1,0:T(8,128)(2,1)} %get-tuple-element.18.refs_2_.refs_3_), channel_id=1, source_target_pairs={{1,2},{3,4},{5,6},{7,0},{0,7},{2,1},{4,3},{6,5},{9,10},{11,12},{13... | collective-permute-start | bytes 2359304 | tf_op jit(solution)/shard_map/ppermute | solution.py:163
  133.6 41.5 %collective-permute-start.13 = (bf16[2,3,256,256]{3,2,1,0:T(8,128)(2,1)}, bf16[2,3,256,256]{3,2,1,0:T(8,128)(2,1)}, u32[]{:S(2)}, u32[]{:S(2)}) collective-permute-start(bf16[2,3,256,256]{3,2,1,0:T(8,128)(2,1)} %collective-permute-done.11.refs_3_.refs_4_), channel_id=1, source_target_pairs={{0,2},{2,4},{4,6},{6,0},{1,7},{3,1},{5,3},{7,5},{8,10},{10,12},{12... | collective-permute-start | bytes 2359304 | tf_op jit(solution)/shard_map/ppermute | solution.py:163
  150.7 2.3 collective-permute-start.8
  150.7 0.7 copy-start.17
  151.4 2.2 collective-permute-start.9
  153.6 1.0 copy-start.3
  154.7 1.0 copy-start.16
  155.7 1.0 copy-start.18
  159.4 0.8 copy-start.14
  160.2 31.7 %all-to-all-start.1 = ((bf16[32,32,256]{2,1,0:T(8,128)(2,1)}), bf16[32,32,256]{2,1,0:T(8,128)(2,1)}, u32[]{:S(2)}, u32[]{:S(2)}) async-start(bf16[32,32,256]{2,1,0:T(8,128)(2,1)} %copy-done.14), calls=%async_computation.1 | async-start | bytes 1048576 | tf_op jit(solution)/shard_map/all_to_all | solution.py:191
  174.5 2.6 %collective-permute-start.14 = (bf16[2,3,256,256]{3,2,1,0:T(8,128)(2,1)}, bf16[2,3,256,256]{3,2,1,0:T(8,128)(2,1)S(1)}, u32[]{:S(2)}, u32[]{:S(2)}) collective-permute-start(bf16[2,3,256,256]{3,2,1,0:T(8,128)(2,1)} %collective-permute-done.11.refs_3_.refs_4_), channel_id=1, source_target_pairs={{0,1},{1,0},{2,3},{3,2},{4,5},{5,4},{6,7},{7,6},{8,9},{9,8},{10,11... | collective-permute-start | bytes 2359304 | tf_op jit(solution)/shard_map/ppermute | solution.py:163
  174.6 3.6 %collective-permute-start.15 = (bf16[2,3,256,256]{3,2,1,0:T(8,128)(2,1)}, bf16[2,3,256,256]{3,2,1,0:T(8,128)(2,1)S(1)}, u32[]{:S(2)}, u32[]{:S(2)}) collective-permute-start(bf16[2,3,256,256]{3,2,1,0:T(8,128)(2,1)} %collective-permute-done.12.refs_4_.refs_5_), channel_id=1, source_target_pairs={{0,1},{1,0},{2,3},{3,2},{4,5},{5,4},{6,7},{7,6},{8,9},{9,8},{10,11... | collective-permute-start | bytes 2359304 | tf_op jit(solution)/shard_map/ppermute | solution.py:163
  175.1 4.2 %collective-permute-start.16 = (bf16[2,3,256,256]{3,2,1,0:T(8,128)(2,1)}, bf16[2,3,256,256]{3,2,1,0:T(8,128)(2,1)S(1)}, u32[]{:S(2)}, u32[]{:S(2)}) collective-permute-start(bf16[2,3,256,256]{3,2,1,0:T(8,128)(2,1)} %collective-permute-done.13.refs_5_.refs_6_), channel_id=1, source_target_pairs={{0,1},{1,0},{2,3},{3,2},{4,5},{5,4},{6,7},{7,6},{8,9},{9,8},{10,11... | collective-permute-start | bytes 2359304 | tf_op jit(solution)/shard_map/ppermute | solution.py:163
  179.3 1.1 copy-start.6
  182.8 0.9 copy-start.8
  183.7 0.9 copy-start.10
  184.6 0.9 copy-start.12
  191.9 1.0 copy-start.4
  192.9 1.1 copy-start.7
  194.1 1.1 copy-start.9
  195.2 1.1 copy-start.11
  196.3 1.1 copy-start.13
  200.1 0.8 copy-start.15
  200.9 21.8 %all-to-all-start.2 = ((bf16[32,32,256]{2,1,0:T(8,128)(2,1)}), bf16[32,32,256]{2,1,0:T(8,128)(2,1)S(1)}, u32[]{:S(2)}, u32[]{:S(2)}) async-start(bf16[32,32,256]{2,1,0:T(8,128)(2,1)} %copy-done.15), calls=%async_computation.2 | async-start | bytes 1048576 | tf_op jit(solution)/shard_map/all_to_all | solution.py:198
  206.5 3.7 %copy-start = (bf16[3,24,256,256]{3,2,1,0:T(8,128)(2,1)S(1)}, bf16[3,24,256,256]{3,2,1,0:T(8,128)(2,1)}, u32[]{:S(2)}) copy-start(bf16[3,24,256,256]{3,2,1,0:T(8,128)(2,1)} %all-gather.2.cloned.1.call-done.refs_3_.refs_4_) | copy-start | bytes 28311556
  210.2 12.5 %copy-start.5 = (bf16[4,256,256]{2,1,0:T(8,128)(2,1)S(1)}, bf16[4,256,256]{2,1,0:T(8,128)(2,1)}, u32[]{:S(2)}) copy-start(bf16[4,256,256]{2,1,0:T(8,128)(2,1)} %refs_1_.5) | copy-start | bytes 1572868
  222.7 3.7 %copy-start.1 = (bf16[3,24,256,256]{3,2,1,0:T(8,128)(2,1)S(1)}, bf16[3,24,256,256]{3,2,1,0:T(8,128)(2,1)}, u32[]{:S(2)}) copy-start(bf16[3,24,256,256]{3,2,1,0:T(8,128)(2,1)} %all-gather.2.cloned.1.call-done.refs_3_.refs_4_) | copy-start | bytes 28311556
  226.4 2.3 copy-start.19
Sparse Core Ops, SparseCore 0:
  81.1 77.5 all-gather.1

commit v3 on v0

v3 whole, which is shorter than its diff:
```python
import functools

import jax
import jax.numpy as jnp
from jax import lax
from jax.experimental import pallas as pl
from jax.experimental.pallas import tpu as pltpu
from jax.sharding import PartitionSpec as P

NT_DIMS = (((1,), (1,)), ((), ()))
BLOCK = 32
SIZE = 256
SLOTS = 3
PLACES = 8
CHIPS = 4
PAIRS = 6
NT = 32
EXTRA = 16
CHUNK = SLOTS * SIZE + EXTRA
VMEM_BYTES = 56 * 1024 * 1024
SMEM = pl.BlockSpec(memory_space=pltpu.SMEM)
ANY = pl.BlockSpec(memory_space=pl.ANY)
F32, BF16 = jnp.float32, jnp.bfloat16
SAME = [(2 * y, 2 * ((y + 1) % CHIPS)) for y in range(CHIPS)] + [
    (2 * y + 1, 2 * ((y - 1) % CHIPS) + 1) for y in range(CHIPS)
]
CROSS = [(2 * y + 1, 2 * ((y + 1) % CHIPS)) for y in range(CHIPS)] + [
    (2 * y, 2 * ((y - 1) % CHIPS) + 1) for y in range(CHIPS)
]
FAR = [(p, (p + 4) % 8) for p in range(8)]
SWAP = [(p, p ^ 1) for p in range(8)]
TURN = [[(p, (p + 2 * d) % 8) for p in range(8)] for d in range(CHIPS)]


def dot_nt(a, b):
    return lax.dot_general(a, b, NT_DIMS, preferred_element_type=F32)


def block_of(shape, *lead):
    return pl.BlockSpec(shape, lambda i: tuple(lead) + (0,) * (len(shape) - len(lead)))


def probe_rows(place, rhs):
    probe = lax.broadcasted_iota(jnp.int32, (BLOCK, rhs.shape[1]), 1)
    mine = lax.broadcasted_iota(jnp.int32, (BLOCK, rhs.shape[1]), 0) + place * BLOCK
    return dot_nt((probe == mine).astype(BF16), rhs)


def owners(place):
    chip, core = lax.div(place, 2), lax.rem(place, 2)
    out = []
    for c in (core, 1 - core):
        near = lax.rem(chip + 3 + 2 * c, CHIPS)
        far = lax.rem(chip + 2, CHIPS)
        out += [chip * 2 + c, near * 2 + c, near * 2 + 1 - c, far * 2 + c]
    return out


def spread_out(result, spread):
    rounded = result.astype(BF16)
    for copy in range(spread.shape[0]):
        spread[copy] = rounded


def call(kernel, name, shapes, in_specs, out_specs, args, scratch=(), flops=0, moved=0):
    return pl.pallas_call(
        kernel,
        grid=(1,),
        out_shape=tuple(jax.ShapeDtypeStruct(s, t) for s, t in shapes),
        in_specs=in_specs,
        out_specs=tuple(out_specs),
        scratch_shapes=list(scratch),
        cost_estimate=pl.CostEstimate(flops=flops, bytes_accessed=moved, transcendentals=0),
        compiler_params=pltpu.CompilerParams(vmem_limit_bytes=VMEM_BYTES),
        name=name,
    )(*args)


def first_kernel(place, cols, rhs, dinv, tiles, answer, spread, chunk):
    residual = probe_rows(place[0], rhs[0]).astype(BF16)
    result = dot_nt(residual, dinv[0])
    answer[...] = result
    spread_out(result, spread)
    for slot in range(SLOTS):
        chunk[slot * SIZE : (slot + 1) * SIZE] = tiles[0, slot]
    lane = lax.broadcasted_iota(jnp.int32, (EXTRA, SIZE), 1)
    packed = jnp.zeros((EXTRA, SIZE), jnp.int32)
    for pair in range(PAIRS):
        for slot in range(SLOTS):
            packed = jnp.where(lane == pair * SLOTS + slot, cols[pair, slot], packed)
    chunk[SLOTS * SIZE :] = packed.astype(F32).astype(BF16)


def first_call(place, cols, rhs, dinv, tiles):
    return call(
        first_kernel,
        "level0",
        [((BLOCK, SIZE), F32), ((NT, BLOCK, SIZE), BF16), ((CHUNK, SIZE), BF16)],
        [SMEM, SMEM, block_of((1, SIZE, SIZE), 0), block_of((1, SIZE, SIZE), 0), block_of((1, SLOTS, SIZE, SIZE), 0)],
        [block_of((BLOCK, SIZE)), block_of((NT, BLOCK, SIZE)), block_of((CHUNK, SIZE))],
        (place, cols, rhs, dinv, tiles),
        moved=2**21,
    )


def decode_kernel(*refs):
    for piece in range(PLACES):
        refs[PLACES][pl.ds(piece, 1), :] = refs[piece][0:1, :].astype(F32).astype(jnp.int32)


def decode_call(chunks):
    spec = pl.BlockSpec((EXTRA, SIZE), lambda i: (SLOTS * SIZE // EXTRA, 0))
    return call(
        decode_kernel,
        "cols",
        [((PLACES, SIZE), jnp.int32)],
        [spec] * PLACES,
        [block_of((PLACES, SIZE))],
        chunks,
    )[0]


def masked(block, alive):
    return jnp.where(alive, block, jnp.zeros_like(block))


def level1_kernel(place, table, live, rhs, dinv, known, *refs):
    chunks, (answer, spread, held, sems) = refs[:PLACES], refs[PLACES:]
    copies = [pltpu.make_async_copy(chunks[n].at[pl.ds(0, SLOTS * SIZE)], held.at[n], sems.at[n]) for n in range(PLACES)]
    for copy in copies:
        copy.start()
    total = probe_rows(place[0], rhs[0])
    owner = owners(place[0])
    for piece in range(PLACES):
        copies[piece].wait()
        for slot in range(SLOTS):
            block = masked(known[table[piece, slot]], owner[piece] * SLOTS + slot < live[0, 0])
            total = total - dot_nt(block, held[piece, slot * SIZE : (slot + 1) * SIZE])
    result = dot_nt(total.astype(BF16), dinv[0])
    answer[...] = result
    spread_out(result, spread)


def level1_call(place, table, live, rhs, dinv, known, chunks):
    pick = block_of((1, SIZE, SIZE), 1)
    return call(
        level1_kernel,
        "level1",
        [((BLOCK, SIZE), F32), ((NT, BLOCK, SIZE), BF16)],
        [SMEM] * 3 + [pick, pick, block_of((NT, BLOCK, SIZE))] + [ANY] * PLACES,
        [block_of((BLOCK, SIZE)), block_of((NT, BLOCK, SIZE))],
        (place, table, live, rhs, dinv, known, *chunks),
        [pltpu.VMEM((PLACES, SLOTS * SIZE, SIZE), BF16), pltpu.SemaphoreType.DMA((PLACES,))],
        flops=2 * 24 * BLOCK * SIZE * SIZE,
        moved=24 * SIZE * SIZE * 2,
    )


def pick_kernel(pairs, place, table, known, *outs):
    owner = owners(place[0])
    chip = lax.div(place[0], 2)
    for step in range(CHIPS):
        for core in range(2):
            want = lax.rem(chip + step, CHIPS) * 2 + core
            piece = jnp.int32(0)
            for n in range(PLACES):
                piece = jnp.where(owner[n] == want, n, piece)
            for n, pair in enumerate(pairs):
                for slot in range(SLOTS):
                    outs[step][n, core * SLOTS + slot] = known[table[piece, pair * SLOTS + slot]]


def pick_call(pairs, place, table, known):
    shape = (len(pairs), 2 * SLOTS, BLOCK, SIZE)
    return call(
        functools.partial(pick_kernel, pairs),
        "pick",
        [(shape, BF16)] * CHIPS,
        [SMEM, SMEM, block_of((NT, BLOCK, SIZE))],
        [block_of(shape)] * CHIPS,
        (place, table, known),
        moved=2**21,
    )


def partial_kernel(pairs, place, live, *refs):
    got, mine, theirs, outs = refs[:CHIPS], refs[CHIPS :: 2], refs[CHIPS + 1 :: 2], refs[-CHIPS:]
    chip, core = lax.div(place[0], 2), lax.rem(place[0], 2)
    for n, pair in enumerate(pairs):
        total = jnp.zeros((CHIPS * BLOCK, SIZE), F32)
        for swapped in range(2):
            side = lax.rem(core + swapped, 2)
            for slot in range(SLOTS):
                at = side * SLOTS + slot
                block = jnp.concatenate([g[n, at] for g in got])
                block = masked(block, chip * 2 * SLOTS + at < live[pair, 0])
                total = total + dot_nt(block, (theirs if swapped else mine)[n][0, slot])
        for step in range(CHIPS):
            outs[step][n] = total[step * BLOCK : (step + 1) * BLOCK]


def partial_call(pairs, place, live, got, tiles, swapped):
    shape = (len(pairs), BLOCK, SIZE)
    args, specs = [place, live, *got], [SMEM, SMEM] + [block_of(g.shape) for g in got]
    for pair in pairs:
        args += [tiles, swapped]
        specs += [block_of((1, SLOTS, SIZE, SIZE), pair)] * 2
    return call(
        functools.partial(partial_kernel, pairs),
        "partial",
        [(shape, F32)] * CHIPS,
        specs,
        [block_of(shape)] * CHIPS,
        args,
        flops=2 * 6 * SIZE**3,
        moved=2**21,
    )


def whole_kernel(index, pair, begin, part, finish, place, table, live, start, known, tiles, *refs):
    refs = list(refs)
    back = [refs.pop(0) for _ in range(CHIPS)] if part is not None else []
    dinv = refs.pop(0) if finish else None
    earlier = [refs.pop(0) for _ in range(3)] if finish == "last" else []
    held, sems = refs[-2:]
    owner = owners(place[0])
    copies = [
        pltpu.make_async_copy(tiles.at[index, pl.ds(owner[n] * SLOTS, SLOTS)], held.at[n], sems.at[n])
        for n in range(PLACES)
    ]
    for copy in copies:
        copy.start()
    total = probe_rows(place[0], start[0]) if begin else start[...]
    for sums in back:
        total = total - sums[part]
    for piece in range(PLACES):
        copies[piece].wait()
        for slot in range(SLOTS):
            block = masked(known[table[piece, pair * SLOTS + slot]], owner[piece] * SLOTS + slot < live[pair, 0])
            total = total - dot_nt(block, held[piece, slot])
    if not finish:
        refs[0][...] = total
        return
    result = dot_nt(total.astype(BF16), dinv[0])
    if finish == "last":
        for n in range(3):
            refs[0][n] = earlier[n][...]
        refs[0][3] = result
        return
    refs[0][...] = result
    spread_out(result, refs[1])


def whole_call(name, level, index, pair, begin, finish, place, table, live, start, known, tiles, part, back, dinv, earlier):
    flat, pick = block_of((BLOCK, SIZE)), block_of((1, SIZE, SIZE), level)
    args = [place, table, live, start, known, tiles]
    specs = [SMEM] * 3 + [pick if begin else flat, block_of((NT, BLOCK, SIZE)), ANY]
    if part is not None:
        args += back
        specs += [block_of(b.shape) for b in back]
    if finish:
        args.append(dinv)
        specs.append(pick)
    if finish == "last":
        args += earlier
        specs += [flat] * 3
        shapes, outs = [((4, BLOCK, SIZE), F32)], [block_of((4, BLOCK, SIZE))]
    else:
        shapes, outs = [((BLOCK, SIZE), F32)], [flat]
        if finish:
            shapes.append(((NT, BLOCK, SIZE), BF16))
            outs.append(block_of((NT, BLOCK, SIZE)))
    return call(
        functools.partial(whole_kernel, index, pair, begin, part, finish),
        name,
        shapes,
        specs,
        outs,
        args,
        [pltpu.VMEM((PLACES, SLOTS, SIZE, SIZE), BF16), pltpu.SemaphoreType.DMA((PLACES,))],
        flops=2 * 24 * BLOCK * SIZE * SIZE,
        moved=24 * SIZE * SIZE * 2,
    )


def local(rhs, dinv, factor, cols, live):
    place = lax.axis_index("col").astype(jnp.int32).reshape(1)
    tiles = factor.transpose(0, 2, 1, 3)
    move = lambda array, pairs: lax.ppermute(array, "col", pairs)
    over_row = lambda array: lax.all_to_all(array, "row", 0, 0, tiled=True)

    answer0, spread0, chunk = first_call(place, cols[:, 0, :], rhs, dinv, tiles)
    here = [chunk, move(chunk, SAME), move(chunk, CROSS), move(chunk, FAR)]
    chunks = here + [move(a, SWAP) for a in here]
    later, chunk = lax.optimization_barrier((tiles, chunk))
    gathered2 = lax.all_gather(later[2:3], "col", axis=1, tiled=True)
    gathered45 = lax.all_gather(later[4:6], "col", axis=1, tiled=True)
    swapped = move(tiles, SWAP)

    known0 = over_row(spread0)
    table = decode_call(chunks)
    answer1, spread1 = level1_call(place, table, live, rhs, dinv, known0, chunks)
    known1 = over_row(spread1)

    known0, spread1 = lax.optimization_barrier((known0, spread1))
    sent = pick_call((1, 3), place, table, known0)
    got = [sent[0]] + [move(sent[d], TURN[d]) for d in range(1, CHIPS)]
    sums = partial_call((1, 3), place, live, got, tiles, swapped)
    back = [sums[0]] + [move(sums[d], TURN[CHIPS - d]) for d in range(1, CHIPS)]

    answer2, spread2 = whole_call(
        "level2", 2, 0, 2, True, "more", place, table, live, rhs, known1, gathered2, 0, back, dinv, None
    )
    known2 = over_row(spread2)
    (early3,) = whole_call(
        "early3", 3, 0, 4, True, "", place, table, live, rhs, known1, gathered45, 1, back, None, None
    )
    (solved,) = whole_call(
        "level3", 3, 1, 5, False, "last", place, table, live, early3, known2, gathered45, None, None, dinv,
        [answer0, answer1, answer2],
    )
    return solved.transpose(0, 2, 1)


def solution(mesh):
    in_specs = (
        P(None, "row", None),
        P(None, "row", None),
        P(None, "row", "col", None),
        P(None, "row", "col"),
        P(None, "row"),
    )
    out_specs = P(None, "row", "col")
    return jax.shard_map(local, mesh=mesh, in_specs=in_specs, out_specs=out_specs, check_vma=False)
```

time: 487 us -> 160 us (0.33)
  waiting for transfers between devices: 412 us -> 64.6 us
  starting transfers between devices: 0.39 us -> 44.8 us
  local copies, waits for them, and re-layouts: 43.2 us -> 6.81 us
  Pallas kernels: 0 us -> 29.7 us
  matrix products: 10.2 us -> 0 us
  other arithmetic: 6.75 us -> 0 us
    all_gather x3 -> x2, waiting for transfers between devices: 316 us -> 0.02 us  [the longest x1 0.02 us: local(): gathered45 = lax.all_gather(later[4:6], 'col', axis=1, tiled=True)]
    reduce_scatter x3 -> x0, waiting for transfers between devices: 96.4 us -> none  [local(): lax.psum_scatter(partial_value, 'col', scatter_dimension=2, tiled=True)]
    ppermute x0 -> x14, waiting for transfers between devices: none -> 54.1 us  [local(): move = lambda array, pairs: lax.ppermute(array, 'col', pairs)]
    all_to_all x0 -> x3, starting transfers between devices: none -> 31.6 us  [local(): over_row = lambda array: lax.all_to_all(array, 'row', 0, 0, tiled=True)]
    pallas_call x0 -> x8, Pallas kernels: none -> 29.7 us  [call(): pl.pallas_call(kernel, grid=(1,), out_shape=tuple((jax.ShapeDtypeStruct(s...]
    gather x6 -> x0, local copies, waits for them, and re-layouts: 16.9 us -> none  [local(): known_rows[lane_index, local_tile[:, :, None]]]
    ppermute x0 -> x14, starting transfers between devices: none -> 13.2 us  [local(): move = lambda array, pairs: lax.ppermute(array, 'col', pairs)]
    all_gather x3 -> x0, local copies, waits for them, and re-layouts: 13.1 us -> none  [local(): lax.all_gather(answer.astype(jnp.bfloat16)[None], ('row', 'col'), axis=0,...]
  transfers between devices with their start and end apart: 6 -> 19, of which waited for: 6 -> 11; matrix products, arithmetic and copies ran while one was open for 3% -> 1% of each run, Pallas kernels for 0% -> 14%
where the time goes in v3:
time: 160 us; the launch traced here: 159 us
  waiting for transfers between devices  64.6 us (40%)
  starting transfers between devices  44.8 us (28%)
  Pallas kernels  29.7 us (19%)
  between operations  13.5 us (8%)
  local copies, waits for them, and re-layouts  6.81 us (4%)
    ppermute x14, waiting for transfers between devices, local(): move = lambda array, pairs: lax.ppermute(array, 'col', pairs)  54.1 us
    all_to_all x3, starting transfers between devices, local(): over_row = lambda array: lax.all_to_all(array, 'row', 0, 0, tiled=True)  31.6 us
    pallas_call x8, Pallas kernels, call(): pl.pallas_call(kernel, grid=(1,), out_shape=tuple((jax.ShapeDtypeStruct(s...  29.7 us
    ppermute x14, starting transfers between devices, local(): move = lambda array, pairs: lax.ppermute(array, 'col', pairs)  13.2 us
    all_to_all x3, waiting for transfers between devices, local(): over_row = lambda array: lax.all_to_all(array, 'row', 0, 0, tiled=True)  10.5 us
    unnamed x25, local copies, waits for them, and re-layouts  3.57 us
  transfers between devices with their start and end apart: 19, of which 11 were waited for; matrix products, arithmetic and copies ran while one was open for 1% of the time, Pallas kernels for 14%

profile of v3, /device:TPU:2, one launch (start us, length us, event | category | flops | bytes accessed | tf_op | source)
XLA Modules:
  0.0 159.5 jit_solution(8562323737787735133)
XLA Ops:
  6.5 0.0 copy-start
  6.5 0.0 all-gather.5.cloned.1.call-start
  6.5 1.5 copy.20
  8.0 2.5 %level0.1 = (f32[32,256]{1,0:T(8,128)}, bf16[32,32,256]{2,1,0:T(8,128)(2,1)}, bf16[784,256]{1,0:T(8,128)(2,1)}) custom-call(s32[1]{0:T(128)} %bitcast.place, s32[6,3]{1,0:T(8,128)} %bitcast.14, bf16[4,256,256]{2,1,0:T(8,128)(2,1)} %start.3, bf16[4,256,256]{2,1,0:T(8,128)(2,1)} %refs_0_.1, bf16[6,3,256,256]{3,2,1,0:T(8,128)(2,1)} %bitcast.7), custom_call_target="tpu_custom_call" | custom-call | bytes 2097152 | tf_op jit(solution)/shard_map/level0/pallas_call | solution.py:66
  10.5 0.0 copy-done
  10.5 0.8 slice_bitcast_fusion
  11.3 0.0 all-gather.5.cloned.1.call-update
  11.3 0.0 all-gather.3.cloned.1.call-start
  11.3 1.0 slice.6
  12.3 0.0 all-gather.3.cloned.1.call-update
  12.3 0.1 collective-permute-start.10
  12.5 11.6 %all-to-all-start = ((bf16[32,32,256]{2,1,0:T(8,128)(2,1)}), bf16[32,32,256]{2,1,0:T(8,128)(2,1)S(1)}, u32[]{:S(2)}, u32[]{:S(2)}) async-start(bf16[32,32,256]{2,1,0:T(8,128)(2,1)} %get-tuple-element.23), calls=%async_computation | async-start | bytes 1048576 | tf_op jit(solution)/shard_map/all_to_all | solution.py:290
  24.1 0.0 copy-done.4
  24.1 1.7 %collective-permute-start = (bf16[784,256]{1,0:T(8,128)(2,1)S(1)}, bf16[784,256]{1,0:T(8,128)(2,1)}, u32[]{:S(2)}, u32[]{:S(2)}) collective-permute-start(bf16[784,256]{1,0:T(8,128)(2,1)S(1)} %copy-done.4), channel_id=1, source_target_pairs={{0,2},{2,4},{4,6},{6,0},{1,7},{3,1},{5,3},{7,5},{8,10},{10,12},{12... | collective-permute-start | bytes 1204232 | tf_op jit(solution)/shard_map/ppermute | solution.py:289
  25.7 1.4 collective-permute-start.1
  27.2 1.5 collective-permute-start.2
  28.7 0.1 collective-permute-start.3
  28.7 14.1 %collective-permute-done.refs_1_ = bf16[784,256]{1,0:T(8,128)(2,1)} collective-permute-done((bf16[784,256]{1,0:T(8,128)(2,1)S(1)}, bf16[784,256]{1,0:T(8,128)(2,1)}, u32[]{:S(2)}, u32[]{:S(2)}) %collective-permute-start) | collective-permute-done | bytes 401440 | tf_op jit(solution)/shard_map/ppermute | solution.py:289
  42.8 3.1 %collective-permute-start.4 = (bf16[784,256]{1,0:T(8,128)(2,1)}, bf16[784,256]{1,0:T(8,128)(2,1)}, u32[]{:S(2)}, u32[]{:S(2)}) collective-permute-start(bf16[784,256]{1,0:T(8,128)(2,1)} %collective-permute-done.refs_1_), channel_id=1, source_target_pairs={{0,1},{1,0},{2,3},{3,2},{4,5},{5,4},{6,7},{7,6},{8,9},{9,8},{10,11... | collective-permute-start | bytes 1204232 | tf_op jit(solution)/shard_map/ppermute | solution.py:289
  45.9 2.2 %collective-permute-done.1.refs_2_ = bf16[784,256]{1,0:T(8,128)(2,1)} collective-permute-done((bf16[784,256]{1,0:T(8,128)(2,1)S(1)}, bf16[784,256]{1,0:T(8,128)(2,1)}, u32[]{:S(2)}, u32[]{:S(2)}) %collective-permute-start.1) | collective-permute-done | bytes 401440 | tf_op jit(solution)/shard_map/ppermute | solution.py:289
  48.2 0.0 collective-permute-start.5
  48.2 11.6 %collective-permute-done.2.refs_3_ = bf16[784,256]{1,0:T(8,128)(2,1)} collective-permute-done((bf16[784,256]{1,0:T(8,128)(2,1)S(1)}, bf16[784,256]{1,0:T(8,128)(2,1)}, u32[]{:S(2)}, u32[]{:S(2)}) %collective-permute-start.2) | collective-permute-done | bytes 401440 | tf_op jit(solution)/shard_map/ppermute | solution.py:289
  59.8 0.0 collective-permute-start.6
  59.8 0.0 copy-done.11
  59.8 0.7 copy.19.live
  60.5 0.0 collective-permute-done.3.refs_4_
  60.5 0.0 collective-permute-done.4.refs_5_
  60.5 0.0 collective-permute-done.5.refs_6_
  60.5 1.4 collective-permute-done.6.refs_7_
  61.9 1.4 cols.1.table
  63.3 0.0 all-to-all-done.known
  63.3 0.8 copy-done.2
  64.1 5.4 %level1.1 = (f32[32,256]{1,0:T(8,128)}, bf16[32,32,256]{2,1,0:T(8,128)(2,1)}) custom-call(s32[1]{0:T(128)} %bitcast.place, s32[8,256]{1,0:T(8,128)} %cols.1.table, s32[6,1]{1,0:T(8,128)} %copy.19.live, bf16[4,256,256]{2,1,0:T(8,128)(2,1)} %start.3, bf16[4,256,256]{2,1,0:T(8,128)(2,1)} %refs_0_.1, bf16[32,32,256]{2,1,0:T(8,128)(2,1)} %copy-done.2, ...), custom_call_target="tpu_custom_call" | custom-call | flops 100663296 | bytes 3145728 | tf_op jit(solution)/shard_map/level1/pallas_call | solution.py:66
  69.5 9.8 %all-to-all-start.1 = ((bf16[32,32,256]{2,1,0:T(8,128)(2,1)}), bf16[32,32,256]{2,1,0:T(8,128)(2,1)S(1)}, u32[]{:S(2)}, u32[]{:S(2)}) async-start(bf16[32,32,256]{2,1,0:T(8,128)(2,1)} %get-tuple-element.24), calls=%async_computation.1 | async-start | bytes 1048576 | tf_op jit(solution)/shard_map/all_to_all | solution.py:290
  79.3 2.1 %pick.1 = (bf16[2,6,32,256]{3,2,1,0:T(8,128)(2,1)}, bf16[2,6,32,256]{3,2,1,0:T(8,128)(2,1)}, bf16[2,6,32,256]{3,2,1,0:T(8,128)(2,1)}, bf16[2,6,32,256]{3,2,1,0:T(8,128)(2,1)}) custom-call(s32[1]{0:T(128)} %bitcast.place, s32[8,256]{1,0:T(8,128)} %cols.1.table, bf16[32,32,256]{2,1,0:T(8,128)(2,1)} %copy-done.2), custom_call_target="tpu_custom_call" | custom-call | bytes 2097152 | tf_op jit(solution)/shard_map/pick/pallas_call | solution.py:66
  81.4 0.0 collective-permute-start.7
  81.4 1.1 collective-permute-start.8
  82.5 2.1 %collective-permute-start.9 = (bf16[2,6,32,256]{3,2,1,0:T(8,128)(2,1)}, bf16[2,6,32,256]{3,2,1,0:T(8,128)(2,1)S(1)}, u32[]{:S(2)}, u32[]{:S(2)}) collective-permute-start(bf16[2,6,32,256]{3,2,1,0:T(8,128)(2,1)} %get-tuple-element.30), channel_id=1, source_target_pairs={{0,6},{1,7},{2,0},{3,1},{4,2},{5,3},{6,4},{7,5},{8,14},{9,15},{10,... | collective-permute-start | bytes 589832 | tf_op jit(solution)/shard_map/ppermute | solution.py:289
  84.6 12.1 %collective-permute-done.7.refs_1_ = bf16[2,6,32,256]{3,2,1,0:T(8,128)(2,1)S(1)} collective-permute-done((bf16[2,6,32,256]{3,2,1,0:T(8,128)(2,1)}, bf16[2,6,32,256]{3,2,1,0:T(8,128)(2,1)S(1)}, u32[]{:S(2)}, u32[]{:S(2)}) %collective-permute-start.7) | collective-permute-done | bytes 196640 | tf_op jit(solution)/shard_map/ppermute | solution.py:289
  96.7 3.9 %collective-permute-done.8.refs_2_ = bf16[2,6,32,256]{3,2,1,0:T(8,128)(2,1)S(1)} collective-permute-done((bf16[2,6,32,256]{3,2,1,0:T(8,128)(2,1)}, bf16[2,6,32,256]{3,2,1,0:T(8,128)(2,1)S(1)}, u32[]{:S(2)}, u32[]{:S(2)}) %collective-permute-start.8) | collective-permute-done | bytes 196640 | tf_op jit(solution)/shard_map/ppermute | solution.py:289
  100.7 2.8 %collective-permute-done.9.refs_3_ = bf16[2,6,32,256]{3,2,1,0:T(8,128)(2,1)S(1)} collective-permute-done((bf16[2,6,32,256]{3,2,1,0:T(8,128)(2,1)}, bf16[2,6,32,256]{3,2,1,0:T(8,128)(2,1)S(1)}, u32[]{:S(2)}, u32[]{:S(2)}) %collective-permute-start.9) | collective-permute-done | bytes 196640 | tf_op jit(solution)/shard_map/ppermute | solution.py:289
  103.5 0.0 collective-permute-done.10.refs_5_.refs_7_
  103.5 0.0 copy-done.8
  103.5 0.0 copy-done.9
  103.5 0.6 copy-done.10
  104.1 3.1 %partial.1 = (f32[2,32,256]{2,1,0:T(8,128)}, f32[2,32,256]{2,1,0:T(8,128)}, f32[2,32,256]{2,1,0:T(8,128)}, f32[2,32,256]{2,1,0:T(8,128)}) custom-call(s32[1]{0:T(128)} %bitcast.place, s32[6,1]{1,0:T(8,128)} %copy.19.live, bf16[2,6,32,256]{3,2,1,0:T(8,128)(2,1)} %get-tuple-element.27.refs_0_, bf16[2,6,32,256]{3,2,1,0:T(8,128)(2,1)} %copy-done.8, ...), custom_call_target="tpu_custom_call" | custom-call | flops 201326592 | bytes 2097152 | tf_op jit(solution)/shard_map/partial/pallas_call | solution.py:66
  107.2 0.0 collective-permute-start.11
  107.2 1.7 %collective-permute-start.12 = (f32[2,32,256]{2,1,0:T(8,128)}, f32[2,32,256]{2,1,0:T(8,128)S(1)}, u32[]{:S(2)}, u32[]{:S(2)}) collective-permute-start(f32[2,32,256]{2,1,0:T(8,128)} %get-tuple-element.33), channel_id=1, source_target_pairs={{0,4},{1,5},{2,6},{3,7},{4,0},{5,1},{6,2},{7,3},{8,12},{9,13},{10,... | collective-permute-start | bytes 196616 | tf_op jit(solution)/shard_map/ppermute | solution.py:289
  108.9 0.4 collective-permute-start.13
  109.3 0.0 all-to-all-done.1.known
  109.3 4.3 %collective-permute-done.11.refs_1_ = f32[2,32,256]{2,1,0:T(8,128)S(1)} collective-permute-done((f32[2,32,256]{2,1,0:T(8,128)}, f32[2,32,256]{2,1,0:T(8,128)S(1)}, u32[]{:S(2)}, u32[]{:S(2)}) %collective-permute-start.11) | collective-permute-done | bytes 65568 | tf_op jit(solution)/shard_map/ppermute | solution.py:289
  113.6 1.2 collective-permute-done.12.refs_2_
  114.8 0.4 collective-permute-done.13.refs_3_
  115.2 0.0 copy-done.1
  115.2 0.0 copy-done.5
  115.2 0.2 copy-done.6
  115.4 0.4 copy-done.7
  115.8 5.4 %level2.1 = (f32[32,256]{1,0:T(8,128)}, bf16[32,32,256]{2,1,0:T(8,128)(2,1)}) custom-call(s32[1]{0:T(128)} %bitcast.place, s32[8,256]{1,0:T(8,128)} %cols.1.table, s32[6,1]{1,0:T(8,128)} %copy.19.live, bf16[4,256,256]{2,1,0:T(8,128)(2,1)} %start.3, bf16[32,32,256]{2,1,0:T(8,128)(2,1)} %copy-done.1, bf16[1,24,256,256]{3,2,1,0:T(8,128)(2,1)} %bitcast.13, ...), custom_call_target="tpu_custom_call" | custom-call | flops 100663296 | bytes 3145728 | tf_op jit(solution)/shard_map/level2/pallas_call | solution.py:66
  121.2 10.2 %all-to-all-start.2 = ((bf16[32,32,256]{2,1,0:T(8,128)(2,1)}), bf16[32,32,256]{2,1,0:T(8,128)(2,1)S(1)}, u32[]{:S(2)}, u32[]{:S(2)}) async-start(bf16[32,32,256]{2,1,0:T(8,128)(2,1)} %get-tuple-element.35), calls=%async_computation.2 | async-start | bytes 1048576 | tf_op jit(solution)/shard_map/all_to_all | solution.py:290
  131.4 0.0 all-gather.3.cloned.1.call-done.tiles
  131.4 4.9 %early3.1.start = f32[32,256]{1,0:T(8,128)} custom-call(s32[1]{0:T(128)} %bitcast.place, s32[8,256]{1,0:T(8,128)} %cols.1.table, s32[6,1]{1,0:T(8,128)} %copy.19.live, bf16[4,256,256]{2,1,0:T(8,128)(2,1)} %start.3, bf16[32,32,256]{2,1,0:T(8,128)(2,1)} %copy-done.1, bf16[2,24,256,256]{3,2,1,0:T(8,128)(2,1)} %all-gather.3.cloned.1.call-done.tiles, ...), custom_call_target="tpu_custom_call" | custom-call | flops 100663296 | bytes 3145728 | tf_op jit(solution)/shard_map/early3/pallas_call | solution.py:66
  136.3 10.5 %all-to-all-done.2.known = bf16[32,32,256]{2,1,0:T(8,128)(2,1)S(1)} async-done(((bf16[32,32,256]{2,1,0:T(8,128)(2,1)}), bf16[32,32,256]{2,1,0:T(8,128)(2,1)S(1)}, u32[]{:S(2)}, u32[]{:S(2)}) %all-to-all-start.2) | async-done | bytes 524320 | tf_op jit(solution)/shard_map/all_to_all | solution.py:290
  146.7 0.8 copy-done.3
  147.5 5.0 %level3.1 = f32[4,32,256]{2,1,0:T(8,128)} custom-call(s32[1]{0:T(128)} %bitcast.place, s32[8,256]{1,0:T(8,128)} %cols.1.table, s32[6,1]{1,0:T(8,128)} %copy.19.live, f32[32,256]{1,0:T(8,128)} %early3.1.start, bf16[32,32,256]{2,1,0:T(8,128)(2,1)} %copy-done.3, bf16[2,24,256,256]{3,2,1,0:T(8,128)(2,1)} %all-gather.3.cloned.1.call-done.tiles, ...), custom_call_target="tpu_custom_call" | custom-call | flops 100663296 | bytes 3145728 | tf_op jit(solution)/shard_map/level3/pallas_call | solution.py:66
  (12 shorter events, 0.0 us)
Async XLA Ops:
  6.5 4.0 %copy-start = (bf16[6,256,3,256]{3,1,2,0:T(8,128)(2,1)S(1)}, bf16[6,256,3,256]{3,1,2,0:T(8,128)(2,1)}, u32[]{:S(2)}) copy-start(bf16[6,256,3,256]{3,1,2,0:T(8,128)(2,1)} %param.7) | copy-start | bytes 7077892
  6.5 108.7 %all-gather.5.cloned.1.call-start = ((), (), s32[]{:S(2)}) async-start(), calls=%async_computation.4 | async-start | bytes 3538944 | tf_op jit(solution)/shard_map/all_gather | solution.py:296
  10.5 13.6 %copy-start.4 = (bf16[784,256]{1,0:T(8,128)(2,1)S(1)}, bf16[784,256]{1,0:T(8,128)(2,1)}, u32[]{:S(2)}) copy-start(bf16[784,256]{1,0:T(8,128)(2,1)} %get-tuple-element.22.refs_0_) | copy-start | bytes 1204228
  10.5 49.3 %copy-start.11 = (s32[6,1]{0,1:T(1,128)S(1)}, s32[6,1]{0,1:T(1,128)}, u32[]{:S(2)}) copy-start(s32[6,1]{0,1:T(1,128)} %param.9) | copy-start | bytes 76
  11.3 120.1 %all-gather.3.cloned.1.call-start = ((), (), s32[]{:S(2)}) async-start(), calls=%async_computation.3 | async-start | bytes 7077888 | tf_op jit(solution)/shard_map/all_gather | solution.py:297
  12.3 91.1 %collective-permute-start.10 = (bf16[6,3,256,256]{3,2,1,0:T(8,128)(2,1)S(1)}, bf16[6,3,256,256]{3,2,1,0:T(8,128)(2,1)}, u32[]{:S(2)}, u32[]{:S(2)}) collective-permute-start(bf16[6,3,256,256]{3,2,1,0:T(8,128)(2,1)S(1)} %bitcast.12), channel_id=1, source_target_pairs={{0,1},{1,0},{2,3},{3,2},{4,5},{5,4},{6,7},{7,6},{8,9},{9,8},{10,11... | collective-permute-start | bytes 7077896 | tf_op jit(solution)/shard_map/ppermute | solution.py:289
  12.5 50.8 %all-to-all-start = ((bf16[32,32,256]{2,1,0:T(8,128)(2,1)}), bf16[32,32,256]{2,1,0:T(8,128)(2,1)S(1)}, u32[]{:S(2)}, u32[]{:S(2)}) async-start(bf16[32,32,256]{2,1,0:T(8,128)(2,1)} %get-tuple-element.23), calls=%async_computation | async-start | bytes 1048576 | tf_op jit(solution)/shard_map/all_to_all | solution.py:290
  24.1 18.7 %collective-permute-start = (bf16[784,256]{1,0:T(8,128)(2,1)S(1)}, bf16[784,256]{1,0:T(8,128)(2,1)}, u32[]{:S(2)}, u32[]{:S(2)}) collective-permute-start(bf16[784,256]{1,0:T(8,128)(2,1)S(1)} %copy-done.4), channel_id=1, source_target_pairs={{0,2},{2,4},{4,6},{6,0},{1,7},{3,1},{5,3},{7,5},{8,10},{10,12},{12... | collective-permute-start | bytes 1204232 | tf_op jit(solution)/shard_map/ppermute | solution.py:289
  25.7 22.4 %collective-permute-start.1 = (bf16[784,256]{1,0:T(8,128)(2,1)S(1)}, bf16[784,256]{1,0:T(8,128)(2,1)}, u32[]{:S(2)}, u32[]{:S(2)}) collective-permute-start(bf16[784,256]{1,0:T(8,128)(2,1)S(1)} %copy-done.4), channel_id=1, source_target_pairs={{1,2},{3,4},{5,6},{7,0},{0,7},{2,1},{4,3},{6,5},{9,10},{11,12},{13... | collective-permute-start | bytes 1204232 | tf_op jit(solution)/shard_map/ppermute | solution.py:289
  27.2 32.6 %collective-permute-start.2 = (bf16[784,256]{1,0:T(8,128)(2,1)S(1)}, bf16[784,256]{1,0:T(8,128)(2,1)}, u32[]{:S(2)}, u32[]{:S(2)}) collective-permute-start(bf16[784,256]{1,0:T(8,128)(2,1)S(1)} %copy-done.4), channel_id=1, source_target_pairs={{0,4},{1,5},{2,6},{3,7},{4,0},{5,1},{6,2},{7,3},{8,12},{9,13},{10,... | collective-permute-start | bytes 1204232 | tf_op jit(solution)/shard_map/ppermute | solution.py:289
  28.7 31.8 %collective-permute-start.3 = (bf16[784,256]{1,0:T(8,128)(2,1)S(1)}, bf16[784,256]{1,0:T(8,128)(2,1)}, u32[]{:S(2)}, u32[]{:S(2)}) collective-permute-start(bf16[784,256]{1,0:T(8,128)(2,1)S(1)} %copy-done.4), channel_id=1, source_target_pairs={{0,1},{1,0},{2,3},{3,2},{4,5},{5,4},{6,7},{7,6},{8,9},{9,8},{10,11... | collective-permute-start | bytes 1204232 | tf_op jit(solution)/shard_map/ppermute | solution.py:289
  42.8 17.7 %collective-permute-start.4 = (bf16[784,256]{1,0:T(8,128)(2,1)}, bf16[784,256]{1,0:T(8,128)(2,1)}, u32[]{:S(2)}, u32[]{:S(2)}) collective-permute-start(bf16[784,256]{1,0:T(8,128)(2,1)} %collective-permute-done.refs_1_), channel_id=1, source_target_pairs={{0,1},{1,0},{2,3},{3,2},{4,5},{5,4},{6,7},{7,6},{8,9},{9,8},{10,11... | collective-permute-start | bytes 1204232 | tf_op jit(solution)/shard_map/ppermute | solution.py:289
  48.2 12.3 %collective-permute-start.5 = (bf16[784,256]{1,0:T(8,128)(2,1)}, bf16[784,256]{1,0:T(8,128)(2,1)}, u32[]{:S(2)}, u32[]{:S(2)}) collective-permute-start(bf16[784,256]{1,0:T(8,128)(2,1)} %collective-permute-done.1.refs_2_), channel_id=1, source_target_pairs={{0,1},{1,0},{2,3},{3,2},{4,5},{5,4},{6,7},{7,6},{8,9},{9,8},{10,11... | collective-permute-start | bytes 1204232 | tf_op jit(solution)/shard_map/ppermute | solution.py:289
  59.8 2.1 %collective-permute-start.6 = (bf16[784,256]{1,0:T(8,128)(2,1)}, bf16[784,256]{1,0:T(8,128)(2,1)}, u32[]{:S(2)}, u32[]{:S(2)}) collective-permute-start(bf16[784,256]{1,0:T(8,128)(2,1)} %collective-permute-done.2.refs_3_), channel_id=1, source_target_pairs={{0,1},{1,0},{2,3},{3,2},{4,5},{5,4},{6,7},{7,6},{8,9},{9,8},{10,11... | collective-permute-start | bytes 1204232 | tf_op jit(solution)/shard_map/ppermute | solution.py:289
  63.3 0.8 copy-start.2
  69.5 39.8 %all-to-all-start.1 = ((bf16[32,32,256]{2,1,0:T(8,128)(2,1)}), bf16[32,32,256]{2,1,0:T(8,128)(2,1)S(1)}, u32[]{:S(2)}, u32[]{:S(2)}) async-start(bf16[32,32,256]{2,1,0:T(8,128)(2,1)} %get-tuple-element.24), calls=%async_computation.1 | async-start | bytes 1048576 | tf_op jit(solution)/shard_map/all_to_all | solution.py:290
  81.4 15.4 %collective-permute-start.7 = (bf16[2,6,32,256]{3,2,1,0:T(8,128)(2,1)}, bf16[2,6,32,256]{3,2,1,0:T(8,128)(2,1)S(1)}, u32[]{:S(2)}, u32[]{:S(2)}) collective-permute-start(bf16[2,6,32,256]{3,2,1,0:T(8,128)(2,1)} %get-tuple-element.28), channel_id=1, source_target_pairs={{0,2},{1,3},{2,4},{3,5},{4,6},{5,7},{6,0},{7,1},{8,10},{9,11},{10,... | collective-permute-start | bytes 589832 | tf_op jit(solution)/shard_map/ppermute | solution.py:289
  81.4 19.3 %collective-permute-start.8 = (bf16[2,6,32,256]{3,2,1,0:T(8,128)(2,1)}, bf16[2,6,32,256]{3,2,1,0:T(8,128)(2,1)S(1)}, u32[]{:S(2)}, u32[]{:S(2)}) collective-permute-start(bf16[2,6,32,256]{3,2,1,0:T(8,128)(2,1)} %get-tuple-element.29), channel_id=1, source_target_pairs={{0,4},{1,5},{2,6},{3,7},{4,0},{5,1},{6,2},{7,3},{8,12},{9,13},{10,... | collective-permute-start | bytes 589832 | tf_op jit(solution)/shard_map/ppermute | solution.py:289
  82.5 21.0 %collective-permute-start.9 = (bf16[2,6,32,256]{3,2,1,0:T(8,128)(2,1)}, bf16[2,6,32,256]{3,2,1,0:T(8,128)(2,1)S(1)}, u32[]{:S(2)}, u32[]{:S(2)}) collective-permute-start(bf16[2,6,32,256]{3,2,1,0:T(8,128)(2,1)} %get-tuple-element.30), channel_id=1, source_target_pairs={{0,6},{1,7},{2,0},{3,1},{4,2},{5,3},{6,4},{7,5},{8,14},{9,15},{10,... | collective-permute-start | bytes 589832 | tf_op jit(solution)/shard_map/ppermute | solution.py:289
  96.7 6.7 %copy-start.8 = (bf16[2,6,32,256]{3,2,1,0:T(8,128)(2,1)}, bf16[2,6,32,256]{3,2,1,0:T(8,128)(2,1)S(1)}, u32[]{:S(2)}) copy-start(bf16[2,6,32,256]{3,2,1,0:T(8,128)(2,1)S(1)} %collective-permute-done.7.refs_1_) | copy-start | bytes 589828
  100.7 2.8 %copy-start.9 = (bf16[2,6,32,256]{3,2,1,0:T(8,128)(2,1)}, bf16[2,6,32,256]{3,2,1,0:T(8,128)(2,1)S(1)}, u32[]{:S(2)}) copy-start(bf16[2,6,32,256]{3,2,1,0:T(8,128)(2,1)S(1)} %collective-permute-done.8.refs_2_) | copy-start | bytes 589828
  103.5 0.7 copy-start.10
  107.2 6.4 %collective-permute-start.11 = (f32[2,32,256]{2,1,0:T(8,128)}, f32[2,32,256]{2,1,0:T(8,128)S(1)}, u32[]{:S(2)}, u32[]{:S(2)}) collective-permute-start(f32[2,32,256]{2,1,0:T(8,128)} %get-tuple-element.32), channel_id=1, source_target_pairs={{0,6},{1,7},{2,0},{3,1},{4,2},{5,3},{6,4},{7,5},{8,14},{9,15},{10,... | collective-permute-start | bytes 196616 | tf_op jit(solution)/shard_map/ppermute | solution.py:289
  107.2 7.6 %collective-permute-start.12 = (f32[2,32,256]{2,1,0:T(8,128)}, f32[2,32,256]{2,1,0:T(8,128)S(1)}, u32[]{:S(2)}, u32[]{:S(2)}) collective-permute-start(f32[2,32,256]{2,1,0:T(8,128)} %get-tuple-element.33), channel_id=1, source_target_pairs={{0,4},{1,5},{2,6},{3,7},{4,0},{5,1},{6,2},{7,3},{8,12},{9,13},{10,... | collective-permute-start | bytes 196616 | tf_op jit(solution)/shard_map/ppermute | solution.py:289
  108.9 6.3 %collective-permute-start.13 = (f32[2,32,256]{2,1,0:T(8,128)}, f32[2,32,256]{2,1,0:T(8,128)S(1)}, u32[]{:S(2)}, u32[]{:S(2)}) collective-permute-start(f32[2,32,256]{2,1,0:T(8,128)} %get-tuple-element.34), channel_id=1, source_target_pairs={{0,2},{1,3},{2,4},{3,5},{4,6},{5,7},{6,0},{7,1},{8,10},{9,11},{10,... | collective-permute-start | bytes 196616 | tf_op jit(solution)/shard_map/ppermute | solution.py:289
  109.3 5.9 %copy-start.1 = (bf16[32,32,256]{2,1,0:T(8,128)(2,1)}, bf16[32,32,256]{2,1,0:T(8,128)(2,1)S(1)}, u32[]{:S(2)}) copy-start(bf16[32,32,256]{2,1,0:T(8,128)(2,1)S(1)} %all-to-all-done.1.known) | copy-start | bytes 1572868
  113.6 1.7 %copy-start.5 = (f32[2,32,256]{2,1,0:T(8,128)}, f32[2,32,256]{2,1,0:T(8,128)S(1)}, u32[]{:S(2)}) copy-start(f32[2,32,256]{2,1,0:T(8,128)S(1)} %collective-permute-done.11.refs_1_) | copy-start | bytes 196612
  114.8 0.6 copy-start.6
  115.2 0.6 copy-start.7
  121.2 25.5 %all-to-all-start.2 = ((bf16[32,32,256]{2,1,0:T(8,128)(2,1)}), bf16[32,32,256]{2,1,0:T(8,128)(2,1)S(1)}, u32[]{:S(2)}, u32[]{:S(2)}) async-start(bf16[32,32,256]{2,1,0:T(8,128)(2,1)} %get-tuple-element.35), calls=%async_computation.2 | async-start | bytes 1048576 | tf_op jit(solution)/shard_map/all_to_all | solution.py:290
  146.7 0.8 copy-start.3
Sparse Core Ops, SparseCore 0:
  11.4 45.7 all-gather.4
  59.0 57.3 all-gather.2

commit v4 on v3

v4 whole, which is shorter than its diff:
```python
import functools

import jax
import jax.numpy as jnp
from jax import lax
from jax.experimental import pallas as pl
from jax.experimental.pallas import tpu as pltpu
from jax.sharding import PartitionSpec as P

NT_DIMS = (((1,), (1,)), ((), ()))
BLOCK = 32
SIZE = 256
SLOTS = 3
PLACES = 8
CHIPS = 4
PAIRS = 6
NT = 32
EXTRA = 16
CHUNK = SLOTS * SIZE + EXTRA
VMEM_BYTES = 56 * 1024 * 1024
SMEM = pl.BlockSpec(memory_space=pltpu.SMEM)
ANY = pl.BlockSpec(memory_space=pl.ANY)
F32, BF16 = jnp.float32, jnp.bfloat16
SWAP = [(p, p ^ 1) for p in range(PLACES)]
TURN = [[(p, (p + 2 * d) % PLACES) for p in range(PLACES)] for d in range(CHIPS)]


def dot_nt(a, b):
    return lax.dot_general(a, b, NT_DIMS, preferred_element_type=F32)


def block_of(shape, *lead):
    return pl.BlockSpec(shape, lambda i: tuple(lead) + (0,) * (len(shape) - len(lead)))


def probe_rows(place, rhs):
    probe = lax.broadcasted_iota(jnp.int32, (BLOCK, rhs.shape[1]), 1)
    mine = lax.broadcasted_iota(jnp.int32, (BLOCK, rhs.shape[1]), 0) + place * BLOCK
    return dot_nt((probe == mine).astype(BF16), rhs)


def spread_out(result, spread):
    rounded = result.astype(BF16)
    for copy in range(spread.shape[0]):
        spread[copy] = rounded


def call(kernel, name, shapes, in_specs, out_specs, args, scratch=(), flops=0, moved=0):
    return pl.pallas_call(
        kernel,
        grid=(1,),
        out_shape=tuple(jax.ShapeDtypeStruct(s, t) for s, t in shapes),
        in_specs=in_specs,
        out_specs=tuple(out_specs),
        scratch_shapes=list(scratch),
        cost_estimate=pl.CostEstimate(flops=flops, bytes_accessed=moved, transcendentals=0),
        compiler_params=pltpu.CompilerParams(vmem_limit_bytes=VMEM_BYTES),
        name=name,
    )(*args)


def first_kernel(place, cols, rhs, dinv, tiles, answer, spread, chunk):
    residual = probe_rows(place[0], rhs[0]).astype(BF16)
    result = dot_nt(residual, dinv[0])
    answer[...] = result
    spread_out(result, spread)
    for slot in range(SLOTS):
        chunk[slot * SIZE : (slot + 1) * SIZE] = tiles[0, slot]
    lane = lax.broadcasted_iota(jnp.int32, (EXTRA, SIZE), 1)
    packed = jnp.zeros((EXTRA, SIZE), jnp.int32)
    for pair in range(PAIRS):
        for slot in range(SLOTS):
            packed = jnp.where(lane == pair * SLOTS + slot, cols[slot, 0, pair], packed)
    chunk[SLOTS * SIZE :] = packed.astype(F32).astype(BF16)


def first_call(place, cols, rhs, dinv, tiles):
    return call(
        first_kernel,
        "level0",
        [((BLOCK, SIZE), F32), ((NT, BLOCK, SIZE), BF16), ((CHUNK, SIZE), BF16)],
        [SMEM, SMEM, block_of((1, SIZE, SIZE), 0), block_of((1, SIZE, SIZE), 0), block_of((1, SLOTS, SIZE, SIZE), 0)],
        [block_of((BLOCK, SIZE)), block_of((NT, BLOCK, SIZE)), block_of((CHUNK, SIZE))],
        (place, cols, rhs, dinv, tiles),
        moved=2**21,
    )


def decode_kernel(gathered, out):
    for place in range(PLACES):
        out[pl.ds(place, 1), :] = gathered[place, 0:1, :].astype(F32).astype(jnp.int32)


def decode_call(gathered):
    return call(
        decode_kernel,
        "cols",
        [((PLACES, SIZE), jnp.int32)],
        [pl.BlockSpec((PLACES, EXTRA, SIZE), lambda i: (0, SLOTS * SIZE // EXTRA, 0))],
        [block_of((PLACES, SIZE))],
        (gathered,),
    )[0]


def masked(block, alive):
    return jnp.where(alive, block, jnp.zeros_like(block))


def pick_kernel(pairs, place, table, known, *outs):
    chip = lax.div(place[0], 2)
    for step in range(CHIPS):
        for core in range(2):
            want = lax.rem(chip + step, CHIPS) * 2 + core
            for n, pair in enumerate(pairs):
                for slot in range(SLOTS):
                    outs[step][n, core * SLOTS + slot] = known[table[want, pair * SLOTS + slot]]


def pick_call(name, pairs, place, table, known):
    shape = (len(pairs), 2 * SLOTS, BLOCK, SIZE)
    return call(
        functools.partial(pick_kernel, pairs),
        name,
        [(shape, BF16)] * CHIPS,
        [SMEM, SMEM, block_of((NT, BLOCK, SIZE))],
        [block_of(shape)] * CHIPS,
        (place, table, known),
        moved=2**21,
    )


def partial_kernel(pairs, kept, place, live, *refs):
    refs = list(refs)
    got = [refs.pop(0) for _ in range(CHIPS)]
    before = [refs.pop(0) for _ in range(CHIPS)] if kept else []
    tiles = [(refs.pop(0), refs.pop(0)) for _ in pairs]
    chip, core = lax.div(place[0], 2), lax.rem(place[0], 2)
    for n, pair in enumerate(pairs):
        total = jnp.zeros((CHIPS * BLOCK, SIZE), F32)
        for swapped in range(2):
            side = lax.rem(core + swapped, 2)
            for slot in range(SLOTS):
                at = side * SLOTS + slot
                block = jnp.concatenate([g[n, at] for g in got])
                block = masked(block, chip * 2 * SLOTS + at < live[0, pair])
                total = total + dot_nt(block, tiles[n][swapped][0, slot])
        for step in range(CHIPS):
            sums = total[step * BLOCK : (step + 1) * BLOCK]
            refs[n * CHIPS + step][...] = sums + before[step][...] if kept else sums


def partial_call(name, pairs, place, live, got, kept, tiles, swapped):
    shape = (BLOCK, SIZE)
    args = [place, live, *got, *kept]
    specs = [SMEM, SMEM] + [block_of(g.shape) for g in args[2:]]
    for pair in pairs:
        args += [tiles, swapped]
        specs += [block_of((1, SLOTS, SIZE, SIZE), pair)] * 2
    return call(
        functools.partial(partial_kernel, pairs, bool(kept)),
        name,
        [(shape, F32)] * (CHIPS * len(pairs)),
        specs,
        [block_of(shape)] * (CHIPS * len(pairs)),
        args,
        flops=2 * 6 * SIZE**3,
        moved=2**21,
    )


def level_kernel(pair, returned, earlier, place, table, live, rhs, dinv, known, tiles, *refs):
    refs = list(refs)
    back = [refs.pop(0) for _ in range(returned)]
    before = [refs.pop(0) for _ in range(earlier)]
    held, sems = refs[-2:]
    copies = []
    for n in range(CHIPS):
        two = pl.ds(2 * n, 2)
        source = tiles.at[two, pl.ds(0, SLOTS * SIZE)]
        copies.append(pltpu.make_async_copy(source, held.at[two], sems.at[n]))
    for copy in copies:
        copy.start()
    total = probe_rows(place[0], rhs[0])
    for sums in back:
        total = total - sums[...]
    for owner in range(PLACES):
        if owner % 2 == 0:
            copies[owner // 2].wait()
        for slot in range(SLOTS):
            block = masked(known[table[owner, pair * SLOTS + slot]], owner * SLOTS + slot < live[0, pair])
            total = total - dot_nt(block, held[owner, slot * SIZE : (slot + 1) * SIZE])
    result = dot_nt(total.astype(BF16), dinv[0])
    if earlier:
        for n in range(earlier):
            refs[0][n] = before[n][...]
        refs[0][earlier] = result
        return
    refs[0][...] = result
    spread_out(result, refs[1])


def level_call(level, pair, place, table, live, rhs, dinv, known, tiles, back, earlier):
    flat, pick = block_of((BLOCK, SIZE)), block_of((1, SIZE, SIZE), level)
    if earlier:
        shapes, outs = [((level + 1, BLOCK, SIZE), F32)], [block_of((level + 1, BLOCK, SIZE))]
    else:
        shapes = [((BLOCK, SIZE), F32), ((NT, BLOCK, SIZE), BF16)]
        outs = [flat, block_of((NT, BLOCK, SIZE))]
    return call(
        functools.partial(level_kernel, pair, len(back), len(earlier)),
        "level%d" % level,
        shapes,
        [SMEM] * 3 + [pick, pick, block_of((NT, BLOCK, SIZE)), ANY] + [flat] * (len(back) + len(earlier)),
        outs,
        (place, table, live, rhs, dinv, known, tiles, *back, *earlier),
        [pltpu.VMEM((PLACES, SLOTS * SIZE, SIZE), BF16), pltpu.SemaphoreType.DMA((CHIPS,))],
        flops=2 * 24 * BLOCK * SIZE * SIZE,
        moved=24 * SIZE * SIZE * 2,
    )


def local(rhs, dinv, factor, cols, live):
    place = lax.axis_index("col").astype(jnp.int32).reshape(1)
    tiles = factor.transpose(0, 2, 1, 3)
    move = lambda array, pairs: lax.ppermute(array, "col", pairs)
    over_row = lambda array: lax.all_to_all(array, "row", 0, 0, tiled=True)

    gather = lambda array: lax.all_gather(array, "col", axis=0, tiled=False)
    piece = lambda array, pair: array[pair].reshape(SLOTS * SIZE, SIZE)
    live = live.transpose(1, 0)

    answer0, spread0, chunk = first_call(place, cols.transpose(2, 1, 0), rhs, dinv, tiles)
    gathered0 = gather(chunk)
    later, spread0 = lax.optimization_barrier((tiles, spread0))
    gathered2 = gather(piece(later, 2))
    gathered5 = gather(piece(later, 5))
    swapped = move(tiles, SWAP)

    def send(picked):
        return [picked[0]] + [move(picked[d], TURN[d]) for d in range(1, CHIPS)]

    def give_back(sums):
        return [sums[0]] + [move(sums[d], TURN[CHIPS - d]) for d in range(1, CHIPS)]

    known0 = over_row(spread0)
    table = decode_call(gathered0)
    answer1, spread1 = level_call(1, 0, place, table, live, rhs, dinv, known0, gathered0, [], [])
    known1 = over_row(spread1)

    known0, spread1 = lax.optimization_barrier((known0, spread1))
    got = send(pick_call("pick13", (1, 3), place, table, known0))
    sums = partial_call("partial13", (1, 3), place, live, got, [], tiles, swapped)
    sums2, sums3 = sums[:CHIPS], sums[CHIPS:]
    answer2, spread2 = level_call(2, 2, place, table, live, rhs, dinv, known1, gathered2, give_back(sums2), [])
    known2 = over_row(spread2)

    known1, spread2 = lax.optimization_barrier((known1, spread2))
    got = send(pick_call("pick4", (4,), place, table, known1))
    sums3 = partial_call("partial4", (4,), place, live, got, sums3, tiles, swapped)
    (solved,) = level_call(
        3, 5, place, table, live, rhs, dinv, known2, gathered5, give_back(sums3), [answer0, answer1, answer2]
    )
    return solved.transpose(0, 2, 1)


def solution(mesh):
    in_specs = (
        P(None, "row", None),
        P(None, "row", None),
        P(None, "row", "col", None),
        P(None, "row", "col"),
        P(None, "row"),
    )
    out_specs = P(None, "row", "col")
    return jax.shard_map(local, mesh=mesh, in_specs=in_specs, out_specs=out_specs, check_vma=False)
```

time: 160 us -> 142 us (0.89)
  waiting for transfers between devices: 64.6 us -> 50.2 us
  Pallas kernels: 29.7 us -> 27.4 us
  local copies, waits for them, and re-layouts: 6.81 us -> 4.78 us
    ppermute x14 -> x13, waiting for transfers between devices: 54.1 us -> 29.2 us  [local(): move = lambda array, pairs: lax.ppermute(array, 'col', pairs)]
    all_gather x2 -> x3, waiting for transfers between devices: 0.02 us -> 20.2 us  [local(): gather = lambda array: lax.all_gather(array, 'col', axis=0, tiled=False)]
    all_to_all x3, waiting for transfers between devices: 10.5 us -> 0.01 us  [local(): over_row = lambda array: lax.all_to_all(array, 'row', 0, 0, tiled=True)]
    pallas_call x8 -> x9, Pallas kernels: 29.7 us -> 27.4 us  [call(): pl.pallas_call(kernel, grid=(1,), out_shape=tuple((jax.ShapeDtypeStruct(s...]
    ppermute x14 -> x13, starting transfers between devices: 13.2 us -> 14.3 us  [local(): move = lambda array, pairs: lax.ppermute(array, 'col', pairs)]
    unnamed x25 -> x32, local copies, waits for them, and re-layouts: 3.57 us -> 3.83 us
  transfers between devices with their start and end apart: 19 -> 19, of which waited for: 11 -> 12; matrix products, arithmetic and copies ran while one was open for 1% -> 1% of each run, Pallas kernels for 14% -> 14%
where the time goes in v4:
time: 142 us
  waiting for transfers between devices  50.2 us (35%)
  starting transfers between devices  46.3 us (33%)
  Pallas kernels  27.4 us (19%)
  between operations  13.2 us (9%)
  local copies, waits for them, and re-layouts  4.78 us (3%)
    all_to_all x3, starting transfers between devices, local(): over_row = lambda array: lax.all_to_all(array, 'row', 0, 0, tiled=True)  31.9 us
    ppermute x13, waiting for transfers between devices, local(): move = lambda array, pairs: lax.ppermute(array, 'col', pairs)  29.2 us
    pallas_call x9, Pallas kernels, call(): pl.pallas_call(kernel, grid=(1,), out_shape=tuple((jax.ShapeDtypeStruct(s...  27.4 us
    all_gather x3, waiting for transfers between devices, local(): gather = lambda array: lax.all_gather(array, 'col', axis=0, tiled=False)  20.2 us
    ppermute x13, starting transfers between devices, local(): move = lambda array, pairs: lax.ppermute(array, 'col', pairs)  14.3 us
    unnamed x32, local copies, waits for them, and re-layouts  3.83 us
  transfers between devices with their start and end apart: 19, of which 12 were waited for; matrix products, arithmetic and copies ran while one was open for 1% of the time, Pallas kernels for 14%

profile of v4, /device:TPU:2, one launch (start us, length us, event | category | flops | bytes accessed | tf_op | source)
XLA Modules:
  0.0 141.8 jit_solution(16514766784630908541)
XLA Ops:
  6.5 0.0 all-gather.9.cloned.1.call-start
  6.5 2.6 %level0.1 = (f32[32,256]{1,0:T(8,128)}, bf16[32,32,256]{2,1,0:T(8,128)(2,1)}, bf16[784,256]{1,0:T(8,128)(2,1)}) custom-call(s32[1]{0:T(128)} %bitcast.place, s32[3,1,6]{2,1,0:T(1,128)} %bitcast.23, bf16[4,256,256]{2,1,0:T(8,128)(2,1)} %rhs.7, bf16[4,256,256]{2,1,0:T(8,128)(2,1)} %dinv.7, bf16[6,3,256,256]{3,2,1,0:T(8,128)(2,1)} %bitcast.8), custom_call_target="tpu_custom_call" | custom-call | bytes 2097152 | tf_op jit(solution)/shard_map/level0/pallas_call | solution.py:49
  9.2 0.0 all-gather.9.cloned.1.call-update
  9.2 0.0 all-gather.5.cloned.1.call-start
  9.3 0.0 copy-done
  9.3 1.0 fusion
  10.2 0.0 all-gather.5.cloned.1.call-update
  10.2 0.0 all-gather.7.cloned.1.call-start
  10.3 0.7 all-gather.7.cloned.1.call-update
  11.0 0.1 collective-permute-start.3
  11.1 11.6 %all-to-all-start = ((bf16[32,32,256]{2,1,0:T(8,128)(2,1)}), bf16[32,32,256]{2,1,0:T(8,128)(2,1)S(1)}, u32[]{:S(2)}, u32[]{:S(2)}) async-start(bf16[32,32,256]{2,1,0:T(8,128)(2,1)} %get-tuple-element.38), calls=%async_computation | async-start | bytes 1048576 | tf_op jit(solution)/shard_map/all_to_all | solution.py:226
  22.7 20.2 %all-gather.9.cloned.1.call-done = bf16[6272,256]{1,0:T(8,128)(2,1)} async-done(((bf16[784,256]{1,0:T(8,128)(2,1)}), bf16[6272,256]{1,0:T(8,128)(2,1)}) %all-gather.9.cloned.1.call-update) | async-done | bytes 3211280 | tf_op jit(solution)/shard_map/all_gather | solution.py:228
  42.9 1.4 %cols.1.table = s32[8,256]{1,0:T(8,128)} custom-call(bf16[8,784,256]{2,1,0:T(8,128)(2,1)} %bitcast.14), custom_call_target="tpu_custom_call" | custom-call | tf_op jit(solution)/shard_map/cols/pallas_call | solution.py:49
  44.4 0.0 all-to-all-done.known
  44.4 0.8 copy-done.2
  45.2 4.7 %level1.1 = (f32[32,256]{1,0:T(8,128)}, bf16[32,32,256]{2,1,0:T(8,128)(2,1)}) custom-call(s32[1]{0:T(128)} %bitcast.place, s32[8,256]{1,0:T(8,128)} %cols.1.table, s32[1,6]{1,0:T(1,128)} %bitcast.18, bf16[4,256,256]{2,1,0:T(8,128)(2,1)} %rhs.7, bf16[4,256,256]{2,1,0:T(8,128)(2,1)} %dinv.7, bf16[32,32,256]{2,1,0:T(8,128)(2,1)} %copy-done.2, ...), custom_call_target="tpu_custom_call" | custom-call | flops 100663296 | bytes 3145728 | tf_op jit(solution)/shard_map/level1/pallas_call | solution.py:49
  49.9 10.2 %all-to-all-start.1 = ((bf16[32,32,256]{2,1,0:T(8,128)(2,1)}), bf16[32,32,256]{2,1,0:T(8,128)(2,1)S(1)}, u32[]{:S(2)}, u32[]{:S(2)}) async-start(bf16[32,32,256]{2,1,0:T(8,128)(2,1)} %get-tuple-element.39), calls=%async_computation.1 | async-start | bytes 1048576 | tf_op jit(solution)/shard_map/all_to_all | solution.py:226
  60.1 2.0 %pick13.1 = (bf16[2,6,32,256]{3,2,1,0:T(8,128)(2,1)}, bf16[2,6,32,256]{3,2,1,0:T(8,128)(2,1)}, bf16[2,6,32,256]{3,2,1,0:T(8,128)(2,1)}, bf16[2,6,32,256]{3,2,1,0:T(8,128)(2,1)}) custom-call(s32[1]{0:T(128)} %bitcast.place, s32[8,256]{1,0:T(8,128)} %cols.1.table, bf16[32,32,256]{2,1,0:T(8,128)(2,1)} %copy-done.2), custom_call_target="tpu_custom_call" | custom-call | bytes 2097152 | tf_op jit(solution)/shard_map/pick13/pallas_call | solution.py:49
  62.1 0.4 collective-permute-start
  62.5 2.6 %collective-permute-start.1 = (bf16[2,6,32,256]{3,2,1,0:T(8,128)(2,1)}, bf16[2,6,32,256]{3,2,1,0:T(8,128)(2,1)S(1)}, u32[]{:S(2)}, u32[]{:S(2)}) collective-permute-start(bf16[2,6,32,256]{3,2,1,0:T(8,128)(2,1)} %get-tuple-element.44), channel_id=1, source_target_pairs={{0,4},{1,5},{2,6},{3,7},{4,0},{5,1},{6,2},{7,3},{8,12},{9,13},{10,... | collective-permute-start | bytes 589832 | tf_op jit(solution)/shard_map/ppermute | solution.py:225
  65.1 1.3 collective-permute-start.2
  66.3 0.0 collective-permute-done.3.refs_5_.refs_7_.refs_9_
  66.3 9.4 %collective-permute-done.refs_1_ = bf16[2,6,32,256]{3,2,1,0:T(8,128)(2,1)S(1)} collective-permute-done((bf16[2,6,32,256]{3,2,1,0:T(8,128)(2,1)}, bf16[2,6,32,256]{3,2,1,0:T(8,128)(2,1)S(1)}, u32[]{:S(2)}, u32[]{:S(2)}) %collective-permute-start) | collective-permute-done | bytes 196640 | tf_op jit(solution)/shard_map/ppermute | solution.py:225
  75.7 6.4 %collective-permute-done.1.refs_2_ = bf16[2,6,32,256]{3,2,1,0:T(8,128)(2,1)S(1)} collective-permute-done((bf16[2,6,32,256]{3,2,1,0:T(8,128)(2,1)}, bf16[2,6,32,256]{3,2,1,0:T(8,128)(2,1)S(1)}, u32[]{:S(2)}, u32[]{:S(2)}) %collective-permute-start.1) | collective-permute-done | bytes 196640 | tf_op jit(solution)/shard_map/ppermute | solution.py:225
  82.1 0.0 collective-permute-done.2.refs_3_
  82.1 0.0 copy-done.4
  82.1 0.7 copy-done.5
  82.8 0.1 copy-done.6
  82.8 3.0 %partial13.1 = (f32[32,256]{1,0:T(8,128)}, f32[32,256]{1,0:T(8,128)}, f32[32,256]{1,0:T(8,128)}, f32[32,256]{1,0:T(8,128)}, f32[32,256]{1,0:T(8,128)}, /*index=5...) custom-call(s32[1]{0:T(128)} %bitcast.place, s32[1,6]{1,0:T(1,128)} %bitcast.19, ...), custom_call_target="tpu_custom_call" | custom-call | flops 201326592 | bytes 2097152 | tf_op jit(solution)/shard_map/partial13/pallas_call | solution.py:49
  85.8 0.5 collective-permute-start.4
  86.3 1.0 collective-permute-start.5
  87.3 1.3 collective-permute-start.6
  88.6 1.4 collective-permute-done.4.refs_1_
  90.0 2.0 %collective-permute-done.5.refs_2_ = f32[32,256]{1,0:T(8,128)S(1)} collective-permute-done((f32[32,256]{1,0:T(8,128)}, f32[32,256]{1,0:T(8,128)S(1)}, u32[]{:S(2)}, u32[]{:S(2)}) %collective-permute-start.5) | collective-permute-done | bytes 32800 | tf_op jit(solution)/shard_map/ppermute | solution.py:225
  92.0 0.7 collective-permute-done.6.refs_3_
  92.7 0.0 all-to-all-done.1.known
  92.7 0.0 copy-done.13
  92.7 0.0 copy-done.14
  92.7 0.6 copy-done.15
  93.3 0.2 copy-done.1
  93.5 4.7 %level2.1 = (f32[32,256]{1,0:T(8,128)}, bf16[32,32,256]{2,1,0:T(8,128)(2,1)}) custom-call(s32[1]{0:T(128)} %bitcast.place, s32[8,256]{1,0:T(8,128)} %cols.1.table, s32[1,6]{1,0:T(1,128)} %bitcast.20, bf16[4,256,256]{2,1,0:T(8,128)(2,1)} %rhs.7, bf16[4,256,256]{2,1,0:T(8,128)(2,1)} %dinv.7, bf16[32,32,256]{2,1,0:T(8,128)(2,1)} %copy-done.1, ...), custom_call_target="tpu_custom_call" | custom-call | flops 100663296 | bytes 3145728 | tf_op jit(solution)/shard_map/level2/pallas_call | solution.py:49
  98.2 10.2 %all-to-all-start.2 = ((bf16[32,32,256]{2,1,0:T(8,128)(2,1)}), bf16[32,32,256]{2,1,0:T(8,128)(2,1)S(1)}, u32[]{:S(2)}, u32[]{:S(2)}) async-start(bf16[32,32,256]{2,1,0:T(8,128)(2,1)} %get-tuple-element.50), calls=%async_computation.2 | async-start | bytes 1048576 | tf_op jit(solution)/shard_map/all_to_all | solution.py:226
  108.4 1.8 %pick4.1 = (bf16[1,6,32,256]{3,2,1,0:T(8,128)(2,1)}, bf16[1,6,32,256]{3,2,1,0:T(8,128)(2,1)}, bf16[1,6,32,256]{3,2,1,0:T(8,128)(2,1)}, bf16[1,6,32,256]{3,2,1,0:T(8,128)(2,1)}) custom-call(s32[1]{0:T(128)} %bitcast.place, s32[8,256]{1,0:T(8,128)} %cols.1.table, bf16[32,32,256]{2,1,0:T(8,128)(2,1)} %copy-done.1), custom_call_target="tpu_custom_call" | custom-call | bytes 2097152 | tf_op jit(solution)/shard_map/pick4/pallas_call | solution.py:49
  110.2 0.9 collective-permute-start.7
  111.1 2.6 %collective-permute-start.8 = (bf16[1,6,32,256]{3,2,1,0:T(8,128)(2,1)}, bf16[1,6,32,256]{3,2,1,0:T(8,128)(2,1)S(1)}, u32[]{:S(2)}, u32[]{:S(2)}) collective-permute-start(bf16[1,6,32,256]{3,2,1,0:T(8,128)(2,1)} %get-tuple-element.54), channel_id=1, source_target_pairs={{0,4},{1,5},{2,6},{3,7},{4,0},{5,1},{6,2},{7,3},{8,12},{9,13},{10,... | collective-permute-start | bytes 294920 | tf_op jit(solution)/shard_map/ppermute | solution.py:225
  113.7 0.4 collective-permute-start.9
  114.1 3.1 %collective-permute-done.7.refs_1_ = bf16[1,6,32,256]{3,2,1,0:T(8,128)(2,1)S(1)} collective-permute-done((bf16[1,6,32,256]{3,2,1,0:T(8,128)(2,1)}, bf16[1,6,32,256]{3,2,1,0:T(8,128)(2,1)S(1)}, u32[]{:S(2)}, u32[]{:S(2)}) %collective-permute-start.7) | collective-permute-done | bytes 98336 | tf_op jit(solution)/shard_map/ppermute | solution.py:225
  117.3 1.1 collective-permute-done.8.refs_2_
  118.4 0.2 collective-permute-done.9.refs_3_
  118.6 0.0 copy-done.7
  118.6 0.5 copy-done.8
  119.0 0.2 copy-done.9
  119.2 2.4 %partial4.1 = (f32[32,256]{1,0:T(8,128)}, f32[32,256]{1,0:T(8,128)}, f32[32,256]{1,0:T(8,128)}, f32[32,256]{1,0:T(8,128)}) custom-call(s32[1]{0:T(128)} %bitcast.place, s32[1,6]{1,0:T(1,128)} %bitcast.21, bf16[1,6,32,256]{3,2,1,0:T(8,128)(2,1)} %get-tuple-element.52.refs_0_, bf16[1,6,32,256]{3,2,1,0:T(8,128)(2,1)} %copy-done.7, ...), custom_call_target="tpu_custom_call" | custom-call | flops 201326592 | bytes 2097152 | tf_op jit(solution)/shard_map/partial4/pallas_call | solution.py:49
  121.6 2.3 %collective-permute-start.10 = (f32[32,256]{1,0:T(8,128)}, f32[32,256]{1,0:T(8,128)S(1)}, u32[]{:S(2)}, u32[]{:S(2)}) collective-permute-start(f32[32,256]{1,0:T(8,128)} %get-tuple-element.61), channel_id=1, source_target_pairs={{0,6},{1,7},{2,0},{3,1},{4,2},{5,3},{6,4},{7,5},{8,14},{9,15},{10,... | collective-permute-start | bytes 98312 | tf_op jit(solution)/shard_map/ppermute | solution.py:225
  123.9 0.4 collective-permute-start.11
  124.3 0.6 collective-permute-start.12
  124.9 1.0 collective-permute-done.10.refs_1_
  125.8 3.7 %collective-permute-done.11.refs_2_ = f32[32,256]{1,0:T(8,128)S(1)} collective-permute-done((f32[32,256]{1,0:T(8,128)}, f32[32,256]{1,0:T(8,128)S(1)}, u32[]{:S(2)}, u32[]{:S(2)}) %collective-permute-start.11) | collective-permute-done | bytes 32800 | tf_op jit(solution)/shard_map/ppermute | solution.py:225
  129.6 0.3 collective-permute-done.12.refs_3_
  129.9 0.0 all-to-all-done.2.known
  129.9 0.3 copy-done.11
  130.2 0.3 copy-done.12
  130.5 0.2 copy-done.3
  130.7 4.6 %level3.1 = f32[4,32,256]{2,1,0:T(8,128)} custom-call(s32[1]{0:T(128)} %bitcast.place, s32[8,256]{1,0:T(8,128)} %cols.1.table, s32[1,6]{1,0:T(1,128)} %bitcast.22, bf16[4,256,256]{2,1,0:T(8,128)(2,1)} %rhs.7, bf16[4,256,256]{2,1,0:T(8,128)(2,1)} %dinv.7, bf16[32,32,256]{2,1,0:T(8,128)(2,1)} %copy-done.3, ...), custom_call_target="tpu_custom_call" | custom-call | flops 100663296 | bytes 3145728 | tf_op jit(solution)/shard_map/level3/pallas_call | solution.py:49
  (19 shorter events, 0.0 us)
Async XLA Ops:
  6.5 2.7 %copy-start = (bf16[6,256,3,256]{3,1,2,0:T(8,128)(2,1)S(1)}, bf16[6,256,3,256]{3,1,2,0:T(8,128)(2,1)}, u32[]{:S(2)}) copy-start(bf16[6,256,3,256]{3,1,2,0:T(8,128)(2,1)} %param.7) | copy-start | bytes 7077892
  6.5 36.4 %all-gather.9.cloned.1.call-start = ((), (), s32[]{:S(2)}) async-start(), calls=%async_computation.5 | async-start | bytes 3612672 | tf_op jit(solution)/shard_map/all_gather | solution.py:228
  9.2 79.4 %all-gather.5.cloned.1.call-start = ((), (), s32[]{:S(2)}) async-start(), calls=%async_computation.3 | async-start | bytes 3538944 | tf_op jit(solution)/shard_map/all_gather | solution.py:228
  10.2 114.6 %all-gather.7.cloned.1.call-start = ((), (), s32[]{:S(2)}) async-start(), calls=%async_computation.4 | async-start | bytes 3538944 | tf_op jit(solution)/shard_map/all_gather | solution.py:228
  11.0 55.4 %collective-permute-start.3 = (bf16[6,3,256,256]{3,2,1,0:T(8,128)(2,1)S(1)}, bf16[6,3,256,256]{3,2,1,0:T(8,128)(2,1)}, u32[]{:S(2)}, u32[]{:S(2)}) collective-permute-start(bf16[6,3,256,256]{3,2,1,0:T(8,128)(2,1)S(1)} %bitcast.13), channel_id=1, source_target_pairs={{0,1},{1,0},{2,3},{3,2},{4,5},{5,4},{6,7},{7,6},{8,9},{9,8},{10,11... | collective-permute-start | bytes 7077896 | tf_op jit(solution)/shard_map/ppermute | solution.py:225
  11.1 33.3 %all-to-all-start = ((bf16[32,32,256]{2,1,0:T(8,128)(2,1)}), bf16[32,32,256]{2,1,0:T(8,128)(2,1)S(1)}, u32[]{:S(2)}, u32[]{:S(2)}) async-start(bf16[32,32,256]{2,1,0:T(8,128)(2,1)} %get-tuple-element.38), calls=%async_computation | async-start | bytes 1048576 | tf_op jit(solution)/shard_map/all_to_all | solution.py:226
  44.4 0.8 copy-start.2
  49.9 42.8 %all-to-all-start.1 = ((bf16[32,32,256]{2,1,0:T(8,128)(2,1)}), bf16[32,32,256]{2,1,0:T(8,128)(2,1)S(1)}, u32[]{:S(2)}, u32[]{:S(2)}) async-start(bf16[32,32,256]{2,1,0:T(8,128)(2,1)} %get-tuple-element.39), calls=%async_computation.1 | async-start | bytes 1048576 | tf_op jit(solution)/shard_map/all_to_all | solution.py:226
  62.1 13.6 %collective-permute-start = (bf16[2,6,32,256]{3,2,1,0:T(8,128)(2,1)}, bf16[2,6,32,256]{3,2,1,0:T(8,128)(2,1)S(1)}, u32[]{:S(2)}, u32[]{:S(2)}) collective-permute-start(bf16[2,6,32,256]{3,2,1,0:T(8,128)(2,1)} %get-tuple-element.43), channel_id=1, source_target_pairs={{0,2},{1,3},{2,4},{3,5},{4,6},{5,7},{6,0},{7,1},{8,10},{9,11},{10,... | collective-permute-start | bytes 589832 | tf_op jit(solution)/shard_map/ppermute | solution.py:225
  62.5 19.6 %collective-permute-start.1 = (bf16[2,6,32,256]{3,2,1,0:T(8,128)(2,1)}, bf16[2,6,32,256]{3,2,1,0:T(8,128)(2,1)S(1)}, u32[]{:S(2)}, u32[]{:S(2)}) collective-permute-start(bf16[2,6,32,256]{3,2,1,0:T(8,128)(2,1)} %get-tuple-element.44), channel_id=1, source_target_pairs={{0,4},{1,5},{2,6},{3,7},{4,0},{5,1},{6,2},{7,3},{8,12},{9,13},{10,... | collective-permute-start | bytes 589832 | tf_op jit(solution)/shard_map/ppermute | solution.py:225
  65.1 17.0 %collective-permute-start.2 = (bf16[2,6,32,256]{3,2,1,0:T(8,128)(2,1)}, bf16[2,6,32,256]{3,2,1,0:T(8,128)(2,1)S(1)}, u32[]{:S(2)}, u32[]{:S(2)}) collective-permute-start(bf16[2,6,32,256]{3,2,1,0:T(8,128)(2,1)} %get-tuple-element.45), channel_id=1, source_target_pairs={{0,6},{1,7},{2,0},{3,1},{4,2},{5,3},{6,4},{7,5},{8,14},{9,15},{10,... | collective-permute-start | bytes 589832 | tf_op jit(solution)/shard_map/ppermute | solution.py:225
  75.7 6.4 %copy-start.4 = (bf16[2,6,32,256]{3,2,1,0:T(8,128)(2,1)}, bf16[2,6,32,256]{3,2,1,0:T(8,128)(2,1)S(1)}, u32[]{:S(2)}) copy-start(bf16[2,6,32,256]{3,2,1,0:T(8,128)(2,1)S(1)} %collective-permute-done.refs_1_) | copy-start | bytes 589828
  82.1 0.7 copy-start.5
  82.1 0.8 copy-start.6
  85.8 4.2 %collective-permute-start.4 = (f32[32,256]{1,0:T(8,128)}, f32[32,256]{1,0:T(8,128)S(1)}, u32[]{:S(2)}, u32[]{:S(2)}) collective-permute-start(f32[32,256]{1,0:T(8,128)} %get-tuple-element.47), channel_id=1, source_target_pairs={{0,6},{1,7},{2,0},{3,1},{4,2},{5,3},{6,4},{7,5},{8,14},{9,15},{10,... | collective-permute-start | bytes 98312 | tf_op jit(solution)/shard_map/ppermute | solution.py:225
  86.3 5.7 %collective-permute-start.5 = (f32[32,256]{1,0:T(8,128)}, f32[32,256]{1,0:T(8,128)S(1)}, u32[]{:S(2)}, u32[]{:S(2)}) collective-permute-start(f32[32,256]{1,0:T(8,128)} %get-tuple-element.48), channel_id=1, source_target_pairs={{0,4},{1,5},{2,6},{3,7},{4,0},{5,1},{6,2},{7,3},{8,12},{9,13},{10,... | collective-permute-start | bytes 98312 | tf_op jit(solution)/shard_map/ppermute | solution.py:225
  87.3 5.4 %collective-permute-start.6 = (f32[32,256]{1,0:T(8,128)}, f32[32,256]{1,0:T(8,128)S(1)}, u32[]{:S(2)}, u32[]{:S(2)}) collective-permute-start(f32[32,256]{1,0:T(8,128)} %get-tuple-element.49), channel_id=1, source_target_pairs={{0,2},{1,3},{2,4},{3,5},{4,6},{5,7},{6,0},{7,1},{8,10},{9,11},{10,... | collective-permute-start | bytes 98312 | tf_op jit(solution)/shard_map/ppermute | solution.py:225
  90.0 2.7 %copy-start.13 = (f32[32,256]{1,0:T(8,128)}, f32[32,256]{1,0:T(8,128)S(1)}, u32[]{:S(2)}) copy-start(f32[32,256]{1,0:T(8,128)S(1)} %collective-permute-done.4.refs_1_) | copy-start | bytes 98308
  92.0 0.7 copy-start.14
  92.7 0.6 copy-start.15
  92.7 0.8 copy-start.1
  98.2 31.6 %all-to-all-start.2 = ((bf16[32,32,256]{2,1,0:T(8,128)(2,1)}), bf16[32,32,256]{2,1,0:T(8,128)(2,1)S(1)}, u32[]{:S(2)}, u32[]{:S(2)}) async-start(bf16[32,32,256]{2,1,0:T(8,128)(2,1)} %get-tuple-element.50), calls=%async_computation.2 | async-start | bytes 1048576 | tf_op jit(solution)/shard_map/all_to_all | solution.py:226
  110.2 7.0 %collective-permute-start.7 = (bf16[1,6,32,256]{3,2,1,0:T(8,128)(2,1)}, bf16[1,6,32,256]{3,2,1,0:T(8,128)(2,1)S(1)}, u32[]{:S(2)}, u32[]{:S(2)}) collective-permute-start(bf16[1,6,32,256]{3,2,1,0:T(8,128)(2,1)} %get-tuple-element.53), channel_id=1, source_target_pairs={{0,2},{1,3},{2,4},{3,5},{4,6},{5,7},{6,0},{7,1},{8,10},{9,11},{10,... | collective-permute-start | bytes 294920 | tf_op jit(solution)/shard_map/ppermute | solution.py:225
  111.1 7.3 %collective-permute-start.8 = (bf16[1,6,32,256]{3,2,1,0:T(8,128)(2,1)}, bf16[1,6,32,256]{3,2,1,0:T(8,128)(2,1)S(1)}, u32[]{:S(2)}, u32[]{:S(2)}) collective-permute-start(bf16[1,6,32,256]{3,2,1,0:T(8,128)(2,1)} %get-tuple-element.54), channel_id=1, source_target_pairs={{0,4},{1,5},{2,6},{3,7},{4,0},{5,1},{6,2},{7,3},{8,12},{9,13},{10,... | collective-permute-start | bytes 294920 | tf_op jit(solution)/shard_map/ppermute | solution.py:225
  113.7 4.8 %collective-permute-start.9 = (bf16[1,6,32,256]{3,2,1,0:T(8,128)(2,1)}, bf16[1,6,32,256]{3,2,1,0:T(8,128)(2,1)S(1)}, u32[]{:S(2)}, u32[]{:S(2)}) collective-permute-start(bf16[1,6,32,256]{3,2,1,0:T(8,128)(2,1)} %get-tuple-element.55), channel_id=1, source_target_pairs={{0,6},{1,7},{2,0},{3,1},{4,2},{5,3},{6,4},{7,5},{8,14},{9,15},{10,... | collective-permute-start | bytes 294920 | tf_op jit(solution)/shard_map/ppermute | solution.py:225
  117.3 1.3 copy-start.7
  118.4 0.6 copy-start.8
  118.6 0.6 copy-start.9
  121.6 4.2 %collective-permute-start.10 = (f32[32,256]{1,0:T(8,128)}, f32[32,256]{1,0:T(8,128)S(1)}, u32[]{:S(2)}, u32[]{:S(2)}) collective-permute-start(f32[32,256]{1,0:T(8,128)} %get-tuple-element.61), channel_id=1, source_target_pairs={{0,6},{1,7},{2,0},{3,1},{4,2},{5,3},{6,4},{7,5},{8,14},{9,15},{10,... | collective-permute-start | bytes 98312 | tf_op jit(solution)/shard_map/ppermute | solution.py:225
  123.9 5.7 %collective-permute-start.11 = (f32[32,256]{1,0:T(8,128)}, f32[32,256]{1,0:T(8,128)S(1)}, u32[]{:S(2)}, u32[]{:S(2)}) collective-permute-start(f32[32,256]{1,0:T(8,128)} %get-tuple-element.62), channel_id=1, source_target_pairs={{0,4},{1,5},{2,6},{3,7},{4,0},{5,1},{6,2},{7,3},{8,12},{9,13},{10,... | collective-permute-start | bytes 98312 | tf_op jit(solution)/shard_map/ppermute | solution.py:225
  124.3 5.6 %collective-permute-start.12 = (f32[32,256]{1,0:T(8,128)}, f32[32,256]{1,0:T(8,128)S(1)}, u32[]{:S(2)}, u32[]{:S(2)}) collective-permute-start(f32[32,256]{1,0:T(8,128)} %get-tuple-element.63), channel_id=1, source_target_pairs={{0,2},{1,3},{2,4},{3,5},{4,6},{5,7},{6,0},{7,1},{8,10},{9,11},{10,... | collective-permute-start | bytes 98312 | tf_op jit(solution)/shard_map/ppermute | solution.py:225
  125.8 4.1 %copy-start.10 = (f32[32,256]{1,0:T(8,128)}, f32[32,256]{1,0:T(8,128)S(1)}, u32[]{:S(2)}) copy-start(f32[32,256]{1,0:T(8,128)S(1)} %collective-permute-done.10.refs_1_) | copy-start | bytes 98308
  129.6 0.6 copy-start.11
  129.9 0.6 copy-start.12
  129.9 0.8 copy-start.3
Sparse Core Ops, SparseCore 0:
  9.3 33.5 all-gather.8
  44.7 37.6 all-gather.4
  84.3 32.2 all-gather.6

commit v5 on v4

--- a/solution.py
+++ b/solution.py
@@ -13,10 +13,7 @@
 SLOTS = 3
 PLACES = 8
 CHIPS = 4
-PAIRS = 6
 NT = 32
-EXTRA = 16
-CHUNK = SLOTS * SIZE + EXTRA
 VMEM_BYTES = 56 * 1024 * 1024
 SMEM = pl.BlockSpec(memory_space=pltpu.SMEM)
 ANY = pl.BlockSpec(memory_space=pl.ANY)
@@ -59,72 +56,49 @@
     )(*args)
 
 
-def first_kernel(place, cols, rhs, dinv, tiles, answer, spread, chunk):
+def first_kernel(place, rhs, dinv, answer, spread):
     residual = probe_rows(place[0], rhs[0]).astype(BF16)
     result = dot_nt(residual, dinv[0])
     answer[...] = result
     spread_out(result, spread)
-    for slot in range(SLOTS):
-        chunk[slot * SIZE : (slot + 1) * SIZE] = tiles[0, slot]
-    lane = lax.broadcasted_iota(jnp.int32, (EXTRA, SIZE), 1)
-    packed = jnp.zeros((EXTRA, SIZE), jnp.int32)
-    for pair in range(PAIRS):
-        for slot in range(SLOTS):
-            packed = jnp.where(lane == pair * SLOTS + slot, cols[slot, 0, pair], packed)
-    chunk[SLOTS * SIZE :] = packed.astype(F32).astype(BF16)
-
-
-def first_call(place, cols, rhs, dinv, tiles):
+
+
+def first_call(place, rhs, dinv):
     return call(
         first_kernel,
         "level0",
-        [((BLOCK, SIZE), F32), ((NT, BLOCK, SIZE), BF16), ((CHUNK, SIZE), BF16)],
-        [SMEM, SMEM, block_of((1, SIZE, SIZE), 0), block_of((1, SIZE, SIZE), 0), block_of((1, SLOTS, SIZE, SIZE), 0)],
-        [block_of((BLOCK, SIZE)), block_of((NT, BLOCK, SIZE)), block_of((CHUNK, SIZE))],
-        (place, cols, rhs, dinv, tiles),
-        moved=2**21,
-    )
-
-
-def decode_kernel(gathered, out):
-    for place in range(PLACES):
-        out[pl.ds(place, 1), :] = gathered[place, 0:1, :].astype(F32).astype(jnp.int32)
-
-
-def decode_call(gathered):
-    return call(
-        decode_kernel,
-        "cols",
-        [((PLACES, SIZE), jnp.int32)],
-        [pl.BlockSpec((PLACES, EXTRA, SIZE), lambda i: (0, SLOTS * SIZE // EXTRA, 0))],
-        [block_of((PLACES, SIZE))],
-        (gathered,),
-    )[0]
+        [((BLOCK, SIZE), F32), ((NT, BLOCK, SIZE), BF16)],
+        [SMEM, block_of((1, SIZE, SIZE), 0), block_of((1, SIZE, SIZE), 0)],
+        [block_of((BLOCK, SIZE)), block_of((NT, BLOCK, SIZE))],
+        (place, rhs, dinv),
+        moved=2**22,
+    )
 
 
 def masked(block, alive):
     return jnp.where(alive, block, jnp.zeros_like(block))
 
 
-def pick_kernel(pairs, place, table, known, *outs):
-    chip = lax.div(place[0], 2)
+def pick_kernel(pairs, place, here, there, known, *outs):
+    mine = lax.rem(place[0], 2)
     for step in range(CHIPS):
+        turn = (CHIPS - step) % CHIPS
         for core in range(2):
-            want = lax.rem(chip + step, CHIPS) * 2 + core
             for n, pair in enumerate(pairs):
                 for slot in range(SLOTS):
-                    outs[step][n, core * SLOTS + slot] = known[table[want, pair * SLOTS + slot]]
-
-
-def pick_call(name, pairs, place, table, known):
+                    at = jnp.where(mine == core, here[turn, slot, pair], there[turn, slot, pair])
+                    outs[step][n, core * SLOTS + slot] = known[at]
+
+
+def pick_call(name, pairs, place, here, there, known):
     shape = (len(pairs), 2 * SLOTS, BLOCK, SIZE)
     return call(
         functools.partial(pick_kernel, pairs),
         name,
         [(shape, BF16)] * CHIPS,
-        [SMEM, SMEM, block_of((NT, BLOCK, SIZE))],
+        [SMEM, SMEM, SMEM, block_of((NT, BLOCK, SIZE))],
         [block_of(shape)] * CHIPS,
-        (place, table, known),
+        (place, here, there, known),
         moved=2**21,
     )
 
@@ -168,27 +142,28 @@
     )
 
 
-def level_kernel(pair, returned, earlier, place, table, live, rhs, dinv, known, tiles, *refs):
+def level_kernel(pair, returned, earlier, place, here, there, live, rhs, dinv, known, tiles, *refs):
     refs = list(refs)
     back = [refs.pop(0) for _ in range(returned)]
     before = [refs.pop(0) for _ in range(earlier)]
     held, sems = refs[-2:]
-    copies = []
-    for n in range(CHIPS):
-        two = pl.ds(2 * n, 2)
-        source = tiles.at[two, pl.ds(0, SLOTS * SIZE)]
-        copies.append(pltpu.make_async_copy(source, held.at[two], sems.at[n]))
+    chip, core = lax.div(place[0], 2), lax.rem(place[0], 2)
+    chips = [lax.rem(chip + CHIPS - d, CHIPS) for d in range(CHIPS)]
+    copies = [
+        pltpu.make_async_copy(tiles.at[pl.ds(2 * chips[d], 2)], held.at[pl.ds(2 * d, 2)], sems.at[d]) for d in range(CHIPS)
+    ]
     for copy in copies:
         copy.start()
     total = probe_rows(place[0], rhs[0])
     for sums in back:
         total = total - sums[...]
-    for owner in range(PLACES):
-        if owner % 2 == 0:
-            copies[owner // 2].wait()
-        for slot in range(SLOTS):
-            block = masked(known[table[owner, pair * SLOTS + slot]], owner * SLOTS + slot < live[0, pair])
-            total = total - dot_nt(block, held[owner, slot * SIZE : (slot + 1) * SIZE])
+    for d in range(CHIPS):
+        copies[d].wait()
+        for cols, side in ((here, core), (there, 1 - core)):
+            first = (2 * chips[d] + side) * SLOTS
+            for slot in range(SLOTS):
+                block = masked(known[cols[d, slot, pair]], first + slot < live[0, pair])
+                total = total - dot_nt(block, held[2 * d + side, slot * SIZE : (slot + 1) * SIZE])
     result = dot_nt(total.astype(BF16), dinv[0])
     if earlier:
         for n in range(earlier):
@@ -199,7 +174,7 @@
     spread_out(result, refs[1])
 
 
-def level_call(level, pair, place, table, live, rhs, dinv, known, tiles, back, earlier):
+def level_call(level, pair, place, here, there, live, rhs, dinv, known, tiles, back, earlier):
     flat, pick = block_of((BLOCK, SIZE)), block_of((1, SIZE, SIZE), level)
     if earlier:
         shapes, outs = [((level + 1, BLOCK, SIZE), F32)], [block_of((level + 1, BLOCK, SIZE))]
@@ -210,9 +185,9 @@
         functools.partial(level_kernel, pair, len(back), len(earlier)),
         "level%d" % level,
         shapes,
-        [SMEM] * 3 + [pick, pick, block_of((NT, BLOCK, SIZE)), ANY] + [flat] * (len(back) + len(earlier)),
+        [SMEM] * 4 + [pick, pick, block_of((NT, BLOCK, SIZE)), ANY] + [flat] * (len(back) + len(earlier)),
         outs,
-        (place, table, live, rhs, dinv, known, tiles, *back, *earlier),
+        (place, here, there, live, rhs, dinv, known, tiles, *back, *earlier),
         [pltpu.VMEM((PLACES, SLOTS * SIZE, SIZE), BF16), pltpu.SemaphoreType.DMA((CHIPS,))],
         flops=2 * 24 * BLOCK * SIZE * SIZE,
         moved=24 * SIZE * SIZE * 2,
@@ -229,12 +204,15 @@
     piece = lambda array, pair: array[pair].reshape(SLOTS * SIZE, SIZE)
     live = live.transpose(1, 0)
 
-    answer0, spread0, chunk = first_call(place, cols.transpose(2, 1, 0), rhs, dinv, tiles)
-    gathered0 = gather(chunk)
+    own = cols.transpose(2, 1, 0).reshape(SLOTS, -1)
+    here = jnp.stack([own] + [move(own, TURN[d]) for d in range(1, CHIPS)])
+    there = move(here, SWAP)
+    answer0, spread0 = first_call(place, rhs, dinv)
+    gathered0 = gather(piece(tiles, 0))
     later, spread0 = lax.optimization_barrier((tiles, spread0))
     gathered2 = gather(piece(later, 2))
     gathered5 = gather(piece(later, 5))
-    swapped = move(tiles, SWAP)
+    swapped = move(later, SWAP)
 
     def send(picked):
         return [picked[0]] + [move(picked[d], TURN[d]) for d in range(1, CHIPS)]
@@ -243,22 +221,27 @@
         return [sums[0]] + [move(sums[d], TURN[CHIPS - d]) for d in range(1, CHIPS)]
 
     known0 = over_row(spread0)
-    table = decode_call(gathered0)
-    answer1, spread1 = level_call(1, 0, place, table, live, rhs, dinv, known0, gathered0, [], [])
+    picked = pick_call("pick13", (1, 3), place, here, there, known0)
+    known0, *picked = lax.optimization_barrier((known0, *picked))
+    got = send(picked)
+    answer1, spread1 = level_call(1, 0, place, here, there, live, rhs, dinv, known0, gathered0, [], [])
+    spread1, *got = lax.optimization_barrier((spread1, *got))
     known1 = over_row(spread1)
 
-    known0, spread1 = lax.optimization_barrier((known0, spread1))
-    got = send(pick_call("pick13", (1, 3), place, table, known0))
     sums = partial_call("partial13", (1, 3), place, live, got, [], tiles, swapped)
     sums2, sums3 = sums[:CHIPS], sums[CHIPS:]
-    answer2, spread2 = level_call(2, 2, place, table, live, rhs, dinv, known1, gathered2, give_back(sums2), [])
+    back2 = give_back(sums2)
+    known1, *back2 = lax.optimization_barrier((known1, *back2))
+    picked = pick_call("pick4", (4,), place, here, there, known1)
+    known1, *picked = lax.optimization_barrier((known1, *picked))
+    got = send(picked)
+    answer2, spread2 = level_call(2, 2, place, here, there, live, rhs, dinv, known1, gathered2, back2, [])
+    spread2, *got = lax.optimization_barrier((spread2, *got))
     known2 = over_row(spread2)
 
-    known1, spread2 = lax.optimization_barrier((known1, spread2))
-    got = send(pick_call("pick4", (4,), place, table, known1))
     sums3 = partial_call("partial4", (4,), place, live, got, sums3, tiles, swapped)
     (solved,) = level_call(
-        3, 5, place, table, live, rhs, dinv, known2, gathered5, give_back(sums3), [answer0, answer1, answer2]
+        3, 5, place, here, there, live, rhs, dinv, known2, gathered5, give_back(sums3), [answer0, answer1, answer2]
     )
     return solved.transpose(0, 2, 1)
 

time: 142 us -> 125 us (0.88)
  waiting for transfers between devices: 50.2 us -> 31 us
  Pallas kernels: 27.4 us -> 25.5 us
  starting transfers between devices: 46.3 us -> 48 us
  local copies, waits for them, and re-layouts: 4.78 us -> 6.41 us
    ppermute x13 -> x17, waiting for transfers between devices: 29.2 us -> 9.87 us  [local(): move = lambda array, pairs: lax.ppermute(array, 'col', pairs)]
    all_to_all x3, waiting for transfers between devices: 0.01 us -> 14.5 us  [local(): over_row = lambda array: lax.all_to_all(array, 'row', 0, 0, tiled=True)]
    all_gather x3, waiting for transfers between devices: 20.2 us -> 5.9 us  [local(): gather = lambda array: lax.all_gather(array, 'col', axis=0, tiled=False)]
    ppermute x13 -> x17, starting transfers between devices: 14.3 us -> 25 us  [local(): move = lambda array, pairs: lax.ppermute(array, 'col', pairs)]
    all_to_all x3, starting transfers between devices: 31.9 us -> 22.9 us  [local(): over_row = lambda array: lax.all_to_all(array, 'row', 0, 0, tiled=True)]
    slice x1 -> x2, local copies, waits for them, and re-layouts: 0.95 us -> 3.97 us  [local(): piece = lambda array, pair: array[pair].reshape(SLOTS * SIZE, SIZE)]
    pallas_call x9 -> x8, Pallas kernels: 27.4 us -> 25.5 us  [call(): pl.pallas_call(kernel, grid=(1,), out_shape=tuple((jax.ShapeDtypeStruct(s...]
    unnamed x32 -> x39, local copies, waits for them, and re-layouts: 3.83 us -> 2.43 us
  transfers between devices with their start and end apart: 19 -> 23, of which waited for: 12 -> 10; matrix products, arithmetic and copies ran while one was open for 1% -> 2% of each run, Pallas kernels for 14% -> 17%
where the time goes in v5:
time: 125 us; the launch traced here: 124 us
  starting transfers between devices  48 us (38%)
  waiting for transfers between devices  31 us (25%)
  Pallas kernels  25.5 us (20%)
  between operations  13.4 us (11%)
  local copies, waits for them, and re-layouts  6.41 us (5%)
    pallas_call x8, Pallas kernels, call(): pl.pallas_call(kernel, grid=(1,), out_shape=tuple((jax.ShapeDtypeStruct(s...  25.5 us
    ppermute x17, starting transfers between devices, local(): move = lambda array, pairs: lax.ppermute(array, 'col', pairs)  25 us
    all_to_all x3, starting transfers between devices, local(): over_row = lambda array: lax.all_to_all(array, 'row', 0, 0, tiled=True)  22.9 us
    all_to_all x3, waiting for transfers between devices, local(): over_row = lambda array: lax.all_to_all(array, 'row', 0, 0, tiled=True)  14.5 us
    ppermute x17, waiting for transfers between devices, local(): move = lambda array, pairs: lax.ppermute(array, 'col', pairs)  9.87 us
    all_gather x3, waiting for transfers between devices, local(): gather = lambda array: lax.all_gather(array, 'col', axis=0, tiled=False)  5.9 us
    slice x2, local copies, waits for them, and re-layouts, local(): piece = lambda array, pair: array[pair].reshape(SLOTS * SIZE, SIZE)  3.97 us
  transfers between devices with their start and end apart: 23, of which 10 were waited for; matrix products, arithmetic and copies ran while one was open for 2% of the time, Pallas kernels for 17%

profile of v5, /device:TPU:2, one launch (start us, length us, event | category | flops | bytes accessed | tf_op | source)
XLA Modules:
  0.0 124.3 jit_solution(11472437109779327041)
XLA Ops:
  6.5 1.9 %slice.12 = bf16[1,3,256,256]{3,2,1,0:T(8,128)(2,1)} slice(bf16[6,3,256,256]{3,2,1,0:T(8,128)(2,1)} %bitcast.16), slice={[0:1], [0:3], [0:256], [0:256]} | slice | bytes 786432 | tf_op jit(solution)/shard_map/slice | solution.py:204
  8.5 0.0 all-gather.4.cloned.1.call-update
  8.5 0.0 all-gather.6.cloned.1.call-start
  8.6 2.1 %level0.1 = (f32[32,256]{1,0:T(8,128)}, bf16[32,32,256]{2,1,0:T(8,128)(2,1)}) custom-call(s32[1]{0:T(128)} %bitcast.place, bf16[4,256,256]{2,1,0:T(8,128)(2,1)} %rhs.7, bf16[4,256,256]{2,1,0:T(8,128)(2,1)} %dinv.7), custom_call_target="tpu_custom_call" | custom-call | bytes 4194304 | tf_op jit(solution)/shard_map/level0/pallas_call | solution.py:46
  10.7 2.0 %fusion = (bf16[1,3,256,256]{3,2,1,0:T(8,128)(2,1)}, bf16[1,3,256,256]{3,2,1,0:T(8,128)(2,1)}) fusion(bf16[6,3,256,256]{3,2,1,0:T(8,128)(2,1)} %bitcast.17), kind=kLoop, calls=%fused_computation.2 | loop fusion | bytes 1572864 | tf_op jit(solution)/shard_map/slice | solution.py:204
  12.7 0.0 all-gather.6.cloned.1.call-update
  12.7 0.0 all-gather.8.cloned.1.call-start
  12.8 0.7 all-gather.8.cloned.1.call-update
  13.5 0.1 collective-permute-start.7
  13.6 11.6 %all-to-all-start = ((bf16[32,32,256]{2,1,0:T(8,128)(2,1)}), bf16[32,32,256]{2,1,0:T(8,128)(2,1)S(1)}, u32[]{:S(2)}, u32[]{:S(2)}) async-start(bf16[32,32,256]{2,1,0:T(8,128)(2,1)} %get-tuple-element.59), calls=%async_computation | async-start | bytes 1048576 | tf_op jit(solution)/shard_map/all_to_all | solution.py:201
  25.2 1.7 %collective-permute-start = (s32[3,6]{1,0:T(4,128)S(1)}, s32[3,6]{1,0:T(4,128)S(1)}, u32[]{:S(2)}, u32[]{:S(2)}) collective-permute-start(s32[3,6]{1,0:T(4,128)S(1)} %bitcast.32), channel_id=1, source_target_pairs={{0,2},{1,3},{2,4},{3,5},{4,6},{5,7},{6,0},{7,1},{8,10},{9,11},{10,... | collective-permute-start | bytes 224 | tf_op jit(solution)/shard_map/ppermute | solution.py:200
  26.9 2.9 %collective-permute-start.1 = (s32[3,6]{1,0:T(4,128)S(1)}, s32[3,6]{1,0:T(4,128)S(1)}, u32[]{:S(2)}, u32[]{:S(2)}) collective-permute-start(s32[3,6]{1,0:T(4,128)S(1)} %bitcast.33), channel_id=1, source_target_pairs={{0,4},{1,5},{2,6},{3,7},{4,0},{5,1},{6,2},{7,3},{8,12},{9,13},{10,... | collective-permute-start | bytes 224 | tf_op jit(solution)/shard_map/ppermute | solution.py:200
  29.8 1.3 %collective-permute-start.2 = (s32[3,6]{1,0:T(4,128)S(1)}, s32[3,6]{1,0:T(4,128)S(1)}, u32[]{:S(2)}, u32[]{:S(2)}) collective-permute-start(s32[3,6]{1,0:T(4,128)S(1)} %bitcast.34), channel_id=1, source_target_pairs={{0,6},{1,7},{2,0},{3,1},{4,2},{5,3},{6,4},{7,5},{8,14},{9,15},{10,... | collective-permute-start | bytes 224 | tf_op jit(solution)/shard_map/ppermute | solution.py:200
  31.1 0.0 collective-permute-done
  31.1 0.9 collective-permute-done.1
  32.1 1.3 %collective-permute-done.2 = s32[3,6]{1,0:T(4,128)S(1)} collective-permute-done((s32[3,6]{1,0:T(4,128)S(1)}, s32[3,6]{1,0:T(4,128)S(1)}, u32[]{:S(2)}, u32[]{:S(2)}) %collective-permute-start.2) | collective-permute-done | bytes 104 | tf_op jit(solution)/shard_map/ppermute | solution.py:200
  33.4 0.1 collective-permute-start.3
  33.5 1.2 collective-permute-done.3.there
  34.6 8.0 %all-to-all-done.known = bf16[32,32,256]{2,1,0:T(8,128)(2,1)S(1)} async-done(((bf16[32,32,256]{2,1,0:T(8,128)(2,1)}), bf16[32,32,256]{2,1,0:T(8,128)(2,1)S(1)}, u32[]{:S(2)}, u32[]{:S(2)}) %all-to-all-start) | async-done | bytes 524320 | tf_op jit(solution)/shard_map/all_to_all | solution.py:201
  42.7 0.0 copy-done.5
  42.7 0.8 copy-done.2
  43.5 2.0 %pick13.1 = (bf16[2,6,32,256]{3,2,1,0:T(8,128)(2,1)}, bf16[2,6,32,256]{3,2,1,0:T(8,128)(2,1)}, bf16[2,6,32,256]{3,2,1,0:T(8,128)(2,1)}, bf16[2,6,32,256]{3,2,1,0:T(8,128)(2,1)}) custom-call(s32[1]{0:T(128)} %bitcast.place, s32[4,3,6]{2,1,0:T(4,128)} %copy-done.4, s32[4,3,6]{2,1,0:T(4,128)} %copy-done.5, bf16[32,32,256]{2,1,0:T(8,128)(2,1)} %copy-done.2), custom_call_target="tpu_custom_call" | custom-call | bytes 2097152 | tf_op jit(solution)/shard_map/pick13/pallas_call | solution.py:46
  45.5 1.6 %collective-permute-start.4 = (bf16[2,6,32,256]{3,2,1,0:T(8,128)(2,1)}, bf16[2,6,32,256]{3,2,1,0:T(8,128)(2,1)S(1)}, u32[]{:S(2)}, u32[]{:S(2)}) collective-permute-start(bf16[2,6,32,256]{3,2,1,0:T(8,128)(2,1)} %get-tuple-element.67), channel_id=1, source_target_pairs={{0,2},{1,3},{2,4},{3,5},{4,6},{5,7},{6,0},{7,1},{8,10},{9,11},{10,... | collective-permute-start | bytes 589832 | tf_op jit(solution)/shard_map/ppermute | solution.py:200
  47.1 2.9 %collective-permute-start.5 = (bf16[2,6,32,256]{3,2,1,0:T(8,128)(2,1)}, bf16[2,6,32,256]{3,2,1,0:T(8,128)(2,1)S(1)}, u32[]{:S(2)}, u32[]{:S(2)}) collective-permute-start(bf16[2,6,32,256]{3,2,1,0:T(8,128)(2,1)} %get-tuple-element.68), channel_id=1, source_target_pairs={{0,4},{1,5},{2,6},{3,7},{4,0},{5,1},{6,2},{7,3},{8,12},{9,13},{10,... | collective-permute-start | bytes 589832 | tf_op jit(solution)/shard_map/ppermute | solution.py:200
  50.0 1.3 %collective-permute-start.6 = (bf16[2,6,32,256]{3,2,1,0:T(8,128)(2,1)}, bf16[2,6,32,256]{3,2,1,0:T(8,128)(2,1)S(1)}, u32[]{:S(2)}, u32[]{:S(2)}) collective-permute-start(bf16[2,6,32,256]{3,2,1,0:T(8,128)(2,1)} %get-tuple-element.69), channel_id=1, source_target_pairs={{0,6},{1,7},{2,0},{3,1},{4,2},{5,3},{6,4},{7,5},{8,14},{9,15},{10,... | collective-permute-start | bytes 589832 | tf_op jit(solution)/shard_map/ppermute | solution.py:200
  51.3 4.7 %level1.1 = (f32[32,256]{1,0:T(8,128)}, bf16[32,32,256]{2,1,0:T(8,128)(2,1)}) custom-call(s32[1]{0:T(128)} %bitcast.place, s32[4,3,6]{2,1,0:T(4,128)} %copy-done.4, s32[4,3,6]{2,1,0:T(4,128)} %copy-done.5, s32[1,6]{1,0:T(1,128)} %bitcast.25, bf16[4,256,256]{2,1,0:T(8,128)(2,1)} %rhs.7, bf16[4,256,256]{2,1,0:T(8,128)(2,1)} %dinv.7, ...), custom_call_target="tpu_custom_call" | custom-call | flops 100663296 | bytes 3145728 | tf_op jit(solution)/shard_map/level1/pallas_call | solution.py:46
  56.1 0.0 collective-permute-done.4.refs_1_
  56.1 0.0 copy-start.6
  56.1 2.2 %collective-permute-done.5.refs_2_ = bf16[2,6,32,256]{3,2,1,0:T(8,128)(2,1)S(1)} collective-permute-done((bf16[2,6,32,256]{3,2,1,0:T(8,128)(2,1)}, bf16[2,6,32,256]{3,2,1,0:T(8,128)(2,1)S(1)}, u32[]{:S(2)}, u32[]{:S(2)}) %collective-permute-start.5) | collective-permute-done | bytes 196640 | tf_op jit(solution)/shard_map/ppermute | solution.py:200
  58.2 0.0 collective-permute-done.6.refs_3_
  58.2 5.7 %all-to-all-start.1 = ((bf16[32,32,256]{2,1,0:T(8,128)(2,1)}), bf16[32,32,256]{2,1,0:T(8,128)(2,1)S(1)}, u32[]{:S(2)}, u32[]{:S(2)}) async-start(bf16[32,32,256]{2,1,0:T(8,128)(2,1)} %get-tuple-element.70), calls=%async_computation.1 | async-start | bytes 1048576 | tf_op jit(solution)/shard_map/all_to_all | solution.py:201
  64.0 0.0 collective-permute-done.7.refs_5_.refs_7_.refs_9_
  64.0 0.0 copy-done.6
  64.0 0.0 copy-done.7
  64.0 0.0 copy-done.8
  64.0 3.0 %partial13.1 = (f32[32,256]{1,0:T(8,128)}, f32[32,256]{1,0:T(8,128)}, f32[32,256]{1,0:T(8,128)}, f32[32,256]{1,0:T(8,128)}, f32[32,256]{1,0:T(8,128)}, /*index=5...) custom-call(s32[1]{0:T(128)} %bitcast.place, s32[1,6]{1,0:T(1,128)} %bitcast.26, ...), custom_call_target="tpu_custom_call" | custom-call | flops 201326592 | bytes 2097152 | tf_op jit(solution)/shard_map/partial13/pallas_call | solution.py:46
  67.1 1.2 collective-permute-start.10
  68.2 2.1 %collective-permute-start.8 = (f32[32,256]{1,0:T(8,128)}, f32[32,256]{1,0:T(8,128)S(1)}, u32[]{:S(2)}, u32[]{:S(2)}) collective-permute-start(f32[32,256]{1,0:T(8,128)} %get-tuple-element.77), channel_id=1, source_target_pairs={{0,6},{1,7},{2,0},{3,1},{4,2},{5,3},{6,4},{7,5},{8,14},{9,15},{10,... | collective-permute-start | bytes 98312 | tf_op jit(solution)/shard_map/ppermute | solution.py:200
  70.4 1.3 %collective-permute-start.9 = (f32[32,256]{1,0:T(8,128)}, f32[32,256]{1,0:T(8,128)S(1)}, u32[]{:S(2)}, u32[]{:S(2)}) collective-permute-start(f32[32,256]{1,0:T(8,128)} %get-tuple-element.78), channel_id=1, source_target_pairs={{0,4},{1,5},{2,6},{3,7},{4,0},{5,1},{6,2},{7,3},{8,12},{9,13},{10,... | collective-permute-start | bytes 98312 | tf_op jit(solution)/shard_map/ppermute | solution.py:200
  71.7 1.7 %collective-permute-done.10.refs_3_ = f32[32,256]{1,0:T(8,128)S(1)} collective-permute-done((f32[32,256]{1,0:T(8,128)}, f32[32,256]{1,0:T(8,128)S(1)}, u32[]{:S(2)}, u32[]{:S(2)}) %collective-permute-start.10) | collective-permute-done | bytes 32800 | tf_op jit(solution)/shard_map/ppermute | solution.py:200
  73.4 0.0 collective-permute-done.8.refs_1_
  73.4 2.6 %collective-permute-done.9.refs_2_ = f32[32,256]{1,0:T(8,128)S(1)} collective-permute-done((f32[32,256]{1,0:T(8,128)}, f32[32,256]{1,0:T(8,128)S(1)}, u32[]{:S(2)}, u32[]{:S(2)}) %collective-permute-start.9) | collective-permute-done | bytes 32800 | tf_op jit(solution)/shard_map/ppermute | solution.py:200
  76.0 3.3 %all-to-all-done.1.known = bf16[32,32,256]{2,1,0:T(8,128)(2,1)S(1)} async-done(((bf16[32,32,256]{2,1,0:T(8,128)(2,1)}), bf16[32,32,256]{2,1,0:T(8,128)(2,1)S(1)}, u32[]{:S(2)}, u32[]{:S(2)}) %all-to-all-start.1) | async-done | bytes 524320 | tf_op jit(solution)/shard_map/all_to_all | solution.py:201
  79.3 0.8 copy-done.1
  80.1 1.8 %pick4.1 = (bf16[1,6,32,256]{3,2,1,0:T(8,128)(2,1)}, bf16[1,6,32,256]{3,2,1,0:T(8,128)(2,1)}, bf16[1,6,32,256]{3,2,1,0:T(8,128)(2,1)}, bf16[1,6,32,256]{3,2,1,0:T(8,128)(2,1)}) custom-call(s32[1]{0:T(128)} %bitcast.place, s32[4,3,6]{2,1,0:T(4,128)} %copy-done.4, s32[4,3,6]{2,1,0:T(4,128)} %copy-done.5, bf16[32,32,256]{2,1,0:T(8,128)(2,1)} %copy-done.1), custom_call_target="tpu_custom_call" | custom-call | bytes 2097152 | tf_op jit(solution)/shard_map/pick4/pallas_call | solution.py:46
  81.9 2.0 %collective-permute-start.11 = (bf16[1,6,32,256]{3,2,1,0:T(8,128)(2,1)}, bf16[1,6,32,256]{3,2,1,0:T(8,128)(2,1)S(1)}, u32[]{:S(2)}, u32[]{:S(2)}) collective-permute-start(bf16[1,6,32,256]{3,2,1,0:T(8,128)(2,1)} %get-tuple-element.92), channel_id=1, source_target_pairs={{0,2},{1,3},{2,4},{3,5},{4,6},{5,7},{6,0},{7,1},{8,10},{9,11},{10,... | collective-permute-start | bytes 294920 | tf_op jit(solution)/shard_map/ppermute | solution.py:200
  83.9 2.2 %collective-permute-start.12 = (bf16[1,6,32,256]{3,2,1,0:T(8,128)(2,1)}, bf16[1,6,32,256]{3,2,1,0:T(8,128)(2,1)S(1)}, u32[]{:S(2)}, u32[]{:S(2)}) collective-permute-start(bf16[1,6,32,256]{3,2,1,0:T(8,128)(2,1)} %get-tuple-element.93), channel_id=1, source_target_pairs={{0,4},{1,5},{2,6},{3,7},{4,0},{5,1},{6,2},{7,3},{8,12},{9,13},{10,... | collective-permute-start | bytes 294920 | tf_op jit(solution)/shard_map/ppermute | solution.py:200
  86.1 0.7 collective-permute-start.13
  86.8 4.8 %level2.1 = (f32[32,256]{1,0:T(8,128)}, bf16[32,32,256]{2,1,0:T(8,128)(2,1)}) custom-call(s32[1]{0:T(128)} %bitcast.place, s32[4,3,6]{2,1,0:T(4,128)} %copy-done.4, s32[4,3,6]{2,1,0:T(4,128)} %copy-done.5, s32[1,6]{1,0:T(1,128)} %bitcast.27, bf16[4,256,256]{2,1,0:T(8,128)(2,1)} %rhs.7, bf16[4,256,256]{2,1,0:T(8,128)(2,1)} %dinv.7, ...), custom_call_target="tpu_custom_call" | custom-call | flops 100663296 | bytes 3145728 | tf_op jit(solution)/shard_map/level2/pallas_call | solution.py:46
  91.7 0.0 collective-permute-done.11.refs_1_
  91.7 0.0 collective-permute-done.12.refs_2_
  91.7 0.0 collective-permute-done.13.refs_3_
  91.7 5.6 %all-to-all-start.2 = ((bf16[32,32,256]{2,1,0:T(8,128)(2,1)}), bf16[32,32,256]{2,1,0:T(8,128)(2,1)S(1)}, u32[]{:S(2)}, u32[]{:S(2)}) async-start(bf16[32,32,256]{2,1,0:T(8,128)(2,1)} %get-tuple-element.95), calls=%async_computation.2 | async-start | bytes 1048576 | tf_op jit(solution)/shard_map/all_to_all | solution.py:201
  97.3 2.5 %partial4.1 = (f32[32,256]{1,0:T(8,128)}, f32[32,256]{1,0:T(8,128)}, f32[32,256]{1,0:T(8,128)}, f32[32,256]{1,0:T(8,128)}) custom-call(s32[1]{0:T(128)} %bitcast.place, s32[1,6]{1,0:T(1,128)} %bitcast.28, bf16[1,6,32,256]{3,2,1,0:T(8,128)(2,1)} %get-tuple-element.96.refs_0_, bf16[1,6,32,256]{3,2,1,0:T(8,128)(2,1)} %copy-done.9, ...), custom_call_target="tpu_custom_call" | custom-call | flops 201326592 | bytes 2097152 | tf_op jit(solution)/shard_map/partial4/pallas_call | solution.py:46
  99.8 1.7 %collective-permute-start.14 = (f32[32,256]{1,0:T(8,128)}, f32[32,256]{1,0:T(8,128)S(1)}, u32[]{:S(2)}, u32[]{:S(2)}) collective-permute-start(f32[32,256]{1,0:T(8,128)} %get-tuple-element.105), channel_id=1, source_target_pairs={{0,6},{1,7},{2,0},{3,1},{4,2},{5,3},{6,4},{7,5},{8,14},{9,15},{10,... | collective-permute-start | bytes 98312 | tf_op jit(solution)/shard_map/ppermute | solution.py:200
  101.4 1.7 %collective-permute-start.15 = (f32[32,256]{1,0:T(8,128)}, f32[32,256]{1,0:T(8,128)S(1)}, u32[]{:S(2)}, u32[]{:S(2)}) collective-permute-start(f32[32,256]{1,0:T(8,128)} %get-tuple-element.106), channel_id=1, source_target_pairs={{0,4},{1,5},{2,6},{3,7},{4,0},{5,1},{6,2},{7,3},{8,12},{9,13},{10,... | collective-permute-start | bytes 98312 | tf_op jit(solution)/shard_map/ppermute | solution.py:200
  103.1 0.2 collective-permute-start.16
  103.3 5.9 %all-gather.8.cloned.1.call-done.tiles = bf16[8,768,256]{2,1,0:T(8,128)(2,1)} async-done(((bf16[1,768,256]{2,1,0:T(8,128)(2,1)}), bf16[8,768,256]{2,1,0:T(8,128)(2,1)}) %all-gather.8.cloned.1.call-update) | async-done | bytes 3145744 | tf_op jit(solution)/shard_map/all_gather | solution.py:203
  109.2 0.0 collective-permute-done.14.refs_1_
  109.2 0.0 collective-permute-done.15.refs_2_
  109.2 0.0 collective-permute-done.16.refs_3_
  109.2 3.1 %all-to-all-done.2.known = bf16[32,32,256]{2,1,0:T(8,128)(2,1)S(1)} async-done(((bf16[32,32,256]{2,1,0:T(8,128)(2,1)}), bf16[32,32,256]{2,1,0:T(8,128)(2,1)S(1)}, u32[]{:S(2)}, u32[]{:S(2)}) %all-to-all-start.2) | async-done | bytes 524320 | tf_op jit(solution)/shard_map/all_to_all | solution.py:201
  112.4 0.8 copy-done.3
  113.2 4.6 %level3.1 = f32[4,32,256]{2,1,0:T(8,128)} custom-call(s32[1]{0:T(128)} %bitcast.place, s32[4,3,6]{2,1,0:T(4,128)} %copy-done.4, s32[4,3,6]{2,1,0:T(4,128)} %copy-done.5, s32[1,6]{1,0:T(1,128)} %bitcast.29, bf16[4,256,256]{2,1,0:T(8,128)(2,1)} %rhs.7, bf16[4,256,256]{2,1,0:T(8,128)(2,1)} %dinv.7, bf16[32,32,256]{2,1,0:T(8,128)(2,1)} %copy-done.3, ...), custom_call_target="tpu_custom_call" | custom-call | flops 100663296 | bytes 3145728 | tf_op jit(solution)/shard_map/level3/pallas_call | solution.py:46
  (36 shorter events, 0.1 us)
Async XLA Ops:
  6.5 6.9 %copy-start = (bf16[6,256,3,256]{3,1,2,0:T(8,128)(2,1)S(1)}, bf16[6,256,3,256]{3,1,2,0:T(8,128)(2,1)}, u32[]{:S(2)}) copy-start(bf16[6,256,3,256]{3,1,2,0:T(8,128)(2,1)} %param.7) | copy-start | bytes 7077892
  6.5 18.7 %copy-start.18 = (s32[6,1,3]{0,1,2:T(1,128)S(1)}, s32[6,1,3]{0,1,2:T(1,128)}, u32[]{:S(2)}) copy-start(s32[6,1,3]{0,1,2:T(1,128)} %param.8) | copy-start | bytes 220
  6.5 44.8 %all-gather.4.cloned.1.call-start = ((), (), s32[]{:S(2)}) async-start(), calls=%async_computation.3 | async-start | bytes 3538944 | tf_op jit(solution)/shard_map/all_gather | solution.py:203
  8.5 78.3 %all-gather.6.cloned.1.call-start = ((), (), s32[]{:S(2)}) async-start(), calls=%async_computation.4 | async-start | bytes 3538944 | tf_op jit(solution)/shard_map/all_gather | solution.py:203
  12.7 96.5 %all-gather.8.cloned.1.call-start = ((), (), s32[]{:S(2)}) async-start(), calls=%async_computation.5 | async-start | bytes 3538944 | tf_op jit(solution)/shard_map/all_gather | solution.py:203
  13.5 50.5 %collective-permute-start.7 = (bf16[6,3,256,256]{3,2,1,0:T(8,128)(2,1)S(1)}, bf16[6,3,256,256]{3,2,1,0:T(8,128)(2,1)}, u32[]{:S(2)}, u32[]{:S(2)}) collective-permute-start(bf16[6,3,256,256]{3,2,1,0:T(8,128)(2,1)S(1)} %bitcast.21), channel_id=1, source_target_pairs={{0,1},{1,0},{2,3},{3,2},{4,5},{5,4},{6,7},{7,6},{8,9},{9,8},{10,11... | collective-permute-start | bytes 7077896 | tf_op jit(solution)/shard_map/ppermute | solution.py:200
  13.6 29.1 %all-to-all-start = ((bf16[32,32,256]{2,1,0:T(8,128)(2,1)}), bf16[32,32,256]{2,1,0:T(8,128)(2,1)S(1)}, u32[]{:S(2)}, u32[]{:S(2)}) async-start(bf16[32,32,256]{2,1,0:T(8,128)(2,1)} %get-tuple-element.59), calls=%async_computation | async-start | bytes 1048576 | tf_op jit(solution)/shard_map/all_to_all | solution.py:201
  25.2 5.9 %collective-permute-start = (s32[3,6]{1,0:T(4,128)S(1)}, s32[3,6]{1,0:T(4,128)S(1)}, u32[]{:S(2)}, u32[]{:S(2)}) collective-permute-start(s32[3,6]{1,0:T(4,128)S(1)} %bitcast.32), channel_id=1, source_target_pairs={{0,2},{1,3},{2,4},{3,5},{4,6},{5,7},{6,0},{7,1},{8,10},{9,11},{10,... | collective-permute-start | bytes 224 | tf_op jit(solution)/shard_map/ppermute | solution.py:200
  26.9 5.2 %collective-permute-start.1 = (s32[3,6]{1,0:T(4,128)S(1)}, s32[3,6]{1,0:T(4,128)S(1)}, u32[]{:S(2)}, u32[]{:S(2)}) collective-permute-start(s32[3,6]{1,0:T(4,128)S(1)} %bitcast.33), channel_id=1, source_target_pairs={{0,4},{1,5},{2,6},{3,7},{4,0},{5,1},{6,2},{7,3},{8,12},{9,13},{10,... | collective-permute-start | bytes 224 | tf_op jit(solution)/shard_map/ppermute | solution.py:200
  29.8 3.6 %collective-permute-start.2 = (s32[3,6]{1,0:T(4,128)S(1)}, s32[3,6]{1,0:T(4,128)S(1)}, u32[]{:S(2)}, u32[]{:S(2)}) collective-permute-start(s32[3,6]{1,0:T(4,128)S(1)} %bitcast.34), channel_id=1, source_target_pairs={{0,6},{1,7},{2,0},{3,1},{4,2},{5,3},{6,4},{7,5},{8,14},{9,15},{10,... | collective-permute-start | bytes 224 | tf_op jit(solution)/shard_map/ppermute | solution.py:200
  33.4 9.3 %copy-start.4 = (s32[4,3,6]{2,1,0:T(4,128)}, s32[4,3,6]{2,1,0:T(4,128)S(1)}, u32[]{:S(2)}) copy-start(s32[4,3,6]{2,1,0:T(4,128)S(1)} %pad_add_fusion.here) | copy-start | bytes 868
  33.4 1.3 %collective-permute-start.3 = (s32[4,3,6]{2,1,0:T(4,128)S(1)}, s32[4,3,6]{2,1,0:T(4,128)S(1)}, u32[]{:S(2)}, u32[]{:S(2)}) collective-permute-start(s32[4,3,6]{2,1,0:T(4,128)S(1)} %pad_add_fusion.here), channel_id=1, source_target_pairs={{0,1},{1,0},{2,3},{3,2},{4,5},{5,4},{6,7},{7,6},{8,9},{9,8},{10,11... | collective-permute-start | bytes 872 | tf_op jit(solution)/shard_map/ppermute | solution.py:200
  34.6 8.1 %copy-start.5 = (s32[4,3,6]{2,1,0:T(4,128)}, s32[4,3,6]{2,1,0:T(4,128)S(1)}, u32[]{:S(2)}) copy-start(s32[4,3,6]{2,1,0:T(4,128)S(1)} %collective-permute-done.3.there) | copy-start | bytes 868
  42.7 0.8 copy-start.2
  45.5 10.6 %collective-permute-start.4 = (bf16[2,6,32,256]{3,2,1,0:T(8,128)(2,1)}, bf16[2,6,32,256]{3,2,1,0:T(8,128)(2,1)S(1)}, u32[]{:S(2)}, u32[]{:S(2)}) collective-permute-start(bf16[2,6,32,256]{3,2,1,0:T(8,128)(2,1)} %get-tuple-element.67), channel_id=1, source_target_pairs={{0,2},{1,3},{2,4},{3,5},{4,6},{5,7},{6,0},{7,1},{8,10},{9,11},{10,... | collective-permute-start | bytes 589832 | tf_op jit(solution)/shard_map/ppermute | solution.py:200
  47.1 11.2 %collective-permute-start.5 = (bf16[2,6,32,256]{3,2,1,0:T(8,128)(2,1)}, bf16[2,6,32,256]{3,2,1,0:T(8,128)(2,1)S(1)}, u32[]{:S(2)}, u32[]{:S(2)}) collective-permute-start(bf16[2,6,32,256]{3,2,1,0:T(8,128)(2,1)} %get-tuple-element.68), channel_id=1, source_target_pairs={{0,4},{1,5},{2,6},{3,7},{4,0},{5,1},{6,2},{7,3},{8,12},{9,13},{10,... | collective-permute-start | bytes 589832 | tf_op jit(solution)/shard_map/ppermute | solution.py:200
  50.0 8.3 %collective-permute-start.6 = (bf16[2,6,32,256]{3,2,1,0:T(8,128)(2,1)}, bf16[2,6,32,256]{3,2,1,0:T(8,128)(2,1)S(1)}, u32[]{:S(2)}, u32[]{:S(2)}) collective-permute-start(bf16[2,6,32,256]{3,2,1,0:T(8,128)(2,1)} %get-tuple-element.69), channel_id=1, source_target_pairs={{0,6},{1,7},{2,0},{3,1},{4,2},{5,3},{6,4},{7,5},{8,14},{9,15},{10,... | collective-permute-start | bytes 589832 | tf_op jit(solution)/shard_map/ppermute | solution.py:200
  56.1 7.9 %copy-start.6 = (bf16[2,6,32,256]{3,2,1,0:T(8,128)(2,1)}, bf16[2,6,32,256]{3,2,1,0:T(8,128)(2,1)S(1)}, u32[]{:S(2)}) copy-start(bf16[2,6,32,256]{3,2,1,0:T(8,128)(2,1)S(1)} %collective-permute-done.4.refs_1_) | copy-start | bytes 589828
  58.2 5.8 %copy-start.7 = (bf16[2,6,32,256]{3,2,1,0:T(8,128)(2,1)}, bf16[2,6,32,256]{3,2,1,0:T(8,128)(2,1)S(1)}, u32[]{:S(2)}) copy-start(bf16[2,6,32,256]{3,2,1,0:T(8,128)(2,1)S(1)} %collective-permute-done.5.refs_2_) | copy-start | bytes 589828
  58.2 5.8 %copy-start.8 = (bf16[2,6,32,256]{3,2,1,0:T(8,128)(2,1)}, bf16[2,6,32,256]{3,2,1,0:T(8,128)(2,1)S(1)}, u32[]{:S(2)}) copy-start(bf16[2,6,32,256]{3,2,1,0:T(8,128)(2,1)S(1)} %collective-permute-done.6.refs_3_) | copy-start | bytes 589828
  58.2 21.1 %all-to-all-start.1 = ((bf16[32,32,256]{2,1,0:T(8,128)(2,1)}), bf16[32,32,256]{2,1,0:T(8,128)(2,1)S(1)}, u32[]{:S(2)}, u32[]{:S(2)}) async-start(bf16[32,32,256]{2,1,0:T(8,128)(2,1)} %get-tuple-element.70), calls=%async_computation.1 | async-start | bytes 1048576 | tf_op jit(solution)/shard_map/all_to_all | solution.py:201
  67.1 6.3 %collective-permute-start.10 = (f32[32,256]{1,0:T(8,128)}, f32[32,256]{1,0:T(8,128)S(1)}, u32[]{:S(2)}, u32[]{:S(2)}) collective-permute-start(f32[32,256]{1,0:T(8,128)} %get-tuple-element.79), channel_id=1, source_target_pairs={{0,2},{1,3},{2,4},{3,5},{4,6},{5,7},{6,0},{7,1},{8,10},{9,11},{10,... | collective-permute-start | bytes 98312 | tf_op jit(solution)/shard_map/ppermute | solution.py:200
  68.2 5.2 %collective-permute-start.8 = (f32[32,256]{1,0:T(8,128)}, f32[32,256]{1,0:T(8,128)S(1)}, u32[]{:S(2)}, u32[]{:S(2)}) collective-permute-start(f32[32,256]{1,0:T(8,128)} %get-tuple-element.77), channel_id=1, source_target_pairs={{0,6},{1,7},{2,0},{3,1},{4,2},{5,3},{6,4},{7,5},{8,14},{9,15},{10,... | collective-permute-start | bytes 98312 | tf_op jit(solution)/shard_map/ppermute | solution.py:200
  70.4 5.6 %collective-permute-start.9 = (f32[32,256]{1,0:T(8,128)}, f32[32,256]{1,0:T(8,128)S(1)}, u32[]{:S(2)}, u32[]{:S(2)}) collective-permute-start(f32[32,256]{1,0:T(8,128)} %get-tuple-element.78), channel_id=1, source_target_pairs={{0,4},{1,5},{2,6},{3,7},{4,0},{5,1},{6,2},{7,3},{8,12},{9,13},{10,... | collective-permute-start | bytes 98312 | tf_op jit(solution)/shard_map/ppermute | solution.py:200
  73.4 13.4 %copy-start.12 = (f32[32,256]{1,0:T(8,128)}, f32[32,256]{1,0:T(8,128)S(1)}, u32[]{:S(2)}) copy-start(f32[32,256]{1,0:T(8,128)S(1)} %collective-permute-done.10.refs_3_) | copy-start | bytes 98308
  73.4 13.4 %copy-start.13 = (f32[32,256]{1,0:T(8,128)}, f32[32,256]{1,0:T(8,128)S(1)}, u32[]{:S(2)}) copy-start(f32[32,256]{1,0:T(8,128)S(1)} %collective-permute-done.8.refs_1_) | copy-start | bytes 98308
  76.0 10.9 %copy-start.14 = (f32[32,256]{1,0:T(8,128)}, f32[32,256]{1,0:T(8,128)S(1)}, u32[]{:S(2)}) copy-start(f32[32,256]{1,0:T(8,128)S(1)} %collective-permute-done.9.refs_2_) | copy-start | bytes 98308
  79.3 0.8 copy-start.1
  81.9 9.7 %collective-permute-start.11 = (bf16[1,6,32,256]{3,2,1,0:T(8,128)(2,1)}, bf16[1,6,32,256]{3,2,1,0:T(8,128)(2,1)S(1)}, u32[]{:S(2)}, u32[]{:S(2)}) collective-permute-start(bf16[1,6,32,256]{3,2,1,0:T(8,128)(2,1)} %get-tuple-element.92), channel_id=1, source_target_pairs={{0,2},{1,3},{2,4},{3,5},{4,6},{5,7},{6,0},{7,1},{8,10},{9,11},{10,... | collective-permute-start | bytes 294920 | tf_op jit(solution)/shard_map/ppermute | solution.py:200
  83.9 7.8 %collective-permute-start.12 = (bf16[1,6,32,256]{3,2,1,0:T(8,128)(2,1)}, bf16[1,6,32,256]{3,2,1,0:T(8,128)(2,1)S(1)}, u32[]{:S(2)}, u32[]{:S(2)}) collective-permute-start(bf16[1,6,32,256]{3,2,1,0:T(8,128)(2,1)} %get-tuple-element.93), channel_id=1, source_target_pairs={{0,4},{1,5},{2,6},{3,7},{4,0},{5,1},{6,2},{7,3},{8,12},{9,13},{10,... | collective-permute-start | bytes 294920 | tf_op jit(solution)/shard_map/ppermute | solution.py:200
  86.1 5.6 %collective-permute-start.13 = (bf16[1,6,32,256]{3,2,1,0:T(8,128)(2,1)}, bf16[1,6,32,256]{3,2,1,0:T(8,128)(2,1)S(1)}, u32[]{:S(2)}, u32[]{:S(2)}) collective-permute-start(bf16[1,6,32,256]{3,2,1,0:T(8,128)(2,1)} %get-tuple-element.94), channel_id=1, source_target_pairs={{0,6},{1,7},{2,0},{3,1},{4,2},{5,3},{6,4},{7,5},{8,14},{9,15},{10,... | collective-permute-start | bytes 294920 | tf_op jit(solution)/shard_map/ppermute | solution.py:200
  91.7 5.6 %copy-start.9 = (bf16[1,6,32,256]{3,2,1,0:T(8,128)(2,1)}, bf16[1,6,32,256]{3,2,1,0:T(8,128)(2,1)S(1)}, u32[]{:S(2)}) copy-start(bf16[1,6,32,256]{3,2,1,0:T(8,128)(2,1)S(1)} %collective-permute-done.11.refs_1_) | copy-start | bytes 294916
  91.7 5.6 %copy-start.10 = (bf16[1,6,32,256]{3,2,1,0:T(8,128)(2,1)}, bf16[1,6,32,256]{3,2,1,0:T(8,128)(2,1)S(1)}, u32[]{:S(2)}) copy-start(bf16[1,6,32,256]{3,2,1,0:T(8,128)(2,1)S(1)} %collective-permute-done.12.refs_2_) | copy-start | bytes 294916
  91.7 5.6 %copy-start.11 = (bf16[1,6,32,256]{3,2,1,0:T(8,128)(2,1)}, bf16[1,6,32,256]{3,2,1,0:T(8,128)(2,1)S(1)}, u32[]{:S(2)}) copy-start(bf16[1,6,32,256]{3,2,1,0:T(8,128)(2,1)S(1)} %collective-permute-done.13.refs_3_) | copy-start | bytes 294916
  91.7 20.7 %all-to-all-start.2 = ((bf16[32,32,256]{2,1,0:T(8,128)(2,1)}), bf16[32,32,256]{2,1,0:T(8,128)(2,1)S(1)}, u32[]{:S(2)}, u32[]{:S(2)}) async-start(bf16[32,32,256]{2,1,0:T(8,128)(2,1)} %get-tuple-element.95), calls=%async_computation.2 | async-start | bytes 1048576 | tf_op jit(solution)/shard_map/all_to_all | solution.py:201
  99.8 9.5 %collective-permute-start.14 = (f32[32,256]{1,0:T(8,128)}, f32[32,256]{1,0:T(8,128)S(1)}, u32[]{:S(2)}, u32[]{:S(2)}) collective-permute-start(f32[32,256]{1,0:T(8,128)} %get-tuple-element.105), channel_id=1, source_target_pairs={{0,6},{1,7},{2,0},{3,1},{4,2},{5,3},{6,4},{7,5},{8,14},{9,15},{10,... | collective-permute-start | bytes 98312 | tf_op jit(solution)/shard_map/ppermute | solution.py:200
  101.4 7.8 %collective-permute-start.15 = (f32[32,256]{1,0:T(8,128)}, f32[32,256]{1,0:T(8,128)S(1)}, u32[]{:S(2)}, u32[]{:S(2)}) collective-permute-start(f32[32,256]{1,0:T(8,128)} %get-tuple-element.106), channel_id=1, source_target_pairs={{0,4},{1,5},{2,6},{3,7},{4,0},{5,1},{6,2},{7,3},{8,12},{9,13},{10,... | collective-permute-start | bytes 98312 | tf_op jit(solution)/shard_map/ppermute | solution.py:200
  103.1 6.1 %collective-permute-start.16 = (f32[32,256]{1,0:T(8,128)}, f32[32,256]{1,0:T(8,128)S(1)}, u32[]{:S(2)}, u32[]{:S(2)}) collective-permute-start(f32[32,256]{1,0:T(8,128)} %get-tuple-element.107), channel_id=1, source_target_pairs={{0,2},{1,3},{2,4},{3,5},{4,6},{5,7},{6,0},{7,1},{8,10},{9,11},{10,... | collective-permute-start | bytes 98312 | tf_op jit(solution)/shard_map/ppermute | solution.py:200
  109.2 3.2 %copy-start.15 = (f32[32,256]{1,0:T(8,128)}, f32[32,256]{1,0:T(8,128)S(1)}, u32[]{:S(2)}) copy-start(f32[32,256]{1,0:T(8,128)S(1)} %collective-permute-done.14.refs_1_) | copy-start | bytes 98308
  109.2 3.2 %copy-start.16 = (f32[32,256]{1,0:T(8,128)}, f32[32,256]{1,0:T(8,128)S(1)}, u32[]{:S(2)}) copy-start(f32[32,256]{1,0:T(8,128)S(1)} %collective-permute-done.15.refs_2_) | copy-start | bytes 98308
  109.2 3.2 %copy-start.17 = (f32[32,256]{1,0:T(8,128)}, f32[32,256]{1,0:T(8,128)S(1)}, u32[]{:S(2)}) copy-start(f32[32,256]{1,0:T(8,128)S(1)} %collective-permute-done.16.refs_3_) | copy-start | bytes 98308
  112.4 0.8 copy-start.3
Sparse Core Ops, SparseCore 0:
  9.2 33.3 all-gather.3
  44.4 31.4 all-gather.5
  77.7 31.4 all-gather.7

commit v6 on v5

--- a/solution.py
+++ b/solution.py
@@ -142,7 +142,7 @@
     )
 
 
-def level_kernel(pair, returned, earlier, place, here, there, live, rhs, dinv, known, tiles, *refs):
+def level_kernel(pair, index, begin, finish, returned, earlier, place, here, there, live, start, dinv, known, tiles, *refs):
     refs = list(refs)
     back = [refs.pop(0) for _ in range(returned)]
     before = [refs.pop(0) for _ in range(earlier)]
@@ -150,11 +150,11 @@
     chip, core = lax.div(place[0], 2), lax.rem(place[0], 2)
     chips = [lax.rem(chip + CHIPS - d, CHIPS) for d in range(CHIPS)]
     copies = [
-        pltpu.make_async_copy(tiles.at[pl.ds(2 * chips[d], 2)], held.at[pl.ds(2 * d, 2)], sems.at[d]) for d in range(CHIPS)
+        pltpu.make_async_copy(tiles.at[pl.ds(2 * chips[d], 2), index], held.at[pl.ds(2 * d, 2)], sems.at[d]) for d in range(CHIPS)
     ]
     for copy in copies:
         copy.start()
-    total = probe_rows(place[0], rhs[0])
+    total = probe_rows(place[0], start[0]) if begin else start[...]
     for sums in back:
         total = total - sums[...]
     for d in range(CHIPS):
@@ -164,6 +164,9 @@
             for slot in range(SLOTS):
                 block = masked(known[cols[d, slot, pair]], first + slot < live[0, pair])
                 total = total - dot_nt(block, held[2 * d + side, slot * SIZE : (slot + 1) * SIZE])
+    if not finish:
+        refs[0][...] = total
+        return
     result = dot_nt(total.astype(BF16), dinv[0])
     if earlier:
         for n in range(earlier):
@@ -174,20 +177,22 @@
     spread_out(result, refs[1])
 
 
-def level_call(level, pair, place, here, there, live, rhs, dinv, known, tiles, back, earlier):
+def level_call(name, level, pair, index, begin, finish, place, here, there, live, start, dinv, known, tiles, back, earlier):
     flat, pick = block_of((BLOCK, SIZE)), block_of((1, SIZE, SIZE), level)
-    if earlier:
+    if not finish:
+        shapes, outs = [((BLOCK, SIZE), F32)], [flat]
+    elif earlier:
         shapes, outs = [((level + 1, BLOCK, SIZE), F32)], [block_of((level + 1, BLOCK, SIZE))]
     else:
         shapes = [((BLOCK, SIZE), F32), ((NT, BLOCK, SIZE), BF16)]
         outs = [flat, block_of((NT, BLOCK, SIZE))]
     return call(
-        functools.partial(level_kernel, pair, len(back), len(earlier)),
-        "level%d" % level,
+        functools.partial(level_kernel, pair, index, begin, finish, len(back), len(earlier)),
+        name,
         shapes,
-        [SMEM] * 4 + [pick, pick, block_of((NT, BLOCK, SIZE)), ANY] + [flat] * (len(back) + len(earlier)),
+        [SMEM] * 4 + [pick if begin else flat, pick, block_of((NT, BLOCK, SIZE)), ANY] + [flat] * (len(back) + len(earlier)),
         outs,
-        (place, here, there, live, rhs, dinv, known, tiles, *back, *earlier),
+        (place, here, there, live, start, dinv, known, tiles, *back, *earlier),
         [pltpu.VMEM((PLACES, SLOTS * SIZE, SIZE), BF16), pltpu.SemaphoreType.DMA((CHIPS,))],
         flops=2 * 24 * BLOCK * SIZE * SIZE,
         moved=24 * SIZE * SIZE * 2,
@@ -201,18 +206,13 @@
     over_row = lambda array: lax.all_to_all(array, "row", 0, 0, tiled=True)
 
     gather = lambda array: lax.all_gather(array, "col", axis=0, tiled=False)
-    piece = lambda array, pair: array[pair].reshape(SLOTS * SIZE, SIZE)
     live = live.transpose(1, 0)
 
     own = cols.transpose(2, 1, 0).reshape(SLOTS, -1)
     here = jnp.stack([own] + [move(own, TURN[d]) for d in range(1, CHIPS)])
     there = move(here, SWAP)
     answer0, spread0 = first_call(place, rhs, dinv)
-    gathered0 = gather(piece(tiles, 0))
-    later, spread0 = lax.optimization_barrier((tiles, spread0))
-    gathered2 = gather(piece(later, 2))
-    gathered5 = gather(piece(later, 5))
-    swapped = move(later, SWAP)
+    gathered02 = gather(tiles[0:3:2].reshape(2, SLOTS * SIZE, SIZE))
 
     def send(picked):
         return [picked[0]] + [move(picked[d], TURN[d]) for d in range(1, CHIPS)]
@@ -220,28 +220,24 @@
     def give_back(sums):
         return [sums[0]] + [move(sums[d], TURN[CHIPS - d]) for d in range(1, CHIPS)]
 
+    scalars = (place, here, there, live)
     known0 = over_row(spread0)
     picked = pick_call("pick13", (1, 3), place, here, there, known0)
-    known0, *picked = lax.optimization_barrier((known0, *picked))
+    later, known0, *picked = lax.optimization_barrier((tiles, known0, *picked))
+    gathered45 = gather(later[4:6].reshape(2, SLOTS * SIZE, SIZE))
+    swapped = move(later, SWAP)
     got = send(picked)
-    answer1, spread1 = level_call(1, 0, place, here, there, live, rhs, dinv, known0, gathered0, [], [])
+    answer1, spread1 = level_call("level1", 1, 0, 0, True, True, *scalars, rhs, dinv, known0, gathered02, [], [])
     spread1, *got = lax.optimization_barrier((spread1, *got))
     known1 = over_row(spread1)
 
     sums = partial_call("partial13", (1, 3), place, live, got, [], tiles, swapped)
-    sums2, sums3 = sums[:CHIPS], sums[CHIPS:]
-    back2 = give_back(sums2)
-    known1, *back2 = lax.optimization_barrier((known1, *back2))
-    picked = pick_call("pick4", (4,), place, here, there, known1)
-    known1, *picked = lax.optimization_barrier((known1, *picked))
-    got = send(picked)
-    answer2, spread2 = level_call(2, 2, place, here, there, live, rhs, dinv, known1, gathered2, back2, [])
-    spread2, *got = lax.optimization_barrier((spread2, *got))
+    back2, back3 = give_back(sums[:CHIPS]), give_back(sums[CHIPS:])
+    answer2, spread2 = level_call("level2", 2, 2, 1, True, True, *scalars, rhs, dinv, known1, gathered02, back2, [])
     known2 = over_row(spread2)
-
-    sums3 = partial_call("partial4", (4,), place, live, got, sums3, tiles, swapped)
+    (early3,) = level_call("early3", 3, 4, 0, True, False, *scalars, rhs, dinv, known1, gathered45, back3, [])
     (solved,) = level_call(
-        3, 5, place, here, there, live, rhs, dinv, known2, gathered5, give_back(sums3), [answer0, answer1, answer2]
+        "level3", 3, 5, 1, False, True, *scalars, early3, dinv, known2, gathered45, [], [answer0, answer1, answer2]
     )
     return solved.transpose(0, 2, 1)
 

time: 125 us -> 136 us (1.088)
  waiting for transfers between devices: 31 us -> 36.8 us
  local copies, waits for them, and re-layouts: 6.41 us -> 8.74 us
  starting transfers between devices: 48 us -> 50.1 us
    all_to_all x3, starting transfers between devices: 22.9 us -> 31.2 us  [local(): over_row = lambda array: lax.all_to_all(array, 'row', 0, 0, tiled=True)]
    ppermute x17 -> x14, starting transfers between devices: 25 us -> 18.8 us  [local(): move = lambda array, pairs: lax.ppermute(array, 'col', pairs)]
    all_gather x3 -> x2, waiting for transfers between devices: 5.9 us -> 9.56 us  [local(): gather = lambda array: lax.all_gather(array, 'col', axis=0, tiled=False)]
    ppermute x17 -> x14, waiting for transfers between devices: 9.87 us -> 13.4 us  [local(): move = lambda array, pairs: lax.ppermute(array, 'col', pairs)]
    unnamed x39 -> x37, local copies, waits for them, and re-layouts: 2.43 us -> 3.72 us
    pallas_call x8 -> x7, Pallas kernels: 25.5 us -> 26.2 us  [call(): pl.pallas_call(kernel, grid=(1,), out_shape=tuple((jax.ShapeDtypeStruct(s...]
  transfers between devices with their start and end apart: 23 -> 19, of which waited for: 10 -> 12; matrix products, arithmetic and copies ran while one was open for 2% -> 3% of each run, Pallas kernels for 17% -> 16%
where the time goes in v6:
time: 136 us; the launch traced here: 135 us
  starting transfers between devices  50.1 us (37%)
  waiting for transfers between devices  36.8 us (27%)
  Pallas kernels  26.2 us (19%)
  between operations  13.6 us (10%)
  local copies, waits for them, and re-layouts  8.74 us (6%)
    all_to_all x3, starting transfers between devices, local(): over_row = lambda array: lax.all_to_all(array, 'row', 0, 0, tiled=True)  31.2 us
    pallas_call x7, Pallas kernels, call(): pl.pallas_call(kernel, grid=(1,), out_shape=tuple((jax.ShapeDtypeStruct(s...  26.2 us
    ppermute x14, starting transfers between devices, local(): move = lambda array, pairs: lax.ppermute(array, 'col', pairs)  18.8 us
    all_to_all x3, waiting for transfers between devices, local(): over_row = lambda array: lax.all_to_all(array, 'row', 0, 0, tiled=True)  13.8 us
    ppermute x14, waiting for transfers between devices, local(): move = lambda array, pairs: lax.ppermute(array, 'col', pairs)  13.4 us
    all_gather x2, waiting for transfers between devices, local(): gather = lambda array: lax.all_gather(array, 'col', axis=0, tiled=False)  9.56 us
    unnamed x37, local copies, waits for them, and re-layouts  3.72 us
  transfers between devices with their start and end apart: 19, of which 12 were waited for; matrix products, arithmetic and copies ran while one was open for 3% of the time, Pallas kernels for 16%

profile of v6, /device:TPU:2, one launch (start us, length us, event | category | flops | bytes accessed | tf_op | source)
XLA Modules:
  0.0 135.4 jit_solution(5819000797694298232)
XLA Ops:
  6.5 0.0 all-gather.3.cloned.1.call-start
  6.5 2.2 %slice.6 = bf16[2,3,256,256]{3,2,1,0:T(8,128)(2,1)} slice(bf16[6,3,256,256]{3,2,1,0:T(8,128)(2,1)} %bitcast.15), slice={[0:3:2], [0:3:1], [0:256:1], [0:256:1]} | slice | bytes 1572864 | tf_op jit(solution)/shard_map/slice | solution.py:215
  8.8 0.0 all-gather.3.cloned.1.call-update
  8.8 2.1 %level0.1 = (f32[32,256]{1,0:T(8,128)}, bf16[32,32,256]{2,1,0:T(8,128)(2,1)}) custom-call(s32[1]{0:T(128)} %bitcast.place, bf16[4,256,256]{2,1,0:T(8,128)(2,1)} %start.5, bf16[4,256,256]{2,1,0:T(8,128)(2,1)} %dinv.9), custom_call_target="tpu_custom_call" | custom-call | bytes 4194304 | tf_op jit(solution)/shard_map/level0/pallas_call | solution.py:46
  11.0 11.6 %all-to-all-start = ((bf16[32,32,256]{2,1,0:T(8,128)(2,1)}), bf16[32,32,256]{2,1,0:T(8,128)(2,1)S(1)}, u32[]{:S(2)}, u32[]{:S(2)}) async-start(bf16[32,32,256]{2,1,0:T(8,128)(2,1)} %get-tuple-element.34), calls=%async_computation | async-start | bytes 1048576 | tf_op jit(solution)/shard_map/all_to_all | solution.py:206
  22.6 0.0 all-gather.5.cloned.1.call-start
  22.6 0.7 copy.10
  23.3 1.6 %collective-permute-start = (s32[3,6]{1,0:T(4,128)S(1)}, s32[3,6]{1,0:T(4,128)S(1)}, u32[]{:S(2)}, u32[]{:S(2)}) collective-permute-start(s32[3,6]{1,0:T(4,128)S(1)} %bitcast.29), channel_id=1, source_target_pairs={{0,2},{1,3},{2,4},{3,5},{4,6},{5,7},{6,0},{7,1},{8,10},{9,11},{10,... | collective-permute-start | bytes 224 | tf_op jit(solution)/shard_map/ppermute | solution.py:205
  24.9 2.9 %collective-permute-start.1 = (s32[3,6]{1,0:T(4,128)S(1)}, s32[3,6]{1,0:T(4,128)S(1)}, u32[]{:S(2)}, u32[]{:S(2)}) collective-permute-start(s32[3,6]{1,0:T(4,128)S(1)} %bitcast.30), channel_id=1, source_target_pairs={{0,4},{1,5},{2,6},{3,7},{4,0},{5,1},{6,2},{7,3},{8,12},{9,13},{10,... | collective-permute-start | bytes 224 | tf_op jit(solution)/shard_map/ppermute | solution.py:205
  27.8 1.3 collective-permute-start.2
  29.1 0.7 copy.7
  29.8 0.0 collective-permute-done
  29.8 0.3 collective-permute-done.1
  30.1 1.3 collective-permute-done.2
  31.4 0.1 collective-permute-start.3
  31.5 1.2 collective-permute-done.3.there
  32.6 6.8 %all-to-all-done.known = bf16[32,32,256]{2,1,0:T(8,128)(2,1)S(1)} async-done(((bf16[32,32,256]{2,1,0:T(8,128)(2,1)}), bf16[32,32,256]{2,1,0:T(8,128)(2,1)S(1)}, u32[]{:S(2)}, u32[]{:S(2)}) %all-to-all-start) | async-done | bytes 524320 | tf_op jit(solution)/shard_map/all_to_all | solution.py:206
  39.4 0.0 copy-done.4
  39.4 0.0 copy-done.5
  39.4 0.8 copy-done.2
  40.2 2.0 %pick13.1 = (bf16[2,6,32,256]{3,2,1,0:T(8,128)(2,1)}, bf16[2,6,32,256]{3,2,1,0:T(8,128)(2,1)}, bf16[2,6,32,256]{3,2,1,0:T(8,128)(2,1)}, bf16[2,6,32,256]{3,2,1,0:T(8,128)(2,1)}) custom-call(s32[1]{0:T(128)} %bitcast.place, s32[4,3,6]{2,1,0:T(4,128)} %copy-done.4, s32[4,3,6]{2,1,0:T(4,128)} %copy-done.5, bf16[32,32,256]{2,1,0:T(8,128)(2,1)} %copy-done.2), custom_call_target="tpu_custom_call" | custom-call | bytes 2097152 | tf_op jit(solution)/shard_map/pick13/pallas_call | solution.py:46
  42.2 2.1 %slice.7 = bf16[2,3,256,256]{3,2,1,0:T(8,128)(2,1)} slice(bf16[6,3,256,256]{3,2,1,0:T(8,128)(2,1)} %bitcast.16), slice={[4:6], [0:3], [0:256], [0:256]} | slice | bytes 1572864 | tf_op jit(solution)/shard_map/slice | solution.py:227
  44.3 0.0 all-gather.5.cloned.1.call-update
  44.4 0.0 copy-done
  44.4 0.1 collective-permute-start.7
  44.5 1.6 %collective-permute-start.4 = (bf16[2,6,32,256]{3,2,1,0:T(8,128)(2,1)}, bf16[2,6,32,256]{3,2,1,0:T(8,128)(2,1)S(1)}, u32[]{:S(2)}, u32[]{:S(2)}) collective-permute-start(bf16[2,6,32,256]{3,2,1,0:T(8,128)(2,1)} %get-tuple-element.42), channel_id=1, source_target_pairs={{0,2},{1,3},{2,4},{3,5},{4,6},{5,7},{6,0},{7,1},{8,10},{9,11},{10,... | collective-permute-start | bytes 589832 | tf_op jit(solution)/shard_map/ppermute | solution.py:205
  46.1 2.9 %collective-permute-start.5 = (bf16[2,6,32,256]{3,2,1,0:T(8,128)(2,1)}, bf16[2,6,32,256]{3,2,1,0:T(8,128)(2,1)S(1)}, u32[]{:S(2)}, u32[]{:S(2)}) collective-permute-start(bf16[2,6,32,256]{3,2,1,0:T(8,128)(2,1)} %get-tuple-element.43), channel_id=1, source_target_pairs={{0,4},{1,5},{2,6},{3,7},{4,0},{5,1},{6,2},{7,3},{8,12},{9,13},{10,... | collective-permute-start | bytes 589832 | tf_op jit(solution)/shard_map/ppermute | solution.py:205
  49.0 1.3 collective-permute-start.6
  50.4 9.6 %all-gather.3.cloned.1.call-done.tiles = bf16[8,2,768,256]{3,2,1,0:T(8,128)(2,1)} async-done(((bf16[1,2,768,256]{3,2,1,0:T(8,128)(2,1)}), bf16[8,2,768,256]{3,2,1,0:T(8,128)(2,1)}) %all-gather.3.cloned.1.call-update) | async-done | bytes 6291472 | tf_op jit(solution)/shard_map/all_gather | solution.py:208
  59.9 4.7 %level1.1 = (f32[32,256]{1,0:T(8,128)}, bf16[32,32,256]{2,1,0:T(8,128)(2,1)}) custom-call(s32[1]{0:T(128)} %bitcast.place, s32[4,3,6]{2,1,0:T(4,128)} %copy-done.4, s32[4,3,6]{2,1,0:T(4,128)} %copy-done.5, s32[1,6]{1,0:T(1,128)} %bitcast.22, bf16[4,256,256]{2,1,0:T(8,128)(2,1)} %start.5, bf16[4,256,256]{2,1,0:T(8,128)(2,1)} %dinv.9, ...), custom_call_target="tpu_custom_call" | custom-call | flops 100663296 | bytes 3145728 | tf_op jit(solution)/shard_map/level1/pallas_call | solution.py:46
  64.7 0.0 collective-permute-done.4.refs_1_
  64.7 0.0 copy-start.6
  64.7 0.0 collective-permute-done.5.refs_2_
  64.7 0.0 copy-start.7
  64.7 0.0 collective-permute-done.6.refs_3_
  64.7 0.0 copy-start.8
  64.7 14.1 %all-to-all-start.1 = ((bf16[32,32,256]{2,1,0:T(8,128)(2,1)}), bf16[32,32,256]{2,1,0:T(8,128)(2,1)S(1)}, u32[]{:S(2)}, u32[]{:S(2)}) async-start(bf16[32,32,256]{2,1,0:T(8,128)(2,1)} %get-tuple-element.45), calls=%async_computation.1 | async-start | bytes 1048576 | tf_op jit(solution)/shard_map/all_to_all | solution.py:206
  78.8 0.0 collective-permute-done.7.refs_5_.refs_7_
  78.9 3.5 %partial13.1 = (f32[32,256]{1,0:T(8,128)}, f32[32,256]{1,0:T(8,128)}, f32[32,256]{1,0:T(8,128)}, f32[32,256]{1,0:T(8,128)}, f32[32,256]{1,0:T(8,128)}, /*index=5...) custom-call(s32[1]{0:T(128)} %bitcast.place, s32[1,6]{1,0:T(1,128)} %bitcast.23, ...), custom_call_target="tpu_custom_call" | custom-call | flops 201326592 | bytes 2097152 | tf_op jit(solution)/shard_map/partial13/pallas_call | solution.py:46
  82.3 0.0 copy-start.16
  82.3 0.0 copy-start.15
  82.3 1.0 collective-permute-start.11
  83.4 1.8 %collective-permute-start.12 = (f32[32,256]{1,0:T(8,128)}, f32[32,256]{1,0:T(8,128)S(1)}, u32[]{:S(2)}, u32[]{:S(2)}) collective-permute-start(f32[32,256]{1,0:T(8,128)} %get-tuple-element.57), channel_id=1, source_target_pairs={{0,4},{1,5},{2,6},{3,7},{4,0},{5,1},{6,2},{7,3},{8,12},{9,13},{10,... | collective-permute-start | bytes 98312 | tf_op jit(solution)/shard_map/ppermute | solution.py:205
  85.2 0.2 collective-permute-start.13
  85.4 2.1 %collective-permute-done.11.refs_1_ = f32[32,256]{1,0:T(8,128)S(1)} collective-permute-done((f32[32,256]{1,0:T(8,128)}, f32[32,256]{1,0:T(8,128)S(1)}, u32[]{:S(2)}, u32[]{:S(2)}) %collective-permute-start.11) | collective-permute-done | bytes 32800 | tf_op jit(solution)/shard_map/ppermute | solution.py:205
  87.5 2.5 %collective-permute-done.12.refs_2_ = f32[32,256]{1,0:T(8,128)S(1)} collective-permute-done((f32[32,256]{1,0:T(8,128)}, f32[32,256]{1,0:T(8,128)S(1)}, u32[]{:S(2)}, u32[]{:S(2)}) %collective-permute-start.12) | collective-permute-done | bytes 32800 | tf_op jit(solution)/shard_map/ppermute | solution.py:205
  89.9 1.3 collective-permute-done.13.refs_3_
  91.2 4.9 %all-to-all-done.1.known = bf16[32,32,256]{2,1,0:T(8,128)(2,1)S(1)} async-done(((bf16[32,32,256]{2,1,0:T(8,128)(2,1)}), bf16[32,32,256]{2,1,0:T(8,128)(2,1)S(1)}, u32[]{:S(2)}, u32[]{:S(2)}) %all-to-all-start.1) | async-done | bytes 524320 | tf_op jit(solution)/shard_map/all_to_all | solution.py:206
  96.1 0.0 copy-done.11
  96.1 0.8 copy-done.1
  96.9 4.9 %level2.1 = (f32[32,256]{1,0:T(8,128)}, bf16[32,32,256]{2,1,0:T(8,128)(2,1)}) custom-call(s32[1]{0:T(128)} %bitcast.place, s32[4,3,6]{2,1,0:T(4,128)} %copy-done.4, s32[4,3,6]{2,1,0:T(4,128)} %copy-done.5, s32[1,6]{1,0:T(1,128)} %bitcast.24, bf16[4,256,256]{2,1,0:T(8,128)(2,1)} %start.5, bf16[4,256,256]{2,1,0:T(8,128)(2,1)} %dinv.9, ...), custom_call_target="tpu_custom_call" | custom-call | flops 100663296 | bytes 3145728 | tf_op jit(solution)/shard_map/level2/pallas_call | solution.py:46
  101.7 5.5 %all-to-all-start.2 = ((bf16[32,32,256]{2,1,0:T(8,128)(2,1)}), bf16[32,32,256]{2,1,0:T(8,128)(2,1)S(1)}, u32[]{:S(2)}, u32[]{:S(2)}) async-start(bf16[32,32,256]{2,1,0:T(8,128)(2,1)} %get-tuple-element.59), calls=%async_computation.2 | async-start | bytes 1048576 | tf_op jit(solution)/shard_map/all_to_all | solution.py:206
  107.3 0.9 collective-permute-start.10
  108.2 2.4 %collective-permute-start.8 = (f32[32,256]{1,0:T(8,128)S(1)}, f32[32,256]{1,0:T(8,128)S(1)}, u32[]{:S(2)}, u32[]{:S(2)}) collective-permute-start(f32[32,256]{1,0:T(8,128)S(1)} %copy-done.16), channel_id=1, source_target_pairs={{0,6},{1,7},{2,0},{3,1},{4,2},{5,3},{6,4},{7,5},{8,14},{9,15},{10,... | collective-permute-start | bytes 98312 | tf_op jit(solution)/shard_map/ppermute | solution.py:205
  110.6 0.0 copy-done.15
  110.6 0.6 collective-permute-start.9
  111.2 1.3 collective-permute-done.10.refs_3_
  112.5 0.0 collective-permute-done.8.refs_1_
  112.5 3.5 %collective-permute-done.9.refs_2_ = f32[32,256]{1,0:T(8,128)S(1)} collective-permute-done((f32[32,256]{1,0:T(8,128)S(1)}, f32[32,256]{1,0:T(8,128)S(1)}, u32[]{:S(2)}, u32[]{:S(2)}) %collective-permute-start.9) | collective-permute-done | bytes 32800 | tf_op jit(solution)/shard_map/ppermute | solution.py:205
  116.0 0.6 copy-done.14
  116.6 4.5 %early3.1.start = f32[32,256]{1,0:T(8,128)} custom-call(s32[1]{0:T(128)} %bitcast.place, s32[4,3,6]{2,1,0:T(4,128)} %copy-done.4, s32[4,3,6]{2,1,0:T(4,128)} %copy-done.5, s32[1,6]{1,0:T(1,128)} %bitcast.25, bf16[4,256,256]{2,1,0:T(8,128)(2,1)} %start.5, bf16[4,256,256]{2,1,0:T(8,128)(2,1)} %dinv.9, bf16[32,32,256]{2,1,0:T(8,128)(2,1)} %copy-done.1, ...), custom_call_target="tpu_custom_call" | custom-call | flops 100663296 | bytes 3145728 | tf_op jit(solution)/shard_map/early3/pallas_call | solution.py:46
  121.1 2.2 %all-to-all-done.2.known = bf16[32,32,256]{2,1,0:T(8,128)(2,1)S(1)} async-done(((bf16[32,32,256]{2,1,0:T(8,128)(2,1)}), bf16[32,32,256]{2,1,0:T(8,128)(2,1)S(1)}, u32[]{:S(2)}, u32[]{:S(2)}) %all-to-all-start.2) | async-done | bytes 524320 | tf_op jit(solution)/shard_map/all_to_all | solution.py:206
  123.3 0.8 copy-done.3
  124.0 4.5 %level3.1 = f32[4,32,256]{2,1,0:T(8,128)} custom-call(s32[1]{0:T(128)} %bitcast.place, s32[4,3,6]{2,1,0:T(4,128)} %copy-done.4, s32[4,3,6]{2,1,0:T(4,128)} %copy-done.5, s32[1,6]{1,0:T(1,128)} %bitcast.26, f32[32,256]{1,0:T(8,128)} %early3.1.start, bf16[4,256,256]{2,1,0:T(8,128)(2,1)} %dinv.9, bf16[32,32,256]{2,1,0:T(8,128)(2,1)} %copy-done.3, ...), custom_call_target="tpu_custom_call" | custom-call | flops 100663296 | bytes 3145728 | tf_op jit(solution)/shard_map/level3/pallas_call | solution.py:46
  (24 shorter events, 0.0 us)
Async XLA Ops:
  6.5 37.8 %copy-start = (bf16[6,256,3,256]{3,1,2,0:T(8,128)(2,1)S(1)}, bf16[6,256,3,256]{3,1,2,0:T(8,128)(2,1)}, u32[]{:S(2)}) copy-start(bf16[6,256,3,256]{3,1,2,0:T(8,128)(2,1)} %param.7) | copy-start | bytes 7077892
  6.5 53.4 %all-gather.3.cloned.1.call-start = ((), (), s32[]{:S(2)}) async-start(), calls=%async_computation.3 | async-start | bytes 7077888 | tf_op jit(solution)/shard_map/all_gather | solution.py:208
  11.0 28.4 %all-to-all-start = ((bf16[32,32,256]{2,1,0:T(8,128)(2,1)}), bf16[32,32,256]{2,1,0:T(8,128)(2,1)S(1)}, u32[]{:S(2)}, u32[]{:S(2)}) async-start(bf16[32,32,256]{2,1,0:T(8,128)(2,1)} %get-tuple-element.34), calls=%async_computation | async-start | bytes 1048576 | tf_op jit(solution)/shard_map/all_to_all | solution.py:206
  22.6 93.4 %all-gather.5.cloned.1.call-start = ((), (), s32[]{:S(2)}) async-start(), calls=%async_computation.4 | async-start | bytes 7077888 | tf_op jit(solution)/shard_map/all_gather | solution.py:208
  23.3 6.5 %collective-permute-start = (s32[3,6]{1,0:T(4,128)S(1)}, s32[3,6]{1,0:T(4,128)S(1)}, u32[]{:S(2)}, u32[]{:S(2)}) collective-permute-start(s32[3,6]{1,0:T(4,128)S(1)} %bitcast.29), channel_id=1, source_target_pairs={{0,2},{1,3},{2,4},{3,5},{4,6},{5,7},{6,0},{7,1},{8,10},{9,11},{10,... | collective-permute-start | bytes 224 | tf_op jit(solution)/shard_map/ppermute | solution.py:205
  24.9 5.2 %collective-permute-start.1 = (s32[3,6]{1,0:T(4,128)S(1)}, s32[3,6]{1,0:T(4,128)S(1)}, u32[]{:S(2)}, u32[]{:S(2)}) collective-permute-start(s32[3,6]{1,0:T(4,128)S(1)} %bitcast.30), channel_id=1, source_target_pairs={{0,4},{1,5},{2,6},{3,7},{4,0},{5,1},{6,2},{7,3},{8,12},{9,13},{10,... | collective-permute-start | bytes 224 | tf_op jit(solution)/shard_map/ppermute | solution.py:205
  27.8 3.6 %collective-permute-start.2 = (s32[3,6]{1,0:T(4,128)S(1)}, s32[3,6]{1,0:T(4,128)S(1)}, u32[]{:S(2)}, u32[]{:S(2)}) collective-permute-start(s32[3,6]{1,0:T(4,128)S(1)} %bitcast.31), channel_id=1, source_target_pairs={{0,6},{1,7},{2,0},{3,1},{4,2},{5,3},{6,4},{7,5},{8,14},{9,15},{10,... | collective-permute-start | bytes 224 | tf_op jit(solution)/shard_map/ppermute | solution.py:205
  31.4 8.0 %copy-start.4 = (s32[4,3,6]{2,1,0:T(4,128)}, s32[4,3,6]{2,1,0:T(4,128)S(1)}, u32[]{:S(2)}) copy-start(s32[4,3,6]{2,1,0:T(4,128)S(1)} %pad_add_fusion.here) | copy-start | bytes 868
  31.4 1.3 collective-permute-start.3
  32.6 6.8 %copy-start.5 = (s32[4,3,6]{2,1,0:T(4,128)}, s32[4,3,6]{2,1,0:T(4,128)S(1)}, u32[]{:S(2)}) copy-start(s32[4,3,6]{2,1,0:T(4,128)S(1)} %collective-permute-done.3.there) | copy-start | bytes 868
  39.4 0.8 copy-start.2
  44.4 34.4 %collective-permute-start.7 = (bf16[6,3,256,256]{3,2,1,0:T(8,128)(2,1)S(1)}, bf16[6,3,256,256]{3,2,1,0:T(8,128)(2,1)}, u32[]{:S(2)}, u32[]{:S(2)}) collective-permute-start(bf16[6,3,256,256]{3,2,1,0:T(8,128)(2,1)S(1)} %bitcast.19), channel_id=1, source_target_pairs={{0,1},{1,0},{2,3},{3,2},{4,5},{5,4},{6,7},{7,6},{8,9},{9,8},{10,11... | collective-permute-start | bytes 7077896 | tf_op jit(solution)/shard_map/ppermute | solution.py:205
  44.5 20.2 %collective-permute-start.4 = (bf16[2,6,32,256]{3,2,1,0:T(8,128)(2,1)}, bf16[2,6,32,256]{3,2,1,0:T(8,128)(2,1)S(1)}, u32[]{:S(2)}, u32[]{:S(2)}) collective-permute-start(bf16[2,6,32,256]{3,2,1,0:T(8,128)(2,1)} %get-tuple-element.42), channel_id=1, source_target_pairs={{0,2},{1,3},{2,4},{3,5},{4,6},{5,7},{6,0},{7,1},{8,10},{9,11},{10,... | collective-permute-start | bytes 589832 | tf_op jit(solution)/shard_map/ppermute | solution.py:205
  46.1 18.6 %collective-permute-start.5 = (bf16[2,6,32,256]{3,2,1,0:T(8,128)(2,1)}, bf16[2,6,32,256]{3,2,1,0:T(8,128)(2,1)S(1)}, u32[]{:S(2)}, u32[]{:S(2)}) collective-permute-start(bf16[2,6,32,256]{3,2,1,0:T(8,128)(2,1)} %get-tuple-element.43), channel_id=1, source_target_pairs={{0,4},{1,5},{2,6},{3,7},{4,0},{5,1},{6,2},{7,3},{8,12},{9,13},{10,... | collective-permute-start | bytes 589832 | tf_op jit(solution)/shard_map/ppermute | solution.py:205
  49.0 15.7 %collective-permute-start.6 = (bf16[2,6,32,256]{3,2,1,0:T(8,128)(2,1)}, bf16[2,6,32,256]{3,2,1,0:T(8,128)(2,1)S(1)}, u32[]{:S(2)}, u32[]{:S(2)}) collective-permute-start(bf16[2,6,32,256]{3,2,1,0:T(8,128)(2,1)} %get-tuple-element.44), channel_id=1, source_target_pairs={{0,6},{1,7},{2,0},{3,1},{4,2},{5,3},{6,4},{7,5},{8,14},{9,15},{10,... | collective-permute-start | bytes 589832 | tf_op jit(solution)/shard_map/ppermute | solution.py:205
  64.7 14.1 %copy-start.6 = (bf16[2,6,32,256]{3,2,1,0:T(8,128)(2,1)}, bf16[2,6,32,256]{3,2,1,0:T(8,128)(2,1)S(1)}, u32[]{:S(2)}) copy-start(bf16[2,6,32,256]{3,2,1,0:T(8,128)(2,1)S(1)} %collective-permute-done.4.refs_1_) | copy-start | bytes 589828
  64.7 14.1 %copy-start.7 = (bf16[2,6,32,256]{3,2,1,0:T(8,128)(2,1)}, bf16[2,6,32,256]{3,2,1,0:T(8,128)(2,1)S(1)}, u32[]{:S(2)}) copy-start(bf16[2,6,32,256]{3,2,1,0:T(8,128)(2,1)S(1)} %collective-permute-done.5.refs_2_) | copy-start | bytes 589828
  64.7 14.1 %copy-start.8 = (bf16[2,6,32,256]{3,2,1,0:T(8,128)(2,1)}, bf16[2,6,32,256]{3,2,1,0:T(8,128)(2,1)S(1)}, u32[]{:S(2)}) copy-start(bf16[2,6,32,256]{3,2,1,0:T(8,128)(2,1)S(1)} %collective-permute-done.6.refs_3_) | copy-start | bytes 589828
  64.7 31.3 %all-to-all-start.1 = ((bf16[32,32,256]{2,1,0:T(8,128)(2,1)}), bf16[32,32,256]{2,1,0:T(8,128)(2,1)S(1)}, u32[]{:S(2)}, u32[]{:S(2)}) async-start(bf16[32,32,256]{2,1,0:T(8,128)(2,1)} %get-tuple-element.45), calls=%async_computation.1 | async-start | bytes 1048576 | tf_op jit(solution)/shard_map/all_to_all | solution.py:206
  82.3 24.9 %copy-start.17 = (f32[32,256]{1,0:T(8,128)S(1)}, f32[32,256]{1,0:T(8,128)}, u32[]{:S(2)}) copy-start(f32[32,256]{1,0:T(8,128)} %get-tuple-element.54) | copy-start | bytes 98308
  82.3 25.9 %copy-start.16 = (f32[32,256]{1,0:T(8,128)S(1)}, f32[32,256]{1,0:T(8,128)}, u32[]{:S(2)}) copy-start(f32[32,256]{1,0:T(8,128)} %get-tuple-element.52) | copy-start | bytes 98308
  82.3 28.2 %copy-start.15 = (f32[32,256]{1,0:T(8,128)S(1)}, f32[32,256]{1,0:T(8,128)}, u32[]{:S(2)}) copy-start(f32[32,256]{1,0:T(8,128)} %get-tuple-element.53) | copy-start | bytes 98308
  82.3 5.1 %collective-permute-start.11 = (f32[32,256]{1,0:T(8,128)}, f32[32,256]{1,0:T(8,128)S(1)}, u32[]{:S(2)}, u32[]{:S(2)}) collective-permute-start(f32[32,256]{1,0:T(8,128)} %get-tuple-element.56), channel_id=1, source_target_pairs={{0,6},{1,7},{2,0},{3,1},{4,2},{5,3},{6,4},{7,5},{8,14},{9,15},{10,... | collective-permute-start | bytes 98312 | tf_op jit(solution)/shard_map/ppermute | solution.py:205
  83.4 6.6 %collective-permute-start.12 = (f32[32,256]{1,0:T(8,128)}, f32[32,256]{1,0:T(8,128)S(1)}, u32[]{:S(2)}, u32[]{:S(2)}) collective-permute-start(f32[32,256]{1,0:T(8,128)} %get-tuple-element.57), channel_id=1, source_target_pairs={{0,4},{1,5},{2,6},{3,7},{4,0},{5,1},{6,2},{7,3},{8,12},{9,13},{10,... | collective-permute-start | bytes 98312 | tf_op jit(solution)/shard_map/ppermute | solution.py:205
  85.2 6.0 %collective-permute-start.13 = (f32[32,256]{1,0:T(8,128)}, f32[32,256]{1,0:T(8,128)S(1)}, u32[]{:S(2)}, u32[]{:S(2)}) collective-permute-start(f32[32,256]{1,0:T(8,128)} %get-tuple-element.58), channel_id=1, source_target_pairs={{0,2},{1,3},{2,4},{3,5},{4,6},{5,7},{6,0},{7,1},{8,10},{9,11},{10,... | collective-permute-start | bytes 98312 | tf_op jit(solution)/shard_map/ppermute | solution.py:205
  87.4 8.6 %copy-start.9 = (f32[32,256]{1,0:T(8,128)}, f32[32,256]{1,0:T(8,128)S(1)}, u32[]{:S(2)}) copy-start(f32[32,256]{1,0:T(8,128)S(1)} %collective-permute-done.11.refs_1_) | copy-start | bytes 98308
  89.9 6.2 %copy-start.11 = (f32[32,256]{1,0:T(8,128)}, f32[32,256]{1,0:T(8,128)S(1)}, u32[]{:S(2)}) copy-start(f32[32,256]{1,0:T(8,128)S(1)} %collective-permute-done.12.refs_2_) | copy-start | bytes 98308
  91.2 4.9 %copy-start.13 = (f32[32,256]{1,0:T(8,128)}, f32[32,256]{1,0:T(8,128)S(1)}, u32[]{:S(2)}) copy-start(f32[32,256]{1,0:T(8,128)S(1)} %collective-permute-done.13.refs_3_) | copy-start | bytes 98308
  96.1 0.8 copy-start.1
  101.7 21.5 %all-to-all-start.2 = ((bf16[32,32,256]{2,1,0:T(8,128)(2,1)}), bf16[32,32,256]{2,1,0:T(8,128)(2,1)S(1)}, u32[]{:S(2)}, u32[]{:S(2)}) async-start(bf16[32,32,256]{2,1,0:T(8,128)(2,1)} %get-tuple-element.59), calls=%async_computation.2 | async-start | bytes 1048576 | tf_op jit(solution)/shard_map/all_to_all | solution.py:206
  107.3 5.2 %collective-permute-start.10 = (f32[32,256]{1,0:T(8,128)S(1)}, f32[32,256]{1,0:T(8,128)S(1)}, u32[]{:S(2)}, u32[]{:S(2)}) collective-permute-start(f32[32,256]{1,0:T(8,128)S(1)} %copy-done.17), channel_id=1, source_target_pairs={{0,2},{1,3},{2,4},{3,5},{4,6},{5,7},{6,0},{7,1},{8,10},{9,11},{10,... | collective-permute-start | bytes 98312 | tf_op jit(solution)/shard_map/ppermute | solution.py:205
  108.2 4.3 %collective-permute-start.8 = (f32[32,256]{1,0:T(8,128)S(1)}, f32[32,256]{1,0:T(8,128)S(1)}, u32[]{:S(2)}, u32[]{:S(2)}) collective-permute-start(f32[32,256]{1,0:T(8,128)S(1)} %copy-done.16), channel_id=1, source_target_pairs={{0,6},{1,7},{2,0},{3,1},{4,2},{5,3},{6,4},{7,5},{8,14},{9,15},{10,... | collective-permute-start | bytes 98312 | tf_op jit(solution)/shard_map/ppermute | solution.py:205
  110.6 5.4 %collective-permute-start.9 = (f32[32,256]{1,0:T(8,128)S(1)}, f32[32,256]{1,0:T(8,128)S(1)}, u32[]{:S(2)}, u32[]{:S(2)}) collective-permute-start(f32[32,256]{1,0:T(8,128)S(1)} %copy-done.15), channel_id=1, source_target_pairs={{0,4},{1,5},{2,6},{3,7},{4,0},{5,1},{6,2},{7,3},{8,12},{9,13},{10,... | collective-permute-start | bytes 98312 | tf_op jit(solution)/shard_map/ppermute | solution.py:205
  112.5 3.5 %copy-start.10 = (f32[32,256]{1,0:T(8,128)}, f32[32,256]{1,0:T(8,128)S(1)}, u32[]{:S(2)}) copy-start(f32[32,256]{1,0:T(8,128)S(1)} %collective-permute-done.10.refs_3_) | copy-start | bytes 98308
  112.5 3.5 %copy-start.12 = (f32[32,256]{1,0:T(8,128)}, f32[32,256]{1,0:T(8,128)S(1)}, u32[]{:S(2)}) copy-start(f32[32,256]{1,0:T(8,128)S(1)} %collective-permute-done.8.refs_1_) | copy-start | bytes 98308
  116.0 0.6 copy-start.14
  123.3 0.8 copy-start.3
Sparse Core Ops, SparseCore 0:
  9.2 50.6 all-gather.2
  61.8 48.9 all-gather.4

commit v7 on v6

--- a/solution.py
+++ b/solution.py
@@ -56,22 +56,49 @@
     )(*args)
 
 
-def first_kernel(place, rhs, dinv, answer, spread):
+def first_kernel(place, rhs, dinv, *refs):
+    tiles, answer, spread, cuts = refs[:4], refs[4], refs[5], refs[6:]
     residual = probe_rows(place[0], rhs[0]).astype(BF16)
     result = dot_nt(residual, dinv[0])
     answer[...] = result
     spread_out(result, spread)
-
-
-def first_call(place, rhs, dinv):
+    for n in range(4):
+        for slot in range(SLOTS):
+            cuts[n // 2][n % 2, slot * SIZE : (slot + 1) * SIZE] = tiles[n][0, slot]
+
+
+def first_call(place, rhs, dinv, tiles, pairs):
+    diag, cut = block_of((1, SIZE, SIZE), 0), (2, SLOTS * SIZE, SIZE)
     return call(
         first_kernel,
         "level0",
+        [((BLOCK, SIZE), F32), ((NT, BLOCK, SIZE), BF16), (cut, BF16), (cut, BF16)],
+        [SMEM, diag, diag] + [block_of((1, SLOTS, SIZE, SIZE), p) for p in pairs],
+        [block_of((BLOCK, SIZE)), block_of((NT, BLOCK, SIZE)), block_of(cut), block_of(cut)],
+        (place, rhs, dinv) + (tiles,) * 4,
+        moved=2**22,
+    )
+
+
+def solve_kernel(place, rhs, dinv, *refs):
+    total = probe_rows(place[0], rhs[0])
+    for sums in refs[:CHIPS]:
+        total = total - sums[...]
+    result = dot_nt(total.astype(BF16), dinv[0])
+    refs[CHIPS][...] = result
+    spread_out(result, refs[CHIPS + 1])
+
+
+def solve_call(name, level, place, rhs, dinv, back):
+    diag, flat = block_of((1, SIZE, SIZE), level), block_of((BLOCK, SIZE))
+    return call(
+        solve_kernel,
+        name,
         [((BLOCK, SIZE), F32), ((NT, BLOCK, SIZE), BF16)],
-        [SMEM, block_of((1, SIZE, SIZE), 0), block_of((1, SIZE, SIZE), 0)],
-        [block_of((BLOCK, SIZE)), block_of((NT, BLOCK, SIZE))],
-        (place, rhs, dinv),
-        moved=2**22,
+        [SMEM, diag, diag] + [flat] * CHIPS,
+        [flat, block_of((NT, BLOCK, SIZE))],
+        (place, rhs, dinv, *back),
+        moved=2**20,
     )
 
 
@@ -211,8 +238,8 @@
     own = cols.transpose(2, 1, 0).reshape(SLOTS, -1)
     here = jnp.stack([own] + [move(own, TURN[d]) for d in range(1, CHIPS)])
     there = move(here, SWAP)
-    answer0, spread0 = first_call(place, rhs, dinv)
-    gathered02 = gather(tiles[0:3:2].reshape(2, SLOTS * SIZE, SIZE))
+    answer0, spread0, cut12, cut45 = first_call(place, rhs, dinv, tiles, (1, 2, 4, 5))
+    gathered12, gathered45 = gather(cut12), gather(cut45)
 
     def send(picked):
         return [picked[0]] + [move(picked[d], TURN[d]) for d in range(1, CHIPS)]
@@ -222,18 +249,19 @@
 
     scalars = (place, here, there, live)
     known0 = over_row(spread0)
-    picked = pick_call("pick13", (1, 3), place, here, there, known0)
-    later, known0, *picked = lax.optimization_barrier((tiles, known0, *picked))
-    gathered45 = gather(later[4:6].reshape(2, SLOTS * SIZE, SIZE))
+    later, *picked = lax.optimization_barrier((tiles, *pick_call("pick0", (0,), place, here, there, known0)))
     swapped = move(later, SWAP)
     got = send(picked)
-    answer1, spread1 = level_call("level1", 1, 0, 0, True, True, *scalars, rhs, dinv, known0, gathered02, [], [])
-    spread1, *got = lax.optimization_barrier((spread1, *got))
+    back1 = give_back(partial_call("partial0", (0,), place, live, got, [], tiles, swapped))
+    answer1, spread1 = solve_call("level1", 1, place, rhs, dinv, back1)
     known1 = over_row(spread1)
 
-    sums = partial_call("partial13", (1, 3), place, live, got, [], tiles, swapped)
-    back2, back3 = give_back(sums[:CHIPS]), give_back(sums[CHIPS:])
-    answer2, spread2 = level_call("level2", 2, 2, 1, True, True, *scalars, rhs, dinv, known1, gathered02, back2, [])
+    known0, spread1 = lax.optimization_barrier((known0, spread1))
+    got = send(pick_call("pick3", (3,), place, here, there, known0))
+    (early2,) = level_call("early2", 2, 1, 0, True, False, *scalars, rhs, dinv, known0, gathered12, [], [])
+    known1, early2, *got = lax.optimization_barrier((known1, early2, *got))
+    back3 = give_back(partial_call("partial3", (3,), place, live, got, [], tiles, swapped))
+    answer2, spread2 = level_call("level2", 2, 2, 1, False, True, *scalars, early2, dinv, known1, gathered12, [], [])
     known2 = over_row(spread2)
     (early3,) = level_call("early3", 3, 4, 0, True, False, *scalars, rhs, dinv, known1, gathered45, back3, [])
     (solved,) = level_call(

time: 136 us -> 134 us (0.985)
  Pallas kernels: 26.2 us -> 31.7 us
  local copies, waits for them, and re-layouts: 8.74 us -> 5.02 us
  waiting for transfers between devices: 36.8 us -> 33.2 us
    ppermute x14 -> x17, waiting for transfers between devices: 13.4 us -> 24.9 us  [local(): move = lambda array, pairs: lax.ppermute(array, 'col', pairs)]
    all_gather x2, waiting for transfers between devices: 9.56 us -> 0.01 us  [local(): gather = lambda array: lax.all_gather(array, 'col', axis=0, tiled=False)]
    all_to_all x3, waiting for transfers between devices: 13.8 us -> 7.53 us  [local(): over_row = lambda array: lax.all_to_all(array, 'row', 0, 0, tiled=True)]
    pallas_call x7 -> x10, Pallas kernels: 26.2 us -> 31.7 us  [call(): pl.pallas_call(kernel, grid=(1,), out_shape=tuple((jax.ShapeDtypeStruct(s...]
    ppermute x14 -> x17, starting transfers between devices: 18.8 us -> 23.3 us  [local(): move = lambda array, pairs: lax.ppermute(array, 'col', pairs)]
    slice x2 -> x0, local copies, waits for them, and re-layouts: 4.34 us -> none  [the longest x1 2.23 us: local(): gathered02 = gather(tiles[0:3:2].reshape(2, SLOTS * SIZE, SIZE))]
    all_to_all x3, starting transfers between devices: 31.2 us -> 27.1 us  [local(): over_row = lambda array: lax.all_to_all(array, 'row', 0, 0, tiled=True)]
    unnamed x37 -> x41, local copies, waits for them, and re-layouts: 3.72 us -> 5.02 us
  transfers between devices with their start and end apart: 19 -> 22, of which waited for: 12 -> 15; matrix products, arithmetic and copies ran while one was open for 3% -> 0% of each run, Pallas kernels for 16% -> 18%
where the time goes in v7:
time: 134 us
  starting transfers between devices  50.4 us (38%)
  waiting for transfers between devices  33.2 us (25%)
  Pallas kernels  31.7 us (24%)
  between operations  13.6 us (10%)
  local copies, waits for them, and re-layouts  5.02 us (4%)
    pallas_call x10, Pallas kernels, call(): pl.pallas_call(kernel, grid=(1,), out_shape=tuple((jax.ShapeDtypeStruct(s...  31.7 us
    all_to_all x3, starting transfers between devices, local(): over_row = lambda array: lax.all_to_all(array, 'row', 0, 0, tiled=True)  27.1 us
    ppermute x17, waiting for transfers between devices, local(): move = lambda array, pairs: lax.ppermute(array, 'col', pairs)  24.9 us
    ppermute x17, starting transfers between devices, local(): move = lambda array, pairs: lax.ppermute(array, 'col', pairs)  23.3 us
    all_to_all x3, waiting for transfers between devices, local(): over_row = lambda array: lax.all_to_all(array, 'row', 0, 0, tiled=True)  7.53 us
    unnamed x41, local copies, waits for them, and re-layouts  5.02 us
  transfers between devices with their start and end apart: 22, of which 15 were waited for; matrix products, arithmetic and copies ran while one was open for 0% of the time, Pallas kernels for 18%

profile of v7, /device:TPU:2, one launch (start us, length us, event | category | flops | bytes accessed | tf_op | source)
XLA Modules:
  0.0 133.9 jit_solution(15789587173677384191)
XLA Ops:
  6.5 0.0 all-gather.5.cloned.1.call-start
  6.5 3.1 %level0.1 = (f32[32,256]{1,0:T(8,128)}, bf16[32,32,256]{2,1,0:T(8,128)(2,1)}, bf16[2,768,256]{2,1,0:T(8,128)(2,1)}, bf16[2,768,256]{2,1,0:T(8,128)(2,1)}) custom-call(s32[1]{0:T(128)} %bitcast.place, bf16[4,256,256]{2,1,0:T(8,128)(2,1)} %start.3, bf16[4,256,256]{2,1,0:T(8,128)(2,1)} %dinv.11, bf16[6,3,256,256]{3,2,1,0:T(8,128)(2,1)} %bitcast.15, ...), custom_call_target="tpu_custom_call" | custom-call | bytes 4194304 | tf_op jit(solution)/shard_map/level0/pallas_call | solution.py:46
  9.7 0.0 all-gather.5.cloned.1.call-update
  9.7 0.0 all-gather.7.cloned.1.call-start
  9.8 0.7 all-gather.7.cloned.1.call-update
  10.5 11.6 %all-to-all-start = ((bf16[32,32,256]{2,1,0:T(8,128)(2,1)}), bf16[32,32,256]{2,1,0:T(8,128)(2,1)S(1)}, u32[]{:S(2)}, u32[]{:S(2)}) async-start(bf16[32,32,256]{2,1,0:T(8,128)(2,1)} %get-tuple-element.41), calls=%async_computation | async-start | bytes 1048576 | tf_op jit(solution)/shard_map/all_to_all | solution.py:233
  22.1 1.7 %collective-permute-start = (s32[3,6]{1,0:T(4,128)S(1)}, s32[3,6]{1,0:T(4,128)S(1)}, u32[]{:S(2)}, u32[]{:S(2)}) collective-permute-start(s32[3,6]{1,0:T(4,128)S(1)} %bitcast.34), channel_id=1, source_target_pairs={{0,2},{1,3},{2,4},{3,5},{4,6},{5,7},{6,0},{7,1},{8,10},{9,11},{10,... | collective-permute-start | bytes 224 | tf_op jit(solution)/shard_map/ppermute | solution.py:232
  23.8 2.9 %collective-permute-start.1 = (s32[3,6]{1,0:T(4,128)S(1)}, s32[3,6]{1,0:T(4,128)S(1)}, u32[]{:S(2)}, u32[]{:S(2)}) collective-permute-start(s32[3,6]{1,0:T(4,128)S(1)} %bitcast.35), channel_id=1, source_target_pairs={{0,4},{1,5},{2,6},{3,7},{4,0},{5,1},{6,2},{7,3},{8,12},{9,13},{10,... | collective-permute-start | bytes 224 | tf_op jit(solution)/shard_map/ppermute | solution.py:232
  26.7 1.3 %collective-permute-start.2 = (s32[3,6]{1,0:T(4,128)S(1)}, s32[3,6]{1,0:T(4,128)S(1)}, u32[]{:S(2)}, u32[]{:S(2)}) collective-permute-start(s32[3,6]{1,0:T(4,128)S(1)} %bitcast.36), channel_id=1, source_target_pairs={{0,6},{1,7},{2,0},{3,1},{4,2},{5,3},{6,4},{7,5},{8,14},{9,15},{10,... | collective-permute-start | bytes 224 | tf_op jit(solution)/shard_map/ppermute | solution.py:232
  28.0 0.0 collective-permute-done
  28.0 0.8 collective-permute-done.1
  28.9 1.4 %collective-permute-done.2 = s32[3,6]{1,0:T(4,128)S(1)} collective-permute-done((s32[3,6]{1,0:T(4,128)S(1)}, s32[3,6]{1,0:T(4,128)S(1)}, u32[]{:S(2)}, u32[]{:S(2)}) %collective-permute-start.2) | collective-permute-done | bytes 104 | tf_op jit(solution)/shard_map/ppermute | solution.py:232
  30.3 0.1 collective-permute-start.3
  30.4 1.2 collective-permute-done.3.there
  31.5 7.4 %all-to-all-done.known = bf16[32,32,256]{2,1,0:T(8,128)(2,1)S(1)} async-done(((bf16[32,32,256]{2,1,0:T(8,128)(2,1)}), bf16[32,32,256]{2,1,0:T(8,128)(2,1)S(1)}, u32[]{:S(2)}, u32[]{:S(2)}) %all-to-all-start) | async-done | bytes 524320 | tf_op jit(solution)/shard_map/all_to_all | solution.py:233
  38.9 0.0 copy-done.5
  38.9 0.8 copy-done.2
  39.7 1.8 %pick0.1 = (bf16[1,6,32,256]{3,2,1,0:T(8,128)(2,1)}, bf16[1,6,32,256]{3,2,1,0:T(8,128)(2,1)}, bf16[1,6,32,256]{3,2,1,0:T(8,128)(2,1)}, bf16[1,6,32,256]{3,2,1,0:T(8,128)(2,1)}) custom-call(s32[1]{0:T(128)} %bitcast.place, s32[4,3,6]{2,1,0:T(4,128)} %copy-done.5, s32[4,3,6]{2,1,0:T(4,128)} %copy-done.6, bf16[32,32,256]{2,1,0:T(8,128)(2,1)} %copy-done.2), custom_call_target="tpu_custom_call" | custom-call | bytes 2097152 | tf_op jit(solution)/shard_map/pick0/pallas_call | solution.py:46
  41.5 0.0 collective-permute-start.7
  41.5 1.7 %collective-permute-start.4 = (bf16[1,6,32,256]{3,2,1,0:T(8,128)(2,1)}, bf16[1,6,32,256]{3,2,1,0:T(8,128)(2,1)S(1)}, u32[]{:S(2)}, u32[]{:S(2)}) collective-permute-start(bf16[1,6,32,256]{3,2,1,0:T(8,128)(2,1)} %get-tuple-element.47), channel_id=1, source_target_pairs={{0,2},{1,3},{2,4},{3,5},{4,6},{5,7},{6,0},{7,1},{8,10},{9,11},{10,... | collective-permute-start | bytes 294920 | tf_op jit(solution)/shard_map/ppermute | solution.py:232
  43.2 2.9 %collective-permute-start.5 = (bf16[1,6,32,256]{3,2,1,0:T(8,128)(2,1)}, bf16[1,6,32,256]{3,2,1,0:T(8,128)(2,1)S(1)}, u32[]{:S(2)}, u32[]{:S(2)}) collective-permute-start(bf16[1,6,32,256]{3,2,1,0:T(8,128)(2,1)} %get-tuple-element.48), channel_id=1, source_target_pairs={{0,4},{1,5},{2,6},{3,7},{4,0},{5,1},{6,2},{7,3},{8,12},{9,13},{10,... | collective-permute-start | bytes 294920 | tf_op jit(solution)/shard_map/ppermute | solution.py:232
  46.1 1.4 %collective-permute-start.6 = (bf16[1,6,32,256]{3,2,1,0:T(8,128)(2,1)}, bf16[1,6,32,256]{3,2,1,0:T(8,128)(2,1)S(1)}, u32[]{:S(2)}, u32[]{:S(2)}) collective-permute-start(bf16[1,6,32,256]{3,2,1,0:T(8,128)(2,1)} %get-tuple-element.49), channel_id=1, source_target_pairs={{0,6},{1,7},{2,0},{3,1},{4,2},{5,3},{6,4},{7,5},{8,14},{9,15},{10,... | collective-permute-start | bytes 294920 | tf_op jit(solution)/shard_map/ppermute | solution.py:232
  47.5 3.2 %collective-permute-done.4.refs_1_ = bf16[1,6,32,256]{3,2,1,0:T(8,128)(2,1)S(1)} collective-permute-done((bf16[1,6,32,256]{3,2,1,0:T(8,128)(2,1)}, bf16[1,6,32,256]{3,2,1,0:T(8,128)(2,1)S(1)}, u32[]{:S(2)}, u32[]{:S(2)}) %collective-permute-start.4) | collective-permute-done | bytes 98336 | tf_op jit(solution)/shard_map/ppermute | solution.py:232
  50.6 5.4 %collective-permute-done.5.refs_2_ = bf16[1,6,32,256]{3,2,1,0:T(8,128)(2,1)S(1)} collective-permute-done((bf16[1,6,32,256]{3,2,1,0:T(8,128)(2,1)}, bf16[1,6,32,256]{3,2,1,0:T(8,128)(2,1)S(1)}, u32[]{:S(2)}, u32[]{:S(2)}) %collective-permute-start.5) | collective-permute-done | bytes 98336 | tf_op jit(solution)/shard_map/ppermute | solution.py:232
  56.1 0.0 collective-permute-done.6.refs_3_
  56.1 0.0 collective-permute-done.7.refs_5_
  56.1 0.6 copy-done.11
  56.7 0.1 copy-done.12
  56.7 0.8 copy-done.1
  57.5 2.3 %partial0.1 = (f32[32,256]{1,0:T(8,128)}, f32[32,256]{1,0:T(8,128)}, f32[32,256]{1,0:T(8,128)}, f32[32,256]{1,0:T(8,128)}) custom-call(s32[1]{0:T(128)} %bitcast.place, s32[1,6]{1,0:T(1,128)} %bitcast.26, bf16[1,6,32,256]{3,2,1,0:T(8,128)(2,1)} %get-tuple-element.46.refs_0_, bf16[1,6,32,256]{3,2,1,0:T(8,128)(2,1)} %copy-done.10, ...), custom_call_target="tpu_custom_call" | custom-call | flops 201326592 | bytes 2097152 | tf_op jit(solution)/shard_map/partial0/pallas_call | solution.py:46
  59.8 0.0 collective-permute-start.10
  59.9 3.2 %collective-permute-start.8 = (f32[32,256]{1,0:T(8,128)}, f32[32,256]{1,0:T(8,128)S(1)}, u32[]{:S(2)}, u32[]{:S(2)}) collective-permute-start(f32[32,256]{1,0:T(8,128)} %get-tuple-element.52), channel_id=1, source_target_pairs={{0,6},{1,7},{2,0},{3,1},{4,2},{5,3},{6,4},{7,5},{8,14},{9,15},{10,... | collective-permute-start | bytes 98312 | tf_op jit(solution)/shard_map/ppermute | solution.py:232
  63.1 1.5 %collective-permute-start.9 = (f32[32,256]{1,0:T(8,128)}, f32[32,256]{1,0:T(8,128)S(1)}, u32[]{:S(2)}, u32[]{:S(2)}) collective-permute-start(f32[32,256]{1,0:T(8,128)} %get-tuple-element.53), channel_id=1, source_target_pairs={{0,4},{1,5},{2,6},{3,7},{4,0},{5,1},{6,2},{7,3},{8,12},{9,13},{10,... | collective-permute-start | bytes 98312 | tf_op jit(solution)/shard_map/ppermute | solution.py:232
  64.6 0.6 collective-permute-done.10.refs_3_
  65.2 0.0 collective-permute-done.8.refs_1_
  65.2 3.5 %collective-permute-done.9.refs_2_ = f32[32,256]{1,0:T(8,128)S(1)} collective-permute-done((f32[32,256]{1,0:T(8,128)}, f32[32,256]{1,0:T(8,128)S(1)}, u32[]{:S(2)}, u32[]{:S(2)}) %collective-permute-start.9) | collective-permute-done | bytes 32800 | tf_op jit(solution)/shard_map/ppermute | solution.py:232
  68.7 0.0 copy-done.17
  68.7 0.6 copy-done.18
  69.3 2.2 %level1.1 = (f32[32,256]{1,0:T(8,128)}, bf16[32,32,256]{2,1,0:T(8,128)(2,1)}) custom-call(s32[1]{0:T(128)} %bitcast.place, bf16[4,256,256]{2,1,0:T(8,128)(2,1)} %start.3, bf16[4,256,256]{2,1,0:T(8,128)(2,1)} %dinv.11, f32[32,256]{1,0:T(8,128)} %get-tuple-element.51.refs_0_, f32[32,256]{1,0:T(8,128)} %copy-done.17, f32[32,256]{1,0:T(8,128)} %copy-done.18, ...), custom_call_target="tpu_custom_call" | custom-call | bytes 1048576 | tf_op jit(solution)/shard_map/level1/pallas_call | solution.py:46
  71.5 5.6 %all-to-all-start.1 = ((bf16[32,32,256]{2,1,0:T(8,128)(2,1)}), bf16[32,32,256]{2,1,0:T(8,128)(2,1)S(1)}, u32[]{:S(2)}, u32[]{:S(2)}) async-start(bf16[32,32,256]{2,1,0:T(8,128)(2,1)} %get-tuple-element.55), calls=%async_computation.1 | async-start | bytes 1048576 | tf_op jit(solution)/shard_map/all_to_all | solution.py:233
  77.1 1.8 %pick3.1 = (bf16[1,6,32,256]{3,2,1,0:T(8,128)(2,1)}, bf16[1,6,32,256]{3,2,1,0:T(8,128)(2,1)}, bf16[1,6,32,256]{3,2,1,0:T(8,128)(2,1)}, bf16[1,6,32,256]{3,2,1,0:T(8,128)(2,1)}) custom-call(s32[1]{0:T(128)} %bitcast.place, s32[4,3,6]{2,1,0:T(4,128)} %copy-done.5, s32[4,3,6]{2,1,0:T(4,128)} %copy-done.6, bf16[32,32,256]{2,1,0:T(8,128)(2,1)} %copy-done.2), custom_call_target="tpu_custom_call" | custom-call | bytes 2097152 | tf_op jit(solution)/shard_map/pick3/pallas_call | solution.py:46
  79.0 0.0 collective-permute-start.11
  79.0 1.6 %collective-permute-start.12 = (bf16[1,6,32,256]{3,2,1,0:T(8,128)(2,1)}, bf16[1,6,32,256]{3,2,1,0:T(8,128)(2,1)S(1)}, u32[]{:S(2)}, u32[]{:S(2)}) collective-permute-start(bf16[1,6,32,256]{3,2,1,0:T(8,128)(2,1)} %get-tuple-element.60), channel_id=1, source_target_pairs={{0,4},{1,5},{2,6},{3,7},{4,0},{5,1},{6,2},{7,3},{8,12},{9,13},{10,... | collective-permute-start | bytes 294920 | tf_op jit(solution)/shard_map/ppermute | solution.py:232
  80.5 2.5 %collective-permute-start.13 = (bf16[1,6,32,256]{3,2,1,0:T(8,128)(2,1)}, bf16[1,6,32,256]{3,2,1,0:T(8,128)(2,1)S(1)}, u32[]{:S(2)}, u32[]{:S(2)}) collective-permute-start(bf16[1,6,32,256]{3,2,1,0:T(8,128)(2,1)} %get-tuple-element.61), channel_id=1, source_target_pairs={{0,6},{1,7},{2,0},{3,1},{4,2},{5,3},{6,4},{7,5},{8,14},{9,15},{10,... | collective-permute-start | bytes 294920 | tf_op jit(solution)/shard_map/ppermute | solution.py:232
  83.0 4.5 %early2.1.start = f32[32,256]{1,0:T(8,128)} custom-call(s32[1]{0:T(128)} %bitcast.place, s32[4,3,6]{2,1,0:T(4,128)} %copy-done.5, s32[4,3,6]{2,1,0:T(4,128)} %copy-done.6, s32[1,6]{1,0:T(1,128)} %bitcast.27, bf16[4,256,256]{2,1,0:T(8,128)(2,1)} %start.3, bf16[4,256,256]{2,1,0:T(8,128)(2,1)} %dinv.11, bf16[32,32,256]{2,1,0:T(8,128)(2,1)} %copy-done.2, ...), custom_call_target="tpu_custom_call" | custom-call | flops 100663296 | bytes 3145728 | tf_op jit(solution)/shard_map/early2/pallas_call | solution.py:46
  87.5 0.5 collective-permute-done.11.refs_1_
  88.0 1.3 collective-permute-done.12.refs_2_
  89.3 2.6 %collective-permute-done.13.refs_3_ = bf16[1,6,32,256]{3,2,1,0:T(8,128)(2,1)S(1)} collective-permute-done((bf16[1,6,32,256]{3,2,1,0:T(8,128)(2,1)}, bf16[1,6,32,256]{3,2,1,0:T(8,128)(2,1)S(1)}, u32[]{:S(2)}, u32[]{:S(2)}) %collective-permute-start.13) | collective-permute-done | bytes 98336 | tf_op jit(solution)/shard_map/ppermute | solution.py:232
  91.9 0.1 all-to-all-done.1.known
  92.0 0.8 copy-done.3
  92.8 4.7 %level2.1 = (f32[32,256]{1,0:T(8,128)}, bf16[32,32,256]{2,1,0:T(8,128)(2,1)}) custom-call(s32[1]{0:T(128)} %bitcast.place, s32[4,3,6]{2,1,0:T(4,128)} %copy-done.5, s32[4,3,6]{2,1,0:T(4,128)} %copy-done.6, s32[1,6]{1,0:T(1,128)} %bitcast.28, f32[32,256]{1,0:T(8,128)} %early2.1.start, bf16[4,256,256]{2,1,0:T(8,128)(2,1)} %dinv.11, ...), custom_call_target="tpu_custom_call" | custom-call | flops 100663296 | bytes 3145728 | tf_op jit(solution)/shard_map/level2/pallas_call | solution.py:46
  97.5 9.8 %all-to-all-start.2 = ((bf16[32,32,256]{2,1,0:T(8,128)(2,1)}), bf16[32,32,256]{2,1,0:T(8,128)(2,1)S(1)}, u32[]{:S(2)}, u32[]{:S(2)}) async-start(bf16[32,32,256]{2,1,0:T(8,128)(2,1)} %get-tuple-element.73), calls=%async_computation.2 | async-start | bytes 1048576 | tf_op jit(solution)/shard_map/all_to_all | solution.py:233
  107.3 2.4 %partial3.1 = (f32[32,256]{1,0:T(8,128)}, f32[32,256]{1,0:T(8,128)}, f32[32,256]{1,0:T(8,128)}, f32[32,256]{1,0:T(8,128)}) custom-call(s32[1]{0:T(128)} %bitcast.place, s32[1,6]{1,0:T(1,128)} %bitcast.29, bf16[1,6,32,256]{3,2,1,0:T(8,128)(2,1)} %get-tuple-element.64.refs_0_, bf16[1,6,32,256]{3,2,1,0:T(8,128)(2,1)} %copy-done.7, ...), custom_call_target="tpu_custom_call" | custom-call | flops 201326592 | bytes 2097152 | tf_op jit(solution)/shard_map/partial3/pallas_call | solution.py:46
  109.7 0.1 collective-permute-start.14
  109.8 1.6 %collective-permute-start.15 = (f32[32,256]{1,0:T(8,128)}, f32[32,256]{1,0:T(8,128)S(1)}, u32[]{:S(2)}, u32[]{:S(2)}) collective-permute-start(f32[32,256]{1,0:T(8,128)} %get-tuple-element.70), channel_id=1, source_target_pairs={{0,4},{1,5},{2,6},{3,7},{4,0},{5,1},{6,2},{7,3},{8,12},{9,13},{10,... | collective-permute-start | bytes 98312 | tf_op jit(solution)/shard_map/ppermute | solution.py:232
  111.3 0.9 collective-permute-start.16
  112.2 1.6 %collective-permute-done.14.refs_1_ = f32[32,256]{1,0:T(8,128)S(1)} collective-permute-done((f32[32,256]{1,0:T(8,128)}, f32[32,256]{1,0:T(8,128)S(1)}, u32[]{:S(2)}, u32[]{:S(2)}) %collective-permute-start.14) | collective-permute-done | bytes 32800 | tf_op jit(solution)/shard_map/ppermute | solution.py:232
  113.8 1.6 %collective-permute-done.15.refs_2_ = f32[32,256]{1,0:T(8,128)S(1)} collective-permute-done((f32[32,256]{1,0:T(8,128)}, f32[32,256]{1,0:T(8,128)S(1)}, u32[]{:S(2)}, u32[]{:S(2)}) %collective-permute-start.15) | collective-permute-done | bytes 32800 | tf_op jit(solution)/shard_map/ppermute | solution.py:232
  115.4 1.3 collective-permute-done.16.refs_3_
  116.7 0.6 copy-done.15
  117.3 4.4 %early3.1.start = f32[32,256]{1,0:T(8,128)} custom-call(s32[1]{0:T(128)} %bitcast.place, s32[4,3,6]{2,1,0:T(4,128)} %copy-done.5, s32[4,3,6]{2,1,0:T(4,128)} %copy-done.6, s32[1,6]{1,0:T(1,128)} %bitcast.30, bf16[4,256,256]{2,1,0:T(8,128)(2,1)} %start.3, bf16[4,256,256]{2,1,0:T(8,128)(2,1)} %dinv.11, bf16[32,32,256]{2,1,0:T(8,128)(2,1)} %copy-done.3, ...), custom_call_target="tpu_custom_call" | custom-call | flops 100663296 | bytes 3145728 | tf_op jit(solution)/shard_map/early3/pallas_call | solution.py:46
  121.7 0.0 all-to-all-done.2.known
  121.7 0.8 copy-done.4
  122.5 4.5 %level3.1 = f32[4,32,256]{2,1,0:T(8,128)} custom-call(s32[1]{0:T(128)} %bitcast.place, s32[4,3,6]{2,1,0:T(4,128)} %copy-done.5, s32[4,3,6]{2,1,0:T(4,128)} %copy-done.6, s32[1,6]{1,0:T(1,128)} %bitcast.31, f32[32,256]{1,0:T(8,128)} %early3.1.start, bf16[4,256,256]{2,1,0:T(8,128)(2,1)} %dinv.11, bf16[32,32,256]{2,1,0:T(8,128)(2,1)} %copy-done.4, ...), custom_call_target="tpu_custom_call" | custom-call | flops 100663296 | bytes 3145728 | tf_op jit(solution)/shard_map/level3/pallas_call | solution.py:46
  (35 shorter events, 0.1 us)
Async XLA Ops:
  6.5 76.5 %all-gather.5.cloned.1.call-start = ((), (), s32[]{:S(2)}) async-start(), calls=%async_computation.3 | async-start | bytes 7077888 | tf_op jit(solution)/shard_map/all_gather | solution.py:235
  6.5 15.6 %copy-start.19 = (s32[6,1,3]{0,1,2:T(1,128)S(1)}, s32[6,1,3]{0,1,2:T(1,128)}, u32[]{:S(2)}) copy-start(s32[6,1,3]{0,1,2:T(1,128)} %param.8) | copy-start | bytes 220
  6.5 35.0 %copy-start = (bf16[6,256,3,256]{3,1,2,0:T(8,128)(2,1)S(1)}, bf16[6,256,3,256]{3,1,2,0:T(8,128)(2,1)}, u32[]{:S(2)}) copy-start(bf16[6,256,3,256]{3,1,2,0:T(8,128)(2,1)} %param.7) | copy-start | bytes 7077892
  9.7 102.5 %all-gather.7.cloned.1.call-start = ((), (), s32[]{:S(2)}) async-start(), calls=%async_computation.4 | async-start | bytes 7077888 | tf_op jit(solution)/shard_map/all_gather | solution.py:235
  10.5 28.5 %all-to-all-start = ((bf16[32,32,256]{2,1,0:T(8,128)(2,1)}), bf16[32,32,256]{2,1,0:T(8,128)(2,1)S(1)}, u32[]{:S(2)}, u32[]{:S(2)}) async-start(bf16[32,32,256]{2,1,0:T(8,128)(2,1)} %get-tuple-element.41), calls=%async_computation | async-start | bytes 1048576 | tf_op jit(solution)/shard_map/all_to_all | solution.py:233
  22.1 5.9 %collective-permute-start = (s32[3,6]{1,0:T(4,128)S(1)}, s32[3,6]{1,0:T(4,128)S(1)}, u32[]{:S(2)}, u32[]{:S(2)}) collective-permute-start(s32[3,6]{1,0:T(4,128)S(1)} %bitcast.34), channel_id=1, source_target_pairs={{0,2},{1,3},{2,4},{3,5},{4,6},{5,7},{6,0},{7,1},{8,10},{9,11},{10,... | collective-permute-start | bytes 224 | tf_op jit(solution)/shard_map/ppermute | solution.py:232
  23.8 5.1 %collective-permute-start.1 = (s32[3,6]{1,0:T(4,128)S(1)}, s32[3,6]{1,0:T(4,128)S(1)}, u32[]{:S(2)}, u32[]{:S(2)}) collective-permute-start(s32[3,6]{1,0:T(4,128)S(1)} %bitcast.35), channel_id=1, source_target_pairs={{0,4},{1,5},{2,6},{3,7},{4,0},{5,1},{6,2},{7,3},{8,12},{9,13},{10,... | collective-permute-start | bytes 224 | tf_op jit(solution)/shard_map/ppermute | solution.py:232
  26.7 3.6 %collective-permute-start.2 = (s32[3,6]{1,0:T(4,128)S(1)}, s32[3,6]{1,0:T(4,128)S(1)}, u32[]{:S(2)}, u32[]{:S(2)}) collective-permute-start(s32[3,6]{1,0:T(4,128)S(1)} %bitcast.36), channel_id=1, source_target_pairs={{0,6},{1,7},{2,0},{3,1},{4,2},{5,3},{6,4},{7,5},{8,14},{9,15},{10,... | collective-permute-start | bytes 224 | tf_op jit(solution)/shard_map/ppermute | solution.py:232
  30.3 8.7 %copy-start.5 = (s32[4,3,6]{2,1,0:T(4,128)}, s32[4,3,6]{2,1,0:T(4,128)S(1)}, u32[]{:S(2)}) copy-start(s32[4,3,6]{2,1,0:T(4,128)S(1)} %pad_add_fusion.here) | copy-start | bytes 868
  30.3 1.3 collective-permute-start.3
  31.5 7.4 %copy-start.6 = (s32[4,3,6]{2,1,0:T(4,128)}, s32[4,3,6]{2,1,0:T(4,128)S(1)}, u32[]{:S(2)}) copy-start(s32[4,3,6]{2,1,0:T(4,128)S(1)} %collective-permute-done.3.there) | copy-start | bytes 868
  38.9 0.8 copy-start.2
  41.5 14.5 %collective-permute-start.7 = (bf16[6,3,256,256]{3,2,1,0:T(8,128)(2,1)S(1)}, bf16[6,3,256,256]{3,2,1,0:T(8,128)(2,1)S(1)}, u32[]{:S(2)}, u32[]{:S(2)}) collective-permute-start(bf16[6,3,256,256]{3,2,1,0:T(8,128)(2,1)S(1)} %bitcast.21), channel_id=1, source_target_pairs={{0,1},{1,0},{2,3},{3,2},{4,5},{5,4},{6,7},{7,6},{8,9},{9,8},{10,11... | collective-permute-start | bytes 7077896 | tf_op jit(solution)/shard_map/ppermute | solution.py:232
  41.5 9.1 %collective-permute-start.4 = (bf16[1,6,32,256]{3,2,1,0:T(8,128)(2,1)}, bf16[1,6,32,256]{3,2,1,0:T(8,128)(2,1)S(1)}, u32[]{:S(2)}, u32[]{:S(2)}) collective-permute-start(bf16[1,6,32,256]{3,2,1,0:T(8,128)(2,1)} %get-tuple-element.47), channel_id=1, source_target_pairs={{0,2},{1,3},{2,4},{3,5},{4,6},{5,7},{6,0},{7,1},{8,10},{9,11},{10,... | collective-permute-start | bytes 294920 | tf_op jit(solution)/shard_map/ppermute | solution.py:232
  43.2 12.8 %collective-permute-start.5 = (bf16[1,6,32,256]{3,2,1,0:T(8,128)(2,1)}, bf16[1,6,32,256]{3,2,1,0:T(8,128)(2,1)S(1)}, u32[]{:S(2)}, u32[]{:S(2)}) collective-permute-start(bf16[1,6,32,256]{3,2,1,0:T(8,128)(2,1)} %get-tuple-element.48), channel_id=1, source_target_pairs={{0,4},{1,5},{2,6},{3,7},{4,0},{5,1},{6,2},{7,3},{8,12},{9,13},{10,... | collective-permute-start | bytes 294920 | tf_op jit(solution)/shard_map/ppermute | solution.py:232
  46.1 10.0 %collective-permute-start.6 = (bf16[1,6,32,256]{3,2,1,0:T(8,128)(2,1)}, bf16[1,6,32,256]{3,2,1,0:T(8,128)(2,1)S(1)}, u32[]{:S(2)}, u32[]{:S(2)}) collective-permute-start(bf16[1,6,32,256]{3,2,1,0:T(8,128)(2,1)} %get-tuple-element.49), channel_id=1, source_target_pairs={{0,6},{1,7},{2,0},{3,1},{4,2},{5,3},{6,4},{7,5},{8,14},{9,15},{10,... | collective-permute-start | bytes 294920 | tf_op jit(solution)/shard_map/ppermute | solution.py:232
  50.6 5.5 %copy-start.10 = (bf16[1,6,32,256]{3,2,1,0:T(8,128)(2,1)}, bf16[1,6,32,256]{3,2,1,0:T(8,128)(2,1)S(1)}, u32[]{:S(2)}) copy-start(bf16[1,6,32,256]{3,2,1,0:T(8,128)(2,1)S(1)} %collective-permute-done.4.refs_1_) | copy-start | bytes 294916
  56.1 0.6 copy-start.11
  56.1 0.7 copy-start.12
  56.1 1.4 %copy-start.1 = (bf16[6,3,256,256]{3,2,1,0:T(8,128)(2,1)}, bf16[6,3,256,256]{3,2,1,0:T(8,128)(2,1)S(1)}, u32[]{:S(2)}) copy-start(bf16[6,3,256,256]{3,2,1,0:T(8,128)(2,1)S(1)} %collective-permute-done.7.refs_5_) | copy-start | bytes 7077892
  59.8 5.3 %collective-permute-start.10 = (f32[32,256]{1,0:T(8,128)}, f32[32,256]{1,0:T(8,128)S(1)}, u32[]{:S(2)}, u32[]{:S(2)}) collective-permute-start(f32[32,256]{1,0:T(8,128)} %get-tuple-element.54), channel_id=1, source_target_pairs={{0,2},{1,3},{2,4},{3,5},{4,6},{5,7},{6,0},{7,1},{8,10},{9,11},{10,... | collective-permute-start | bytes 98312 | tf_op jit(solution)/shard_map/ppermute | solution.py:232
  59.9 5.3 %collective-permute-start.8 = (f32[32,256]{1,0:T(8,128)}, f32[32,256]{1,0:T(8,128)S(1)}, u32[]{:S(2)}, u32[]{:S(2)}) collective-permute-start(f32[32,256]{1,0:T(8,128)} %get-tuple-element.52), channel_id=1, source_target_pairs={{0,6},{1,7},{2,0},{3,1},{4,2},{5,3},{6,4},{7,5},{8,14},{9,15},{10,... | collective-permute-start | bytes 98312 | tf_op jit(solution)/shard_map/ppermute | solution.py:232
  63.1 5.6 %collective-permute-start.9 = (f32[32,256]{1,0:T(8,128)}, f32[32,256]{1,0:T(8,128)S(1)}, u32[]{:S(2)}, u32[]{:S(2)}) collective-permute-start(f32[32,256]{1,0:T(8,128)} %get-tuple-element.53), channel_id=1, source_target_pairs={{0,4},{1,5},{2,6},{3,7},{4,0},{5,1},{6,2},{7,3},{8,12},{9,13},{10,... | collective-permute-start | bytes 98312 | tf_op jit(solution)/shard_map/ppermute | solution.py:232
  65.2 3.5 %copy-start.16 = (f32[32,256]{1,0:T(8,128)}, f32[32,256]{1,0:T(8,128)S(1)}, u32[]{:S(2)}) copy-start(f32[32,256]{1,0:T(8,128)S(1)} %collective-permute-done.10.refs_3_) | copy-start | bytes 98308
  65.2 3.5 %copy-start.17 = (f32[32,256]{1,0:T(8,128)}, f32[32,256]{1,0:T(8,128)S(1)}, u32[]{:S(2)}) copy-start(f32[32,256]{1,0:T(8,128)S(1)} %collective-permute-done.8.refs_1_) | copy-start | bytes 98308
  68.7 0.6 copy-start.18
  71.5 20.5 %all-to-all-start.1 = ((bf16[32,32,256]{2,1,0:T(8,128)(2,1)}), bf16[32,32,256]{2,1,0:T(8,128)(2,1)S(1)}, u32[]{:S(2)}, u32[]{:S(2)}) async-start(bf16[32,32,256]{2,1,0:T(8,128)(2,1)} %get-tuple-element.55), calls=%async_computation.1 | async-start | bytes 1048576 | tf_op jit(solution)/shard_map/all_to_all | solution.py:233
  79.0 9.1 %collective-permute-start.11 = (bf16[1,6,32,256]{3,2,1,0:T(8,128)(2,1)}, bf16[1,6,32,256]{3,2,1,0:T(8,128)(2,1)S(1)}, u32[]{:S(2)}, u32[]{:S(2)}) collective-permute-start(bf16[1,6,32,256]{3,2,1,0:T(8,128)(2,1)} %get-tuple-element.59), channel_id=1, source_target_pairs={{0,2},{1,3},{2,4},{3,5},{4,6},{5,7},{6,0},{7,1},{8,10},{9,11},{10,... | collective-permute-start | bytes 294920 | tf_op jit(solution)/shard_map/ppermute | solution.py:232
  79.0 10.3 %collective-permute-start.12 = (bf16[1,6,32,256]{3,2,1,0:T(8,128)(2,1)}, bf16[1,6,32,256]{3,2,1,0:T(8,128)(2,1)S(1)}, u32[]{:S(2)}, u32[]{:S(2)}) collective-permute-start(bf16[1,6,32,256]{3,2,1,0:T(8,128)(2,1)} %get-tuple-element.60), channel_id=1, source_target_pairs={{0,4},{1,5},{2,6},{3,7},{4,0},{5,1},{6,2},{7,3},{8,12},{9,13},{10,... | collective-permute-start | bytes 294920 | tf_op jit(solution)/shard_map/ppermute | solution.py:232
  80.5 11.4 %collective-permute-start.13 = (bf16[1,6,32,256]{3,2,1,0:T(8,128)(2,1)}, bf16[1,6,32,256]{3,2,1,0:T(8,128)(2,1)S(1)}, u32[]{:S(2)}, u32[]{:S(2)}) collective-permute-start(bf16[1,6,32,256]{3,2,1,0:T(8,128)(2,1)} %get-tuple-element.61), channel_id=1, source_target_pairs={{0,6},{1,7},{2,0},{3,1},{4,2},{5,3},{6,4},{7,5},{8,14},{9,15},{10,... | collective-permute-start | bytes 294920 | tf_op jit(solution)/shard_map/ppermute | solution.py:232
  88.0 19.3 %copy-start.7 = (bf16[1,6,32,256]{3,2,1,0:T(8,128)(2,1)}, bf16[1,6,32,256]{3,2,1,0:T(8,128)(2,1)S(1)}, u32[]{:S(2)}) copy-start(bf16[1,6,32,256]{3,2,1,0:T(8,128)(2,1)S(1)} %collective-permute-done.11.refs_1_) | copy-start | bytes 294916
  89.3 18.0 %copy-start.8 = (bf16[1,6,32,256]{3,2,1,0:T(8,128)(2,1)}, bf16[1,6,32,256]{3,2,1,0:T(8,128)(2,1)S(1)}, u32[]{:S(2)}) copy-start(bf16[1,6,32,256]{3,2,1,0:T(8,128)(2,1)S(1)} %collective-permute-done.12.refs_2_) | copy-start | bytes 294916
  91.9 15.4 %copy-start.9 = (bf16[1,6,32,256]{3,2,1,0:T(8,128)(2,1)}, bf16[1,6,32,256]{3,2,1,0:T(8,128)(2,1)S(1)}, u32[]{:S(2)}) copy-start(bf16[1,6,32,256]{3,2,1,0:T(8,128)(2,1)S(1)} %collective-permute-done.13.refs_3_) | copy-start | bytes 294916
  92.0 0.8 copy-start.3
  97.5 24.2 %all-to-all-start.2 = ((bf16[32,32,256]{2,1,0:T(8,128)(2,1)}), bf16[32,32,256]{2,1,0:T(8,128)(2,1)S(1)}, u32[]{:S(2)}, u32[]{:S(2)}) async-start(bf16[32,32,256]{2,1,0:T(8,128)(2,1)} %get-tuple-element.73), calls=%async_computation.2 | async-start | bytes 1048576 | tf_op jit(solution)/shard_map/all_to_all | solution.py:233
  109.7 4.1 %collective-permute-start.14 = (f32[32,256]{1,0:T(8,128)}, f32[32,256]{1,0:T(8,128)S(1)}, u32[]{:S(2)}, u32[]{:S(2)}) collective-permute-start(f32[32,256]{1,0:T(8,128)} %get-tuple-element.69), channel_id=1, source_target_pairs={{0,6},{1,7},{2,0},{3,1},{4,2},{5,3},{6,4},{7,5},{8,14},{9,15},{10,... | collective-permute-start | bytes 98312 | tf_op jit(solution)/shard_map/ppermute | solution.py:232
  109.8 5.6 %collective-permute-start.15 = (f32[32,256]{1,0:T(8,128)}, f32[32,256]{1,0:T(8,128)S(1)}, u32[]{:S(2)}, u32[]{:S(2)}) collective-permute-start(f32[32,256]{1,0:T(8,128)} %get-tuple-element.70), channel_id=1, source_target_pairs={{0,4},{1,5},{2,6},{3,7},{4,0},{5,1},{6,2},{7,3},{8,12},{9,13},{10,... | collective-permute-start | bytes 98312 | tf_op jit(solution)/shard_map/ppermute | solution.py:232
  111.3 5.3 %collective-permute-start.16 = (f32[32,256]{1,0:T(8,128)}, f32[32,256]{1,0:T(8,128)S(1)}, u32[]{:S(2)}, u32[]{:S(2)}) collective-permute-start(f32[32,256]{1,0:T(8,128)} %get-tuple-element.71), channel_id=1, source_target_pairs={{0,2},{1,3},{2,4},{3,5},{4,6},{5,7},{6,0},{7,1},{8,10},{9,11},{10,... | collective-permute-start | bytes 98312 | tf_op jit(solution)/shard_map/ppermute | solution.py:232
  113.8 2.9 %copy-start.13 = (f32[32,256]{1,0:T(8,128)}, f32[32,256]{1,0:T(8,128)S(1)}, u32[]{:S(2)}) copy-start(f32[32,256]{1,0:T(8,128)S(1)} %collective-permute-done.14.refs_1_) | copy-start | bytes 98308
  115.4 1.3 copy-start.14
  116.7 0.6 copy-start.15
  121.7 0.8 copy-start.4
Sparse Core Ops, SparseCore 0:
  9.8 50.6 all-gather.4
  62.4 48.0 all-gather.6

commit v8 on v6

--- a/solution.py
+++ b/solution.py
@@ -19,6 +19,12 @@
 ANY = pl.BlockSpec(memory_space=pl.ANY)
 F32, BF16 = jnp.float32, jnp.bfloat16
 SWAP = [(p, p ^ 1) for p in range(PLACES)]
+SAME = [(2 * y, 2 * ((y + 1) % CHIPS)) for y in range(CHIPS)] + [
+    (2 * y + 1, 2 * ((y - 1) % CHIPS) + 1) for y in range(CHIPS)
+]
+CROSS = [(2 * y + 1, 2 * ((y + 1) % CHIPS)) for y in range(CHIPS)] + [
+    (2 * y, 2 * ((y - 1) % CHIPS) + 1) for y in range(CHIPS)
+]
 TURN = [[(p, (p + 2 * d) % PLACES) for p in range(PLACES)] for d in range(CHIPS)]
 
 
@@ -56,21 +62,26 @@
     )(*args)
 
 
-def first_kernel(place, rhs, dinv, answer, spread):
+def first_kernel(place, rhs, dinv, *refs):
+    tiles, answer, spread, cuts = refs[:4], refs[4], refs[5], refs[6:]
     residual = probe_rows(place[0], rhs[0]).astype(BF16)
     result = dot_nt(residual, dinv[0])
     answer[...] = result
     spread_out(result, spread)
-
-
-def first_call(place, rhs, dinv):
+    for n in range(4):
+        for slot in range(SLOTS):
+            cuts[min(n, 2)][max(n - 2, 0), slot * SIZE : (slot + 1) * SIZE] = tiles[n][0, slot]
+
+
+def first_call(place, rhs, dinv, tiles, pairs):
+    diag, cuts = block_of((1, SIZE, SIZE), 0), [(n, SLOTS * SIZE, SIZE) for n in (1, 1, 2)]
     return call(
         first_kernel,
         "level0",
-        [((BLOCK, SIZE), F32), ((NT, BLOCK, SIZE), BF16)],
-        [SMEM, block_of((1, SIZE, SIZE), 0), block_of((1, SIZE, SIZE), 0)],
-        [block_of((BLOCK, SIZE)), block_of((NT, BLOCK, SIZE))],
-        (place, rhs, dinv),
+        [((BLOCK, SIZE), F32), ((NT, BLOCK, SIZE), BF16)] + [(cut, BF16) for cut in cuts],
+        [SMEM, diag, diag] + [block_of((1, SLOTS, SIZE, SIZE), p) for p in pairs],
+        [block_of((BLOCK, SIZE)), block_of((NT, BLOCK, SIZE))] + [block_of(cut) for cut in cuts],
+        (place, rhs, dinv) + (tiles,) * 4,
         moved=2**22,
     )
 
@@ -199,6 +210,48 @@
     )
 
 
+def pieces_kernel(pair, returned, place, here, there, live, rhs, dinv, known, *refs):
+    refs = list(refs)
+    back = [refs.pop(0) for _ in range(returned)]
+    sources = [refs.pop(0) for _ in range(PLACES)]
+    answer, spread, held, sems = refs
+    sources = [s.at[pair] if s.shape[0] > 1 else s.at[0] for s in sources]
+    copies = [pltpu.make_async_copy(sources[n], held.at[n], sems.at[n]) for n in range(PLACES)]
+    for copy in copies:
+        copy.start()
+    total = probe_rows(place[0], rhs[0])
+    for sums in back:
+        total = total - sums[...]
+    chip, core = lax.div(place[0], 2), lax.rem(place[0], 2)
+    near, other = 1 + 2 * core, 3 - 2 * core
+    kinds = [(0, 0), (near, 0), (near, 1), (2, 0), (0, 1), (other, 1), (other, 0), (2, 1)]
+    for n, (turn, side) in enumerate(kinds):
+        copies[n].wait()
+        cols = there if side else here
+        owner = 2 * lax.rem(chip + CHIPS - turn, CHIPS) + (1 - core if side else core)
+        for slot in range(SLOTS):
+            block = masked(known[cols[turn, slot, pair]], owner * SLOTS + slot < live[0, pair])
+            total = total - dot_nt(block, held[n, slot])
+    result = dot_nt(total.astype(BF16), dinv[0])
+    answer[...] = result
+    spread_out(result, spread)
+
+
+def pieces_call(name, level, pair, place, here, there, live, rhs, dinv, known, back, sources):
+    flat, diag = block_of((BLOCK, SIZE)), block_of((1, SIZE, SIZE), level)
+    return call(
+        functools.partial(pieces_kernel, pair, len(back)),
+        name,
+        [((BLOCK, SIZE), F32), ((NT, BLOCK, SIZE), BF16)],
+        [SMEM] * 4 + [diag, diag, block_of((NT, BLOCK, SIZE))] + [flat] * len(back) + [ANY] * PLACES,
+        [flat, block_of((NT, BLOCK, SIZE))],
+        (place, here, there, live, rhs, dinv, known, *back, *sources),
+        [pltpu.VMEM((PLACES, SLOTS, SIZE, SIZE), BF16), pltpu.SemaphoreType.DMA((PLACES,))],
+        flops=2 * 24 * BLOCK * SIZE * SIZE,
+        moved=24 * SIZE * SIZE * 2,
+    )
+
+
 def local(rhs, dinv, factor, cols, live):
     place = lax.axis_index("col").astype(jnp.int32).reshape(1)
     tiles = factor.transpose(0, 2, 1, 3)
@@ -211,8 +264,10 @@
     own = cols.transpose(2, 1, 0).reshape(SLOTS, -1)
     here = jnp.stack([own] + [move(own, TURN[d]) for d in range(1, CHIPS)])
     there = move(here, SWAP)
-    answer0, spread0 = first_call(place, rhs, dinv)
-    gathered02 = gather(tiles[0:3:2].reshape(2, SLOTS * SIZE, SIZE))
+    answer0, spread0, cut0, cut2, cut45 = first_call(place, rhs, dinv, tiles, (0, 2, 4, 5))
+    gathered0, gathered45 = gather(cut0), gather(cut45)
+    cut2 = cut2.reshape(1, SLOTS, SIZE, SIZE)
+    same, cross = move(cut2, SAME), move(cut2, CROSS)
 
     def send(picked):
         return [picked[0]] + [move(picked[d], TURN[d]) for d in range(1, CHIPS)]
@@ -222,18 +277,21 @@
 
     scalars = (place, here, there, live)
     known0 = over_row(spread0)
+    known0, same, cross = lax.optimization_barrier((known0, same, cross))
     picked = pick_call("pick13", (1, 3), place, here, there, known0)
     later, known0, *picked = lax.optimization_barrier((tiles, known0, *picked))
-    gathered45 = gather(later[4:6].reshape(2, SLOTS * SIZE, SIZE))
     swapped = move(later, SWAP)
     got = send(picked)
-    answer1, spread1 = level_call("level1", 1, 0, 0, True, True, *scalars, rhs, dinv, known0, gathered02, [], [])
-    spread1, *got = lax.optimization_barrier((spread1, *got))
+    far = move(same, SAME)
+    answer1, spread1 = level_call("level1", 1, 0, 0, True, True, *scalars, rhs, dinv, known0, gathered0, [], [])
+    spread1, far, *got = lax.optimization_barrier((spread1, far, *got))
     known1 = over_row(spread1)
 
     sums = partial_call("partial13", (1, 3), place, live, got, [], tiles, swapped)
     back2, back3 = give_back(sums[:CHIPS]), give_back(sums[CHIPS:])
-    answer2, spread2 = level_call("level2", 2, 2, 1, True, True, *scalars, rhs, dinv, known1, gathered02, back2, [])
+    near = [same, cross, far]
+    sources = [tiles] + near + [swapped] + [move(a, SWAP) for a in near]
+    answer2, spread2 = pieces_call("level2", 2, 2, *scalars, rhs, dinv, known1, back2, sources)
     known2 = over_row(spread2)
     (early3,) = level_call("early3", 3, 4, 0, True, False, *scalars, rhs, dinv, known1, gathered45, back3, [])
     (solved,) = level_call(

time: 136 us -> 133 us (0.978)
  waiting for transfers between devices: 36.8 us -> 42.1 us
  local copies, waits for them, and re-layouts: 8.74 us -> 3.63 us
  starting transfers between devices: 50.1 us -> 46.1 us
    ppermute x14 -> x20, waiting for transfers between devices: 13.4 us -> 34.1 us  [local(): move = lambda array, pairs: lax.ppermute(array, 'col', pairs)]
    all_gather x2, waiting for transfers between devices: 9.56 us -> 0.01 us  [local(): gather = lambda array: lax.all_gather(array, 'col', axis=0, tiled=False)]
    all_to_all x3, waiting for transfers between devices: 13.8 us -> 7.28 us  [local(): over_row = lambda array: lax.all_to_all(array, 'row', 0, 0, tiled=True)]
    slice x2 -> x0, local copies, waits for them, and re-layouts: 4.34 us -> none  [the longest x1 2.23 us: local(): gathered02 = gather(tiles[0:3:2].reshape(2, SLOTS * SIZE, SIZE))]
    all_to_all x3, starting transfers between devices: 31.2 us -> 27.2 us  [local(): over_row = lambda array: lax.all_to_all(array, 'row', 0, 0, tiled=True)]
    unnamed x37 -> x43, local copies, waits for them, and re-layouts: 3.72 us -> 3.63 us
    ppermute x14 -> x20, starting transfers between devices: 18.8 us -> 18.9 us  [local(): move = lambda array, pairs: lax.ppermute(array, 'col', pairs)]
  transfers between devices with their start and end apart: 19 -> 25, of which waited for: 12 -> 12; matrix products, arithmetic and copies ran while one was open for 3% -> 0% of each run, Pallas kernels for 16% -> 15%
where the time goes in v8:
time: 133 us
  starting transfers between devices  46.1 us (35%)
  waiting for transfers between devices  42.1 us (32%)
  Pallas kernels  27.2 us (20%)
  between operations  13.6 us (10%)
  local copies, waits for them, and re-layouts  3.63 us (3%)
    ppermute x20, waiting for transfers between devices, local(): move = lambda array, pairs: lax.ppermute(array, 'col', pairs)  34.1 us
    all_to_all x3, starting transfers between devices, local(): over_row = lambda array: lax.all_to_all(array, 'row', 0, 0, tiled=True)  27.2 us
    pallas_call x7, Pallas kernels, call(): pl.pallas_call(kernel, grid=(1,), out_shape=tuple((jax.ShapeDtypeStruct(s...  27.2 us
    ppermute x20, starting transfers between devices, local(): move = lambda array, pairs: lax.ppermute(array, 'col', pairs)  18.9 us
    all_to_all x3, waiting for transfers between devices, local(): over_row = lambda array: lax.all_to_all(array, 'row', 0, 0, tiled=True)  7.28 us
    unnamed x43, local copies, waits for them, and re-layouts  3.63 us
  transfers between devices with their start and end apart: 25, of which 12 were waited for; matrix products, arithmetic and copies ran while one was open for 0% of the time, Pallas kernels for 15%

profile of v8, /device:TPU:2, one launch (start us, length us, event | category | flops | bytes accessed | tf_op | source)
XLA Modules:
  0.0 132.6 jit_solution(2018101995913424020)
XLA Ops:
  6.5 3.2 %level0.1 = (f32[32,256]{1,0:T(8,128)}, bf16[32,32,256]{2,1,0:T(8,128)(2,1)}, bf16[1,768,256]{2,1,0:T(8,128)(2,1)}, bf16[1,768,256]{2,1,0:T(8,128)(2,1)}, bf16[2,768,256]{2,1,0:T(8,128)(2,1)}) custom-call(s32[1]{0:T(128)} %bitcast.place, bf16[4,256,256]{2,1,0:T(8,128)(2,1)} %rhs.3, bf16[4,256,256]{2,1,0:T(8,128)(2,1)} %dinv.9, ...), custom_call_target="tpu_custom_call" | custom-call | bytes 4194304 | tf_op jit(solution)/shard_map/level0/pallas_call | solution.py:52
  9.7 0.0 all-gather.5.cloned.1.call-update
  9.7 0.0 all-gather.7.cloned.1.call-start
  9.8 0.7 all-gather.7.cloned.1.call-update
  10.5 11.6 %all-to-all-start = ((bf16[32,32,256]{2,1,0:T(8,128)(2,1)}), bf16[32,32,256]{2,1,0:T(8,128)(2,1)S(1)}, u32[]{:S(2)}, u32[]{:S(2)}) async-start(bf16[32,32,256]{2,1,0:T(8,128)(2,1)} %get-tuple-element.41), calls=%async_computation | async-start | bytes 1048576 | tf_op jit(solution)/shard_map/all_to_all | solution.py:259
  22.1 1.7 %collective-permute-start.4 = (bf16[1,3,256,256]{3,2,1,0:T(8,128)(2,1)}, bf16[1,3,256,256]{3,2,1,0:T(8,128)(2,1)S(1)}, u32[]{:S(2)}, u32[]{:S(2)}) collective-permute-start(bf16[1,3,256,256]{3,2,1,0:T(8,128)(2,1)} %bitcast.40), channel_id=1, source_target_pairs={{0,2},{2,4},{4,6},{6,0},{1,7},{3,1},{5,3},{7,5},{8,10},{10,12},{12... | collective-permute-start | bytes 1179656 | tf_op jit(solution)/shard_map/ppermute | solution.py:258
  23.8 0.8 collective-permute-start.5
  24.5 0.0 copy-done.17
  24.6 1.3 collective-permute-start
  25.8 1.1 collective-permute-start.1
  27.0 2.4 %collective-permute-start.2 = (s32[3,6]{1,0:T(4,128)S(1)}, s32[3,6]{1,0:T(4,128)S(1)}, u32[]{:S(2)}, u32[]{:S(2)}) collective-permute-start(s32[3,6]{1,0:T(4,128)S(1)} %bitcast.36), channel_id=1, source_target_pairs={{0,6},{1,7},{2,0},{3,1},{4,2},{5,3},{6,4},{7,5},{8,14},{9,15},{10,... | collective-permute-start | bytes 224 | tf_op jit(solution)/shard_map/ppermute | solution.py:258
  29.4 11.1 %collective-permute-done = s32[3,6]{1,0:T(4,128)S(1)} collective-permute-done((s32[3,6]{1,0:T(4,128)S(1)}, s32[3,6]{1,0:T(4,128)S(1)}, u32[]{:S(2)}, u32[]{:S(2)}) %collective-permute-start) | collective-permute-done | bytes 104 | tf_op jit(solution)/shard_map/ppermute | solution.py:258
  40.5 3.9 %collective-permute-done.1 = s32[3,6]{1,0:T(4,128)S(1)} collective-permute-done((s32[3,6]{1,0:T(4,128)S(1)}, s32[3,6]{1,0:T(4,128)S(1)}, u32[]{:S(2)}, u32[]{:S(2)}) %collective-permute-start.1) | collective-permute-done | bytes 104 | tf_op jit(solution)/shard_map/ppermute | solution.py:258
  44.3 0.0 collective-permute-done.2
  44.3 0.1 collective-permute-start.3
  44.4 0.0 collective-permute-done.4.refs_5_
  44.5 0.0 copy-start.4
  44.5 0.0 collective-permute-done.5.refs_6_
  44.5 0.0 all-to-all-done.known
  44.5 1.1 collective-permute-done.3.there
  45.6 0.0 copy-done.2
  45.6 0.6 copy-done.9
  46.2 2.0 %pick13.1 = (bf16[2,6,32,256]{3,2,1,0:T(8,128)(2,1)}, bf16[2,6,32,256]{3,2,1,0:T(8,128)(2,1)}, bf16[2,6,32,256]{3,2,1,0:T(8,128)(2,1)}, bf16[2,6,32,256]{3,2,1,0:T(8,128)(2,1)}) custom-call(s32[1]{0:T(128)} %bitcast.place, s32[4,3,6]{2,1,0:T(4,128)} %copy-done.8, s32[4,3,6]{2,1,0:T(4,128)} %copy-done.9, bf16[32,32,256]{2,1,0:T(8,128)(2,1)} %copy-done.2), custom_call_target="tpu_custom_call" | custom-call | bytes 2097152 | tf_op jit(solution)/shard_map/pick13/pallas_call | solution.py:52
  48.2 0.2 collective-permute-start.10
  48.4 0.2 collective-permute-start.6
  48.6 1.6 %collective-permute-start.7 = (bf16[2,6,32,256]{3,2,1,0:T(8,128)(2,1)}, bf16[2,6,32,256]{3,2,1,0:T(8,128)(2,1)S(1)}, u32[]{:S(2)}, u32[]{:S(2)}) collective-permute-start(bf16[2,6,32,256]{3,2,1,0:T(8,128)(2,1)} %get-tuple-element.53), channel_id=1, source_target_pairs={{0,2},{1,3},{2,4},{3,5},{4,6},{5,7},{6,0},{7,1},{8,10},{9,11},{10,... | collective-permute-start | bytes 589832 | tf_op jit(solution)/shard_map/ppermute | solution.py:258
  50.2 2.9 %collective-permute-start.8 = (bf16[2,6,32,256]{3,2,1,0:T(8,128)(2,1)}, bf16[2,6,32,256]{3,2,1,0:T(8,128)(2,1)}, u32[]{:S(2)}, u32[]{:S(2)}) collective-permute-start(bf16[2,6,32,256]{3,2,1,0:T(8,128)(2,1)} %get-tuple-element.54), channel_id=1, source_target_pairs={{0,4},{1,5},{2,6},{3,7},{4,0},{5,1},{6,2},{7,3},{8,12},{9,13},{10,... | collective-permute-start | bytes 589832 | tf_op jit(solution)/shard_map/ppermute | solution.py:258
  53.1 0.5 collective-permute-start.9
  53.6 4.7 %level1.1 = (f32[32,256]{1,0:T(8,128)}, bf16[32,32,256]{2,1,0:T(8,128)(2,1)}) custom-call(s32[1]{0:T(128)} %bitcast.place, s32[4,3,6]{2,1,0:T(4,128)} %copy-done.8, s32[4,3,6]{2,1,0:T(4,128)} %copy-done.9, s32[1,6]{1,0:T(1,128)} %bitcast.27, bf16[4,256,256]{2,1,0:T(8,128)(2,1)} %rhs.3, bf16[4,256,256]{2,1,0:T(8,128)(2,1)} %dinv.9, ...), custom_call_target="tpu_custom_call" | custom-call | flops 100663296 | bytes 3145728 | tf_op jit(solution)/shard_map/level1/pallas_call | solution.py:52
  58.3 7.5 %collective-permute-done.7.refs_1_ = bf16[2,6,32,256]{3,2,1,0:T(8,128)(2,1)S(1)} collective-permute-done((bf16[2,6,32,256]{3,2,1,0:T(8,128)(2,1)}, bf16[2,6,32,256]{3,2,1,0:T(8,128)(2,1)S(1)}, u32[]{:S(2)}, u32[]{:S(2)}) %collective-permute-start.7) | collective-permute-done | bytes 196640 | tf_op jit(solution)/shard_map/ppermute | solution.py:258
  65.8 0.0 collective-permute-done.8.refs_2_
  65.8 0.0 collective-permute-done.9.refs_3_
  65.8 0.0 collective-permute-done.6.refs_7_
  65.9 0.8 copy-done.5
  66.7 9.3 %all-to-all-start.1 = ((bf16[32,32,256]{2,1,0:T(8,128)(2,1)}), bf16[32,32,256]{2,1,0:T(8,128)(2,1)S(1)}, u32[]{:S(2)}, u32[]{:S(2)}) async-start(bf16[32,32,256]{2,1,0:T(8,128)(2,1)} %get-tuple-element.56), calls=%async_computation.1 | async-start | bytes 1048576 | tf_op jit(solution)/shard_map/all_to_all | solution.py:259
  76.0 0.1 collective-permute-start.17
  76.1 0.5 collective-permute-start.18
  76.6 0.1 collective-permute-start.19
  76.7 0.0 collective-permute-done.10.refs_5_.refs_7_.refs_8_
  76.7 3.0 %partial13.1 = (f32[32,256]{1,0:T(8,128)}, f32[32,256]{1,0:T(8,128)}, f32[32,256]{1,0:T(8,128)}, f32[32,256]{1,0:T(8,128)}, f32[32,256]{1,0:T(8,128)}, /*index=5...) custom-call(s32[1]{0:T(128)} %bitcast.place, s32[1,6]{1,0:T(1,128)} %bitcast.28, ...), custom_call_target="tpu_custom_call" | custom-call | flops 201326592 | bytes 2097152 | tf_op jit(solution)/shard_map/partial13/pallas_call | solution.py:52
  79.7 0.8 collective-permute-start.14
  80.5 0.5 collective-permute-start.15
  81.0 0.0 collective-permute-done.17.refs_9_
  81.0 1.3 collective-permute-start.16
  82.3 0.0 collective-permute-done.18.refs_10_
  82.3 2.7 %collective-permute-done.14.refs_1_ = f32[32,256]{1,0:T(8,128)S(1)} collective-permute-done((f32[32,256]{1,0:T(8,128)}, f32[32,256]{1,0:T(8,128)S(1)}, u32[]{:S(2)}, u32[]{:S(2)}) %collective-permute-start.14) | collective-permute-done | bytes 32800 | tf_op jit(solution)/shard_map/ppermute | solution.py:258
  85.0 1.9 %collective-permute-done.15.refs_2_ = f32[32,256]{1,0:T(8,128)S(1)} collective-permute-done((f32[32,256]{1,0:T(8,128)}, f32[32,256]{1,0:T(8,128)S(1)}, u32[]{:S(2)}, u32[]{:S(2)}) %collective-permute-start.15) | collective-permute-done | bytes 32800 | tf_op jit(solution)/shard_map/ppermute | solution.py:258
  86.9 0.8 collective-permute-done.16.refs_3_
  87.8 0.0 collective-permute-done.19.refs_11_
  87.8 3.5 %all-to-all-done.1.known = bf16[32,32,256]{2,1,0:T(8,128)(2,1)S(1)} async-done(((bf16[32,32,256]{2,1,0:T(8,128)(2,1)}), bf16[32,32,256]{2,1,0:T(8,128)(2,1)S(1)}, u32[]{:S(2)}, u32[]{:S(2)}) %all-to-all-start.1) | async-done | bytes 524320 | tf_op jit(solution)/shard_map/all_to_all | solution.py:259
  91.3 0.8 copy-done.1
  92.1 5.4 %level2.1 = (f32[32,256]{1,0:T(8,128)}, bf16[32,32,256]{2,1,0:T(8,128)(2,1)}) custom-call(s32[1]{0:T(128)} %bitcast.place, s32[4,3,6]{2,1,0:T(4,128)} %copy-done.8, s32[4,3,6]{2,1,0:T(4,128)} %copy-done.9, s32[1,6]{1,0:T(1,128)} %bitcast.29, bf16[4,256,256]{2,1,0:T(8,128)(2,1)} %rhs.3, bf16[4,256,256]{2,1,0:T(8,128)(2,1)} %dinv.9, ...), custom_call_target="tpu_custom_call" | custom-call | flops 100663296 | bytes 3145728 | tf_op jit(solution)/shard_map/level2/pallas_call | solution.py:52
  97.5 6.3 %all-to-all-start.2 = ((bf16[32,32,256]{2,1,0:T(8,128)(2,1)}), bf16[32,32,256]{2,1,0:T(8,128)(2,1)S(1)}, u32[]{:S(2)}, u32[]{:S(2)}) async-start(bf16[32,32,256]{2,1,0:T(8,128)(2,1)} %get-tuple-element.73), calls=%async_computation.2 | async-start | bytes 1048576 | tf_op jit(solution)/shard_map/all_to_all | solution.py:259
  103.8 1.7 %collective-permute-start.11 = (f32[32,256]{1,0:T(8,128)S(1)}, f32[32,256]{1,0:T(8,128)S(1)}, u32[]{:S(2)}, u32[]{:S(2)}) collective-permute-start(f32[32,256]{1,0:T(8,128)S(1)} %copy-done.20), channel_id=1, source_target_pairs={{0,6},{1,7},{2,0},{3,1},{4,2},{5,3},{6,4},{7,5},{8,14},{9,15},{10,... | collective-permute-start | bytes 98312 | tf_op jit(solution)/shard_map/ppermute | solution.py:258
  105.5 1.0 collective-permute-start.12
  106.6 0.0 collective-permute-start.13
  106.6 1.2 collective-permute-done.11.refs_1_
  107.8 3.2 %collective-permute-done.12.refs_2_ = f32[32,256]{1,0:T(8,128)S(1)} collective-permute-done((f32[32,256]{1,0:T(8,128)S(1)}, f32[32,256]{1,0:T(8,128)S(1)}, u32[]{:S(2)}, u32[]{:S(2)}) %collective-permute-start.12) | collective-permute-done | bytes 32800 | tf_op jit(solution)/shard_map/ppermute | solution.py:258
  110.9 0.8 collective-permute-done.13.refs_3_
  111.7 0.6 copy-done.16
  112.3 4.5 %early3.1.start = f32[32,256]{1,0:T(8,128)} custom-call(s32[1]{0:T(128)} %bitcast.place, s32[4,3,6]{2,1,0:T(4,128)} %copy-done.8, s32[4,3,6]{2,1,0:T(4,128)} %copy-done.9, s32[1,6]{1,0:T(1,128)} %bitcast.30, bf16[4,256,256]{2,1,0:T(8,128)(2,1)} %rhs.3, bf16[4,256,256]{2,1,0:T(8,128)(2,1)} %dinv.9, bf16[32,32,256]{2,1,0:T(8,128)(2,1)} %copy-done.1, ...), custom_call_target="tpu_custom_call" | custom-call | flops 100663296 | bytes 3145728 | tf_op jit(solution)/shard_map/early3/pallas_call | solution.py:52
  116.8 3.7 %all-to-all-done.2.known = bf16[32,32,256]{2,1,0:T(8,128)(2,1)S(1)} async-done(((bf16[32,32,256]{2,1,0:T(8,128)(2,1)}), bf16[32,32,256]{2,1,0:T(8,128)(2,1)S(1)}, u32[]{:S(2)}, u32[]{:S(2)}) %all-to-all-start.2) | async-done | bytes 524320 | tf_op jit(solution)/shard_map/all_to_all | solution.py:259
  120.5 0.8 copy-done.3
  121.3 4.5 %level3.1 = f32[4,32,256]{2,1,0:T(8,128)} custom-call(s32[1]{0:T(128)} %bitcast.place, s32[4,3,6]{2,1,0:T(4,128)} %copy-done.8, s32[4,3,6]{2,1,0:T(4,128)} %copy-done.9, s32[1,6]{1,0:T(1,128)} %bitcast.31, f32[32,256]{1,0:T(8,128)} %early3.1.start, bf16[4,256,256]{2,1,0:T(8,128)(2,1)} %dinv.9, bf16[32,32,256]{2,1,0:T(8,128)(2,1)} %copy-done.3, ...), custom_call_target="tpu_custom_call" | custom-call | flops 100663296 | bytes 3145728 | tf_op jit(solution)/shard_map/level3/pallas_call | solution.py:52
  (40 shorter events, 0.1 us)
Async XLA Ops:
  6.5 47.0 %all-gather.5.cloned.1.call-start = ((), (), s32[]{:S(2)}) async-start(), calls=%async_computation.3 | async-start | bytes 3538944 | tf_op jit(solution)/shard_map/all_gather | solution.py:261
  6.5 18.0 %copy-start.17 = (s32[6,1,3]{0,1,2:T(1,128)S(1)}, s32[6,1,3]{0,1,2:T(1,128)}, u32[]{:S(2)}) copy-start(s32[6,1,3]{0,1,2:T(1,128)} %param.8) | copy-start | bytes 220
  6.5 41.7 %copy-start = (bf16[6,256,3,256]{3,1,2,0:T(8,128)(2,1)S(1)}, bf16[6,256,3,256]{3,1,2,0:T(8,128)(2,1)}, u32[]{:S(2)}) copy-start(bf16[6,256,3,256]{3,1,2,0:T(8,128)(2,1)} %param.7) | copy-start | bytes 7077892
  9.7 102.0 %all-gather.7.cloned.1.call-start = ((), (), s32[]{:S(2)}) async-start(), calls=%async_computation.4 | async-start | bytes 7077888 | tf_op jit(solution)/shard_map/all_gather | solution.py:261
  10.5 34.0 %all-to-all-start = ((bf16[32,32,256]{2,1,0:T(8,128)(2,1)}), bf16[32,32,256]{2,1,0:T(8,128)(2,1)S(1)}, u32[]{:S(2)}, u32[]{:S(2)}) async-start(bf16[32,32,256]{2,1,0:T(8,128)(2,1)} %get-tuple-element.41), calls=%async_computation | async-start | bytes 1048576 | tf_op jit(solution)/shard_map/all_to_all | solution.py:259
  22.1 22.3 %collective-permute-start.4 = (bf16[1,3,256,256]{3,2,1,0:T(8,128)(2,1)}, bf16[1,3,256,256]{3,2,1,0:T(8,128)(2,1)S(1)}, u32[]{:S(2)}, u32[]{:S(2)}) collective-permute-start(bf16[1,3,256,256]{3,2,1,0:T(8,128)(2,1)} %bitcast.40), channel_id=1, source_target_pairs={{0,2},{2,4},{4,6},{6,0},{1,7},{3,1},{5,3},{7,5},{8,10},{10,12},{12... | collective-permute-start | bytes 1179656 | tf_op jit(solution)/shard_map/ppermute | solution.py:258
  23.8 20.7 %collective-permute-start.5 = (bf16[1,3,256,256]{3,2,1,0:T(8,128)(2,1)}, bf16[1,3,256,256]{3,2,1,0:T(8,128)(2,1)}, u32[]{:S(2)}, u32[]{:S(2)}) collective-permute-start(bf16[1,3,256,256]{3,2,1,0:T(8,128)(2,1)} %bitcast.41), channel_id=1, source_target_pairs={{1,2},{3,4},{5,6},{7,0},{0,7},{2,1},{4,3},{6,5},{9,10},{11,12},{13... | collective-permute-start | bytes 1179656 | tf_op jit(solution)/shard_map/ppermute | solution.py:258
  24.6 15.9 %collective-permute-start = (s32[3,6]{1,0:T(4,128)S(1)}, s32[3,6]{1,0:T(4,128)S(1)}, u32[]{:S(2)}, u32[]{:S(2)}) collective-permute-start(s32[3,6]{1,0:T(4,128)S(1)} %bitcast.34), channel_id=1, source_target_pairs={{0,2},{1,3},{2,4},{3,5},{4,6},{5,7},{6,0},{7,1},{8,10},{9,11},{10,... | collective-permute-start | bytes 224 | tf_op jit(solution)/shard_map/ppermute | solution.py:258
  25.8 18.5 %collective-permute-start.1 = (s32[3,6]{1,0:T(4,128)S(1)}, s32[3,6]{1,0:T(4,128)S(1)}, u32[]{:S(2)}, u32[]{:S(2)}) collective-permute-start(s32[3,6]{1,0:T(4,128)S(1)} %bitcast.35), channel_id=1, source_target_pairs={{0,4},{1,5},{2,6},{3,7},{4,0},{5,1},{6,2},{7,3},{8,12},{9,13},{10,... | collective-permute-start | bytes 224 | tf_op jit(solution)/shard_map/ppermute | solution.py:258
  27.0 17.4 %collective-permute-start.2 = (s32[3,6]{1,0:T(4,128)S(1)}, s32[3,6]{1,0:T(4,128)S(1)}, u32[]{:S(2)}, u32[]{:S(2)}) collective-permute-start(s32[3,6]{1,0:T(4,128)S(1)} %bitcast.36), channel_id=1, source_target_pairs={{0,6},{1,7},{2,0},{3,1},{4,2},{5,3},{6,4},{7,5},{8,14},{9,15},{10,... | collective-permute-start | bytes 224 | tf_op jit(solution)/shard_map/ppermute | solution.py:258
  44.3 1.3 copy-start.8
  44.3 1.3 collective-permute-start.3
  44.5 46.9 %copy-start.4 = (bf16[1,3,256,256]{3,2,1,0:T(8,128)(2,1)}, bf16[1,3,256,256]{3,2,1,0:T(8,128)(2,1)S(1)}, u32[]{:S(2)}) copy-start(bf16[1,3,256,256]{3,2,1,0:T(8,128)(2,1)S(1)} %collective-permute-done.4.refs_5_) | copy-start | bytes 1179652
  44.5 1.1 copy-start.2
  45.6 0.6 copy-start.9
  48.2 28.5 %collective-permute-start.10 = (bf16[6,3,256,256]{3,2,1,0:T(8,128)(2,1)S(1)}, bf16[6,3,256,256]{3,2,1,0:T(8,128)(2,1)}, u32[]{:S(2)}, u32[]{:S(2)}) collective-permute-start(bf16[6,3,256,256]{3,2,1,0:T(8,128)(2,1)S(1)} %bitcast.23), channel_id=1, source_target_pairs={{0,1},{1,0},{2,3},{3,2},{4,5},{5,4},{6,7},{7,6},{8,9},{9,8},{10,11... | collective-permute-start | bytes 7077896 | tf_op jit(solution)/shard_map/ppermute | solution.py:258
  48.4 17.4 %collective-permute-start.6 = (bf16[1,3,256,256]{3,2,1,0:T(8,128)(2,1)S(1)}, bf16[1,3,256,256]{3,2,1,0:T(8,128)(2,1)S(1)}, u32[]{:S(2)}, u32[]{:S(2)}) collective-permute-start(bf16[1,3,256,256]{3,2,1,0:T(8,128)(2,1)S(1)} %collective-permute-done.4.refs_5_), channel_id=1, source_target_pairs={{0,2},{2,4},{4,6},{6,0},{1,7},{3,1},{5,3},{7,5},{8,10},{10,12},{12... | collective-permute-start | bytes 1179656 | tf_op jit(solution)/shard_map/ppermute | solution.py:258
  48.6 17.2 %collective-permute-start.7 = (bf16[2,6,32,256]{3,2,1,0:T(8,128)(2,1)}, bf16[2,6,32,256]{3,2,1,0:T(8,128)(2,1)S(1)}, u32[]{:S(2)}, u32[]{:S(2)}) collective-permute-start(bf16[2,6,32,256]{3,2,1,0:T(8,128)(2,1)} %get-tuple-element.53), channel_id=1, source_target_pairs={{0,2},{1,3},{2,4},{3,5},{4,6},{5,7},{6,0},{7,1},{8,10},{9,11},{10,... | collective-permute-start | bytes 589832 | tf_op jit(solution)/shard_map/ppermute | solution.py:258
  50.2 15.6 %collective-permute-start.8 = (bf16[2,6,32,256]{3,2,1,0:T(8,128)(2,1)}, bf16[2,6,32,256]{3,2,1,0:T(8,128)(2,1)}, u32[]{:S(2)}, u32[]{:S(2)}) collective-permute-start(bf16[2,6,32,256]{3,2,1,0:T(8,128)(2,1)} %get-tuple-element.54), channel_id=1, source_target_pairs={{0,4},{1,5},{2,6},{3,7},{4,0},{5,1},{6,2},{7,3},{8,12},{9,13},{10,... | collective-permute-start | bytes 589832 | tf_op jit(solution)/shard_map/ppermute | solution.py:258
  53.1 12.7 %collective-permute-start.9 = (bf16[2,6,32,256]{3,2,1,0:T(8,128)(2,1)}, bf16[2,6,32,256]{3,2,1,0:T(8,128)(2,1)}, u32[]{:S(2)}, u32[]{:S(2)}) collective-permute-start(bf16[2,6,32,256]{3,2,1,0:T(8,128)(2,1)} %get-tuple-element.55), channel_id=1, source_target_pairs={{0,6},{1,7},{2,0},{3,1},{4,2},{5,3},{6,4},{7,5},{8,14},{9,15},{10,... | collective-permute-start | bytes 589832 | tf_op jit(solution)/shard_map/ppermute | solution.py:258
  65.8 10.9 %copy-start.10 = (bf16[2,6,32,256]{3,2,1,0:T(8,128)(2,1)}, bf16[2,6,32,256]{3,2,1,0:T(8,128)(2,1)S(1)}, u32[]{:S(2)}) copy-start(bf16[2,6,32,256]{3,2,1,0:T(8,128)(2,1)S(1)} %collective-permute-done.7.refs_1_) | copy-start | bytes 589828
  65.8 0.8 copy-start.5
  66.7 24.6 %all-to-all-start.1 = ((bf16[32,32,256]{2,1,0:T(8,128)(2,1)}), bf16[32,32,256]{2,1,0:T(8,128)(2,1)S(1)}, u32[]{:S(2)}, u32[]{:S(2)}) async-start(bf16[32,32,256]{2,1,0:T(8,128)(2,1)} %get-tuple-element.56), calls=%async_computation.1 | async-start | bytes 1048576 | tf_op jit(solution)/shard_map/all_to_all | solution.py:259
  76.0 5.0 %collective-permute-start.17 = (bf16[1,3,256,256]{3,2,1,0:T(8,128)(2,1)S(1)}, bf16[1,3,256,256]{3,2,1,0:T(8,128)(2,1)S(1)}, u32[]{:S(2)}, u32[]{:S(2)}) collective-permute-start(bf16[1,3,256,256]{3,2,1,0:T(8,128)(2,1)S(1)} %collective-permute-done.4.refs_5_), channel_id=1, source_target_pairs={{0,1},{1,0},{2,3},{3,2},{4,5},{5,4},{6,7},{7,6},{8,9},{9,8},{10,11... | collective-permute-start | bytes 1179656 | tf_op jit(solution)/shard_map/ppermute | solution.py:258
  76.1 6.3 %collective-permute-start.18 = (bf16[1,3,256,256]{3,2,1,0:T(8,128)(2,1)}, bf16[1,3,256,256]{3,2,1,0:T(8,128)(2,1)S(1)}, u32[]{:S(2)}, u32[]{:S(2)}) collective-permute-start(bf16[1,3,256,256]{3,2,1,0:T(8,128)(2,1)} %collective-permute-done.5.refs_6_), channel_id=1, source_target_pairs={{0,1},{1,0},{2,3},{3,2},{4,5},{5,4},{6,7},{7,6},{8,9},{9,8},{10,11... | collective-permute-start | bytes 1179656 | tf_op jit(solution)/shard_map/ppermute | solution.py:258
  76.6 11.2 %collective-permute-start.19 = (bf16[1,3,256,256]{3,2,1,0:T(8,128)(2,1)}, bf16[1,3,256,256]{3,2,1,0:T(8,128)(2,1)}, u32[]{:S(2)}, u32[]{:S(2)}) collective-permute-start(bf16[1,3,256,256]{3,2,1,0:T(8,128)(2,1)} %copy-done.5), channel_id=1, source_target_pairs={{0,1},{1,0},{2,3},{3,2},{4,5},{5,4},{6,7},{7,6},{8,9},{9,8},{10,11... | collective-permute-start | bytes 1179656 | tf_op jit(solution)/shard_map/ppermute | solution.py:258
  79.7 5.4 %collective-permute-start.14 = (f32[32,256]{1,0:T(8,128)}, f32[32,256]{1,0:T(8,128)S(1)}, u32[]{:S(2)}, u32[]{:S(2)}) collective-permute-start(f32[32,256]{1,0:T(8,128)} %get-tuple-element.68), channel_id=1, source_target_pairs={{0,6},{1,7},{2,0},{3,1},{4,2},{5,3},{6,4},{7,5},{8,14},{9,15},{10,... | collective-permute-start | bytes 98312 | tf_op jit(solution)/shard_map/ppermute | solution.py:258
  80.5 6.4 %collective-permute-start.15 = (f32[32,256]{1,0:T(8,128)}, f32[32,256]{1,0:T(8,128)S(1)}, u32[]{:S(2)}, u32[]{:S(2)}) collective-permute-start(f32[32,256]{1,0:T(8,128)} %get-tuple-element.69), channel_id=1, source_target_pairs={{0,4},{1,5},{2,6},{3,7},{4,0},{5,1},{6,2},{7,3},{8,12},{9,13},{10,... | collective-permute-start | bytes 98312 | tf_op jit(solution)/shard_map/ppermute | solution.py:258
  81.0 6.7 %copy-start.6 = (bf16[1,3,256,256]{3,2,1,0:T(8,128)(2,1)}, bf16[1,3,256,256]{3,2,1,0:T(8,128)(2,1)S(1)}, u32[]{:S(2)}) copy-start(bf16[1,3,256,256]{3,2,1,0:T(8,128)(2,1)S(1)} %collective-permute-done.17.refs_9_) | copy-start | bytes 1179652
  81.0 6.7 %collective-permute-start.16 = (f32[32,256]{1,0:T(8,128)}, f32[32,256]{1,0:T(8,128)S(1)}, u32[]{:S(2)}, u32[]{:S(2)}) collective-permute-start(f32[32,256]{1,0:T(8,128)} %get-tuple-element.70), channel_id=1, source_target_pairs={{0,2},{1,3},{2,4},{3,5},{4,6},{5,7},{6,0},{7,1},{8,10},{9,11},{10,... | collective-permute-start | bytes 98312 | tf_op jit(solution)/shard_map/ppermute | solution.py:258
  82.3 5.4 %copy-start.7 = (bf16[1,3,256,256]{3,2,1,0:T(8,128)(2,1)}, bf16[1,3,256,256]{3,2,1,0:T(8,128)(2,1)S(1)}, u32[]{:S(2)}) copy-start(bf16[1,3,256,256]{3,2,1,0:T(8,128)(2,1)S(1)} %collective-permute-done.18.refs_10_) | copy-start | bytes 1179652
  85.0 6.3 %copy-start.11 = (f32[32,256]{1,0:T(8,128)}, f32[32,256]{1,0:T(8,128)S(1)}, u32[]{:S(2)}) copy-start(f32[32,256]{1,0:T(8,128)S(1)} %collective-permute-done.14.refs_1_) | copy-start | bytes 98308
  86.9 4.4 %copy-start.12 = (f32[32,256]{1,0:T(8,128)}, f32[32,256]{1,0:T(8,128)S(1)}, u32[]{:S(2)}) copy-start(f32[32,256]{1,0:T(8,128)S(1)} %collective-permute-done.15.refs_2_) | copy-start | bytes 98308
  87.7 3.6 %copy-start.13 = (f32[32,256]{1,0:T(8,128)}, f32[32,256]{1,0:T(8,128)S(1)}, u32[]{:S(2)}) copy-start(f32[32,256]{1,0:T(8,128)S(1)} %collective-permute-done.16.refs_3_) | copy-start | bytes 98308
  91.3 0.8 copy-start.1
  92.1 11.7 %copy-start.20 = (f32[32,256]{1,0:T(8,128)S(1)}, f32[32,256]{1,0:T(8,128)}, u32[]{:S(2)}) copy-start(f32[32,256]{1,0:T(8,128)} %get-tuple-element.64) | copy-start | bytes 98308
  92.1 13.4 %copy-start.19 = (f32[32,256]{1,0:T(8,128)S(1)}, f32[32,256]{1,0:T(8,128)}, u32[]{:S(2)}) copy-start(f32[32,256]{1,0:T(8,128)} %get-tuple-element.65) | copy-start | bytes 98308
  92.1 14.5 %copy-start.18 = (f32[32,256]{1,0:T(8,128)S(1)}, f32[32,256]{1,0:T(8,128)}, u32[]{:S(2)}) copy-start(f32[32,256]{1,0:T(8,128)} %get-tuple-element.66) | copy-start | bytes 98308
  97.5 23.0 %all-to-all-start.2 = ((bf16[32,32,256]{2,1,0:T(8,128)(2,1)}), bf16[32,32,256]{2,1,0:T(8,128)(2,1)S(1)}, u32[]{:S(2)}, u32[]{:S(2)}) async-start(bf16[32,32,256]{2,1,0:T(8,128)(2,1)} %get-tuple-element.73), calls=%async_computation.2 | async-start | bytes 1048576 | tf_op jit(solution)/shard_map/all_to_all | solution.py:259
  103.8 4.0 %collective-permute-start.11 = (f32[32,256]{1,0:T(8,128)S(1)}, f32[32,256]{1,0:T(8,128)S(1)}, u32[]{:S(2)}, u32[]{:S(2)}) collective-permute-start(f32[32,256]{1,0:T(8,128)S(1)} %copy-done.20), channel_id=1, source_target_pairs={{0,6},{1,7},{2,0},{3,1},{4,2},{5,3},{6,4},{7,5},{8,14},{9,15},{10,... | collective-permute-start | bytes 98312 | tf_op jit(solution)/shard_map/ppermute | solution.py:258
  105.5 5.4 %collective-permute-start.12 = (f32[32,256]{1,0:T(8,128)S(1)}, f32[32,256]{1,0:T(8,128)S(1)}, u32[]{:S(2)}, u32[]{:S(2)}) collective-permute-start(f32[32,256]{1,0:T(8,128)S(1)} %copy-done.19), channel_id=1, source_target_pairs={{0,4},{1,5},{2,6},{3,7},{4,0},{5,1},{6,2},{7,3},{8,12},{9,13},{10,... | collective-permute-start | bytes 98312 | tf_op jit(solution)/shard_map/ppermute | solution.py:258
  106.6 5.1 %collective-permute-start.13 = (f32[32,256]{1,0:T(8,128)S(1)}, f32[32,256]{1,0:T(8,128)S(1)}, u32[]{:S(2)}, u32[]{:S(2)}) collective-permute-start(f32[32,256]{1,0:T(8,128)S(1)} %copy-done.18), channel_id=1, source_target_pairs={{0,2},{1,3},{2,4},{3,5},{4,6},{5,7},{6,0},{7,1},{8,10},{9,11},{10,... | collective-permute-start | bytes 98312 | tf_op jit(solution)/shard_map/ppermute | solution.py:258
  107.8 3.9 %copy-start.14 = (f32[32,256]{1,0:T(8,128)}, f32[32,256]{1,0:T(8,128)S(1)}, u32[]{:S(2)}) copy-start(f32[32,256]{1,0:T(8,128)S(1)} %collective-permute-done.11.refs_1_) | copy-start | bytes 98308
  110.9 0.8 copy-start.15
  111.7 0.6 copy-start.16
  120.5 0.8 copy-start.3
Sparse Core Ops, SparseCore 0:
  9.8 43.0 all-gather.4
  54.8 44.4 all-gather.6

commit v9 on v8

--- a/solution.py
+++ b/solution.py
@@ -262,11 +262,12 @@
     live = live.transpose(1, 0)
 
     own = cols.transpose(2, 1, 0).reshape(SLOTS, -1)
-    here = jnp.stack([own] + [move(own, TURN[d]) for d in range(1, CHIPS)])
+    turned = [move(own, TURN[d]) for d in range(1, CHIPS)]
+    here = jnp.stack([own] + turned)
     there = move(here, SWAP)
     answer0, spread0, cut0, cut2, cut45 = first_call(place, rhs, dinv, tiles, (0, 2, 4, 5))
     gathered0, gathered45 = gather(cut0), gather(cut45)
-    cut2 = cut2.reshape(1, SLOTS, SIZE, SIZE)
+    cut2, *turned = lax.optimization_barrier((cut2.reshape(1, SLOTS, SIZE, SIZE), *turned))
     same, cross = move(cut2, SAME), move(cut2, CROSS)
 
     def send(picked):
@@ -277,14 +278,13 @@
 
     scalars = (place, here, there, live)
     known0 = over_row(spread0)
-    known0, same, cross = lax.optimization_barrier((known0, same, cross))
     picked = pick_call("pick13", (1, 3), place, here, there, known0)
-    later, known0, *picked = lax.optimization_barrier((tiles, known0, *picked))
+    later, known0, same, cross, *picked = lax.optimization_barrier((tiles, known0, same, cross, *picked))
     swapped = move(later, SWAP)
     got = send(picked)
     far = move(same, SAME)
     answer1, spread1 = level_call("level1", 1, 0, 0, True, True, *scalars, rhs, dinv, known0, gathered0, [], [])
-    spread1, far, *got = lax.optimization_barrier((spread1, far, *got))
+    spread1, *got = lax.optimization_barrier((spread1, *got))
     known1 = over_row(spread1)
 
     sums = partial_call("partial13", (1, 3), place, live, got, [], tiles, swapped)

time: 133 us -> 148 us (1.11)
  waiting for transfers between devices: 42.1 us -> 50.6 us
  starting transfers between devices: 46.1 us -> 51.5 us
    ppermute x20, waiting for transfers between devices: 34.1 us -> 41.3 us  [local(): move = lambda array, pairs: lax.ppermute(array, 'col', pairs)]
    all_to_all x3, starting transfers between devices: 27.2 us -> 31.6 us  [local(): over_row = lambda array: lax.all_to_all(array, 'row', 0, 0, tiled=True)]
    unnamed x43 -> x49, local copies, waits for them, and re-layouts: 3.63 us -> 3.72 us
  transfers between devices with their start and end apart: 25 -> 25, of which waited for: 12 -> 14; matrix products, arithmetic and copies ran while one was open for 0% -> 0% of each run, Pallas kernels for 15% -> 13%
where the time goes in v9:
time: 148 us; the launch traced here: 147 us
  starting transfers between devices  51.5 us (35%)
  waiting for transfers between devices  50.6 us (34%)
  Pallas kernels  27.3 us (18%)
  between operations  13.6 us (9%)
  local copies, waits for them, and re-layouts  3.72 us (3%)
    ppermute x20, waiting for transfers between devices, local(): move = lambda array, pairs: lax.ppermute(array, 'col', pairs)  41.3 us
    all_to_all x3, starting transfers between devices, local(): over_row = lambda array: lax.all_to_all(array, 'row', 0, 0, tiled=True)  31.6 us
    pallas_call x7, Pallas kernels, call(): pl.pallas_call(kernel, grid=(1,), out_shape=tuple((jax.ShapeDtypeStruct(s...  27.3 us
    ppermute x20, starting transfers between devices, local(): move = lambda array, pairs: lax.ppermute(array, 'col', pairs)  19.8 us
    all_to_all x3, waiting for transfers between devices, local(): over_row = lambda array: lax.all_to_all(array, 'row', 0, 0, tiled=True)  8.58 us
    unnamed x49, local copies, waits for them, and re-layouts  3.72 us
  transfers between devices with their start and end apart: 25, of which 14 were waited for; matrix products, arithmetic and copies ran while one was open for 0% of the time, Pallas kernels for 13%

profile of v9, /device:TPU:2, one launch (start us, length us, event | category | flops | bytes accessed | tf_op | source)
XLA Modules:
  0.0 146.7 jit_solution(3752192595473590521)
XLA Ops:
  6.5 3.2 %level0.1 = (f32[32,256]{1,0:T(8,128)}, bf16[32,32,256]{2,1,0:T(8,128)(2,1)}, bf16[1,768,256]{2,1,0:T(8,128)(2,1)}, bf16[1,768,256]{2,1,0:T(8,128)(2,1)}, bf16[2,768,256]{2,1,0:T(8,128)(2,1)}) custom-call(s32[1]{0:T(128)} %bitcast.place, bf16[4,256,256]{2,1,0:T(8,128)(2,1)} %rhs.3, bf16[4,256,256]{2,1,0:T(8,128)(2,1)} %dinv.9, ...), custom_call_target="tpu_custom_call" | custom-call | bytes 4194304 | tf_op jit(solution)/shard_map/level0/pallas_call | solution.py:52
  9.7 0.0 all-gather.5.cloned.1.call-update
  9.7 0.0 all-gather.7.cloned.1.call-start
  9.8 0.7 all-gather.7.cloned.1.call-update
  10.5 11.6 %all-to-all-start = ((bf16[32,32,256]{2,1,0:T(8,128)(2,1)}), bf16[32,32,256]{2,1,0:T(8,128)(2,1)S(1)}, u32[]{:S(2)}, u32[]{:S(2)}) async-start(bf16[32,32,256]{2,1,0:T(8,128)(2,1)} %get-tuple-element.40), calls=%async_computation | async-start | bytes 1048576 | tf_op jit(solution)/shard_map/all_to_all | solution.py:259
  22.1 1.7 %collective-permute-start = (s32[3,6]{1,0:T(4,128)S(1)}, s32[3,6]{1,0:T(4,128)S(1)}, u32[]{:S(2)}, u32[]{:S(2)}) collective-permute-start(s32[3,6]{1,0:T(4,128)S(1)} %bitcast.34), channel_id=1, source_target_pairs={{0,2},{1,3},{2,4},{3,5},{4,6},{5,7},{6,0},{7,1},{8,10},{9,11},{10,... | collective-permute-start | bytes 224 | tf_op jit(solution)/shard_map/ppermute | solution.py:258
  23.8 2.9 %collective-permute-start.1 = (s32[3,6]{1,0:T(4,128)S(1)}, s32[3,6]{1,0:T(4,128)S(1)}, u32[]{:S(2)}, u32[]{:S(2)}) collective-permute-start(s32[3,6]{1,0:T(4,128)S(1)} %bitcast.35), channel_id=1, source_target_pairs={{0,4},{1,5},{2,6},{3,7},{4,0},{5,1},{6,2},{7,3},{8,12},{9,13},{10,... | collective-permute-start | bytes 224 | tf_op jit(solution)/shard_map/ppermute | solution.py:258
  26.7 1.3 collective-permute-start.2
  28.0 0.0 collective-permute-done
  28.0 0.8 collective-permute-done.1
  28.9 1.4 collective-permute-done.2
  30.3 0.3 collective-permute-start.4
  30.6 0.0 collective-permute-start.5
  30.6 1.5 %collective-permute-start.3 = (s32[4,3,6]{2,1,0:T(4,128)S(1)}, s32[4,3,6]{2,1,0:T(4,128)S(1)}, u32[]{:S(2)}, u32[]{:S(2)}) collective-permute-start(s32[4,3,6]{2,1,0:T(4,128)S(1)} %pad_add_fusion.here), channel_id=1, source_target_pairs={{0,1},{1,0},{2,3},{3,2},{4,5},{5,4},{6,7},{7,6},{8,9},{9,8},{10,11... | collective-permute-start | bytes 872 | tf_op jit(solution)/shard_map/ppermute | solution.py:258
  32.1 0.8 collective-permute-done.3.there
  32.9 6.1 %all-to-all-done.known = bf16[32,32,256]{2,1,0:T(8,128)(2,1)S(1)} async-done(((bf16[32,32,256]{2,1,0:T(8,128)(2,1)}), bf16[32,32,256]{2,1,0:T(8,128)(2,1)S(1)}, u32[]{:S(2)}, u32[]{:S(2)}) %all-to-all-start) | async-done | bytes 524320 | tf_op jit(solution)/shard_map/all_to_all | solution.py:259
  39.0 0.8 copy-done.2
  39.8 2.0 %pick13.1 = (bf16[2,6,32,256]{3,2,1,0:T(8,128)(2,1)}, bf16[2,6,32,256]{3,2,1,0:T(8,128)(2,1)}, bf16[2,6,32,256]{3,2,1,0:T(8,128)(2,1)}, bf16[2,6,32,256]{3,2,1,0:T(8,128)(2,1)}) custom-call(s32[1]{0:T(128)} %bitcast.place, s32[4,3,6]{2,1,0:T(4,128)} %copy-done.9, s32[4,3,6]{2,1,0:T(4,128)} %copy-done.10, bf16[32,32,256]{2,1,0:T(8,128)(2,1)} %copy-done.2), custom_call_target="tpu_custom_call" | custom-call | bytes 2097152 | tf_op jit(solution)/shard_map/pick13/pallas_call | solution.py:52
  41.8 8.2 %collective-permute-done.4.refs_5_ = bf16[1,3,256,256]{3,2,1,0:T(8,128)(2,1)S(1)} collective-permute-done((bf16[1,3,256,256]{3,2,1,0:T(8,128)(2,1)}, bf16[1,3,256,256]{3,2,1,0:T(8,128)(2,1)S(1)}, u32[]{:S(2)}, u32[]{:S(2)}) %collective-permute-start.4) | collective-permute-done | bytes 393248 | tf_op jit(solution)/shard_map/ppermute | solution.py:258
  50.0 0.0 collective-permute-done.5.refs_6_
  50.0 0.1 collective-permute-start.9
  50.1 0.5 collective-permute-start.6
  50.6 2.2 %collective-permute-start.7 = (bf16[2,6,32,256]{3,2,1,0:T(8,128)(2,1)}, bf16[2,6,32,256]{3,2,1,0:T(8,128)(2,1)S(1)}, u32[]{:S(2)}, u32[]{:S(2)}) collective-permute-start(bf16[2,6,32,256]{3,2,1,0:T(8,128)(2,1)} %get-tuple-element.52), channel_id=1, source_target_pairs={{0,4},{1,5},{2,6},{3,7},{4,0},{5,1},{6,2},{7,3},{8,12},{9,13},{10,... | collective-permute-start | bytes 589832 | tf_op jit(solution)/shard_map/ppermute | solution.py:258
  52.8 1.5 %collective-permute-start.8 = (bf16[2,6,32,256]{3,2,1,0:T(8,128)(2,1)}, bf16[2,6,32,256]{3,2,1,0:T(8,128)(2,1)S(1)}, u32[]{:S(2)}, u32[]{:S(2)}) collective-permute-start(bf16[2,6,32,256]{3,2,1,0:T(8,128)(2,1)} %get-tuple-element.53), channel_id=1, source_target_pairs={{0,6},{1,7},{2,0},{3,1},{4,2},{5,3},{6,4},{7,5},{8,14},{9,15},{10,... | collective-permute-start | bytes 589832 | tf_op jit(solution)/shard_map/ppermute | solution.py:258
  54.4 4.7 %level1.1 = (f32[32,256]{1,0:T(8,128)}, bf16[32,32,256]{2,1,0:T(8,128)(2,1)}) custom-call(s32[1]{0:T(128)} %bitcast.place, s32[4,3,6]{2,1,0:T(4,128)} %copy-done.9, s32[4,3,6]{2,1,0:T(4,128)} %copy-done.10, s32[1,6]{1,0:T(1,128)} %bitcast.27, bf16[4,256,256]{2,1,0:T(8,128)(2,1)} %rhs.3, bf16[4,256,256]{2,1,0:T(8,128)(2,1)} %dinv.9, ...), custom_call_target="tpu_custom_call" | custom-call | flops 100663296 | bytes 3145728 | tf_op jit(solution)/shard_map/level1/pallas_call | solution.py:52
  59.1 4.0 %collective-permute-done.6.refs_1_ = bf16[2,6,32,256]{3,2,1,0:T(8,128)(2,1)S(1)} collective-permute-done((bf16[2,6,32,256]{3,2,1,0:T(8,128)(2,1)}, bf16[2,6,32,256]{3,2,1,0:T(8,128)(2,1)S(1)}, u32[]{:S(2)}, u32[]{:S(2)}) %collective-permute-start.6) | collective-permute-done | bytes 196640 | tf_op jit(solution)/shard_map/ppermute | solution.py:258
  63.0 0.0 collective-permute-done.7.refs_2_
  63.0 0.6 collective-permute-done.8.refs_3_
  63.7 0.1 copy-done.12
  63.8 0.6 copy-done.13
  64.3 10.1 %all-to-all-start.1 = ((bf16[32,32,256]{2,1,0:T(8,128)(2,1)}), bf16[32,32,256]{2,1,0:T(8,128)(2,1)S(1)}, u32[]{:S(2)}, u32[]{:S(2)}) async-start(bf16[32,32,256]{2,1,0:T(8,128)(2,1)} %get-tuple-element.54), calls=%async_computation.1 | async-start | bytes 1048576 | tf_op jit(solution)/shard_map/all_to_all | solution.py:259
  74.5 0.7 collective-permute-start.16
  75.2 1.2 collective-permute-start.17
  76.4 0.0 collective-permute-start.18
  76.4 15.6 %collective-permute-done.16.refs_7_ = bf16[1,3,256,256]{3,2,1,0:T(8,128)(2,1)S(1)} collective-permute-done((bf16[1,3,256,256]{3,2,1,0:T(8,128)(2,1)S(1)}, bf16[1,3,256,256]{3,2,1,0:T(8,128)(2,1)S(1)}, u32[]{:S(2)}, u32[]{:S(2)}) %collective-permute-start.16) | collective-permute-done | bytes 393248 | tf_op jit(solution)/shard_map/ppermute | solution.py:258
  91.9 0.0 collective-permute-start.19
  91.9 0.0 collective-permute-done.9.refs_5_.refs_7_.refs_8_
  92.0 3.1 %partial13.1 = (f32[32,256]{1,0:T(8,128)}, f32[32,256]{1,0:T(8,128)}, f32[32,256]{1,0:T(8,128)}, f32[32,256]{1,0:T(8,128)}, f32[32,256]{1,0:T(8,128)}, /*index=5...) custom-call(s32[1]{0:T(128)} %bitcast.place, s32[1,6]{1,0:T(1,128)} %bitcast.28, ...), custom_call_target="tpu_custom_call" | custom-call | flops 201326592 | bytes 2097152 | tf_op jit(solution)/shard_map/partial13/pallas_call | solution.py:52
  95.1 1.8 %collective-permute-start.13 = (f32[32,256]{1,0:T(8,128)}, f32[32,256]{1,0:T(8,128)S(1)}, u32[]{:S(2)}, u32[]{:S(2)}) collective-permute-start(f32[32,256]{1,0:T(8,128)} %get-tuple-element.66), channel_id=1, source_target_pairs={{0,6},{1,7},{2,0},{3,1},{4,2},{5,3},{6,4},{7,5},{8,14},{9,15},{10,... | collective-permute-start | bytes 98312 | tf_op jit(solution)/shard_map/ppermute | solution.py:258
  96.8 0.1 collective-permute-start.14
  96.9 0.0 collective-permute-done.17.refs_9_
  96.9 0.9 collective-permute-start.15
  97.8 0.0 collective-permute-done.18.refs_10_
  97.8 0.0 collective-permute-done.19.refs_11_
  97.8 2.6 %collective-permute-done.13.refs_1_ = f32[32,256]{1,0:T(8,128)S(1)} collective-permute-done((f32[32,256]{1,0:T(8,128)}, f32[32,256]{1,0:T(8,128)S(1)}, u32[]{:S(2)}, u32[]{:S(2)}) %collective-permute-start.13) | collective-permute-done | bytes 32800 | tf_op jit(solution)/shard_map/ppermute | solution.py:258
  100.5 2.3 %collective-permute-done.14.refs_2_ = f32[32,256]{1,0:T(8,128)S(1)} collective-permute-done((f32[32,256]{1,0:T(8,128)}, f32[32,256]{1,0:T(8,128)S(1)}, u32[]{:S(2)}, u32[]{:S(2)}) %collective-permute-start.14) | collective-permute-done | bytes 32800 | tf_op jit(solution)/shard_map/ppermute | solution.py:258
  102.8 0.0 collective-permute-done.15.refs_3_
  102.8 0.0 all-to-all-done.1.known
  102.8 0.6 copy-done.15
  103.4 0.0 copy-done.16
  103.4 0.2 copy-done.1
  103.6 5.4 %level2.1 = (f32[32,256]{1,0:T(8,128)}, bf16[32,32,256]{2,1,0:T(8,128)(2,1)}) custom-call(s32[1]{0:T(128)} %bitcast.place, s32[4,3,6]{2,1,0:T(4,128)} %copy-done.9, s32[4,3,6]{2,1,0:T(4,128)} %copy-done.10, s32[1,6]{1,0:T(1,128)} %bitcast.29, bf16[4,256,256]{2,1,0:T(8,128)(2,1)} %rhs.3, bf16[4,256,256]{2,1,0:T(8,128)(2,1)} %dinv.9, ...), custom_call_target="tpu_custom_call" | custom-call | flops 100663296 | bytes 3145728 | tf_op jit(solution)/shard_map/level2/pallas_call | solution.py:52
  109.0 9.8 %all-to-all-start.2 = ((bf16[32,32,256]{2,1,0:T(8,128)(2,1)}), bf16[32,32,256]{2,1,0:T(8,128)(2,1)S(1)}, u32[]{:S(2)}, u32[]{:S(2)}) async-start(bf16[32,32,256]{2,1,0:T(8,128)(2,1)} %get-tuple-element.71), calls=%async_computation.2 | async-start | bytes 1048576 | tf_op jit(solution)/shard_map/all_to_all | solution.py:259
  118.8 1.6 %collective-permute-start.10 = (f32[32,256]{1,0:T(8,128)S(1)}, f32[32,256]{1,0:T(8,128)S(1)}, u32[]{:S(2)}, u32[]{:S(2)}) collective-permute-start(f32[32,256]{1,0:T(8,128)S(1)} %copy-done.23), channel_id=1, source_target_pairs={{0,6},{1,7},{2,0},{3,1},{4,2},{5,3},{6,4},{7,5},{8,14},{9,15},{10,... | collective-permute-start | bytes 98312 | tf_op jit(solution)/shard_map/ppermute | solution.py:258
  120.4 1.5 %collective-permute-start.11 = (f32[32,256]{1,0:T(8,128)S(1)}, f32[32,256]{1,0:T(8,128)S(1)}, u32[]{:S(2)}, u32[]{:S(2)}) collective-permute-start(f32[32,256]{1,0:T(8,128)S(1)} %copy-done.22), channel_id=1, source_target_pairs={{0,4},{1,5},{2,6},{3,7},{4,0},{5,1},{6,2},{7,3},{8,12},{9,13},{10,... | collective-permute-start | bytes 98312 | tf_op jit(solution)/shard_map/ppermute | solution.py:258
  121.9 0.2 collective-permute-start.12
  122.0 0.8 collective-permute-done.10.refs_1_
  122.8 3.0 %collective-permute-done.11.refs_2_ = f32[32,256]{1,0:T(8,128)S(1)} collective-permute-done((f32[32,256]{1,0:T(8,128)S(1)}, f32[32,256]{1,0:T(8,128)S(1)}, u32[]{:S(2)}, u32[]{:S(2)}) %collective-permute-start.11) | collective-permute-done | bytes 32800 | tf_op jit(solution)/shard_map/ppermute | solution.py:258
  125.8 1.2 collective-permute-done.12.refs_3_
  127.0 0.6 copy-done.19
  127.6 4.5 %early3.1.start = f32[32,256]{1,0:T(8,128)} custom-call(s32[1]{0:T(128)} %bitcast.place, s32[4,3,6]{2,1,0:T(4,128)} %copy-done.9, s32[4,3,6]{2,1,0:T(4,128)} %copy-done.10, s32[1,6]{1,0:T(1,128)} %bitcast.30, bf16[4,256,256]{2,1,0:T(8,128)(2,1)} %rhs.3, bf16[4,256,256]{2,1,0:T(8,128)(2,1)} %dinv.9, bf16[32,32,256]{2,1,0:T(8,128)(2,1)} %copy-done.1, ...), custom_call_target="tpu_custom_call" | custom-call | flops 100663296 | bytes 3145728 | tf_op jit(solution)/shard_map/early3/pallas_call | solution.py:52
  132.1 2.5 %all-to-all-done.2.known = bf16[32,32,256]{2,1,0:T(8,128)(2,1)S(1)} async-done(((bf16[32,32,256]{2,1,0:T(8,128)(2,1)}), bf16[32,32,256]{2,1,0:T(8,128)(2,1)S(1)}, u32[]{:S(2)}, u32[]{:S(2)}) %all-to-all-start.2) | async-done | bytes 524320 | tf_op jit(solution)/shard_map/all_to_all | solution.py:259
  134.6 0.8 copy-done.3
  135.4 4.5 %level3.1 = f32[4,32,256]{2,1,0:T(8,128)} custom-call(s32[1]{0:T(128)} %bitcast.place, s32[4,3,6]{2,1,0:T(4,128)} %copy-done.9, s32[4,3,6]{2,1,0:T(4,128)} %copy-done.10, s32[1,6]{1,0:T(1,128)} %bitcast.31, f32[32,256]{1,0:T(8,128)} %early3.1.start, bf16[4,256,256]{2,1,0:T(8,128)(2,1)} %dinv.9, bf16[32,32,256]{2,1,0:T(8,128)(2,1)} %copy-done.3, ...), custom_call_target="tpu_custom_call" | custom-call | flops 100663296 | bytes 3145728 | tf_op jit(solution)/shard_map/level3/pallas_call | solution.py:52
  (46 shorter events, 0.1 us)
Async XLA Ops:
  6.5 47.8 %all-gather.5.cloned.1.call-start = ((), (), s32[]{:S(2)}) async-start(), calls=%async_computation.3 | async-start | bytes 3538944 | tf_op jit(solution)/shard_map/all_gather | solution.py:261
  6.5 15.6 %copy-start.20 = (s32[6,1,3]{0,1,2:T(1,128)S(1)}, s32[6,1,3]{0,1,2:T(1,128)}, u32[]{:S(2)}) copy-start(s32[6,1,3]{0,1,2:T(1,128)} %param.8) | copy-start | bytes 220
  6.5 43.4 %copy-start = (bf16[6,256,3,256]{3,1,2,0:T(8,128)(2,1)S(1)}, bf16[6,256,3,256]{3,1,2,0:T(8,128)(2,1)}, u32[]{:S(2)}) copy-start(bf16[6,256,3,256]{3,1,2,0:T(8,128)(2,1)} %param.7) | copy-start | bytes 7077892
  9.7 117.3 %all-gather.7.cloned.1.call-start = ((), (), s32[]{:S(2)}) async-start(), calls=%async_computation.4 | async-start | bytes 7077888 | tf_op jit(solution)/shard_map/all_gather | solution.py:261
  10.5 28.5 %all-to-all-start = ((bf16[32,32,256]{2,1,0:T(8,128)(2,1)}), bf16[32,32,256]{2,1,0:T(8,128)(2,1)S(1)}, u32[]{:S(2)}, u32[]{:S(2)}) async-start(bf16[32,32,256]{2,1,0:T(8,128)(2,1)} %get-tuple-element.40), calls=%async_computation | async-start | bytes 1048576 | tf_op jit(solution)/shard_map/all_to_all | solution.py:259
  22.1 5.9 %collective-permute-start = (s32[3,6]{1,0:T(4,128)S(1)}, s32[3,6]{1,0:T(4,128)S(1)}, u32[]{:S(2)}, u32[]{:S(2)}) collective-permute-start(s32[3,6]{1,0:T(4,128)S(1)} %bitcast.34), channel_id=1, source_target_pairs={{0,2},{1,3},{2,4},{3,5},{4,6},{5,7},{6,0},{7,1},{8,10},{9,11},{10,... | collective-permute-start | bytes 224 | tf_op jit(solution)/shard_map/ppermute | solution.py:258
  23.8 5.1 %collective-permute-start.1 = (s32[3,6]{1,0:T(4,128)S(1)}, s32[3,6]{1,0:T(4,128)S(1)}, u32[]{:S(2)}, u32[]{:S(2)}) collective-permute-start(s32[3,6]{1,0:T(4,128)S(1)} %bitcast.35), channel_id=1, source_target_pairs={{0,4},{1,5},{2,6},{3,7},{4,0},{5,1},{6,2},{7,3},{8,12},{9,13},{10,... | collective-permute-start | bytes 224 | tf_op jit(solution)/shard_map/ppermute | solution.py:258
  26.7 3.6 %collective-permute-start.2 = (s32[3,6]{1,0:T(4,128)S(1)}, s32[3,6]{1,0:T(4,128)S(1)}, u32[]{:S(2)}, u32[]{:S(2)}) collective-permute-start(s32[3,6]{1,0:T(4,128)S(1)} %bitcast.36), channel_id=1, source_target_pairs={{0,6},{1,7},{2,0},{3,1},{4,2},{5,3},{6,4},{7,5},{8,14},{9,15},{10,... | collective-permute-start | bytes 224 | tf_op jit(solution)/shard_map/ppermute | solution.py:258
  30.3 19.7 %collective-permute-start.4 = (bf16[1,3,256,256]{3,2,1,0:T(8,128)(2,1)}, bf16[1,3,256,256]{3,2,1,0:T(8,128)(2,1)S(1)}, u32[]{:S(2)}, u32[]{:S(2)}) collective-permute-start(bf16[1,3,256,256]{3,2,1,0:T(8,128)(2,1)} %bitcast.40), channel_id=1, source_target_pairs={{0,2},{2,4},{4,6},{6,0},{1,7},{3,1},{5,3},{7,5},{8,10},{10,12},{12... | collective-permute-start | bytes 1179656 | tf_op jit(solution)/shard_map/ppermute | solution.py:258
  30.6 19.4 %collective-permute-start.5 = (bf16[1,3,256,256]{3,2,1,0:T(8,128)(2,1)}, bf16[1,3,256,256]{3,2,1,0:T(8,128)(2,1)}, u32[]{:S(2)}, u32[]{:S(2)}) collective-permute-start(bf16[1,3,256,256]{3,2,1,0:T(8,128)(2,1)} %bitcast.41), channel_id=1, source_target_pairs={{1,2},{3,4},{5,6},{7,0},{0,7},{2,1},{4,3},{6,5},{9,10},{11,12},{13... | collective-permute-start | bytes 1179656 | tf_op jit(solution)/shard_map/ppermute | solution.py:258
  30.6 8.4 %copy-start.9 = (s32[4,3,6]{2,1,0:T(4,128)}, s32[4,3,6]{2,1,0:T(4,128)S(1)}, u32[]{:S(2)}) copy-start(s32[4,3,6]{2,1,0:T(4,128)S(1)} %pad_add_fusion.here) | copy-start | bytes 868
  30.6 2.3 %collective-permute-start.3 = (s32[4,3,6]{2,1,0:T(4,128)S(1)}, s32[4,3,6]{2,1,0:T(4,128)S(1)}, u32[]{:S(2)}, u32[]{:S(2)}) collective-permute-start(s32[4,3,6]{2,1,0:T(4,128)S(1)} %pad_add_fusion.here), channel_id=1, source_target_pairs={{0,1},{1,0},{2,3},{3,2},{4,5},{5,4},{6,7},{7,6},{8,9},{9,8},{10,11... | collective-permute-start | bytes 872 | tf_op jit(solution)/shard_map/ppermute | solution.py:258
  32.9 6.1 %copy-start.10 = (s32[4,3,6]{2,1,0:T(4,128)}, s32[4,3,6]{2,1,0:T(4,128)S(1)}, u32[]{:S(2)}) copy-start(s32[4,3,6]{2,1,0:T(4,128)S(1)} %collective-permute-done.3.there) | copy-start | bytes 868
  39.0 0.8 copy-start.2
  50.0 45.1 %copy-start.4 = (bf16[1,3,256,256]{3,2,1,0:T(8,128)(2,1)}, bf16[1,3,256,256]{3,2,1,0:T(8,128)(2,1)S(1)}, u32[]{:S(2)}) copy-start(bf16[1,3,256,256]{3,2,1,0:T(8,128)(2,1)S(1)} %collective-permute-done.4.refs_5_) | copy-start | bytes 1179652
  50.0 42.0 %collective-permute-start.9 = (bf16[6,3,256,256]{3,2,1,0:T(8,128)(2,1)S(1)}, bf16[6,3,256,256]{3,2,1,0:T(8,128)(2,1)}, u32[]{:S(2)}, u32[]{:S(2)}) collective-permute-start(bf16[6,3,256,256]{3,2,1,0:T(8,128)(2,1)S(1)} %bitcast.23), channel_id=1, source_target_pairs={{0,1},{1,0},{2,3},{3,2},{4,5},{5,4},{6,7},{7,6},{8,9},{9,8},{10,11... | collective-permute-start | bytes 7077896 | tf_op jit(solution)/shard_map/ppermute | solution.py:258
  50.1 13.0 %collective-permute-start.6 = (bf16[2,6,32,256]{3,2,1,0:T(8,128)(2,1)}, bf16[2,6,32,256]{3,2,1,0:T(8,128)(2,1)S(1)}, u32[]{:S(2)}, u32[]{:S(2)}) collective-permute-start(bf16[2,6,32,256]{3,2,1,0:T(8,128)(2,1)} %get-tuple-element.51), channel_id=1, source_target_pairs={{0,2},{1,3},{2,4},{3,5},{4,6},{5,7},{6,0},{7,1},{8,10},{9,11},{10,... | collective-permute-start | bytes 589832 | tf_op jit(solution)/shard_map/ppermute | solution.py:258
  50.6 12.4 %collective-permute-start.7 = (bf16[2,6,32,256]{3,2,1,0:T(8,128)(2,1)}, bf16[2,6,32,256]{3,2,1,0:T(8,128)(2,1)S(1)}, u32[]{:S(2)}, u32[]{:S(2)}) collective-permute-start(bf16[2,6,32,256]{3,2,1,0:T(8,128)(2,1)} %get-tuple-element.52), channel_id=1, source_target_pairs={{0,4},{1,5},{2,6},{3,7},{4,0},{5,1},{6,2},{7,3},{8,12},{9,13},{10,... | collective-permute-start | bytes 589832 | tf_op jit(solution)/shard_map/ppermute | solution.py:258
  52.8 10.8 %collective-permute-start.8 = (bf16[2,6,32,256]{3,2,1,0:T(8,128)(2,1)}, bf16[2,6,32,256]{3,2,1,0:T(8,128)(2,1)S(1)}, u32[]{:S(2)}, u32[]{:S(2)}) collective-permute-start(bf16[2,6,32,256]{3,2,1,0:T(8,128)(2,1)} %get-tuple-element.53), channel_id=1, source_target_pairs={{0,6},{1,7},{2,0},{3,1},{4,2},{5,3},{6,4},{7,5},{8,14},{9,15},{10,... | collective-permute-start | bytes 589832 | tf_op jit(solution)/shard_map/ppermute | solution.py:258
  63.0 28.9 %copy-start.11 = (bf16[2,6,32,256]{3,2,1,0:T(8,128)(2,1)}, bf16[2,6,32,256]{3,2,1,0:T(8,128)(2,1)S(1)}, u32[]{:S(2)}) copy-start(bf16[2,6,32,256]{3,2,1,0:T(8,128)(2,1)S(1)} %collective-permute-done.6.refs_1_) | copy-start | bytes 589828
  63.0 0.7 copy-start.12
  63.7 0.7 copy-start.13
  64.3 38.5 %all-to-all-start.1 = ((bf16[32,32,256]{2,1,0:T(8,128)(2,1)}), bf16[32,32,256]{2,1,0:T(8,128)(2,1)S(1)}, u32[]{:S(2)}, u32[]{:S(2)}) async-start(bf16[32,32,256]{2,1,0:T(8,128)(2,1)} %get-tuple-element.54), calls=%async_computation.1 | async-start | bytes 1048576 | tf_op jit(solution)/shard_map/all_to_all | solution.py:259
  74.5 17.5 %collective-permute-start.16 = (bf16[1,3,256,256]{3,2,1,0:T(8,128)(2,1)S(1)}, bf16[1,3,256,256]{3,2,1,0:T(8,128)(2,1)S(1)}, u32[]{:S(2)}, u32[]{:S(2)}) collective-permute-start(bf16[1,3,256,256]{3,2,1,0:T(8,128)(2,1)S(1)} %collective-permute-done.4.refs_5_), channel_id=1, source_target_pairs={{0,2},{2,4},{4,6},{6,0},{1,7},{3,1},{5,3},{7,5},{8,10},{10,12},{12... | collective-permute-start | bytes 1179656 | tf_op jit(solution)/shard_map/ppermute | solution.py:258
  75.2 21.7 %collective-permute-start.17 = (bf16[1,3,256,256]{3,2,1,0:T(8,128)(2,1)S(1)}, bf16[1,3,256,256]{3,2,1,0:T(8,128)(2,1)S(1)}, u32[]{:S(2)}, u32[]{:S(2)}) collective-permute-start(bf16[1,3,256,256]{3,2,1,0:T(8,128)(2,1)S(1)} %collective-permute-done.4.refs_5_), channel_id=1, source_target_pairs={{0,1},{1,0},{2,3},{3,2},{4,5},{5,4},{6,7},{7,6},{8,9},{9,8},{10,11... | collective-permute-start | bytes 1179656 | tf_op jit(solution)/shard_map/ppermute | solution.py:258
  76.4 21.5 %collective-permute-start.18 = (bf16[1,3,256,256]{3,2,1,0:T(8,128)(2,1)}, bf16[1,3,256,256]{3,2,1,0:T(8,128)(2,1)S(1)}, u32[]{:S(2)}, u32[]{:S(2)}) collective-permute-start(bf16[1,3,256,256]{3,2,1,0:T(8,128)(2,1)} %collective-permute-done.5.refs_6_), channel_id=1, source_target_pairs={{0,1},{1,0},{2,3},{3,2},{4,5},{5,4},{6,7},{7,6},{8,9},{9,8},{10,11... | collective-permute-start | bytes 1179656 | tf_op jit(solution)/shard_map/ppermute | solution.py:258
  91.9 3.1 %copy-start.5 = (bf16[1,3,256,256]{3,2,1,0:T(8,128)(2,1)}, bf16[1,3,256,256]{3,2,1,0:T(8,128)(2,1)S(1)}, u32[]{:S(2)}) copy-start(bf16[1,3,256,256]{3,2,1,0:T(8,128)(2,1)S(1)} %collective-permute-done.16.refs_7_) | copy-start | bytes 1179652
  91.9 5.9 %collective-permute-start.19 = (bf16[1,3,256,256]{3,2,1,0:T(8,128)(2,1)S(1)}, bf16[1,3,256,256]{3,2,1,0:T(8,128)(2,1)S(1)}, u32[]{:S(2)}, u32[]{:S(2)}) collective-permute-start(bf16[1,3,256,256]{3,2,1,0:T(8,128)(2,1)S(1)} %collective-permute-done.16.refs_7_), channel_id=1, source_target_pairs={{0,1},{1,0},{2,3},{3,2},{4,5},{5,4},{6,7},{7,6},{8,9},{9,8},{10,11... | collective-permute-start | bytes 1179656 | tf_op jit(solution)/shard_map/ppermute | solution.py:258
  95.1 5.4 %collective-permute-start.13 = (f32[32,256]{1,0:T(8,128)}, f32[32,256]{1,0:T(8,128)S(1)}, u32[]{:S(2)}, u32[]{:S(2)}) collective-permute-start(f32[32,256]{1,0:T(8,128)} %get-tuple-element.66), channel_id=1, source_target_pairs={{0,6},{1,7},{2,0},{3,1},{4,2},{5,3},{6,4},{7,5},{8,14},{9,15},{10,... | collective-permute-start | bytes 98312 | tf_op jit(solution)/shard_map/ppermute | solution.py:258
  96.8 5.9 %collective-permute-start.14 = (f32[32,256]{1,0:T(8,128)}, f32[32,256]{1,0:T(8,128)S(1)}, u32[]{:S(2)}, u32[]{:S(2)}) collective-permute-start(f32[32,256]{1,0:T(8,128)} %get-tuple-element.67), channel_id=1, source_target_pairs={{0,4},{1,5},{2,6},{3,7},{4,0},{5,1},{6,2},{7,3},{8,12},{9,13},{10,... | collective-permute-start | bytes 98312 | tf_op jit(solution)/shard_map/ppermute | solution.py:258
  96.9 5.8 %copy-start.6 = (bf16[1,3,256,256]{3,2,1,0:T(8,128)(2,1)}, bf16[1,3,256,256]{3,2,1,0:T(8,128)(2,1)S(1)}, u32[]{:S(2)}) copy-start(bf16[1,3,256,256]{3,2,1,0:T(8,128)(2,1)S(1)} %collective-permute-done.17.refs_9_) | copy-start | bytes 1179652
  96.9 5.9 %collective-permute-start.15 = (f32[32,256]{1,0:T(8,128)}, f32[32,256]{1,0:T(8,128)S(1)}, u32[]{:S(2)}, u32[]{:S(2)}) collective-permute-start(f32[32,256]{1,0:T(8,128)} %get-tuple-element.68), channel_id=1, source_target_pairs={{0,2},{1,3},{2,4},{3,5},{4,6},{5,7},{6,0},{7,1},{8,10},{9,11},{10,... | collective-permute-start | bytes 98312 | tf_op jit(solution)/shard_map/ppermute | solution.py:258
  97.8 4.9 %copy-start.7 = (bf16[1,3,256,256]{3,2,1,0:T(8,128)(2,1)}, bf16[1,3,256,256]{3,2,1,0:T(8,128)(2,1)S(1)}, u32[]{:S(2)}) copy-start(bf16[1,3,256,256]{3,2,1,0:T(8,128)(2,1)S(1)} %collective-permute-done.18.refs_10_) | copy-start | bytes 1179652
  97.8 4.9 %copy-start.8 = (bf16[1,3,256,256]{3,2,1,0:T(8,128)(2,1)}, bf16[1,3,256,256]{3,2,1,0:T(8,128)(2,1)S(1)}, u32[]{:S(2)}) copy-start(bf16[1,3,256,256]{3,2,1,0:T(8,128)(2,1)S(1)} %collective-permute-done.19.refs_11_) | copy-start | bytes 1179652
  100.4 2.4 %copy-start.14 = (f32[32,256]{1,0:T(8,128)}, f32[32,256]{1,0:T(8,128)S(1)}, u32[]{:S(2)}) copy-start(f32[32,256]{1,0:T(8,128)S(1)} %collective-permute-done.13.refs_1_) | copy-start | bytes 98308
  102.8 0.6 copy-start.15
  102.8 0.6 copy-start.16
  102.8 0.8 copy-start.1
  103.6 15.2 %copy-start.23 = (f32[32,256]{1,0:T(8,128)S(1)}, f32[32,256]{1,0:T(8,128)}, u32[]{:S(2)}) copy-start(f32[32,256]{1,0:T(8,128)} %get-tuple-element.62) | copy-start | bytes 98308
  103.6 16.8 %copy-start.22 = (f32[32,256]{1,0:T(8,128)S(1)}, f32[32,256]{1,0:T(8,128)}, u32[]{:S(2)}) copy-start(f32[32,256]{1,0:T(8,128)} %get-tuple-element.63) | copy-start | bytes 98308
  103.6 18.3 %copy-start.21 = (f32[32,256]{1,0:T(8,128)S(1)}, f32[32,256]{1,0:T(8,128)}, u32[]{:S(2)}) copy-start(f32[32,256]{1,0:T(8,128)} %get-tuple-element.64) | copy-start | bytes 98308
  109.0 25.6 %all-to-all-start.2 = ((bf16[32,32,256]{2,1,0:T(8,128)(2,1)}), bf16[32,32,256]{2,1,0:T(8,128)(2,1)S(1)}, u32[]{:S(2)}, u32[]{:S(2)}) async-start(bf16[32,32,256]{2,1,0:T(8,128)(2,1)} %get-tuple-element.71), calls=%async_computation.2 | async-start | bytes 1048576 | tf_op jit(solution)/shard_map/all_to_all | solution.py:259
  118.8 4.0 %collective-permute-start.10 = (f32[32,256]{1,0:T(8,128)S(1)}, f32[32,256]{1,0:T(8,128)S(1)}, u32[]{:S(2)}, u32[]{:S(2)}) collective-permute-start(f32[32,256]{1,0:T(8,128)S(1)} %copy-done.23), channel_id=1, source_target_pairs={{0,6},{1,7},{2,0},{3,1},{4,2},{5,3},{6,4},{7,5},{8,14},{9,15},{10,... | collective-permute-start | bytes 98312 | tf_op jit(solution)/shard_map/ppermute | solution.py:258
  120.4 5.4 %collective-permute-start.11 = (f32[32,256]{1,0:T(8,128)S(1)}, f32[32,256]{1,0:T(8,128)S(1)}, u32[]{:S(2)}, u32[]{:S(2)}) collective-permute-start(f32[32,256]{1,0:T(8,128)S(1)} %copy-done.22), channel_id=1, source_target_pairs={{0,4},{1,5},{2,6},{3,7},{4,0},{5,1},{6,2},{7,3},{8,12},{9,13},{10,... | collective-permute-start | bytes 98312 | tf_op jit(solution)/shard_map/ppermute | solution.py:258
  121.9 5.1 %collective-permute-start.12 = (f32[32,256]{1,0:T(8,128)S(1)}, f32[32,256]{1,0:T(8,128)S(1)}, u32[]{:S(2)}, u32[]{:S(2)}) collective-permute-start(f32[32,256]{1,0:T(8,128)S(1)} %copy-done.21), channel_id=1, source_target_pairs={{0,2},{1,3},{2,4},{3,5},{4,6},{5,7},{6,0},{7,1},{8,10},{9,11},{10,... | collective-permute-start | bytes 98312 | tf_op jit(solution)/shard_map/ppermute | solution.py:258
  122.8 4.2 %copy-start.17 = (f32[32,256]{1,0:T(8,128)}, f32[32,256]{1,0:T(8,128)S(1)}, u32[]{:S(2)}) copy-start(f32[32,256]{1,0:T(8,128)S(1)} %collective-permute-done.10.refs_1_) | copy-start | bytes 98308
  125.8 1.2 copy-start.18
  127.0 0.6 copy-start.19
  134.6 0.8 copy-start.3
Sparse Core Ops, SparseCore 0:
  9.9 40.3 all-gather.4
  52.1 50.7 all-gather.6

commit v10 on v5

--- a/solution.py
+++ b/solution.py
@@ -14,7 +14,7 @@
 PLACES = 8
 CHIPS = 4
 NT = 32
-VMEM_BYTES = 56 * 1024 * 1024
+VMEM_BYTES = 64 * 1024 * 1024
 SMEM = pl.BlockSpec(memory_space=pltpu.SMEM)
 ANY = pl.BlockSpec(memory_space=pl.ANY)
 F32, BF16 = jnp.float32, jnp.bfloat16
@@ -56,21 +56,27 @@
     )(*args)
 
 
-def first_kernel(place, rhs, dinv, answer, spread):
+def first_kernel(place, rhs, dinv, *refs):
+    count = (len(refs) - 2) // 2
+    tiles, (answer, spread), cuts = refs[:count], refs[count : count + 2], refs[count + 2 :]
     residual = probe_rows(place[0], rhs[0]).astype(BF16)
     result = dot_nt(residual, dinv[0])
     answer[...] = result
     spread_out(result, spread)
-
-
-def first_call(place, rhs, dinv):
+    for n in range(count):
+        for slot in range(SLOTS):
+            cuts[n][slot * SIZE : (slot + 1) * SIZE] = tiles[n][0, slot]
+
+
+def first_call(place, rhs, dinv, tiles, pairs):
+    diag, cut = block_of((1, SIZE, SIZE), 0), (SLOTS * SIZE, SIZE)
     return call(
         first_kernel,
         "level0",
-        [((BLOCK, SIZE), F32), ((NT, BLOCK, SIZE), BF16)],
-        [SMEM, block_of((1, SIZE, SIZE), 0), block_of((1, SIZE, SIZE), 0)],
-        [block_of((BLOCK, SIZE)), block_of((NT, BLOCK, SIZE))],
-        (place, rhs, dinv),
+        [((BLOCK, SIZE), F32), ((NT, BLOCK, SIZE), BF16)] + [(cut, BF16)] * len(pairs),
+        [SMEM, diag, diag] + [block_of((1, SLOTS, SIZE, SIZE), p) for p in pairs],
+        [block_of((BLOCK, SIZE)), block_of((NT, BLOCK, SIZE))] + [block_of(cut)] * len(pairs),
+        (place, rhs, dinv) + (tiles,) * len(pairs),
         moved=2**22,
     )
 
@@ -201,18 +207,13 @@
     over_row = lambda array: lax.all_to_all(array, "row", 0, 0, tiled=True)
 
     gather = lambda array: lax.all_gather(array, "col", axis=0, tiled=False)
-    piece = lambda array, pair: array[pair].reshape(SLOTS * SIZE, SIZE)
     live = live.transpose(1, 0)
 
     own = cols.transpose(2, 1, 0).reshape(SLOTS, -1)
     here = jnp.stack([own] + [move(own, TURN[d]) for d in range(1, CHIPS)])
     there = move(here, SWAP)
-    answer0, spread0 = first_call(place, rhs, dinv)
-    gathered0 = gather(piece(tiles, 0))
-    later, spread0 = lax.optimization_barrier((tiles, spread0))
-    gathered2 = gather(piece(later, 2))
-    gathered5 = gather(piece(later, 5))
-    swapped = move(later, SWAP)
+    answer0, spread0, *cuts = first_call(place, rhs, dinv, tiles, (0, 2, 5))
+    gathered0, gathered2, gathered5 = [gather(cut) for cut in cuts]
 
     def send(picked):
         return [picked[0]] + [move(picked[d], TURN[d]) for d in range(1, CHIPS)]
@@ -222,7 +223,8 @@
 
     known0 = over_row(spread0)
     picked = pick_call("pick13", (1, 3), place, here, there, known0)
-    known0, *picked = lax.optimization_barrier((known0, *picked))
+    later, known0, *picked = lax.optimization_barrier((tiles, known0, *picked))
+    swapped = move(later, SWAP)
     got = send(picked)
     answer1, spread1 = level_call(1, 0, place, here, there, live, rhs, dinv, known0, gathered0, [], [])
     spread1, *got = lax.optimization_barrier((spread1, *got))

time: 125 us -> 124 us (level); the launches traced: 124 us -> 122 us
  local copies, waits for them, and re-layouts: 6.41 us -> 1.96 us
  waiting for transfers between devices: 31 us -> 35 us
  starting transfers between devices: 48 us -> 45.5 us
    all_to_all x3, waiting for transfers between devices: 14.5 us -> 10.2 us  [local(): over_row = lambda array: lax.all_to_all(array, 'row', 0, 0, tiled=True)]
    slice x2 -> x0, local copies, waits for them, and re-layouts: 3.97 us -> none  [local(): piece = lambda array, pair: array[pair].reshape(SLOTS * SIZE, SIZE)]
    all_gather x3, waiting for transfers between devices: 5.9 us -> 9.77 us  [local(): gather = lambda array: lax.all_gather(array, 'col', axis=0, tiled=False)]
    ppermute x17, waiting for transfers between devices: 9.87 us -> 13.6 us  [local(): move = lambda array, pairs: lax.ppermute(array, 'col', pairs)]
    ppermute x17, starting transfers between devices: 25 us -> 22.4 us  [local(): move = lambda array, pairs: lax.ppermute(array, 'col', pairs)]
  transfers between devices with their start and end apart: 23 -> 23, of which waited for: 10 -> 10; matrix products, arithmetic and copies ran while one was open for 2% -> 1% of each run, Pallas kernels for 17% -> 15%
where the time goes in v10:
time: 124 us; the launch traced here: 122 us
  starting transfers between devices  45.5 us (37%)
  waiting for transfers between devices  35 us (28%)
  Pallas kernels  26 us (21%)
  between operations  13.2 us (11%)
  local copies, waits for them, and re-layouts  1.96 us (2%)
    pallas_call x8, Pallas kernels, call(): pl.pallas_call(kernel, grid=(1,), out_shape=tuple((jax.ShapeDtypeStruct(s...  26 us
    all_to_all x3, starting transfers between devices, local(): over_row = lambda array: lax.all_to_all(array, 'row', 0, 0, tiled=True)  23 us
    ppermute x17, starting transfers between devices, local(): move = lambda array, pairs: lax.ppermute(array, 'col', pairs)  22.4 us
    ppermute x17, waiting for transfers between devices, local(): move = lambda array, pairs: lax.ppermute(array, 'col', pairs)  13.6 us
    all_to_all x3, waiting for transfers between devices, local(): over_row = lambda array: lax.all_to_all(array, 'row', 0, 0, tiled=True)  10.2 us
    all_gather x3, waiting for transfers between devices, local(): gather = lambda array: lax.all_gather(array, 'col', axis=0, tiled=False)  9.77 us
  transfers between devices with their start and end apart: 23, of which 10 were waited for; matrix products, arithmetic and copies ran while one was open for 1% of the time, Pallas kernels for 15%

profile of v10, /device:TPU:2, one launch (start us, length us, event | category | flops | bytes accessed | tf_op | source)
XLA Modules:
  0.0 121.7 jit_solution(10579086455633991298)
XLA Ops:
  6.5 0.0 all-gather.7.cloned.1.call-start
  6.5 2.7 %level0.1 = (f32[32,256]{1,0:T(8,128)}, bf16[32,32,256]{2,1,0:T(8,128)(2,1)}, bf16[768,256]{1,0:T(8,128)(2,1)}, bf16[768,256]{1,0:T(8,128)(2,1)}, bf16[768,256]{1,0:T(8,128)(2,1)}) custom-call(s32[1]{0:T(128)} %bitcast.place, bf16[4,256,256]{2,1,0:T(8,128)(2,1)} %rhs.7, bf16[4,256,256]{2,1,0:T(8,128)(2,1)} %dinv.7, bf16[6,3,256,256]{3,2,1,0:T(8,128)(2,1)} %bitcast.16, ...), custom_call_target="tpu_custom_call" | custom-call | bytes 4194304 | tf_op jit(solution)/shard_map/level0/pallas_call | solution.py:46
  9.3 0.0 all-gather.7.cloned.1.call-update
  9.3 0.0 all-gather.9.cloned.1.call-start
  9.4 0.7 all-gather.9.cloned.1.call-update
  10.1 0.0 all-gather.11.cloned.1.call-start
  10.1 0.7 all-gather.11.cloned.1.call-update
  10.8 11.7 %all-to-all-start = ((bf16[32,32,256]{2,1,0:T(8,128)(2,1)}), bf16[32,32,256]{2,1,0:T(8,128)(2,1)}, u32[]{:S(2)}, u32[]{:S(2)}) async-start(bf16[32,32,256]{2,1,0:T(8,128)(2,1)} %get-tuple-element.60), calls=%async_computation | async-start | bytes 1048576 | tf_op jit(solution)/shard_map/all_to_all | solution.py:207
  22.5 0.7 copy.9
  23.2 3.0 %collective-permute-start.2 = (s32[3,6]{1,0:T(4,128)S(1)}, s32[3,6]{1,0:T(4,128)S(1)}, u32[]{:S(2)}, u32[]{:S(2)}) collective-permute-start(s32[3,6]{1,0:T(4,128)S(1)} %bitcast.33), channel_id=1, source_target_pairs={{0,6},{1,7},{2,0},{3,1},{4,2},{5,3},{6,4},{7,5},{8,14},{9,15},{10,... | collective-permute-start | bytes 224 | tf_op jit(solution)/shard_map/ppermute | solution.py:206
  26.2 0.6 collective-permute-start.1
  26.8 1.0 collective-permute-start
  27.8 0.7 copy.6
  28.5 0.0 collective-permute-done.2
  28.5 2.9 %collective-permute-done.1 = s32[3,6]{1,0:T(4,128)S(1)} collective-permute-done((s32[3,6]{1,0:T(4,128)S(1)}, s32[3,6]{1,0:T(4,128)S(1)}, u32[]{:S(2)}, u32[]{:S(2)}) %collective-permute-start.1) | collective-permute-done | bytes 104 | tf_op jit(solution)/shard_map/ppermute | solution.py:206
  31.4 0.2 collective-permute-done
  31.6 0.0 copy-start
  31.6 0.6 copy-done
  32.2 0.0 collective-permute-start.3
  32.2 1.3 %collective-permute-done.3.there = s32[4,3,6]{2,1,0:T(4,128)} collective-permute-done((s32[4,3,6]{2,1,0:T(4,128)S(1)}, s32[4,3,6]{2,1,0:T(4,128)}, u32[]{:S(2)}, u32[]{:S(2)}) %collective-permute-start.3) | collective-permute-done | bytes 320 | tf_op jit(solution)/shard_map/ppermute | solution.py:206
  33.5 5.8 %all-to-all-done.known = bf16[32,32,256]{2,1,0:T(8,128)(2,1)} async-done(((bf16[32,32,256]{2,1,0:T(8,128)(2,1)}), bf16[32,32,256]{2,1,0:T(8,128)(2,1)}, u32[]{:S(2)}, u32[]{:S(2)}) %all-to-all-start) | async-done | bytes 524320 | tf_op jit(solution)/shard_map/all_to_all | solution.py:207
  39.4 2.0 %pick13.1 = (bf16[2,6,32,256]{3,2,1,0:T(8,128)(2,1)}, bf16[2,6,32,256]{3,2,1,0:T(8,128)(2,1)}, bf16[2,6,32,256]{3,2,1,0:T(8,128)(2,1)}, bf16[2,6,32,256]{3,2,1,0:T(8,128)(2,1)}) custom-call(s32[1]{0:T(128)} %bitcast.place, s32[4,3,6]{2,1,0:T(4,128)} %copy-done, s32[4,3,6]{2,1,0:T(4,128)} %collective-permute-done.3.there, bf16[32,32,256]{2,1,0:T(8,128)(2,1)} %all-to-all-done.known), custom_call_target="tpu_custom_call" | custom-call | bytes 2097152 | tf_op jit(solution)/shard_map/pick13/pallas_call | solution.py:46
  41.4 0.0 collective-permute-start.7
  41.4 1.6 %collective-permute-start.4 = (bf16[2,6,32,256]{3,2,1,0:T(8,128)(2,1)}, bf16[2,6,32,256]{3,2,1,0:T(8,128)(2,1)}, u32[]{:S(2)}, u32[]{:S(2)}) collective-permute-start(bf16[2,6,32,256]{3,2,1,0:T(8,128)(2,1)} %get-tuple-element.69), channel_id=1, source_target_pairs={{0,2},{1,3},{2,4},{3,5},{4,6},{5,7},{6,0},{7,1},{8,10},{9,11},{10,... | collective-permute-start | bytes 589832 | tf_op jit(solution)/shard_map/ppermute | solution.py:206
  43.0 2.9 %collective-permute-start.5 = (bf16[2,6,32,256]{3,2,1,0:T(8,128)(2,1)}, bf16[2,6,32,256]{3,2,1,0:T(8,128)(2,1)}, u32[]{:S(2)}, u32[]{:S(2)}) collective-permute-start(bf16[2,6,32,256]{3,2,1,0:T(8,128)(2,1)} %get-tuple-element.70), channel_id=1, source_target_pairs={{0,4},{1,5},{2,6},{3,7},{4,0},{5,1},{6,2},{7,3},{8,12},{9,13},{10,... | collective-permute-start | bytes 589832 | tf_op jit(solution)/shard_map/ppermute | solution.py:206
  45.9 1.4 %collective-permute-start.6 = (bf16[2,6,32,256]{3,2,1,0:T(8,128)(2,1)}, bf16[2,6,32,256]{3,2,1,0:T(8,128)(2,1)}, u32[]{:S(2)}, u32[]{:S(2)}) collective-permute-start(bf16[2,6,32,256]{3,2,1,0:T(8,128)(2,1)} %get-tuple-element.71), channel_id=1, source_target_pairs={{0,6},{1,7},{2,0},{3,1},{4,2},{5,3},{6,4},{7,5},{8,14},{9,15},{10,... | collective-permute-start | bytes 589832 | tf_op jit(solution)/shard_map/ppermute | solution.py:206
  47.2 0.0 all-gather.7.cloned.1.call-done
  47.2 4.7 %level1.1 = (f32[32,256]{1,0:T(8,128)}, bf16[32,32,256]{2,1,0:T(8,128)(2,1)}) custom-call(s32[1]{0:T(128)} %bitcast.place, s32[4,3,6]{2,1,0:T(4,128)} %copy-done, s32[4,3,6]{2,1,0:T(4,128)} %collective-permute-done.3.there, s32[1,6]{1,0:T(1,128)} %bitcast.26, bf16[4,256,256]{2,1,0:T(8,128)(2,1)} %rhs.7, bf16[4,256,256]{2,1,0:T(8,128)(2,1)} %dinv.7, ...), custom_call_target="tpu_custom_call" | custom-call | flops 100663296 | bytes 3145728 | tf_op jit(solution)/shard_map/level1/pallas_call | solution.py:46
  51.9 0.0 collective-permute-done.4.refs_1_
  52.0 3.7 %collective-permute-done.5.refs_2_ = bf16[2,6,32,256]{3,2,1,0:T(8,128)(2,1)} collective-permute-done((bf16[2,6,32,256]{3,2,1,0:T(8,128)(2,1)}, bf16[2,6,32,256]{3,2,1,0:T(8,128)(2,1)}, u32[]{:S(2)}, u32[]{:S(2)}) %collective-permute-start.5) | collective-permute-done | bytes 196640 | tf_op jit(solution)/shard_map/ppermute | solution.py:206
  55.7 0.0 collective-permute-done.6.refs_3_
  55.7 5.6 %all-to-all-start.1 = ((bf16[32,32,256]{2,1,0:T(8,128)(2,1)}), bf16[32,32,256]{2,1,0:T(8,128)(2,1)}, u32[]{:S(2)}, u32[]{:S(2)}) async-start(bf16[32,32,256]{2,1,0:T(8,128)(2,1)} %get-tuple-element.72), calls=%async_computation.1 | async-start | bytes 1048576 | tf_op jit(solution)/shard_map/all_to_all | solution.py:207
  61.3 0.0 collective-permute-done.7.refs_5_.refs_7_.refs_9_
  61.3 3.0 %partial13.1 = (f32[32,256]{1,0:T(8,128)}, f32[32,256]{1,0:T(8,128)}, f32[32,256]{1,0:T(8,128)}, f32[32,256]{1,0:T(8,128)}, f32[32,256]{1,0:T(8,128)}, /*index=5...) custom-call(s32[1]{0:T(128)} %bitcast.place, s32[1,6]{1,0:T(1,128)} %bitcast.27, ...), custom_call_target="tpu_custom_call" | custom-call | flops 201326592 | bytes 2097152 | tf_op jit(solution)/shard_map/partial13/pallas_call | solution.py:46
  64.3 2.2 %collective-permute-start.8 = (f32[32,256]{1,0:T(8,128)}, f32[32,256]{1,0:T(8,128)}, u32[]{:S(2)}, u32[]{:S(2)}) collective-permute-start(f32[32,256]{1,0:T(8,128)} %get-tuple-element.79), channel_id=1, source_target_pairs={{0,6},{1,7},{2,0},{3,1},{4,2},{5,3},{6,4},{7,5},{8,14},{9,15},{10,... | collective-permute-start | bytes 98312 | tf_op jit(solution)/shard_map/ppermute | solution.py:206
  66.5 1.1 collective-permute-start.9
  67.6 0.8 collective-permute-start.10
  68.4 1.1 collective-permute-done.8.refs_1_
  69.5 3.5 %collective-permute-done.9.refs_2_ = f32[32,256]{1,0:T(8,128)} collective-permute-done((f32[32,256]{1,0:T(8,128)}, f32[32,256]{1,0:T(8,128)}, u32[]{:S(2)}, u32[]{:S(2)}) %collective-permute-start.9) | collective-permute-done | bytes 32800 | tf_op jit(solution)/shard_map/ppermute | solution.py:206
  73.0 0.8 collective-permute-done.10.refs_3_
  73.8 4.3 %all-to-all-done.1.known = bf16[32,32,256]{2,1,0:T(8,128)(2,1)} async-done(((bf16[32,32,256]{2,1,0:T(8,128)(2,1)}), bf16[32,32,256]{2,1,0:T(8,128)(2,1)}, u32[]{:S(2)}, u32[]{:S(2)}) %all-to-all-start.1) | async-done | bytes 524320 | tf_op jit(solution)/shard_map/all_to_all | solution.py:207
  78.1 1.8 %pick4.1 = (bf16[1,6,32,256]{3,2,1,0:T(8,128)(2,1)}, bf16[1,6,32,256]{3,2,1,0:T(8,128)(2,1)}, bf16[1,6,32,256]{3,2,1,0:T(8,128)(2,1)}, bf16[1,6,32,256]{3,2,1,0:T(8,128)(2,1)}) custom-call(s32[1]{0:T(128)} %bitcast.place, s32[4,3,6]{2,1,0:T(4,128)} %copy-done, s32[4,3,6]{2,1,0:T(4,128)} %collective-permute-done.3.there, ...), custom_call_target="tpu_custom_call" | custom-call | bytes 2097152 | tf_op jit(solution)/shard_map/pick4/pallas_call | solution.py:46
  80.0 0.6 collective-permute-start.11
  80.6 3.2 %collective-permute-start.12 = (bf16[1,6,32,256]{3,2,1,0:T(8,128)(2,1)}, bf16[1,6,32,256]{3,2,1,0:T(8,128)(2,1)}, u32[]{:S(2)}, u32[]{:S(2)}) collective-permute-start(bf16[1,6,32,256]{3,2,1,0:T(8,128)(2,1)} %get-tuple-element.96), channel_id=1, source_target_pairs={{0,4},{1,5},{2,6},{3,7},{4,0},{5,1},{6,2},{7,3},{8,12},{9,13},{10,... | collective-permute-start | bytes 294920 | tf_op jit(solution)/shard_map/ppermute | solution.py:206
  83.8 1.1 collective-permute-start.13
  84.8 0.0 all-gather.9.cloned.1.call-done
  84.8 4.7 %level2.1 = (f32[32,256]{1,0:T(8,128)}, bf16[32,32,256]{2,1,0:T(8,128)(2,1)}) custom-call(s32[1]{0:T(128)} %bitcast.place, s32[4,3,6]{2,1,0:T(4,128)} %copy-done, s32[4,3,6]{2,1,0:T(4,128)} %collective-permute-done.3.there, s32[1,6]{1,0:T(1,128)} %bitcast.28, bf16[4,256,256]{2,1,0:T(8,128)(2,1)} %rhs.7, bf16[4,256,256]{2,1,0:T(8,128)(2,1)} %dinv.7, ...), custom_call_target="tpu_custom_call" | custom-call | flops 100663296 | bytes 3145728 | tf_op jit(solution)/shard_map/level2/pallas_call | solution.py:46
  89.6 0.0 collective-permute-done.11.refs_1_
  89.6 0.0 collective-permute-done.12.refs_2_
  89.6 0.0 collective-permute-done.13.refs_3_
  89.6 5.6 %all-to-all-start.2 = ((bf16[32,32,256]{2,1,0:T(8,128)(2,1)}), bf16[32,32,256]{2,1,0:T(8,128)(2,1)}, u32[]{:S(2)}, u32[]{:S(2)}) async-start(bf16[32,32,256]{2,1,0:T(8,128)(2,1)} %get-tuple-element.98), calls=%async_computation.2 | async-start | bytes 1048576 | tf_op jit(solution)/shard_map/all_to_all | solution.py:207
  95.3 2.4 %partial4.1 = (f32[32,256]{1,0:T(8,128)}, f32[32,256]{1,0:T(8,128)}, f32[32,256]{1,0:T(8,128)}, f32[32,256]{1,0:T(8,128)}) custom-call(s32[1]{0:T(128)} %bitcast.place, s32[1,6]{1,0:T(1,128)} %bitcast.29, bf16[1,6,32,256]{3,2,1,0:T(8,128)(2,1)} %get-tuple-element.100.refs_0_, bf16[1,6,32,256]{3,2,1,0:T(8,128)(2,1)} %collective-permute-done.11.refs_1_, ...), custom_call_target="tpu_custom_call" | custom-call | flops 201326592 | bytes 2097152 | tf_op jit(solution)/shard_map/partial4/pallas_call | solution.py:46
  97.7 1.3 %collective-permute-start.14 = (f32[32,256]{1,0:T(8,128)}, f32[32,256]{1,0:T(8,128)}, u32[]{:S(2)}, u32[]{:S(2)}) collective-permute-start(f32[32,256]{1,0:T(8,128)} %get-tuple-element.109), channel_id=1, source_target_pairs={{0,6},{1,7},{2,0},{3,1},{4,2},{5,3},{6,4},{7,5},{8,14},{9,15},{10,... | collective-permute-start | bytes 98312 | tf_op jit(solution)/shard_map/ppermute | solution.py:206
  99.0 1.7 %collective-permute-start.15 = (f32[32,256]{1,0:T(8,128)}, f32[32,256]{1,0:T(8,128)}, u32[]{:S(2)}, u32[]{:S(2)}) collective-permute-start(f32[32,256]{1,0:T(8,128)} %get-tuple-element.110), channel_id=1, source_target_pairs={{0,4},{1,5},{2,6},{3,7},{4,0},{5,1},{6,2},{7,3},{8,12},{9,13},{10,... | collective-permute-start | bytes 98312 | tf_op jit(solution)/shard_map/ppermute | solution.py:206
  100.7 0.0 collective-permute-start.16
  100.7 9.8 %all-gather.11.cloned.1.call-done = bf16[6144,256]{1,0:T(8,128)(2,1)} async-done(((bf16[768,256]{1,0:T(8,128)(2,1)}), bf16[6144,256]{1,0:T(8,128)(2,1)}) %all-gather.11.cloned.1.call-update) | async-done | bytes 3145744 | tf_op jit(solution)/shard_map/all_gather | solution.py:209
  110.5 0.0 collective-permute-done.14.refs_1_
  110.5 0.0 collective-permute-done.15.refs_2_
  110.5 0.0 collective-permute-done.16.refs_3_
  110.5 0.0 all-to-all-done.2.known
  110.5 4.6 %level3.1 = f32[4,32,256]{2,1,0:T(8,128)} custom-call(s32[1]{0:T(128)} %bitcast.place, s32[4,3,6]{2,1,0:T(4,128)} %copy-done, s32[4,3,6]{2,1,0:T(4,128)} %collective-permute-done.3.there, s32[1,6]{1,0:T(1,128)} %bitcast.30, bf16[4,256,256]{2,1,0:T(8,128)(2,1)} %rhs.7, bf16[4,256,256]{2,1,0:T(8,128)(2,1)} %dinv.7, bf16[32,32,256]{2,1,0:T(8,128)(2,1)} %all-to-all-done.2.known, ...), custom_call_target="tpu_custom_call" | custom-call | flops 100663296 | bytes 3145728 | tf_op jit(solution)/shard_map/level3/pallas_call | solution.py:46
  (1 shorter events, 0.0 us)
Async XLA Ops:
  6.5 40.7 %all-gather.7.cloned.1.call-start = ((), (), s32[]{:S(2)}) async-start(), calls=%async_computation.3 | async-start | bytes 3538944 | tf_op jit(solution)/shard_map/all_gather | solution.py:209
  9.3 75.5 %all-gather.9.cloned.1.call-start = ((), (), s32[]{:S(2)}) async-start(), calls=%async_computation.4 | async-start | bytes 3538944 | tf_op jit(solution)/shard_map/all_gather | solution.py:209
  10.1 100.4 %all-gather.11.cloned.1.call-start = ((), (), s32[]{:S(2)}) async-start(), calls=%async_computation.5 | async-start | bytes 3538944 | tf_op jit(solution)/shard_map/all_gather | solution.py:209
  10.8 28.6 %all-to-all-start = ((bf16[32,32,256]{2,1,0:T(8,128)(2,1)}), bf16[32,32,256]{2,1,0:T(8,128)(2,1)}, u32[]{:S(2)}, u32[]{:S(2)}) async-start(bf16[32,32,256]{2,1,0:T(8,128)(2,1)} %get-tuple-element.60), calls=%async_computation | async-start | bytes 1048576 | tf_op jit(solution)/shard_map/all_to_all | solution.py:207
  23.2 5.3 %collective-permute-start.2 = (s32[3,6]{1,0:T(4,128)S(1)}, s32[3,6]{1,0:T(4,128)S(1)}, u32[]{:S(2)}, u32[]{:S(2)}) collective-permute-start(s32[3,6]{1,0:T(4,128)S(1)} %bitcast.33), channel_id=1, source_target_pairs={{0,6},{1,7},{2,0},{3,1},{4,2},{5,3},{6,4},{7,5},{8,14},{9,15},{10,... | collective-permute-start | bytes 224 | tf_op jit(solution)/shard_map/ppermute | solution.py:206
  26.2 5.2 %collective-permute-start.1 = (s32[3,6]{1,0:T(4,128)S(1)}, s32[3,6]{1,0:T(4,128)S(1)}, u32[]{:S(2)}, u32[]{:S(2)}) collective-permute-start(s32[3,6]{1,0:T(4,128)S(1)} %bitcast.34), channel_id=1, source_target_pairs={{0,4},{1,5},{2,6},{3,7},{4,0},{5,1},{6,2},{7,3},{8,12},{9,13},{10,... | collective-permute-start | bytes 224 | tf_op jit(solution)/shard_map/ppermute | solution.py:206
  26.8 4.8 %collective-permute-start = (s32[3,6]{1,0:T(4,128)S(1)}, s32[3,6]{1,0:T(4,128)S(1)}, u32[]{:S(2)}, u32[]{:S(2)}) collective-permute-start(s32[3,6]{1,0:T(4,128)S(1)} %bitcast.35), channel_id=1, source_target_pairs={{0,2},{1,3},{2,4},{3,5},{4,6},{5,7},{6,0},{7,1},{8,10},{9,11},{10,... | collective-permute-start | bytes 224 | tf_op jit(solution)/shard_map/ppermute | solution.py:206
  31.6 0.6 copy-start
  32.2 1.3 %collective-permute-start.3 = (s32[4,3,6]{2,1,0:T(4,128)S(1)}, s32[4,3,6]{2,1,0:T(4,128)}, u32[]{:S(2)}, u32[]{:S(2)}) collective-permute-start(s32[4,3,6]{2,1,0:T(4,128)S(1)} %pad_add_fusion.here), channel_id=1, source_target_pairs={{0,1},{1,0},{2,3},{3,2},{4,5},{5,4},{6,7},{7,6},{8,9},{9,8},{10,11... | collective-permute-start | bytes 872 | tf_op jit(solution)/shard_map/ppermute | solution.py:206
  41.4 19.9 %collective-permute-start.7 = (bf16[6,3,256,256]{3,2,1,0:T(8,128)(2,1)}, bf16[6,3,256,256]{3,2,1,0:T(8,128)(2,1)}, u32[]{:S(2)}, u32[]{:S(2)}) collective-permute-start(bf16[6,3,256,256]{3,2,1,0:T(8,128)(2,1)} %bitcast.19), channel_id=1, source_target_pairs={{0,1},{1,0},{2,3},{3,2},{4,5},{5,4},{6,7},{7,6},{8,9},{9,8},{10,11... | collective-permute-start | bytes 7077896 | tf_op jit(solution)/shard_map/ppermute | solution.py:206
  41.4 10.6 %collective-permute-start.4 = (bf16[2,6,32,256]{3,2,1,0:T(8,128)(2,1)}, bf16[2,6,32,256]{3,2,1,0:T(8,128)(2,1)}, u32[]{:S(2)}, u32[]{:S(2)}) collective-permute-start(bf16[2,6,32,256]{3,2,1,0:T(8,128)(2,1)} %get-tuple-element.69), channel_id=1, source_target_pairs={{0,2},{1,3},{2,4},{3,5},{4,6},{5,7},{6,0},{7,1},{8,10},{9,11},{10,... | collective-permute-start | bytes 589832 | tf_op jit(solution)/shard_map/ppermute | solution.py:206
  43.0 12.7 %collective-permute-start.5 = (bf16[2,6,32,256]{3,2,1,0:T(8,128)(2,1)}, bf16[2,6,32,256]{3,2,1,0:T(8,128)(2,1)}, u32[]{:S(2)}, u32[]{:S(2)}) collective-permute-start(bf16[2,6,32,256]{3,2,1,0:T(8,128)(2,1)} %get-tuple-element.70), channel_id=1, source_target_pairs={{0,4},{1,5},{2,6},{3,7},{4,0},{5,1},{6,2},{7,3},{8,12},{9,13},{10,... | collective-permute-start | bytes 589832 | tf_op jit(solution)/shard_map/ppermute | solution.py:206
  45.9 9.8 %collective-permute-start.6 = (bf16[2,6,32,256]{3,2,1,0:T(8,128)(2,1)}, bf16[2,6,32,256]{3,2,1,0:T(8,128)(2,1)}, u32[]{:S(2)}, u32[]{:S(2)}) collective-permute-start(bf16[2,6,32,256]{3,2,1,0:T(8,128)(2,1)} %get-tuple-element.71), channel_id=1, source_target_pairs={{0,6},{1,7},{2,0},{3,1},{4,2},{5,3},{6,4},{7,5},{8,14},{9,15},{10,... | collective-permute-start | bytes 589832 | tf_op jit(solution)/shard_map/ppermute | solution.py:206
  55.7 22.5 %all-to-all-start.1 = ((bf16[32,32,256]{2,1,0:T(8,128)(2,1)}), bf16[32,32,256]{2,1,0:T(8,128)(2,1)}, u32[]{:S(2)}, u32[]{:S(2)}) async-start(bf16[32,32,256]{2,1,0:T(8,128)(2,1)} %get-tuple-element.72), calls=%async_computation.1 | async-start | bytes 1048576 | tf_op jit(solution)/shard_map/all_to_all | solution.py:207
  64.3 5.2 %collective-permute-start.8 = (f32[32,256]{1,0:T(8,128)}, f32[32,256]{1,0:T(8,128)}, u32[]{:S(2)}, u32[]{:S(2)}) collective-permute-start(f32[32,256]{1,0:T(8,128)} %get-tuple-element.79), channel_id=1, source_target_pairs={{0,6},{1,7},{2,0},{3,1},{4,2},{5,3},{6,4},{7,5},{8,14},{9,15},{10,... | collective-permute-start | bytes 98312 | tf_op jit(solution)/shard_map/ppermute | solution.py:206
  66.5 6.5 %collective-permute-start.9 = (f32[32,256]{1,0:T(8,128)}, f32[32,256]{1,0:T(8,128)}, u32[]{:S(2)}, u32[]{:S(2)}) collective-permute-start(f32[32,256]{1,0:T(8,128)} %get-tuple-element.80), channel_id=1, source_target_pairs={{0,4},{1,5},{2,6},{3,7},{4,0},{5,1},{6,2},{7,3},{8,12},{9,13},{10,... | collective-permute-start | bytes 98312 | tf_op jit(solution)/shard_map/ppermute | solution.py:206
  67.6 6.2 %collective-permute-start.10 = (f32[32,256]{1,0:T(8,128)}, f32[32,256]{1,0:T(8,128)}, u32[]{:S(2)}, u32[]{:S(2)}) collective-permute-start(f32[32,256]{1,0:T(8,128)} %get-tuple-element.81), channel_id=1, source_target_pairs={{0,2},{1,3},{2,4},{3,5},{4,6},{5,7},{6,0},{7,1},{8,10},{9,11},{10,... | collective-permute-start | bytes 98312 | tf_op jit(solution)/shard_map/ppermute | solution.py:206
  80.0 9.6 %collective-permute-start.11 = (bf16[1,6,32,256]{3,2,1,0:T(8,128)(2,1)}, bf16[1,6,32,256]{3,2,1,0:T(8,128)(2,1)}, u32[]{:S(2)}, u32[]{:S(2)}) collective-permute-start(bf16[1,6,32,256]{3,2,1,0:T(8,128)(2,1)} %get-tuple-element.95), channel_id=1, source_target_pairs={{0,2},{1,3},{2,4},{3,5},{4,6},{5,7},{6,0},{7,1},{8,10},{9,11},{10,... | collective-permute-start | bytes 294920 | tf_op jit(solution)/shard_map/ppermute | solution.py:206
  80.6 9.0 %collective-permute-start.12 = (bf16[1,6,32,256]{3,2,1,0:T(8,128)(2,1)}, bf16[1,6,32,256]{3,2,1,0:T(8,128)(2,1)}, u32[]{:S(2)}, u32[]{:S(2)}) collective-permute-start(bf16[1,6,32,256]{3,2,1,0:T(8,128)(2,1)} %get-tuple-element.96), channel_id=1, source_target_pairs={{0,4},{1,5},{2,6},{3,7},{4,0},{5,1},{6,2},{7,3},{8,12},{9,13},{10,... | collective-permute-start | bytes 294920 | tf_op jit(solution)/shard_map/ppermute | solution.py:206
  83.8 5.9 %collective-permute-start.13 = (bf16[1,6,32,256]{3,2,1,0:T(8,128)(2,1)}, bf16[1,6,32,256]{3,2,1,0:T(8,128)(2,1)}, u32[]{:S(2)}, u32[]{:S(2)}) collective-permute-start(bf16[1,6,32,256]{3,2,1,0:T(8,128)(2,1)} %get-tuple-element.97), channel_id=1, source_target_pairs={{0,6},{1,7},{2,0},{3,1},{4,2},{5,3},{6,4},{7,5},{8,14},{9,15},{10,... | collective-permute-start | bytes 294920 | tf_op jit(solution)/shard_map/ppermute | solution.py:206
  89.6 20.9 %all-to-all-start.2 = ((bf16[32,32,256]{2,1,0:T(8,128)(2,1)}), bf16[32,32,256]{2,1,0:T(8,128)(2,1)}, u32[]{:S(2)}, u32[]{:S(2)}) async-start(bf16[32,32,256]{2,1,0:T(8,128)(2,1)} %get-tuple-element.98), calls=%async_computation.2 | async-start | bytes 1048576 | tf_op jit(solution)/shard_map/all_to_all | solution.py:207
  97.7 12.8 %collective-permute-start.14 = (f32[32,256]{1,0:T(8,128)}, f32[32,256]{1,0:T(8,128)}, u32[]{:S(2)}, u32[]{:S(2)}) collective-permute-start(f32[32,256]{1,0:T(8,128)} %get-tuple-element.109), channel_id=1, source_target_pairs={{0,6},{1,7},{2,0},{3,1},{4,2},{5,3},{6,4},{7,5},{8,14},{9,15},{10,... | collective-permute-start | bytes 98312 | tf_op jit(solution)/shard_map/ppermute | solution.py:206
  99.0 11.5 %collective-permute-start.15 = (f32[32,256]{1,0:T(8,128)}, f32[32,256]{1,0:T(8,128)}, u32[]{:S(2)}, u32[]{:S(2)}) collective-permute-start(f32[32,256]{1,0:T(8,128)} %get-tuple-element.110), channel_id=1, source_target_pairs={{0,4},{1,5},{2,6},{3,7},{4,0},{5,1},{6,2},{7,3},{8,12},{9,13},{10,... | collective-permute-start | bytes 98312 | tf_op jit(solution)/shard_map/ppermute | solution.py:206
  100.7 9.8 %collective-permute-start.16 = (f32[32,256]{1,0:T(8,128)}, f32[32,256]{1,0:T(8,128)}, u32[]{:S(2)}, u32[]{:S(2)}) collective-permute-start(f32[32,256]{1,0:T(8,128)} %get-tuple-element.111), channel_id=1, source_target_pairs={{0,2},{1,3},{2,4},{3,5},{4,6},{5,7},{6,0},{7,1},{8,10},{9,11},{10,... | collective-permute-start | bytes 98312 | tf_op jit(solution)/shard_map/ppermute | solution.py:206
Sparse Core Ops, SparseCore 0:
  9.4 35.6 all-gather.6
  47.0 29.9 all-gather.8
  78.8 31.6 all-gather.10

commit v11 on v10

--- a/solution.py
+++ b/solution.py
@@ -18,6 +18,7 @@
 SMEM = pl.BlockSpec(memory_space=pltpu.SMEM)
 ANY = pl.BlockSpec(memory_space=pl.ANY)
 F32, BF16 = jnp.float32, jnp.bfloat16
+COL = ("chip", "core")
 SWAP = [(p, p ^ 1) for p in range(PLACES)]
 TURN = [[(p, (p + 2 * d) % PLACES) for p in range(PLACES)] for d in range(CHIPS)]
 
@@ -148,28 +149,35 @@
     )
 
 
-def level_kernel(pair, returned, earlier, place, here, there, live, rhs, dinv, known, tiles, *refs):
+def level_kernel(pair, count, returned, earlier, place, here, there, live, rhs, dinv, known, *refs):
     refs = list(refs)
+    tiles = [refs.pop(0) for _ in range(count)]
     back = [refs.pop(0) for _ in range(returned)]
     before = [refs.pop(0) for _ in range(earlier)]
     held, sems = refs[-2:]
     chip, core = lax.div(place[0], 2), lax.rem(place[0], 2)
     chips = [lax.rem(chip + CHIPS - d, CHIPS) for d in range(CHIPS)]
+    split = count == 2
     copies = [
-        pltpu.make_async_copy(tiles.at[pl.ds(2 * chips[d], 2)], held.at[pl.ds(2 * d, 2)], sems.at[d]) for d in range(CHIPS)
+        [pltpu.make_async_copy(tiles[n].at[chips[d]], held.at[2 * d + n], sems.at[2 * d + n]) for n in range(2)]
+        if split
+        else [pltpu.make_async_copy(tiles[0].at[pl.ds(2 * chips[d], 2)], held.at[pl.ds(2 * d, 2)], sems.at[2 * d])]
+        for d in range(CHIPS)
     ]
-    for copy in copies:
+    for copy in sum(copies, []):
         copy.start()
     total = probe_rows(place[0], rhs[0])
     for sums in back:
         total = total - sums[...]
     for d in range(CHIPS):
-        copies[d].wait()
-        for cols, side in ((here, core), (there, 1 - core)):
+        for copy in copies[d]:
+            copy.wait()
+        for n, (cols, side) in enumerate(((here, core), (there, 1 - core))):
             first = (2 * chips[d] + side) * SLOTS
+            at = 2 * d + (n if split else side)
             for slot in range(SLOTS):
                 block = masked(known[cols[d, slot, pair]], first + slot < live[0, pair])
-                total = total - dot_nt(block, held[2 * d + side, slot * SIZE : (slot + 1) * SIZE])
+                total = total - dot_nt(block, held[at, slot * SIZE : (slot + 1) * SIZE])
     result = dot_nt(total.astype(BF16), dinv[0])
     if earlier:
         for n in range(earlier):
@@ -188,32 +196,32 @@
         shapes = [((BLOCK, SIZE), F32), ((NT, BLOCK, SIZE), BF16)]
         outs = [flat, block_of((NT, BLOCK, SIZE))]
     return call(
-        functools.partial(level_kernel, pair, len(back), len(earlier)),
+        functools.partial(level_kernel, pair, len(tiles), len(back), len(earlier)),
         "level%d" % level,
         shapes,
-        [SMEM] * 4 + [pick, pick, block_of((NT, BLOCK, SIZE)), ANY] + [flat] * (len(back) + len(earlier)),
+        [SMEM] * 4 + [pick, pick, block_of((NT, BLOCK, SIZE))] + [ANY] * len(tiles) + [flat] * (len(back) + len(earlier)),
         outs,
-        (place, here, there, live, rhs, dinv, known, tiles, *back, *earlier),
-        [pltpu.VMEM((PLACES, SLOTS * SIZE, SIZE), BF16), pltpu.SemaphoreType.DMA((CHIPS,))],
+        (place, here, there, live, rhs, dinv, known, *tiles, *back, *earlier),
+        [pltpu.VMEM((PLACES, SLOTS * SIZE, SIZE), BF16), pltpu.SemaphoreType.DMA((PLACES,))],
         flops=2 * 24 * BLOCK * SIZE * SIZE,
         moved=24 * SIZE * SIZE * 2,
     )
 
 
 def local(rhs, dinv, factor, cols, live):
-    place = lax.axis_index("col").astype(jnp.int32).reshape(1)
+    place = lax.axis_index(COL).astype(jnp.int32).reshape(1)
     tiles = factor.transpose(0, 2, 1, 3)
-    move = lambda array, pairs: lax.ppermute(array, "col", pairs)
+    move = lambda array, pairs: lax.ppermute(array, COL, pairs)
     over_row = lambda array: lax.all_to_all(array, "row", 0, 0, tiled=True)
 
-    gather = lambda array: lax.all_gather(array, "col", axis=0, tiled=False)
+    gather = lambda array, axes: lax.all_gather(array, axes, axis=0, tiled=False)
     live = live.transpose(1, 0)
 
     own = cols.transpose(2, 1, 0).reshape(SLOTS, -1)
     here = jnp.stack([own] + [move(own, TURN[d]) for d in range(1, CHIPS)])
     there = move(here, SWAP)
     answer0, spread0, *cuts = first_call(place, rhs, dinv, tiles, (0, 2, 5))
-    gathered0, gathered2, gathered5 = [gather(cut) for cut in cuts]
+    gathered0, gathered2, gathered5 = gather(cuts[0], "chip"), gather(cuts[1], COL), gather(cuts[2], COL)
 
     def send(picked):
         return [picked[0]] + [move(picked[d], TURN[d]) for d in range(1, CHIPS)]
@@ -223,11 +231,13 @@
 
     known0 = over_row(spread0)
     picked = pick_call("pick13", (1, 3), place, here, there, known0)
-    later, known0, *picked = lax.optimization_barrier((tiles, known0, *picked))
+    known0, *picked = lax.optimization_barrier((known0, *picked))
+    got = send(picked)
+    gathered0, _ = lax.optimization_barrier((gathered0, picked[0]))
+    gathered0 = [gathered0, move(gathered0, SWAP)]
+    answer1, spread1 = level_call(1, 0, place, here, there, live, rhs, dinv, known0, gathered0, [], [])
+    later, spread1, *got = lax.optimization_barrier((tiles, spread1, *got))
     swapped = move(later, SWAP)
-    got = send(picked)
-    answer1, spread1 = level_call(1, 0, place, here, there, live, rhs, dinv, known0, gathered0, [], [])
-    spread1, *got = lax.optimization_barrier((spread1, *got))
     known1 = over_row(spread1)
 
     sums = partial_call("partial13", (1, 3), place, live, got, [], tiles, swapped)
@@ -237,24 +247,26 @@
     picked = pick_call("pick4", (4,), place, here, there, known1)
     known1, *picked = lax.optimization_barrier((known1, *picked))
     got = send(picked)
-    answer2, spread2 = level_call(2, 2, place, here, there, live, rhs, dinv, known1, gathered2, back2, [])
+    answer2, spread2 = level_call(2, 2, place, here, there, live, rhs, dinv, known1, [gathered2], back2, [])
     spread2, *got = lax.optimization_barrier((spread2, *got))
     known2 = over_row(spread2)
 
     sums3 = partial_call("partial4", (4,), place, live, got, sums3, tiles, swapped)
     (solved,) = level_call(
-        3, 5, place, here, there, live, rhs, dinv, known2, gathered5, give_back(sums3), [answer0, answer1, answer2]
+        3, 5, place, here, there, live, rhs, dinv, known2, [gathered5], give_back(sums3), [answer0, answer1, answer2]
     )
     return solved.transpose(0, 2, 1)
 
 
 def solution(mesh):
+    rows, places = mesh.devices.shape
+    mesh = jax.sharding.Mesh(mesh.devices.reshape(rows, places // 2, 2), ("row",) + COL)
     in_specs = (
         P(None, "row", None),
         P(None, "row", None),
-        P(None, "row", "col", None),
-        P(None, "row", "col"),
+        P(None, "row", COL, None),
+        P(None, "row", COL),
         P(None, "row"),
     )
-    out_specs = P(None, "row", "col")
+    out_specs = P(None, "row", COL)
     return jax.shard_map(local, mesh=mesh, in_specs=in_specs, out_specs=out_specs, check_vma=False)

time: 124 us -> 128 us (1.032); the launches traced: 122 us -> 127 us
  starting transfers between devices: 45.5 us -> 49.5 us
    all_to_all x3, waiting for transfers between devices: 10.2 us -> 18.5 us  [local(): over_row = lambda array: lax.all_to_all(array, 'row', 0, 0, tiled=True)]
    all_gather x3, waiting for transfers between devices: 9.77 us -> 1.82 us  [local(): lax.all_gather(array, axes, axis=0, tiled=False)]
    all_to_all x3, starting transfers between devices: 23 us -> 26.9 us  [local(): over_row = lambda array: lax.all_to_all(array, 'row', 0, 0, tiled=True)]
    ppermute x17 -> x18, waiting for transfers between devices: 13.6 us -> 14.4 us  [local(): move = lambda array, pairs: lax.ppermute(array, COL, pairs)]
    ppermute x17 -> x18, starting transfers between devices: 22.4 us -> 22.6 us  [local(): move = lambda array, pairs: lax.ppermute(array, COL, pairs)]
  transfers between devices with their start and end apart: 23 -> 24, of which waited for: 10 -> 15; matrix products, arithmetic and copies ran while one was open for 1% -> 1% of each run, Pallas kernels for 15% -> 15%
where the time goes in v11:
time: 128 us; the launch traced here: 127 us
  starting transfers between devices  49.5 us (39%)
  waiting for transfers between devices  36.1 us (28%)
  Pallas kernels  26.3 us (21%)
  between operations  13.2 us (10%)
  local copies, waits for them, and re-layouts  1.96 us (2%)
    all_to_all x3, starting transfers between devices, local(): over_row = lambda array: lax.all_to_all(array, 'row', 0, 0, tiled=True)  26.9 us
    pallas_call x8, Pallas kernels, call(): pl.pallas_call(kernel, grid=(1,), out_shape=tuple((jax.ShapeDtypeStruct(s...  26.3 us
    ppermute x18, starting transfers between devices, local(): move = lambda array, pairs: lax.ppermute(array, COL, pairs)  22.6 us
    all_to_all x3, waiting for transfers between devices, local(): over_row = lambda array: lax.all_to_all(array, 'row', 0, 0, tiled=True)  18.5 us
    ppermute x18, waiting for transfers between devices, local(): move = lambda array, pairs: lax.ppermute(array, COL, pairs)  14.4 us
  transfers between devices with their start and end apart: 24, of which 15 were waited for; matrix products, arithmetic and copies ran while one was open for 1% of the time, Pallas kernels for 15%

profile of v11, /device:TPU:2, one launch (start us, length us, event | category | flops | bytes accessed | tf_op | source)
XLA Modules:
  0.0 127.1 jit_solution(296256583583946744)
XLA Ops:
  6.5 0.0 all-gather.7.cloned.1.call-start
  6.5 2.8 %level0.1 = (f32[32,256]{1,0:T(8,128)}, bf16[32,32,256]{2,1,0:T(8,128)(2,1)}, bf16[768,256]{1,0:T(8,128)(2,1)}, bf16[768,256]{1,0:T(8,128)(2,1)}, bf16[768,256]{1,0:T(8,128)(2,1)}) custom-call(s32[1]{0:T(128)} %bitcast.place, bf16[4,256,256]{2,1,0:T(8,128)(2,1)} %rhs.7, bf16[4,256,256]{2,1,0:T(8,128)(2,1)} %dinv.7, bf16[6,3,256,256]{3,2,1,0:T(8,128)(2,1)} %bitcast.16, ...), custom_call_target="tpu_custom_call" | custom-call | bytes 4194304 | tf_op jit(solution)/shard_map/level0/pallas_call | solution.py:47
  9.3 0.0 all-gather.7.cloned.1.call-update
  9.3 0.0 all-gather.9.cloned.1.call-start
  9.4 0.7 all-gather.9.cloned.1.call-update
  10.1 11.7 %all-to-all-start = ((bf16[32,32,256]{2,1,0:T(8,128)(2,1)}), bf16[32,32,256]{2,1,0:T(8,128)(2,1)}, u32[]{:S(2)}, u32[]{:S(2)}) async-start(bf16[32,32,256]{2,1,0:T(8,128)(2,1)} %get-tuple-element.61), calls=%async_computation | async-start | bytes 1048576 | tf_op jit(solution)/shard_map/all_to_all | solution.py:215
  21.8 0.0 all-gather.11.cloned.1.call-start
  21.8 0.7 all-gather.11.cloned.1.call-update
  22.5 0.7 copy.9
  23.2 1.6 %collective-permute-start = (s32[3,6]{1,0:T(4,128)S(1)}, s32[3,6]{1,0:T(4,128)S(1)}, u32[]{:S(2)}, u32[]{:S(2)}) collective-permute-start(s32[3,6]{1,0:T(4,128)S(1)} %bitcast.34), channel_id=1, source_target_pairs={{0,2},{1,3},{2,4},{3,5},{4,6},{5,7},{6,0},{7,1},{8,10},{9,11},{10,... | collective-permute-start | bytes 224 | tf_op jit(solution)/shard_map/ppermute | solution.py:214
  24.8 2.9 %collective-permute-start.1 = (s32[3,6]{1,0:T(4,128)S(1)}, s32[3,6]{1,0:T(4,128)S(1)}, u32[]{:S(2)}, u32[]{:S(2)}) collective-permute-start(s32[3,6]{1,0:T(4,128)S(1)} %bitcast.35), channel_id=1, source_target_pairs={{0,4},{1,5},{2,6},{3,7},{4,0},{5,1},{6,2},{7,3},{8,12},{9,13},{10,... | collective-permute-start | bytes 224 | tf_op jit(solution)/shard_map/ppermute | solution.py:214
  27.7 1.3 %collective-permute-start.2 = (s32[3,6]{1,0:T(4,128)S(1)}, s32[3,6]{1,0:T(4,128)S(1)}, u32[]{:S(2)}, u32[]{:S(2)}) collective-permute-start(s32[3,6]{1,0:T(4,128)S(1)} %bitcast.36), channel_id=1, source_target_pairs={{0,6},{1,7},{2,0},{3,1},{4,2},{5,3},{6,4},{7,5},{8,14},{9,15},{10,... | collective-permute-start | bytes 224 | tf_op jit(solution)/shard_map/ppermute | solution.py:214
  29.0 0.7 copy.6
  29.7 0.0 collective-permute-done
  29.7 0.3 collective-permute-done.1
  30.0 1.3 %collective-permute-done.2 = s32[3,6]{1,0:T(4,128)S(1)} collective-permute-done((s32[3,6]{1,0:T(4,128)S(1)}, s32[3,6]{1,0:T(4,128)S(1)}, u32[]{:S(2)}, u32[]{:S(2)}) %collective-permute-start.2) | collective-permute-done | bytes 104 | tf_op jit(solution)/shard_map/ppermute | solution.py:214
  31.3 0.0 copy-start
  31.3 0.6 copy-done
  31.9 0.0 collective-permute-start.3
  31.9 1.3 %collective-permute-done.3.there = s32[4,3,6]{2,1,0:T(4,128)} collective-permute-done((s32[4,3,6]{2,1,0:T(4,128)S(1)}, s32[4,3,6]{2,1,0:T(4,128)}, u32[]{:S(2)}, u32[]{:S(2)}) %collective-permute-start.3) | collective-permute-done | bytes 320 | tf_op jit(solution)/shard_map/ppermute | solution.py:214
  33.2 5.5 %all-to-all-done.known = bf16[32,32,256]{2,1,0:T(8,128)(2,1)} async-done(((bf16[32,32,256]{2,1,0:T(8,128)(2,1)}), bf16[32,32,256]{2,1,0:T(8,128)(2,1)}, u32[]{:S(2)}, u32[]{:S(2)}) %all-to-all-start) | async-done | bytes 524320 | tf_op jit(solution)/shard_map/all_to_all | solution.py:215
  38.7 2.0 %pick13.1 = (bf16[2,6,32,256]{3,2,1,0:T(8,128)(2,1)}, bf16[2,6,32,256]{3,2,1,0:T(8,128)(2,1)}, bf16[2,6,32,256]{3,2,1,0:T(8,128)(2,1)}, bf16[2,6,32,256]{3,2,1,0:T(8,128)(2,1)}) custom-call(s32[1]{0:T(128)} %bitcast.place, s32[4,3,6]{2,1,0:T(4,128)} %copy-done, s32[4,3,6]{2,1,0:T(4,128)} %collective-permute-done.3.there, bf16[32,32,256]{2,1,0:T(8,128)(2,1)} %all-to-all-done.known), custom_call_target="tpu_custom_call" | custom-call | bytes 2097152 | tf_op jit(solution)/shard_map/pick13/pallas_call | solution.py:47
  40.7 0.9 all-gather.7.cloned.1.call-done
  41.6 0.0 collective-permute-start.4
  41.6 0.8 collective-permute-start.5
  42.3 2.9 %collective-permute-start.6 = (bf16[2,6,32,256]{3,2,1,0:T(8,128)(2,1)}, bf16[2,6,32,256]{3,2,1,0:T(8,128)(2,1)}, u32[]{:S(2)}, u32[]{:S(2)}) collective-permute-start(bf16[2,6,32,256]{3,2,1,0:T(8,128)(2,1)} %get-tuple-element.72), channel_id=1, source_target_pairs={{0,4},{1,5},{2,6},{3,7},{4,0},{5,1},{6,2},{7,3},{8,12},{9,13},{10,... | collective-permute-start | bytes 589832 | tf_op jit(solution)/shard_map/ppermute | solution.py:214
  45.2 1.3 %collective-permute-start.7 = (bf16[2,6,32,256]{3,2,1,0:T(8,128)(2,1)}, bf16[2,6,32,256]{3,2,1,0:T(8,128)(2,1)}, u32[]{:S(2)}, u32[]{:S(2)}) collective-permute-start(bf16[2,6,32,256]{3,2,1,0:T(8,128)(2,1)} %get-tuple-element.73), channel_id=1, source_target_pairs={{0,6},{1,7},{2,0},{3,1},{4,2},{5,3},{6,4},{7,5},{8,14},{9,15},{10,... | collective-permute-start | bytes 589832 | tf_op jit(solution)/shard_map/ppermute | solution.py:214
  46.6 0.0 collective-permute-done.4.refs_1_
  46.6 4.7 %level1.1 = (f32[32,256]{1,0:T(8,128)}, bf16[32,32,256]{2,1,0:T(8,128)(2,1)}) custom-call(s32[1]{0:T(128)} %bitcast.place, s32[4,3,6]{2,1,0:T(4,128)} %copy-done, s32[4,3,6]{2,1,0:T(4,128)} %collective-permute-done.3.there, s32[1,6]{1,0:T(1,128)} %bitcast.27, bf16[4,256,256]{2,1,0:T(8,128)(2,1)} %rhs.7, bf16[4,256,256]{2,1,0:T(8,128)(2,1)} %dinv.7, ...), custom_call_target="tpu_custom_call" | custom-call | flops 100663296 | bytes 3145728 | tf_op jit(solution)/shard_map/level1/pallas_call | solution.py:47
  51.4 0.0 collective-permute-done.5.refs_1_
  51.4 3.6 %collective-permute-done.6.refs_2_ = bf16[2,6,32,256]{3,2,1,0:T(8,128)(2,1)} collective-permute-done((bf16[2,6,32,256]{3,2,1,0:T(8,128)(2,1)}, bf16[2,6,32,256]{3,2,1,0:T(8,128)(2,1)}, u32[]{:S(2)}, u32[]{:S(2)}) %collective-permute-start.6) | collective-permute-done | bytes 196640 | tf_op jit(solution)/shard_map/ppermute | solution.py:214
  55.0 0.3 collective-permute-done.7.refs_3_
  55.3 0.0 collective-permute-start.8
  55.3 10.2 %all-to-all-start.1 = ((bf16[32,32,256]{2,1,0:T(8,128)(2,1)}), bf16[32,32,256]{2,1,0:T(8,128)(2,1)}, u32[]{:S(2)}, u32[]{:S(2)}) async-start(bf16[32,32,256]{2,1,0:T(8,128)(2,1)} %get-tuple-element.74), calls=%async_computation.1 | async-start | bytes 1048576 | tf_op jit(solution)/shard_map/all_to_all | solution.py:215
  65.5 0.0 collective-permute-done.8.refs_5_.refs_7_.refs_9_
  65.5 3.0 %partial13.1 = (f32[32,256]{1,0:T(8,128)}, f32[32,256]{1,0:T(8,128)}, f32[32,256]{1,0:T(8,128)}, f32[32,256]{1,0:T(8,128)}, f32[32,256]{1,0:T(8,128)}, /*index=5...) custom-call(s32[1]{0:T(128)} %bitcast.place, s32[1,6]{1,0:T(1,128)} %bitcast.28, ...), custom_call_target="tpu_custom_call" | custom-call | flops 201326592 | bytes 2097152 | tf_op jit(solution)/shard_map/partial13/pallas_call | solution.py:47
  68.5 1.9 %collective-permute-start.10 = (f32[32,256]{1,0:T(8,128)}, f32[32,256]{1,0:T(8,128)}, u32[]{:S(2)}, u32[]{:S(2)}) collective-permute-start(f32[32,256]{1,0:T(8,128)} %get-tuple-element.82), channel_id=1, source_target_pairs={{0,4},{1,5},{2,6},{3,7},{4,0},{5,1},{6,2},{7,3},{8,12},{9,13},{10,... | collective-permute-start | bytes 98312 | tf_op jit(solution)/shard_map/ppermute | solution.py:214
  70.4 1.7 %collective-permute-start.11 = (f32[32,256]{1,0:T(8,128)}, f32[32,256]{1,0:T(8,128)}, u32[]{:S(2)}, u32[]{:S(2)}) collective-permute-start(f32[32,256]{1,0:T(8,128)} %get-tuple-element.83), channel_id=1, source_target_pairs={{0,2},{1,3},{2,4},{3,5},{4,6},{5,7},{6,0},{7,1},{8,10},{9,11},{10,... | collective-permute-start | bytes 98312 | tf_op jit(solution)/shard_map/ppermute | solution.py:214
  72.1 1.5 %collective-permute-start.9 = (f32[32,256]{1,0:T(8,128)}, f32[32,256]{1,0:T(8,128)}, u32[]{:S(2)}, u32[]{:S(2)}) collective-permute-start(f32[32,256]{1,0:T(8,128)} %get-tuple-element.81), channel_id=1, source_target_pairs={{0,6},{1,7},{2,0},{3,1},{4,2},{5,3},{6,4},{7,5},{8,14},{9,15},{10,... | collective-permute-start | bytes 98312 | tf_op jit(solution)/shard_map/ppermute | solution.py:214
  73.6 9.4 %all-to-all-done.1.known = bf16[32,32,256]{2,1,0:T(8,128)(2,1)} async-done(((bf16[32,32,256]{2,1,0:T(8,128)(2,1)}), bf16[32,32,256]{2,1,0:T(8,128)(2,1)}, u32[]{:S(2)}, u32[]{:S(2)}) %all-to-all-start.1) | async-done | bytes 524320 | tf_op jit(solution)/shard_map/all_to_all | solution.py:215
  83.0 0.0 collective-permute-done.10.refs_3_
  83.0 0.0 collective-permute-done.11.refs_4_
  83.0 0.0 collective-permute-done.9.refs_2_
  83.0 1.8 %pick4.1 = (bf16[1,6,32,256]{3,2,1,0:T(8,128)(2,1)}, bf16[1,6,32,256]{3,2,1,0:T(8,128)(2,1)}, bf16[1,6,32,256]{3,2,1,0:T(8,128)(2,1)}, bf16[1,6,32,256]{3,2,1,0:T(8,128)(2,1)}) custom-call(s32[1]{0:T(128)} %bitcast.place, s32[4,3,6]{2,1,0:T(4,128)} %copy-done, s32[4,3,6]{2,1,0:T(4,128)} %collective-permute-done.3.there, ...), custom_call_target="tpu_custom_call" | custom-call | bytes 2097152 | tf_op jit(solution)/shard_map/pick4/pallas_call | solution.py:47
  84.9 1.1 collective-permute-start.12
  86.0 2.9 %collective-permute-start.13 = (bf16[1,6,32,256]{3,2,1,0:T(8,128)(2,1)}, bf16[1,6,32,256]{3,2,1,0:T(8,128)(2,1)}, u32[]{:S(2)}, u32[]{:S(2)}) collective-permute-start(bf16[1,6,32,256]{3,2,1,0:T(8,128)(2,1)} %get-tuple-element.98), channel_id=1, source_target_pairs={{0,4},{1,5},{2,6},{3,7},{4,0},{5,1},{6,2},{7,3},{8,12},{9,13},{10,... | collective-permute-start | bytes 294920 | tf_op jit(solution)/shard_map/ppermute | solution.py:214
  88.9 0.3 collective-permute-start.14
  89.3 0.0 all-gather.9.cloned.1.call-done
  89.3 4.8 %level2.1 = (f32[32,256]{1,0:T(8,128)}, bf16[32,32,256]{2,1,0:T(8,128)(2,1)}) custom-call(s32[1]{0:T(128)} %bitcast.place, s32[4,3,6]{2,1,0:T(4,128)} %copy-done, s32[4,3,6]{2,1,0:T(4,128)} %collective-permute-done.3.there, s32[1,6]{1,0:T(1,128)} %bitcast.29, bf16[4,256,256]{2,1,0:T(8,128)(2,1)} %rhs.7, bf16[4,256,256]{2,1,0:T(8,128)(2,1)} %dinv.7, ...), custom_call_target="tpu_custom_call" | custom-call | flops 100663296 | bytes 3145728 | tf_op jit(solution)/shard_map/level2/pallas_call | solution.py:47
  94.1 0.0 collective-permute-done.12.refs_1_
  94.1 0.7 collective-permute-done.13.refs_2_
  94.8 2.9 %collective-permute-done.14.refs_3_ = bf16[1,6,32,256]{3,2,1,0:T(8,128)(2,1)} collective-permute-done((bf16[1,6,32,256]{3,2,1,0:T(8,128)(2,1)}, bf16[1,6,32,256]{3,2,1,0:T(8,128)(2,1)}, u32[]{:S(2)}, u32[]{:S(2)}) %collective-permute-start.14) | collective-permute-done | bytes 98336 | tf_op jit(solution)/shard_map/ppermute | solution.py:214
  97.7 5.0 %all-to-all-start.2 = ((bf16[32,32,256]{2,1,0:T(8,128)(2,1)}), bf16[32,32,256]{2,1,0:T(8,128)(2,1)}, u32[]{:S(2)}, u32[]{:S(2)}) async-start(bf16[32,32,256]{2,1,0:T(8,128)(2,1)} %get-tuple-element.100), calls=%async_computation.2 | async-start | bytes 1048576 | tf_op jit(solution)/shard_map/all_to_all | solution.py:215
  102.7 2.5 %partial4.1 = (f32[32,256]{1,0:T(8,128)}, f32[32,256]{1,0:T(8,128)}, f32[32,256]{1,0:T(8,128)}, f32[32,256]{1,0:T(8,128)}) custom-call(s32[1]{0:T(128)} %bitcast.place, s32[1,6]{1,0:T(1,128)} %bitcast.30, bf16[1,6,32,256]{3,2,1,0:T(8,128)(2,1)} %get-tuple-element.102.refs_0_, bf16[1,6,32,256]{3,2,1,0:T(8,128)(2,1)} %collective-permute-done.12.refs_1_, ...), custom_call_target="tpu_custom_call" | custom-call | flops 201326592 | bytes 2097152 | tf_op jit(solution)/shard_map/partial4/pallas_call | solution.py:47
  105.2 1.1 collective-permute-start.15
  106.2 0.6 collective-permute-start.16
  106.8 0.6 collective-permute-start.17
  107.4 0.9 all-gather.11.cloned.1.call-done
  108.3 1.1 collective-permute-done.15.refs_2_
  109.4 2.6 %collective-permute-done.16.refs_3_ = f32[32,256]{1,0:T(8,128)} collective-permute-done((f32[32,256]{1,0:T(8,128)}, f32[32,256]{1,0:T(8,128)}, u32[]{:S(2)}, u32[]{:S(2)}) %collective-permute-start.16) | collective-permute-done | bytes 32800 | tf_op jit(solution)/shard_map/ppermute | solution.py:214
  112.0 0.3 collective-permute-done.17.refs_4_
  112.3 3.7 %all-to-all-done.2.known = bf16[32,32,256]{2,1,0:T(8,128)(2,1)} async-done(((bf16[32,32,256]{2,1,0:T(8,128)(2,1)}), bf16[32,32,256]{2,1,0:T(8,128)(2,1)}, u32[]{:S(2)}, u32[]{:S(2)}) %all-to-all-start.2) | async-done | bytes 524320 | tf_op jit(solution)/shard_map/all_to_all | solution.py:215
  116.0 4.6 %level3.1 = f32[4,32,256]{2,1,0:T(8,128)} custom-call(s32[1]{0:T(128)} %bitcast.place, s32[4,3,6]{2,1,0:T(4,128)} %copy-done, s32[4,3,6]{2,1,0:T(4,128)} %collective-permute-done.3.there, s32[1,6]{1,0:T(1,128)} %bitcast.31, bf16[4,256,256]{2,1,0:T(8,128)(2,1)} %rhs.7, bf16[4,256,256]{2,1,0:T(8,128)(2,1)} %dinv.7, bf16[32,32,256]{2,1,0:T(8,128)(2,1)} %all-to-all-done.2.known, ...), custom_call_target="tpu_custom_call" | custom-call | flops 100663296 | bytes 3145728 | tf_op jit(solution)/shard_map/level3/pallas_call | solution.py:47
  (1 shorter events, 0.0 us)
Async XLA Ops:
  6.5 35.0 %all-gather.7.cloned.1.call-start = ((), (), s32[]{:S(2)}) async-start(), calls=%async_computation.3 | async-start | bytes 1966080 | tf_op jit(solution)/shard_map/all_gather | solution.py:217
  9.3 79.9 %all-gather.9.cloned.1.call-start = ((), (), s32[]{:S(2)}) async-start(), calls=%async_computation.4 | async-start | bytes 3538944 | tf_op jit(solution)/shard_map/all_gather | solution.py:217
  10.1 28.6 %all-to-all-start = ((bf16[32,32,256]{2,1,0:T(8,128)(2,1)}), bf16[32,32,256]{2,1,0:T(8,128)(2,1)}, u32[]{:S(2)}, u32[]{:S(2)}) async-start(bf16[32,32,256]{2,1,0:T(8,128)(2,1)} %get-tuple-element.61), calls=%async_computation | async-start | bytes 1048576 | tf_op jit(solution)/shard_map/all_to_all | solution.py:215
  21.8 86.5 %all-gather.11.cloned.1.call-start = ((), (), s32[]{:S(2)}) async-start(), calls=%async_computation.5 | async-start | bytes 3538944 | tf_op jit(solution)/shard_map/all_gather | solution.py:217
  23.2 6.5 %collective-permute-start = (s32[3,6]{1,0:T(4,128)S(1)}, s32[3,6]{1,0:T(4,128)S(1)}, u32[]{:S(2)}, u32[]{:S(2)}) collective-permute-start(s32[3,6]{1,0:T(4,128)S(1)} %bitcast.34), channel_id=1, source_target_pairs={{0,2},{1,3},{2,4},{3,5},{4,6},{5,7},{6,0},{7,1},{8,10},{9,11},{10,... | collective-permute-start | bytes 224 | tf_op jit(solution)/shard_map/ppermute | solution.py:214
  24.8 5.2 %collective-permute-start.1 = (s32[3,6]{1,0:T(4,128)S(1)}, s32[3,6]{1,0:T(4,128)S(1)}, u32[]{:S(2)}, u32[]{:S(2)}) collective-permute-start(s32[3,6]{1,0:T(4,128)S(1)} %bitcast.35), channel_id=1, source_target_pairs={{0,4},{1,5},{2,6},{3,7},{4,0},{5,1},{6,2},{7,3},{8,12},{9,13},{10,... | collective-permute-start | bytes 224 | tf_op jit(solution)/shard_map/ppermute | solution.py:214
  27.7 3.6 %collective-permute-start.2 = (s32[3,6]{1,0:T(4,128)S(1)}, s32[3,6]{1,0:T(4,128)S(1)}, u32[]{:S(2)}, u32[]{:S(2)}) collective-permute-start(s32[3,6]{1,0:T(4,128)S(1)} %bitcast.36), channel_id=1, source_target_pairs={{0,6},{1,7},{2,0},{3,1},{4,2},{5,3},{6,4},{7,5},{8,14},{9,15},{10,... | collective-permute-start | bytes 224 | tf_op jit(solution)/shard_map/ppermute | solution.py:214
  31.3 0.6 copy-start
  31.9 1.3 %collective-permute-start.3 = (s32[4,3,6]{2,1,0:T(4,128)S(1)}, s32[4,3,6]{2,1,0:T(4,128)}, u32[]{:S(2)}, u32[]{:S(2)}) collective-permute-start(s32[4,3,6]{2,1,0:T(4,128)S(1)} %pad_add_fusion.here), channel_id=1, source_target_pairs={{0,1},{1,0},{2,3},{3,2},{4,5},{5,4},{6,7},{7,6},{8,9},{9,8},{10,11... | collective-permute-start | bytes 872 | tf_op jit(solution)/shard_map/ppermute | solution.py:214
  41.6 5.0 %collective-permute-start.4 = (bf16[4,768,256]{2,1,0:T(8,128)(2,1)}, bf16[4,768,256]{2,1,0:T(8,128)(2,1)}, u32[]{:S(2)}, u32[]{:S(2)}) collective-permute-start(bf16[4,768,256]{2,1,0:T(8,128)(2,1)} %bitcast.25), channel_id=1, source_target_pairs={{0,1},{1,0},{2,3},{3,2},{4,5},{5,4},{6,7},{7,6},{8,9},{9,8},{10,11... | collective-permute-start | bytes 4718600 | tf_op jit(solution)/shard_map/ppermute | solution.py:214
  41.6 9.8 %collective-permute-start.5 = (bf16[2,6,32,256]{3,2,1,0:T(8,128)(2,1)}, bf16[2,6,32,256]{3,2,1,0:T(8,128)(2,1)}, u32[]{:S(2)}, u32[]{:S(2)}) collective-permute-start(bf16[2,6,32,256]{3,2,1,0:T(8,128)(2,1)} %get-tuple-element.71), channel_id=1, source_target_pairs={{0,2},{1,3},{2,4},{3,5},{4,6},{5,7},{6,0},{7,1},{8,10},{9,11},{10,... | collective-permute-start | bytes 589832 | tf_op jit(solution)/shard_map/ppermute | solution.py:214
  42.3 12.6 %collective-permute-start.6 = (bf16[2,6,32,256]{3,2,1,0:T(8,128)(2,1)}, bf16[2,6,32,256]{3,2,1,0:T(8,128)(2,1)}, u32[]{:S(2)}, u32[]{:S(2)}) collective-permute-start(bf16[2,6,32,256]{3,2,1,0:T(8,128)(2,1)} %get-tuple-element.72), channel_id=1, source_target_pairs={{0,4},{1,5},{2,6},{3,7},{4,0},{5,1},{6,2},{7,3},{8,12},{9,13},{10,... | collective-permute-start | bytes 589832 | tf_op jit(solution)/shard_map/ppermute | solution.py:214
  45.2 10.0 %collective-permute-start.7 = (bf16[2,6,32,256]{3,2,1,0:T(8,128)(2,1)}, bf16[2,6,32,256]{3,2,1,0:T(8,128)(2,1)}, u32[]{:S(2)}, u32[]{:S(2)}) collective-permute-start(bf16[2,6,32,256]{3,2,1,0:T(8,128)(2,1)} %get-tuple-element.73), channel_id=1, source_target_pairs={{0,6},{1,7},{2,0},{3,1},{4,2},{5,3},{6,4},{7,5},{8,14},{9,15},{10,... | collective-permute-start | bytes 589832 | tf_op jit(solution)/shard_map/ppermute | solution.py:214
  55.3 10.2 %collective-permute-start.8 = (bf16[6,3,256,256]{3,2,1,0:T(8,128)(2,1)}, bf16[6,3,256,256]{3,2,1,0:T(8,128)(2,1)}, u32[]{:S(2)}, u32[]{:S(2)}) collective-permute-start(bf16[6,3,256,256]{3,2,1,0:T(8,128)(2,1)} %bitcast.19), channel_id=1, source_target_pairs={{0,1},{1,0},{2,3},{3,2},{4,5},{5,4},{6,7},{7,6},{8,9},{9,8},{10,11... | collective-permute-start | bytes 7077896 | tf_op jit(solution)/shard_map/ppermute | solution.py:214
  55.3 27.8 %all-to-all-start.1 = ((bf16[32,32,256]{2,1,0:T(8,128)(2,1)}), bf16[32,32,256]{2,1,0:T(8,128)(2,1)}, u32[]{:S(2)}, u32[]{:S(2)}) async-start(bf16[32,32,256]{2,1,0:T(8,128)(2,1)} %get-tuple-element.74), calls=%async_computation.1 | async-start | bytes 1048576 | tf_op jit(solution)/shard_map/all_to_all | solution.py:215
  68.5 14.5 %collective-permute-start.10 = (f32[32,256]{1,0:T(8,128)}, f32[32,256]{1,0:T(8,128)}, u32[]{:S(2)}, u32[]{:S(2)}) collective-permute-start(f32[32,256]{1,0:T(8,128)} %get-tuple-element.82), channel_id=1, source_target_pairs={{0,4},{1,5},{2,6},{3,7},{4,0},{5,1},{6,2},{7,3},{8,12},{9,13},{10,... | collective-permute-start | bytes 98312 | tf_op jit(solution)/shard_map/ppermute | solution.py:214
  70.4 12.6 %collective-permute-start.11 = (f32[32,256]{1,0:T(8,128)}, f32[32,256]{1,0:T(8,128)}, u32[]{:S(2)}, u32[]{:S(2)}) collective-permute-start(f32[32,256]{1,0:T(8,128)} %get-tuple-element.83), channel_id=1, source_target_pairs={{0,2},{1,3},{2,4},{3,5},{4,6},{5,7},{6,0},{7,1},{8,10},{9,11},{10,... | collective-permute-start | bytes 98312 | tf_op jit(solution)/shard_map/ppermute | solution.py:214
  72.1 10.9 %collective-permute-start.9 = (f32[32,256]{1,0:T(8,128)}, f32[32,256]{1,0:T(8,128)}, u32[]{:S(2)}, u32[]{:S(2)}) collective-permute-start(f32[32,256]{1,0:T(8,128)} %get-tuple-element.81), channel_id=1, source_target_pairs={{0,6},{1,7},{2,0},{3,1},{4,2},{5,3},{6,4},{7,5},{8,14},{9,15},{10,... | collective-permute-start | bytes 98312 | tf_op jit(solution)/shard_map/ppermute | solution.py:214
  84.9 9.2 %collective-permute-start.12 = (bf16[1,6,32,256]{3,2,1,0:T(8,128)(2,1)}, bf16[1,6,32,256]{3,2,1,0:T(8,128)(2,1)}, u32[]{:S(2)}, u32[]{:S(2)}) collective-permute-start(bf16[1,6,32,256]{3,2,1,0:T(8,128)(2,1)} %get-tuple-element.97), channel_id=1, source_target_pairs={{0,2},{1,3},{2,4},{3,5},{4,6},{5,7},{6,0},{7,1},{8,10},{9,11},{10,... | collective-permute-start | bytes 294920 | tf_op jit(solution)/shard_map/ppermute | solution.py:214
  86.0 8.8 %collective-permute-start.13 = (bf16[1,6,32,256]{3,2,1,0:T(8,128)(2,1)}, bf16[1,6,32,256]{3,2,1,0:T(8,128)(2,1)}, u32[]{:S(2)}, u32[]{:S(2)}) collective-permute-start(bf16[1,6,32,256]{3,2,1,0:T(8,128)(2,1)} %get-tuple-element.98), channel_id=1, source_target_pairs={{0,4},{1,5},{2,6},{3,7},{4,0},{5,1},{6,2},{7,3},{8,12},{9,13},{10,... | collective-permute-start | bytes 294920 | tf_op jit(solution)/shard_map/ppermute | solution.py:214
  88.9 8.8 %collective-permute-start.14 = (bf16[1,6,32,256]{3,2,1,0:T(8,128)(2,1)}, bf16[1,6,32,256]{3,2,1,0:T(8,128)(2,1)}, u32[]{:S(2)}, u32[]{:S(2)}) collective-permute-start(bf16[1,6,32,256]{3,2,1,0:T(8,128)(2,1)} %get-tuple-element.99), channel_id=1, source_target_pairs={{0,6},{1,7},{2,0},{3,1},{4,2},{5,3},{6,4},{7,5},{8,14},{9,15},{10,... | collective-permute-start | bytes 294920 | tf_op jit(solution)/shard_map/ppermute | solution.py:214
  97.7 18.3 %all-to-all-start.2 = ((bf16[32,32,256]{2,1,0:T(8,128)(2,1)}), bf16[32,32,256]{2,1,0:T(8,128)(2,1)}, u32[]{:S(2)}, u32[]{:S(2)}) async-start(bf16[32,32,256]{2,1,0:T(8,128)(2,1)} %get-tuple-element.100), calls=%async_computation.2 | async-start | bytes 1048576 | tf_op jit(solution)/shard_map/all_to_all | solution.py:215
  105.2 4.2 %collective-permute-start.15 = (f32[32,256]{1,0:T(8,128)}, f32[32,256]{1,0:T(8,128)}, u32[]{:S(2)}, u32[]{:S(2)}) collective-permute-start(f32[32,256]{1,0:T(8,128)} %get-tuple-element.111), channel_id=1, source_target_pairs={{0,6},{1,7},{2,0},{3,1},{4,2},{5,3},{6,4},{7,5},{8,14},{9,15},{10,... | collective-permute-start | bytes 98312 | tf_op jit(solution)/shard_map/ppermute | solution.py:214
  106.2 5.7 %collective-permute-start.16 = (f32[32,256]{1,0:T(8,128)}, f32[32,256]{1,0:T(8,128)}, u32[]{:S(2)}, u32[]{:S(2)}) collective-permute-start(f32[32,256]{1,0:T(8,128)} %get-tuple-element.112), channel_id=1, source_target_pairs={{0,4},{1,5},{2,6},{3,7},{4,0},{5,1},{6,2},{7,3},{8,12},{9,13},{10,... | collective-permute-start | bytes 98312 | tf_op jit(solution)/shard_map/ppermute | solution.py:214
  106.8 5.5 %collective-permute-start.17 = (f32[32,256]{1,0:T(8,128)}, f32[32,256]{1,0:T(8,128)}, u32[]{:S(2)}, u32[]{:S(2)}) collective-permute-start(f32[32,256]{1,0:T(8,128)} %get-tuple-element.113), channel_id=1, source_target_pairs={{0,2},{1,3},{2,4},{3,5},{4,6},{5,7},{6,0},{7,1},{8,10},{9,11},{10,... | collective-permute-start | bytes 98312 | tf_op jit(solution)/shard_map/ppermute | solution.py:214
Sparse Core Ops, SparseCore 0:
  9.5 32.0 all-gather.6
  43.4 30.3 all-gather.8
  75.7 32.5 all-gather.10

commit v12 on v11

--- a/solution.py
+++ b/solution.py
@@ -229,6 +229,8 @@
     def give_back(sums):
         return [sums[0]] + [move(sums[d], TURN[CHIPS - d]) for d in range(1, CHIPS)]
 
+    later, spread0 = lax.optimization_barrier((tiles, spread0))
+    swapped = move(later, SWAP)
     known0 = over_row(spread0)
     picked = pick_call("pick13", (1, 3), place, here, there, known0)
     known0, *picked = lax.optimization_barrier((known0, *picked))
@@ -236,8 +238,7 @@
     gathered0, _ = lax.optimization_barrier((gathered0, picked[0]))
     gathered0 = [gathered0, move(gathered0, SWAP)]
     answer1, spread1 = level_call(1, 0, place, here, there, live, rhs, dinv, known0, gathered0, [], [])
-    later, spread1, *got = lax.optimization_barrier((tiles, spread1, *got))
-    swapped = move(later, SWAP)
+    spread1, *got = lax.optimization_barrier((spread1, *got))
     known1 = over_row(spread1)
 
     sums = partial_call("partial13", (1, 3), place, live, got, [], tiles, swapped)

time: 128 us -> 127 us (level)
  waiting for transfers between devices: 36.1 us -> 32 us
  starting transfers between devices: 49.5 us -> 52 us
    all_to_all x3, waiting for transfers between devices: 18.5 us -> 14.9 us  [local(): over_row = lambda array: lax.all_to_all(array, 'row', 0, 0, tiled=True)]
    ppermute x18, starting transfers between devices: 22.6 us -> 25.1 us  [local(): move = lambda array, pairs: lax.ppermute(array, COL, pairs)]
where the time goes in v12:
time: 127 us; the launch traced here: 126 us
  starting transfers between devices  52 us (41%)
  waiting for transfers between devices  32 us (25%)
  Pallas kernels  26.4 us (21%)
  between operations  13.2 us (10%)
  local copies, waits for them, and re-layouts  1.96 us (2%)
    all_to_all x3, starting transfers between devices, local(): over_row = lambda array: lax.all_to_all(array, 'row', 0, 0, tiled=True)  26.9 us
    pallas_call x8, Pallas kernels, call(): pl.pallas_call(kernel, grid=(1,), out_shape=tuple((jax.ShapeDtypeStruct(s...  26.4 us
    ppermute x18, starting transfers between devices, local(): move = lambda array, pairs: lax.ppermute(array, COL, pairs)  25.1 us
    all_to_all x3, waiting for transfers between devices, local(): over_row = lambda array: lax.all_to_all(array, 'row', 0, 0, tiled=True)  14.9 us
    ppermute x18, waiting for transfers between devices, local(): move = lambda array, pairs: lax.ppermute(array, COL, pairs)  14.1 us
  transfers between devices with their start and end apart: 24, of which 15 were waited for; matrix products, arithmetic and copies ran while one was open for 1% of the time, Pallas kernels for 15%

profile of v12, /device:TPU:2, one launch (start us, length us, event | category | flops | bytes accessed | tf_op | source)
XLA Modules:
  0.0 125.5 jit_solution(14589221534181084421)
XLA Ops:
  6.5 0.0 all-gather.7.cloned.1.call-start
  6.5 2.7 %level0.1 = (f32[32,256]{1,0:T(8,128)}, bf16[32,32,256]{2,1,0:T(8,128)(2,1)}, bf16[768,256]{1,0:T(8,128)(2,1)}, bf16[768,256]{1,0:T(8,128)(2,1)}, bf16[768,256]{1,0:T(8,128)(2,1)}) custom-call(s32[1]{0:T(128)} %bitcast.place, bf16[4,256,256]{2,1,0:T(8,128)(2,1)} %rhs.7, bf16[4,256,256]{2,1,0:T(8,128)(2,1)} %dinv.7, bf16[6,3,256,256]{3,2,1,0:T(8,128)(2,1)} %bitcast.16, ...), custom_call_target="tpu_custom_call" | custom-call | bytes 4194304 | tf_op jit(solution)/shard_map/level0/pallas_call | solution.py:47
  9.3 0.0 all-gather.7.cloned.1.call-update
  9.3 0.0 all-gather.9.cloned.1.call-start
  9.4 0.7 all-gather.9.cloned.1.call-update
  10.1 0.0 all-gather.11.cloned.1.call-start
  10.1 0.7 all-gather.11.cloned.1.call-update
  10.8 11.7 %all-to-all-start = ((bf16[32,32,256]{2,1,0:T(8,128)(2,1)}), bf16[32,32,256]{2,1,0:T(8,128)(2,1)}, u32[]{:S(2)}, u32[]{:S(2)}) async-start(bf16[32,32,256]{2,1,0:T(8,128)(2,1)} %get-tuple-element.63), calls=%async_computation | async-start | bytes 1048576 | tf_op jit(solution)/shard_map/all_to_all | solution.py:215
  22.5 0.7 copy.9
  23.2 1.6 %collective-permute-start = (s32[3,6]{1,0:T(4,128)S(1)}, s32[3,6]{1,0:T(4,128)S(1)}, u32[]{:S(2)}, u32[]{:S(2)}) collective-permute-start(s32[3,6]{1,0:T(4,128)S(1)} %bitcast.34), channel_id=1, source_target_pairs={{0,2},{1,3},{2,4},{3,5},{4,6},{5,7},{6,0},{7,1},{8,10},{9,11},{10,... | collective-permute-start | bytes 224 | tf_op jit(solution)/shard_map/ppermute | solution.py:214
  24.7 2.9 %collective-permute-start.1 = (s32[3,6]{1,0:T(4,128)S(1)}, s32[3,6]{1,0:T(4,128)S(1)}, u32[]{:S(2)}, u32[]{:S(2)}) collective-permute-start(s32[3,6]{1,0:T(4,128)S(1)} %bitcast.35), channel_id=1, source_target_pairs={{0,4},{1,5},{2,6},{3,7},{4,0},{5,1},{6,2},{7,3},{8,12},{9,13},{10,... | collective-permute-start | bytes 224 | tf_op jit(solution)/shard_map/ppermute | solution.py:214
  27.6 1.3 %collective-permute-start.2 = (s32[3,6]{1,0:T(4,128)S(1)}, s32[3,6]{1,0:T(4,128)S(1)}, u32[]{:S(2)}, u32[]{:S(2)}) collective-permute-start(s32[3,6]{1,0:T(4,128)S(1)} %bitcast.36), channel_id=1, source_target_pairs={{0,6},{1,7},{2,0},{3,1},{4,2},{5,3},{6,4},{7,5},{8,14},{9,15},{10,... | collective-permute-start | bytes 224 | tf_op jit(solution)/shard_map/ppermute | solution.py:214
  29.0 0.7 copy.6
  29.7 0.0 collective-permute-done
  29.7 0.3 collective-permute-done.1
  29.9 1.3 %collective-permute-done.2 = s32[3,6]{1,0:T(4,128)S(1)} collective-permute-done((s32[3,6]{1,0:T(4,128)S(1)}, s32[3,6]{1,0:T(4,128)S(1)}, u32[]{:S(2)}, u32[]{:S(2)}) %collective-permute-start.2) | collective-permute-done | bytes 104 | tf_op jit(solution)/shard_map/ppermute | solution.py:214
  31.3 0.0 copy-start
  31.3 0.6 copy-done
  31.8 0.0 collective-permute-start.3
  31.8 1.3 %collective-permute-done.3.there = s32[4,3,6]{2,1,0:T(4,128)} collective-permute-done((s32[4,3,6]{2,1,0:T(4,128)S(1)}, s32[4,3,6]{2,1,0:T(4,128)}, u32[]{:S(2)}, u32[]{:S(2)}) %collective-permute-start.3) | collective-permute-done | bytes 320 | tf_op jit(solution)/shard_map/ppermute | solution.py:214
  33.2 6.2 %all-to-all-done.known = bf16[32,32,256]{2,1,0:T(8,128)(2,1)} async-done(((bf16[32,32,256]{2,1,0:T(8,128)(2,1)}), bf16[32,32,256]{2,1,0:T(8,128)(2,1)}, u32[]{:S(2)}, u32[]{:S(2)}) %all-to-all-start) | async-done | bytes 524320 | tf_op jit(solution)/shard_map/all_to_all | solution.py:215
  39.4 2.0 %pick13.1 = (bf16[2,6,32,256]{3,2,1,0:T(8,128)(2,1)}, bf16[2,6,32,256]{3,2,1,0:T(8,128)(2,1)}, bf16[2,6,32,256]{3,2,1,0:T(8,128)(2,1)}, bf16[2,6,32,256]{3,2,1,0:T(8,128)(2,1)}) custom-call(s32[1]{0:T(128)} %bitcast.place, s32[4,3,6]{2,1,0:T(4,128)} %copy-done, s32[4,3,6]{2,1,0:T(4,128)} %collective-permute-done.3.there, bf16[32,32,256]{2,1,0:T(8,128)(2,1)} %all-to-all-done.known), custom_call_target="tpu_custom_call" | custom-call | bytes 2097152 | tf_op jit(solution)/shard_map/pick13/pallas_call | solution.py:47
  41.4 0.2 all-gather.7.cloned.1.call-done
  41.5 0.0 collective-permute-start.4
  41.5 0.5 collective-permute-start.8
  42.0 1.4 %collective-permute-start.5 = (bf16[2,6,32,256]{3,2,1,0:T(8,128)(2,1)}, bf16[2,6,32,256]{3,2,1,0:T(8,128)(2,1)}, u32[]{:S(2)}, u32[]{:S(2)}) collective-permute-start(bf16[2,6,32,256]{3,2,1,0:T(8,128)(2,1)} %get-tuple-element.73), channel_id=1, source_target_pairs={{0,2},{1,3},{2,4},{3,5},{4,6},{5,7},{6,0},{7,1},{8,10},{9,11},{10,... | collective-permute-start | bytes 589832 | tf_op jit(solution)/shard_map/ppermute | solution.py:214
  43.5 2.9 %collective-permute-start.6 = (bf16[2,6,32,256]{3,2,1,0:T(8,128)(2,1)}, bf16[2,6,32,256]{3,2,1,0:T(8,128)(2,1)}, u32[]{:S(2)}, u32[]{:S(2)}) collective-permute-start(bf16[2,6,32,256]{3,2,1,0:T(8,128)(2,1)} %get-tuple-element.74), channel_id=1, source_target_pairs={{0,4},{1,5},{2,6},{3,7},{4,0},{5,1},{6,2},{7,3},{8,12},{9,13},{10,... | collective-permute-start | bytes 589832 | tf_op jit(solution)/shard_map/ppermute | solution.py:214
  46.4 1.3 %collective-permute-start.7 = (bf16[2,6,32,256]{3,2,1,0:T(8,128)(2,1)}, bf16[2,6,32,256]{3,2,1,0:T(8,128)(2,1)}, u32[]{:S(2)}, u32[]{:S(2)}) collective-permute-start(bf16[2,6,32,256]{3,2,1,0:T(8,128)(2,1)} %get-tuple-element.75), channel_id=1, source_target_pairs={{0,6},{1,7},{2,0},{3,1},{4,2},{5,3},{6,4},{7,5},{8,14},{9,15},{10,... | collective-permute-start | bytes 589832 | tf_op jit(solution)/shard_map/ppermute | solution.py:214
  47.7 0.0 collective-permute-done.4.refs_1_
  47.7 4.7 %level1.1 = (f32[32,256]{1,0:T(8,128)}, bf16[32,32,256]{2,1,0:T(8,128)(2,1)}) custom-call(s32[1]{0:T(128)} %bitcast.place, s32[4,3,6]{2,1,0:T(4,128)} %copy-done, s32[4,3,6]{2,1,0:T(4,128)} %collective-permute-done.3.there, s32[1,6]{1,0:T(1,128)} %bitcast.27, bf16[4,256,256]{2,1,0:T(8,128)(2,1)} %rhs.7, bf16[4,256,256]{2,1,0:T(8,128)(2,1)} %dinv.7, ...), custom_call_target="tpu_custom_call" | custom-call | flops 100663296 | bytes 3145728 | tf_op jit(solution)/shard_map/level1/pallas_call | solution.py:47
  52.5 0.0 collective-permute-done.5.refs_1_
  52.5 3.3 %collective-permute-done.6.refs_2_ = bf16[2,6,32,256]{3,2,1,0:T(8,128)(2,1)} collective-permute-done((bf16[2,6,32,256]{3,2,1,0:T(8,128)(2,1)}, bf16[2,6,32,256]{3,2,1,0:T(8,128)(2,1)}, u32[]{:S(2)}, u32[]{:S(2)}) %collective-permute-start.6) | collective-permute-done | bytes 196640 | tf_op jit(solution)/shard_map/ppermute | solution.py:214
  55.8 0.0 collective-permute-done.7.refs_3_
  55.8 9.7 %all-to-all-start.1 = ((bf16[32,32,256]{2,1,0:T(8,128)(2,1)}), bf16[32,32,256]{2,1,0:T(8,128)(2,1)}, u32[]{:S(2)}, u32[]{:S(2)}) async-start(bf16[32,32,256]{2,1,0:T(8,128)(2,1)} %get-tuple-element.76), calls=%async_computation.1 | async-start | bytes 1048576 | tf_op jit(solution)/shard_map/all_to_all | solution.py:215
  65.4 0.0 collective-permute-done.8.refs_5_.refs_7_.refs_9_
  65.4 3.0 %partial13.1 = (f32[32,256]{1,0:T(8,128)}, f32[32,256]{1,0:T(8,128)}, f32[32,256]{1,0:T(8,128)}, f32[32,256]{1,0:T(8,128)}, f32[32,256]{1,0:T(8,128)}, /*index=5...) custom-call(s32[1]{0:T(128)} %bitcast.place, s32[1,6]{1,0:T(1,128)} %bitcast.28, ...), custom_call_target="tpu_custom_call" | custom-call | flops 201326592 | bytes 2097152 | tf_op jit(solution)/shard_map/partial13/pallas_call | solution.py:47
  68.5 1.9 %collective-permute-start.10 = (f32[32,256]{1,0:T(8,128)}, f32[32,256]{1,0:T(8,128)}, u32[]{:S(2)}, u32[]{:S(2)}) collective-permute-start(f32[32,256]{1,0:T(8,128)} %get-tuple-element.84), channel_id=1, source_target_pairs={{0,4},{1,5},{2,6},{3,7},{4,0},{5,1},{6,2},{7,3},{8,12},{9,13},{10,... | collective-permute-start | bytes 98312 | tf_op jit(solution)/shard_map/ppermute | solution.py:214
  70.3 1.7 %collective-permute-start.11 = (f32[32,256]{1,0:T(8,128)}, f32[32,256]{1,0:T(8,128)}, u32[]{:S(2)}, u32[]{:S(2)}) collective-permute-start(f32[32,256]{1,0:T(8,128)} %get-tuple-element.85), channel_id=1, source_target_pairs={{0,2},{1,3},{2,4},{3,5},{4,6},{5,7},{6,0},{7,1},{8,10},{9,11},{10,... | collective-permute-start | bytes 98312 | tf_op jit(solution)/shard_map/ppermute | solution.py:214
  72.0 1.5 %collective-permute-start.9 = (f32[32,256]{1,0:T(8,128)}, f32[32,256]{1,0:T(8,128)}, u32[]{:S(2)}, u32[]{:S(2)}) collective-permute-start(f32[32,256]{1,0:T(8,128)} %get-tuple-element.83), channel_id=1, source_target_pairs={{0,6},{1,7},{2,0},{3,1},{4,2},{5,3},{6,4},{7,5},{8,14},{9,15},{10,... | collective-permute-start | bytes 98312 | tf_op jit(solution)/shard_map/ppermute | solution.py:214
  73.6 1.0 collective-permute-done.10.refs_3_
  74.6 1.2 collective-permute-done.11.refs_4_
  75.8 0.5 collective-permute-done.9.refs_2_
  76.3 5.2 %all-to-all-done.1.known = bf16[32,32,256]{2,1,0:T(8,128)(2,1)} async-done(((bf16[32,32,256]{2,1,0:T(8,128)(2,1)}), bf16[32,32,256]{2,1,0:T(8,128)(2,1)}, u32[]{:S(2)}, u32[]{:S(2)}) %all-to-all-start.1) | async-done | bytes 524320 | tf_op jit(solution)/shard_map/all_to_all | solution.py:215
  81.4 1.8 %pick4.1 = (bf16[1,6,32,256]{3,2,1,0:T(8,128)(2,1)}, bf16[1,6,32,256]{3,2,1,0:T(8,128)(2,1)}, bf16[1,6,32,256]{3,2,1,0:T(8,128)(2,1)}, bf16[1,6,32,256]{3,2,1,0:T(8,128)(2,1)}) custom-call(s32[1]{0:T(128)} %bitcast.place, s32[4,3,6]{2,1,0:T(4,128)} %copy-done, s32[4,3,6]{2,1,0:T(4,128)} %collective-permute-done.3.there, ...), custom_call_target="tpu_custom_call" | custom-call | bytes 2097152 | tf_op jit(solution)/shard_map/pick4/pallas_call | solution.py:47
  83.2 2.2 %collective-permute-start.12 = (bf16[1,6,32,256]{3,2,1,0:T(8,128)(2,1)}, bf16[1,6,32,256]{3,2,1,0:T(8,128)(2,1)}, u32[]{:S(2)}, u32[]{:S(2)}) collective-permute-start(bf16[1,6,32,256]{3,2,1,0:T(8,128)(2,1)} %get-tuple-element.99), channel_id=1, source_target_pairs={{0,2},{1,3},{2,4},{3,5},{4,6},{5,7},{6,0},{7,1},{8,10},{9,11},{10,... | collective-permute-start | bytes 294920 | tf_op jit(solution)/shard_map/ppermute | solution.py:214
  85.5 2.9 %collective-permute-start.13 = (bf16[1,6,32,256]{3,2,1,0:T(8,128)(2,1)}, bf16[1,6,32,256]{3,2,1,0:T(8,128)(2,1)}, u32[]{:S(2)}, u32[]{:S(2)}) collective-permute-start(bf16[1,6,32,256]{3,2,1,0:T(8,128)(2,1)} %get-tuple-element.100), channel_id=1, source_target_pairs={{0,4},{1,5},{2,6},{3,7},{4,0},{5,1},{6,2},{7,3},{8,12},{9,13},{10,... | collective-permute-start | bytes 294920 | tf_op jit(solution)/shard_map/ppermute | solution.py:214
  88.4 0.0 collective-permute-start.14
  88.4 0.0 all-gather.9.cloned.1.call-done
  88.4 5.0 %level2.1 = (f32[32,256]{1,0:T(8,128)}, bf16[32,32,256]{2,1,0:T(8,128)(2,1)}) custom-call(s32[1]{0:T(128)} %bitcast.place, s32[4,3,6]{2,1,0:T(4,128)} %copy-done, s32[4,3,6]{2,1,0:T(4,128)} %collective-permute-done.3.there, s32[1,6]{1,0:T(1,128)} %bitcast.29, bf16[4,256,256]{2,1,0:T(8,128)(2,1)} %rhs.7, bf16[4,256,256]{2,1,0:T(8,128)(2,1)} %dinv.7, ...), custom_call_target="tpu_custom_call" | custom-call | flops 100663296 | bytes 3145728 | tf_op jit(solution)/shard_map/level2/pallas_call | solution.py:47
  93.4 0.0 collective-permute-done.12.refs_1_
  93.4 0.0 collective-permute-done.13.refs_2_
  93.4 1.7 %collective-permute-done.14.refs_3_ = bf16[1,6,32,256]{3,2,1,0:T(8,128)(2,1)} collective-permute-done((bf16[1,6,32,256]{3,2,1,0:T(8,128)(2,1)}, bf16[1,6,32,256]{3,2,1,0:T(8,128)(2,1)}, u32[]{:S(2)}, u32[]{:S(2)}) %collective-permute-start.14) | collective-permute-done | bytes 98336 | tf_op jit(solution)/shard_map/ppermute | solution.py:214
  95.1 5.6 %all-to-all-start.2 = ((bf16[32,32,256]{2,1,0:T(8,128)(2,1)}), bf16[32,32,256]{2,1,0:T(8,128)(2,1)}, u32[]{:S(2)}, u32[]{:S(2)}) async-start(bf16[32,32,256]{2,1,0:T(8,128)(2,1)} %get-tuple-element.102), calls=%async_computation.2 | async-start | bytes 1048576 | tf_op jit(solution)/shard_map/all_to_all | solution.py:215
  100.7 2.4 %partial4.1 = (f32[32,256]{1,0:T(8,128)}, f32[32,256]{1,0:T(8,128)}, f32[32,256]{1,0:T(8,128)}, f32[32,256]{1,0:T(8,128)}) custom-call(s32[1]{0:T(128)} %bitcast.place, s32[1,6]{1,0:T(1,128)} %bitcast.30, bf16[1,6,32,256]{3,2,1,0:T(8,128)(2,1)} %get-tuple-element.104.refs_0_, bf16[1,6,32,256]{3,2,1,0:T(8,128)(2,1)} %collective-permute-done.12.refs_1_, ...), custom_call_target="tpu_custom_call" | custom-call | flops 201326592 | bytes 2097152 | tf_op jit(solution)/shard_map/partial4/pallas_call | solution.py:47
  103.1 1.5 %collective-permute-start.15 = (f32[32,256]{1,0:T(8,128)}, f32[32,256]{1,0:T(8,128)}, u32[]{:S(2)}, u32[]{:S(2)}) collective-permute-start(f32[32,256]{1,0:T(8,128)} %get-tuple-element.113), channel_id=1, source_target_pairs={{0,6},{1,7},{2,0},{3,1},{4,2},{5,3},{6,4},{7,5},{8,14},{9,15},{10,... | collective-permute-start | bytes 98312 | tf_op jit(solution)/shard_map/ppermute | solution.py:214
  104.6 0.8 collective-permute-start.16
  105.4 0.5 collective-permute-start.17
  105.9 1.4 %all-gather.11.cloned.1.call-done = bf16[6144,256]{1,0:T(8,128)(2,1)} async-done(((bf16[768,256]{1,0:T(8,128)(2,1)}), bf16[6144,256]{1,0:T(8,128)(2,1)}) %all-gather.11.cloned.1.call-update) | async-done | bytes 3145744 | tf_op jit(solution)/shard_map/all_gather | solution.py:217
  107.3 0.0 collective-permute-done.15.refs_2_
  107.4 3.0 %collective-permute-done.16.refs_3_ = f32[32,256]{1,0:T(8,128)} collective-permute-done((f32[32,256]{1,0:T(8,128)}, f32[32,256]{1,0:T(8,128)}, u32[]{:S(2)}, u32[]{:S(2)}) %collective-permute-start.16) | collective-permute-done | bytes 32800 | tf_op jit(solution)/shard_map/ppermute | solution.py:214
  110.3 0.5 collective-permute-done.17.refs_4_
  110.9 3.5 %all-to-all-done.2.known = bf16[32,32,256]{2,1,0:T(8,128)(2,1)} async-done(((bf16[32,32,256]{2,1,0:T(8,128)(2,1)}), bf16[32,32,256]{2,1,0:T(8,128)(2,1)}, u32[]{:S(2)}, u32[]{:S(2)}) %all-to-all-start.2) | async-done | bytes 524320 | tf_op jit(solution)/shard_map/all_to_all | solution.py:215
  114.4 4.6 %level3.1 = f32[4,32,256]{2,1,0:T(8,128)} custom-call(s32[1]{0:T(128)} %bitcast.place, s32[4,3,6]{2,1,0:T(4,128)} %copy-done, s32[4,3,6]{2,1,0:T(4,128)} %collective-permute-done.3.there, s32[1,6]{1,0:T(1,128)} %bitcast.31, bf16[4,256,256]{2,1,0:T(8,128)(2,1)} %rhs.7, bf16[4,256,256]{2,1,0:T(8,128)(2,1)} %dinv.7, bf16[32,32,256]{2,1,0:T(8,128)(2,1)} %all-to-all-done.2.known, ...), custom_call_target="tpu_custom_call" | custom-call | flops 100663296 | bytes 3145728 | tf_op jit(solution)/shard_map/level3/pallas_call | solution.py:47
  (1 shorter events, 0.0 us)
Async XLA Ops:
  6.5 35.0 %all-gather.7.cloned.1.call-start = ((), (), s32[]{:S(2)}) async-start(), calls=%async_computation.3 | async-start | bytes 1966080 | tf_op jit(solution)/shard_map/all_gather | solution.py:217
  9.3 79.1 %all-gather.9.cloned.1.call-start = ((), (), s32[]{:S(2)}) async-start(), calls=%async_computation.4 | async-start | bytes 3538944 | tf_op jit(solution)/shard_map/all_gather | solution.py:217
  10.1 97.3 %all-gather.11.cloned.1.call-start = ((), (), s32[]{:S(2)}) async-start(), calls=%async_computation.5 | async-start | bytes 3538944 | tf_op jit(solution)/shard_map/all_gather | solution.py:217
  10.8 28.6 %all-to-all-start = ((bf16[32,32,256]{2,1,0:T(8,128)(2,1)}), bf16[32,32,256]{2,1,0:T(8,128)(2,1)}, u32[]{:S(2)}, u32[]{:S(2)}) async-start(bf16[32,32,256]{2,1,0:T(8,128)(2,1)} %get-tuple-element.63), calls=%async_computation | async-start | bytes 1048576 | tf_op jit(solution)/shard_map/all_to_all | solution.py:215
  23.2 6.5 %collective-permute-start = (s32[3,6]{1,0:T(4,128)S(1)}, s32[3,6]{1,0:T(4,128)S(1)}, u32[]{:S(2)}, u32[]{:S(2)}) collective-permute-start(s32[3,6]{1,0:T(4,128)S(1)} %bitcast.34), channel_id=1, source_target_pairs={{0,2},{1,3},{2,4},{3,5},{4,6},{5,7},{6,0},{7,1},{8,10},{9,11},{10,... | collective-permute-start | bytes 224 | tf_op jit(solution)/shard_map/ppermute | solution.py:214
  24.7 5.2 %collective-permute-start.1 = (s32[3,6]{1,0:T(4,128)S(1)}, s32[3,6]{1,0:T(4,128)S(1)}, u32[]{:S(2)}, u32[]{:S(2)}) collective-permute-start(s32[3,6]{1,0:T(4,128)S(1)} %bitcast.35), channel_id=1, source_target_pairs={{0,4},{1,5},{2,6},{3,7},{4,0},{5,1},{6,2},{7,3},{8,12},{9,13},{10,... | collective-permute-start | bytes 224 | tf_op jit(solution)/shard_map/ppermute | solution.py:214
  27.6 3.6 %collective-permute-start.2 = (s32[3,6]{1,0:T(4,128)S(1)}, s32[3,6]{1,0:T(4,128)S(1)}, u32[]{:S(2)}, u32[]{:S(2)}) collective-permute-start(s32[3,6]{1,0:T(4,128)S(1)} %bitcast.36), channel_id=1, source_target_pairs={{0,6},{1,7},{2,0},{3,1},{4,2},{5,3},{6,4},{7,5},{8,14},{9,15},{10,... | collective-permute-start | bytes 224 | tf_op jit(solution)/shard_map/ppermute | solution.py:214
  31.3 0.6 copy-start
  31.8 1.3 %collective-permute-start.3 = (s32[4,3,6]{2,1,0:T(4,128)S(1)}, s32[4,3,6]{2,1,0:T(4,128)}, u32[]{:S(2)}, u32[]{:S(2)}) collective-permute-start(s32[4,3,6]{2,1,0:T(4,128)S(1)} %pad_add_fusion.here), channel_id=1, source_target_pairs={{0,1},{1,0},{2,3},{3,2},{4,5},{5,4},{6,7},{7,6},{8,9},{9,8},{10,11... | collective-permute-start | bytes 872 | tf_op jit(solution)/shard_map/ppermute | solution.py:214
  41.5 6.2 %collective-permute-start.4 = (bf16[4,768,256]{2,1,0:T(8,128)(2,1)}, bf16[4,768,256]{2,1,0:T(8,128)(2,1)}, u32[]{:S(2)}, u32[]{:S(2)}) collective-permute-start(bf16[4,768,256]{2,1,0:T(8,128)(2,1)} %bitcast.25), channel_id=1, source_target_pairs={{0,1},{1,0},{2,3},{3,2},{4,5},{5,4},{6,7},{7,6},{8,9},{9,8},{10,11... | collective-permute-start | bytes 4718600 | tf_op jit(solution)/shard_map/ppermute | solution.py:214
  41.5 23.9 %collective-permute-start.8 = (bf16[6,3,256,256]{3,2,1,0:T(8,128)(2,1)}, bf16[6,3,256,256]{3,2,1,0:T(8,128)(2,1)}, u32[]{:S(2)}, u32[]{:S(2)}) collective-permute-start(bf16[6,3,256,256]{3,2,1,0:T(8,128)(2,1)} %bitcast.19), channel_id=1, source_target_pairs={{0,1},{1,0},{2,3},{3,2},{4,5},{5,4},{6,7},{7,6},{8,9},{9,8},{10,11... | collective-permute-start | bytes 7077896 | tf_op jit(solution)/shard_map/ppermute | solution.py:214
  42.0 10.4 %collective-permute-start.5 = (bf16[2,6,32,256]{3,2,1,0:T(8,128)(2,1)}, bf16[2,6,32,256]{3,2,1,0:T(8,128)(2,1)}, u32[]{:S(2)}, u32[]{:S(2)}) collective-permute-start(bf16[2,6,32,256]{3,2,1,0:T(8,128)(2,1)} %get-tuple-element.73), channel_id=1, source_target_pairs={{0,2},{1,3},{2,4},{3,5},{4,6},{5,7},{6,0},{7,1},{8,10},{9,11},{10,... | collective-permute-start | bytes 589832 | tf_op jit(solution)/shard_map/ppermute | solution.py:214
  43.5 12.3 %collective-permute-start.6 = (bf16[2,6,32,256]{3,2,1,0:T(8,128)(2,1)}, bf16[2,6,32,256]{3,2,1,0:T(8,128)(2,1)}, u32[]{:S(2)}, u32[]{:S(2)}) collective-permute-start(bf16[2,6,32,256]{3,2,1,0:T(8,128)(2,1)} %get-tuple-element.74), channel_id=1, source_target_pairs={{0,4},{1,5},{2,6},{3,7},{4,0},{5,1},{6,2},{7,3},{8,12},{9,13},{10,... | collective-permute-start | bytes 589832 | tf_op jit(solution)/shard_map/ppermute | solution.py:214
  46.4 9.4 %collective-permute-start.7 = (bf16[2,6,32,256]{3,2,1,0:T(8,128)(2,1)}, bf16[2,6,32,256]{3,2,1,0:T(8,128)(2,1)}, u32[]{:S(2)}, u32[]{:S(2)}) collective-permute-start(bf16[2,6,32,256]{3,2,1,0:T(8,128)(2,1)} %get-tuple-element.75), channel_id=1, source_target_pairs={{0,6},{1,7},{2,0},{3,1},{4,2},{5,3},{6,4},{7,5},{8,14},{9,15},{10,... | collective-permute-start | bytes 589832 | tf_op jit(solution)/shard_map/ppermute | solution.py:214
  55.8 25.7 %all-to-all-start.1 = ((bf16[32,32,256]{2,1,0:T(8,128)(2,1)}), bf16[32,32,256]{2,1,0:T(8,128)(2,1)}, u32[]{:S(2)}, u32[]{:S(2)}) async-start(bf16[32,32,256]{2,1,0:T(8,128)(2,1)} %get-tuple-element.76), calls=%async_computation.1 | async-start | bytes 1048576 | tf_op jit(solution)/shard_map/all_to_all | solution.py:215
  68.5 6.1 %collective-permute-start.10 = (f32[32,256]{1,0:T(8,128)}, f32[32,256]{1,0:T(8,128)}, u32[]{:S(2)}, u32[]{:S(2)}) collective-permute-start(f32[32,256]{1,0:T(8,128)} %get-tuple-element.84), channel_id=1, source_target_pairs={{0,4},{1,5},{2,6},{3,7},{4,0},{5,1},{6,2},{7,3},{8,12},{9,13},{10,... | collective-permute-start | bytes 98312 | tf_op jit(solution)/shard_map/ppermute | solution.py:214
  70.3 5.4 %collective-permute-start.11 = (f32[32,256]{1,0:T(8,128)}, f32[32,256]{1,0:T(8,128)}, u32[]{:S(2)}, u32[]{:S(2)}) collective-permute-start(f32[32,256]{1,0:T(8,128)} %get-tuple-element.85), channel_id=1, source_target_pairs={{0,2},{1,3},{2,4},{3,5},{4,6},{5,7},{6,0},{7,1},{8,10},{9,11},{10,... | collective-permute-start | bytes 98312 | tf_op jit(solution)/shard_map/ppermute | solution.py:214
  72.0 4.2 %collective-permute-start.9 = (f32[32,256]{1,0:T(8,128)}, f32[32,256]{1,0:T(8,128)}, u32[]{:S(2)}, u32[]{:S(2)}) collective-permute-start(f32[32,256]{1,0:T(8,128)} %get-tuple-element.83), channel_id=1, source_target_pairs={{0,6},{1,7},{2,0},{3,1},{4,2},{5,3},{6,4},{7,5},{8,14},{9,15},{10,... | collective-permute-start | bytes 98312 | tf_op jit(solution)/shard_map/ppermute | solution.py:214
  83.2 10.1 %collective-permute-start.12 = (bf16[1,6,32,256]{3,2,1,0:T(8,128)(2,1)}, bf16[1,6,32,256]{3,2,1,0:T(8,128)(2,1)}, u32[]{:S(2)}, u32[]{:S(2)}) collective-permute-start(bf16[1,6,32,256]{3,2,1,0:T(8,128)(2,1)} %get-tuple-element.99), channel_id=1, source_target_pairs={{0,2},{1,3},{2,4},{3,5},{4,6},{5,7},{6,0},{7,1},{8,10},{9,11},{10,... | collective-permute-start | bytes 294920 | tf_op jit(solution)/shard_map/ppermute | solution.py:214
  85.5 7.9 %collective-permute-start.13 = (bf16[1,6,32,256]{3,2,1,0:T(8,128)(2,1)}, bf16[1,6,32,256]{3,2,1,0:T(8,128)(2,1)}, u32[]{:S(2)}, u32[]{:S(2)}) collective-permute-start(bf16[1,6,32,256]{3,2,1,0:T(8,128)(2,1)} %get-tuple-element.100), channel_id=1, source_target_pairs={{0,4},{1,5},{2,6},{3,7},{4,0},{5,1},{6,2},{7,3},{8,12},{9,13},{10,... | collective-permute-start | bytes 294920 | tf_op jit(solution)/shard_map/ppermute | solution.py:214
  88.4 6.7 %collective-permute-start.14 = (bf16[1,6,32,256]{3,2,1,0:T(8,128)(2,1)}, bf16[1,6,32,256]{3,2,1,0:T(8,128)(2,1)}, u32[]{:S(2)}, u32[]{:S(2)}) collective-permute-start(bf16[1,6,32,256]{3,2,1,0:T(8,128)(2,1)} %get-tuple-element.101), channel_id=1, source_target_pairs={{0,6},{1,7},{2,0},{3,1},{4,2},{5,3},{6,4},{7,5},{8,14},{9,15},{10,... | collective-permute-start | bytes 294920 | tf_op jit(solution)/shard_map/ppermute | solution.py:214
  95.1 19.2 %all-to-all-start.2 = ((bf16[32,32,256]{2,1,0:T(8,128)(2,1)}), bf16[32,32,256]{2,1,0:T(8,128)(2,1)}, u32[]{:S(2)}, u32[]{:S(2)}) async-start(bf16[32,32,256]{2,1,0:T(8,128)(2,1)} %get-tuple-element.102), calls=%async_computation.2 | async-start | bytes 1048576 | tf_op jit(solution)/shard_map/all_to_all | solution.py:215
  103.1 4.2 %collective-permute-start.15 = (f32[32,256]{1,0:T(8,128)}, f32[32,256]{1,0:T(8,128)}, u32[]{:S(2)}, u32[]{:S(2)}) collective-permute-start(f32[32,256]{1,0:T(8,128)} %get-tuple-element.113), channel_id=1, source_target_pairs={{0,6},{1,7},{2,0},{3,1},{4,2},{5,3},{6,4},{7,5},{8,14},{9,15},{10,... | collective-permute-start | bytes 98312 | tf_op jit(solution)/shard_map/ppermute | solution.py:214
  104.6 5.7 %collective-permute-start.16 = (f32[32,256]{1,0:T(8,128)}, f32[32,256]{1,0:T(8,128)}, u32[]{:S(2)}, u32[]{:S(2)}) collective-permute-start(f32[32,256]{1,0:T(8,128)} %get-tuple-element.114), channel_id=1, source_target_pairs={{0,4},{1,5},{2,6},{3,7},{4,0},{5,1},{6,2},{7,3},{8,12},{9,13},{10,... | collective-permute-start | bytes 98312 | tf_op jit(solution)/shard_map/ppermute | solution.py:214
  105.4 5.4 %collective-permute-start.17 = (f32[32,256]{1,0:T(8,128)}, f32[32,256]{1,0:T(8,128)}, u32[]{:S(2)}, u32[]{:S(2)}) collective-permute-start(f32[32,256]{1,0:T(8,128)} %get-tuple-element.115), channel_id=1, source_target_pairs={{0,2},{1,3},{2,4},{3,5},{4,6},{5,7},{6,0},{7,1},{8,10},{9,11},{10,... | collective-permute-start | bytes 98312 | tf_op jit(solution)/shard_map/ppermute | solution.py:214
Sparse Core Ops, SparseCore 0:
  9.4 32.0 all-gather.6
  43.4 30.7 all-gather.8
  76.0 31.2 all-gather.10

commit v13 on v12

--- a/solution.py
+++ b/solution.py
@@ -221,7 +221,7 @@
     here = jnp.stack([own] + [move(own, TURN[d]) for d in range(1, CHIPS)])
     there = move(here, SWAP)
     answer0, spread0, *cuts = first_call(place, rhs, dinv, tiles, (0, 2, 5))
-    gathered0, gathered2, gathered5 = gather(cuts[0], "chip"), gather(cuts[1], COL), gather(cuts[2], COL)
+    gathered0, gathered2, gathered5 = gather(cuts[0], COL), gather(cuts[1], "chip"), gather(cuts[2], COL)
 
     def send(picked):
         return [picked[0]] + [move(picked[d], TURN[d]) for d in range(1, CHIPS)]
@@ -229,15 +229,12 @@
     def give_back(sums):
         return [sums[0]] + [move(sums[d], TURN[CHIPS - d]) for d in range(1, CHIPS)]
 
-    later, spread0 = lax.optimization_barrier((tiles, spread0))
-    swapped = move(later, SWAP)
     known0 = over_row(spread0)
     picked = pick_call("pick13", (1, 3), place, here, there, known0)
-    known0, *picked = lax.optimization_barrier((known0, *picked))
+    later, known0, *picked = lax.optimization_barrier((tiles, known0, *picked))
+    swapped = move(later, SWAP)
     got = send(picked)
-    gathered0, _ = lax.optimization_barrier((gathered0, picked[0]))
-    gathered0 = [gathered0, move(gathered0, SWAP)]
-    answer1, spread1 = level_call(1, 0, place, here, there, live, rhs, dinv, known0, gathered0, [], [])
+    answer1, spread1 = level_call(1, 0, place, here, there, live, rhs, dinv, known0, [gathered0], [], [])
     spread1, *got = lax.optimization_barrier((spread1, *got))
     known1 = over_row(spread1)
 
@@ -248,7 +245,9 @@
     picked = pick_call("pick4", (4,), place, here, there, known1)
     known1, *picked = lax.optimization_barrier((known1, *picked))
     got = send(picked)
-    answer2, spread2 = level_call(2, 2, place, here, there, live, rhs, dinv, known1, [gathered2], back2, [])
+    gathered2, _ = lax.optimization_barrier((gathered2, picked[0]))
+    gathered2 = [gathered2, move(gathered2, SWAP)]
+    answer2, spread2 = level_call(2, 2, place, here, there, live, rhs, dinv, known1, gathered2, back2, [])
     spread2, *got = lax.optimization_barrier((spread2, *got))
     known2 = over_row(spread2)
 

time: 127 us -> 125 us (0.984)
  starting transfers between devices: 52 us -> 46.8 us
  waiting for transfers between devices: 32 us -> 34.9 us
    all_gather x3, waiting for transfers between devices: 1.55 us -> 7.98 us  [local(): lax.all_gather(array, axes, axis=0, tiled=False)]
    all_to_all x3, starting transfers between devices: 26.9 us -> 23.6 us  [local(): over_row = lambda array: lax.all_to_all(array, 'row', 0, 0, tiled=True)]
    all_to_all x3, waiting for transfers between devices: 14.9 us -> 12 us  [local(): over_row = lambda array: lax.all_to_all(array, 'row', 0, 0, tiled=True)]
    ppermute x18, starting transfers between devices: 25.1 us -> 23.1 us  [local(): move = lambda array, pairs: lax.ppermute(array, COL, pairs)]
  transfers between devices with their start and end apart: 24 -> 24, of which waited for: 15 -> 11; matrix products, arithmetic and copies ran while one was open for 1% -> 1% of each run, Pallas kernels for 15% -> 15%
where the time goes in v13:
time: 125 us; the launch traced here: 123 us
  starting transfers between devices  46.8 us (37%)
  waiting for transfers between devices  34.9 us (28%)
  Pallas kernels  26.3 us (21%)
  between operations  13.2 us (11%)
  local copies, waits for them, and re-layouts  1.96 us (2%)
    pallas_call x8, Pallas kernels, call(): pl.pallas_call(kernel, grid=(1,), out_shape=tuple((jax.ShapeDtypeStruct(s...  26.3 us
    all_to_all x3, starting transfers between devices, local(): over_row = lambda array: lax.all_to_all(array, 'row', 0, 0, tiled=True)  23.6 us
    ppermute x18, starting transfers between devices, local(): move = lambda array, pairs: lax.ppermute(array, COL, pairs)  23.1 us
    ppermute x18, waiting for transfers between devices, local(): move = lambda array, pairs: lax.ppermute(array, COL, pairs)  13.5 us
    all_to_all x3, waiting for transfers between devices, local(): over_row = lambda array: lax.all_to_all(array, 'row', 0, 0, tiled=True)  12 us
    all_gather x3, waiting for transfers between devices, local(): lax.all_gather(array, axes, axis=0, tiled=False)  7.98 us
  transfers between devices with their start and end apart: 24, of which 11 were waited for; matrix products, arithmetic and copies ran while one was open for 1% of the time, Pallas kernels for 15%

profile of v13, /device:TPU:2, one launch (start us, length us, event | category | flops | bytes accessed | tf_op | source)
XLA Modules:
  0.0 123.2 jit_solution(15582075268727582482)
XLA Ops:
  6.5 0.0 all-gather.7.cloned.1.call-start
  6.5 2.8 %level0.1 = (f32[32,256]{1,0:T(8,128)}, bf16[32,32,256]{2,1,0:T(8,128)(2,1)}, bf16[768,256]{1,0:T(8,128)(2,1)}, bf16[768,256]{1,0:T(8,128)(2,1)}, bf16[768,256]{1,0:T(8,128)(2,1)}) custom-call(s32[1]{0:T(128)} %bitcast.place, bf16[4,256,256]{2,1,0:T(8,128)(2,1)} %rhs.7, bf16[4,256,256]{2,1,0:T(8,128)(2,1)} %dinv.7, bf16[6,3,256,256]{3,2,1,0:T(8,128)(2,1)} %bitcast.16, ...), custom_call_target="tpu_custom_call" | custom-call | bytes 4194304 | tf_op jit(solution)/shard_map/level0/pallas_call | solution.py:47
  9.3 0.0 all-gather.7.cloned.1.call-update
  9.3 0.0 all-gather.9.cloned.1.call-start
  9.4 0.7 all-gather.9.cloned.1.call-update
  10.1 11.7 %all-to-all-start = ((bf16[32,32,256]{2,1,0:T(8,128)(2,1)}), bf16[32,32,256]{2,1,0:T(8,128)(2,1)}, u32[]{:S(2)}, u32[]{:S(2)}) async-start(bf16[32,32,256]{2,1,0:T(8,128)(2,1)} %get-tuple-element.61), calls=%async_computation | async-start | bytes 1048576 | tf_op jit(solution)/shard_map/all_to_all | solution.py:215
  21.8 0.0 all-gather.11.cloned.1.call-start
  21.8 0.7 all-gather.11.cloned.1.call-update
  22.5 0.7 copy.9
  23.2 3.0 %collective-permute-start.2 = (s32[3,6]{1,0:T(4,128)S(1)}, s32[3,6]{1,0:T(4,128)S(1)}, u32[]{:S(2)}, u32[]{:S(2)}) collective-permute-start(s32[3,6]{1,0:T(4,128)S(1)} %bitcast.34), channel_id=1, source_target_pairs={{0,6},{1,7},{2,0},{3,1},{4,2},{5,3},{6,4},{7,5},{8,14},{9,15},{10,... | collective-permute-start | bytes 224 | tf_op jit(solution)/shard_map/ppermute | solution.py:214
  26.2 0.6 collective-permute-start.1
  26.9 1.0 collective-permute-start
  27.8 0.7 copy.6
  28.5 0.0 collective-permute-done.2
  28.5 2.9 %collective-permute-done.1 = s32[3,6]{1,0:T(4,128)S(1)} collective-permute-done((s32[3,6]{1,0:T(4,128)S(1)}, s32[3,6]{1,0:T(4,128)S(1)}, u32[]{:S(2)}, u32[]{:S(2)}) %collective-permute-start.1) | collective-permute-done | bytes 104 | tf_op jit(solution)/shard_map/ppermute | solution.py:214
  31.4 0.2 collective-permute-done
  31.7 0.0 copy-start
  31.7 0.6 copy-done
  32.3 0.0 collective-permute-start.3
  32.3 1.3 %collective-permute-done.3.there = s32[4,3,6]{2,1,0:T(4,128)} collective-permute-done((s32[4,3,6]{2,1,0:T(4,128)S(1)}, s32[4,3,6]{2,1,0:T(4,128)}, u32[]{:S(2)}, u32[]{:S(2)}) %collective-permute-start.3) | collective-permute-done | bytes 320 | tf_op jit(solution)/shard_map/ppermute | solution.py:214
  33.6 5.1 %all-to-all-done.known = bf16[32,32,256]{2,1,0:T(8,128)(2,1)} async-done(((bf16[32,32,256]{2,1,0:T(8,128)(2,1)}), bf16[32,32,256]{2,1,0:T(8,128)(2,1)}, u32[]{:S(2)}, u32[]{:S(2)}) %all-to-all-start) | async-done | bytes 524320 | tf_op jit(solution)/shard_map/all_to_all | solution.py:215
  38.7 2.0 %pick13.1 = (bf16[2,6,32,256]{3,2,1,0:T(8,128)(2,1)}, bf16[2,6,32,256]{3,2,1,0:T(8,128)(2,1)}, bf16[2,6,32,256]{3,2,1,0:T(8,128)(2,1)}, bf16[2,6,32,256]{3,2,1,0:T(8,128)(2,1)}) custom-call(s32[1]{0:T(128)} %bitcast.place, s32[4,3,6]{2,1,0:T(4,128)} %copy-done, s32[4,3,6]{2,1,0:T(4,128)} %collective-permute-done.3.there, bf16[32,32,256]{2,1,0:T(8,128)(2,1)} %all-to-all-done.known), custom_call_target="tpu_custom_call" | custom-call | bytes 2097152 | tf_op jit(solution)/shard_map/pick13/pallas_call | solution.py:47
  40.7 0.0 collective-permute-start.7
  40.7 1.5 %collective-permute-start.4 = (bf16[2,6,32,256]{3,2,1,0:T(8,128)(2,1)}, bf16[2,6,32,256]{3,2,1,0:T(8,128)(2,1)}, u32[]{:S(2)}, u32[]{:S(2)}) collective-permute-start(bf16[2,6,32,256]{3,2,1,0:T(8,128)(2,1)} %get-tuple-element.70), channel_id=1, source_target_pairs={{0,2},{1,3},{2,4},{3,5},{4,6},{5,7},{6,0},{7,1},{8,10},{9,11},{10,... | collective-permute-start | bytes 589832 | tf_op jit(solution)/shard_map/ppermute | solution.py:214
  42.2 2.9 %collective-permute-start.5 = (bf16[2,6,32,256]{3,2,1,0:T(8,128)(2,1)}, bf16[2,6,32,256]{3,2,1,0:T(8,128)(2,1)}, u32[]{:S(2)}, u32[]{:S(2)}) collective-permute-start(bf16[2,6,32,256]{3,2,1,0:T(8,128)(2,1)} %get-tuple-element.71), channel_id=1, source_target_pairs={{0,4},{1,5},{2,6},{3,7},{4,0},{5,1},{6,2},{7,3},{8,12},{9,13},{10,... | collective-permute-start | bytes 589832 | tf_op jit(solution)/shard_map/ppermute | solution.py:214
  45.2 1.3 %collective-permute-start.6 = (bf16[2,6,32,256]{3,2,1,0:T(8,128)(2,1)}, bf16[2,6,32,256]{3,2,1,0:T(8,128)(2,1)}, u32[]{:S(2)}, u32[]{:S(2)}) collective-permute-start(bf16[2,6,32,256]{3,2,1,0:T(8,128)(2,1)} %get-tuple-element.72), channel_id=1, source_target_pairs={{0,6},{1,7},{2,0},{3,1},{4,2},{5,3},{6,4},{7,5},{8,14},{9,15},{10,... | collective-permute-start | bytes 589832 | tf_op jit(solution)/shard_map/ppermute | solution.py:214
  46.5 0.0 all-gather.7.cloned.1.call-done
  46.5 4.8 %level1.1 = (f32[32,256]{1,0:T(8,128)}, bf16[32,32,256]{2,1,0:T(8,128)(2,1)}) custom-call(s32[1]{0:T(128)} %bitcast.place, s32[4,3,6]{2,1,0:T(4,128)} %copy-done, s32[4,3,6]{2,1,0:T(4,128)} %collective-permute-done.3.there, s32[1,6]{1,0:T(1,128)} %bitcast.27, bf16[4,256,256]{2,1,0:T(8,128)(2,1)} %rhs.7, bf16[4,256,256]{2,1,0:T(8,128)(2,1)} %dinv.7, ...), custom_call_target="tpu_custom_call" | custom-call | flops 100663296 | bytes 3145728 | tf_op jit(solution)/shard_map/level1/pallas_call | solution.py:47
  51.3 0.0 collective-permute-done.4.refs_1_
  51.3 3.7 %collective-permute-done.5.refs_2_ = bf16[2,6,32,256]{3,2,1,0:T(8,128)(2,1)} collective-permute-done((bf16[2,6,32,256]{3,2,1,0:T(8,128)(2,1)}, bf16[2,6,32,256]{3,2,1,0:T(8,128)(2,1)}, u32[]{:S(2)}, u32[]{:S(2)}) %collective-permute-start.5) | collective-permute-done | bytes 196640 | tf_op jit(solution)/shard_map/ppermute | solution.py:214
  55.0 0.0 collective-permute-done.6.refs_3_
  55.0 5.6 %all-to-all-start.1 = ((bf16[32,32,256]{2,1,0:T(8,128)(2,1)}), bf16[32,32,256]{2,1,0:T(8,128)(2,1)}, u32[]{:S(2)}, u32[]{:S(2)}) async-start(bf16[32,32,256]{2,1,0:T(8,128)(2,1)} %get-tuple-element.73), calls=%async_computation.1 | async-start | bytes 1048576 | tf_op jit(solution)/shard_map/all_to_all | solution.py:215
  60.6 0.0 collective-permute-done.7.refs_5_.refs_7_.refs_9_
  60.6 3.0 %partial13.1 = (f32[32,256]{1,0:T(8,128)}, f32[32,256]{1,0:T(8,128)}, f32[32,256]{1,0:T(8,128)}, f32[32,256]{1,0:T(8,128)}, f32[32,256]{1,0:T(8,128)}, /*index=5...) custom-call(s32[1]{0:T(128)} %bitcast.place, s32[1,6]{1,0:T(1,128)} %bitcast.28, ...), custom_call_target="tpu_custom_call" | custom-call | flops 201326592 | bytes 2097152 | tf_op jit(solution)/shard_map/partial13/pallas_call | solution.py:47
  63.6 2.1 %collective-permute-start.8 = (f32[32,256]{1,0:T(8,128)}, f32[32,256]{1,0:T(8,128)}, u32[]{:S(2)}, u32[]{:S(2)}) collective-permute-start(f32[32,256]{1,0:T(8,128)} %get-tuple-element.80), channel_id=1, source_target_pairs={{0,6},{1,7},{2,0},{3,1},{4,2},{5,3},{6,4},{7,5},{8,14},{9,15},{10,... | collective-permute-start | bytes 98312 | tf_op jit(solution)/shard_map/ppermute | solution.py:214
  65.7 1.2 collective-permute-start.9
  66.9 0.8 collective-permute-start.10
  67.7 1.1 collective-permute-done.8.refs_3_
  68.8 3.5 %collective-permute-done.9.refs_4_ = f32[32,256]{1,0:T(8,128)} collective-permute-done((f32[32,256]{1,0:T(8,128)}, f32[32,256]{1,0:T(8,128)}, u32[]{:S(2)}, u32[]{:S(2)}) %collective-permute-start.9) | collective-permute-done | bytes 32800 | tf_op jit(solution)/shard_map/ppermute | solution.py:214
  72.2 0.8 collective-permute-done.10.refs_5_
  73.1 4.4 %all-to-all-done.1.known = bf16[32,32,256]{2,1,0:T(8,128)(2,1)} async-done(((bf16[32,32,256]{2,1,0:T(8,128)(2,1)}), bf16[32,32,256]{2,1,0:T(8,128)(2,1)}, u32[]{:S(2)}, u32[]{:S(2)}) %all-to-all-start.1) | async-done | bytes 524320 | tf_op jit(solution)/shard_map/all_to_all | solution.py:215
  77.4 1.8 %pick4.1 = (bf16[1,6,32,256]{3,2,1,0:T(8,128)(2,1)}, bf16[1,6,32,256]{3,2,1,0:T(8,128)(2,1)}, bf16[1,6,32,256]{3,2,1,0:T(8,128)(2,1)}, bf16[1,6,32,256]{3,2,1,0:T(8,128)(2,1)}) custom-call(s32[1]{0:T(128)} %bitcast.place, s32[4,3,6]{2,1,0:T(4,128)} %copy-done, s32[4,3,6]{2,1,0:T(4,128)} %collective-permute-done.3.there, ...), custom_call_target="tpu_custom_call" | custom-call | bytes 2097152 | tf_op jit(solution)/shard_map/pick4/pallas_call | solution.py:47
  79.2 0.0 all-gather.9.cloned.1.call-done
  79.2 0.0 collective-permute-start.11
  79.2 0.7 collective-permute-start.12
  80.0 3.2 %collective-permute-start.13 = (bf16[1,6,32,256]{3,2,1,0:T(8,128)(2,1)}, bf16[1,6,32,256]{3,2,1,0:T(8,128)(2,1)}, u32[]{:S(2)}, u32[]{:S(2)}) collective-permute-start(bf16[1,6,32,256]{3,2,1,0:T(8,128)(2,1)} %get-tuple-element.98), channel_id=1, source_target_pairs={{0,4},{1,5},{2,6},{3,7},{4,0},{5,1},{6,2},{7,3},{8,12},{9,13},{10,... | collective-permute-start | bytes 294920 | tf_op jit(solution)/shard_map/ppermute | solution.py:214
  83.1 1.1 collective-permute-start.14
  84.2 0.0 collective-permute-done.11.refs_1_
  84.2 4.8 %level2.1 = (f32[32,256]{1,0:T(8,128)}, bf16[32,32,256]{2,1,0:T(8,128)(2,1)}) custom-call(s32[1]{0:T(128)} %bitcast.place, s32[4,3,6]{2,1,0:T(4,128)} %copy-done, s32[4,3,6]{2,1,0:T(4,128)} %collective-permute-done.3.there, s32[1,6]{1,0:T(1,128)} %bitcast.29, bf16[4,256,256]{2,1,0:T(8,128)(2,1)} %rhs.7, bf16[4,256,256]{2,1,0:T(8,128)(2,1)} %dinv.7, ...), custom_call_target="tpu_custom_call" | custom-call | flops 100663296 | bytes 3145728 | tf_op jit(solution)/shard_map/level2/pallas_call | solution.py:47
  89.0 0.0 collective-permute-done.12.refs_1_
  89.0 0.0 collective-permute-done.13.refs_2_
  89.1 0.0 collective-permute-done.14.refs_3_
  89.1 6.4 %all-to-all-start.2 = ((bf16[32,32,256]{2,1,0:T(8,128)(2,1)}), bf16[32,32,256]{2,1,0:T(8,128)(2,1)}, u32[]{:S(2)}, u32[]{:S(2)}) async-start(bf16[32,32,256]{2,1,0:T(8,128)(2,1)} %get-tuple-element.100), calls=%async_computation.2 | async-start | bytes 1048576 | tf_op jit(solution)/shard_map/all_to_all | solution.py:215
  95.4 2.5 %partial4.1 = (f32[32,256]{1,0:T(8,128)}, f32[32,256]{1,0:T(8,128)}, f32[32,256]{1,0:T(8,128)}, f32[32,256]{1,0:T(8,128)}) custom-call(s32[1]{0:T(128)} %bitcast.place, s32[1,6]{1,0:T(1,128)} %bitcast.30, bf16[1,6,32,256]{3,2,1,0:T(8,128)(2,1)} %get-tuple-element.102.refs_0_, bf16[1,6,32,256]{3,2,1,0:T(8,128)(2,1)} %collective-permute-done.12.refs_1_, ...), custom_call_target="tpu_custom_call" | custom-call | flops 201326592 | bytes 2097152 | tf_op jit(solution)/shard_map/partial4/pallas_call | solution.py:47
  97.9 2.7 %collective-permute-start.15 = (f32[32,256]{1,0:T(8,128)}, f32[32,256]{1,0:T(8,128)}, u32[]{:S(2)}, u32[]{:S(2)}) collective-permute-start(f32[32,256]{1,0:T(8,128)} %get-tuple-element.111), channel_id=1, source_target_pairs={{0,6},{1,7},{2,0},{3,1},{4,2},{5,3},{6,4},{7,5},{8,14},{9,15},{10,... | collective-permute-start | bytes 98312 | tf_op jit(solution)/shard_map/ppermute | solution.py:214
  100.6 0.6 collective-permute-start.16
  101.2 0.4 collective-permute-start.17
  101.5 8.0 %all-gather.11.cloned.1.call-done = bf16[6144,256]{1,0:T(8,128)(2,1)} async-done(((bf16[768,256]{1,0:T(8,128)(2,1)}), bf16[6144,256]{1,0:T(8,128)(2,1)}) %all-gather.11.cloned.1.call-update) | async-done | bytes 3145744 | tf_op jit(solution)/shard_map/all_gather | solution.py:217
  109.5 0.0 collective-permute-done.15.refs_2_
  109.5 0.0 collective-permute-done.16.refs_3_
  109.5 0.0 collective-permute-done.17.refs_4_
  109.5 2.5 %all-to-all-done.2.known = bf16[32,32,256]{2,1,0:T(8,128)(2,1)} async-done(((bf16[32,32,256]{2,1,0:T(8,128)(2,1)}), bf16[32,32,256]{2,1,0:T(8,128)(2,1)}, u32[]{:S(2)}, u32[]{:S(2)}) %all-to-all-start.2) | async-done | bytes 524320 | tf_op jit(solution)/shard_map/all_to_all | solution.py:215
  112.0 4.6 %level3.1 = f32[4,32,256]{2,1,0:T(8,128)} custom-call(s32[1]{0:T(128)} %bitcast.place, s32[4,3,6]{2,1,0:T(4,128)} %copy-done, s32[4,3,6]{2,1,0:T(4,128)} %collective-permute-done.3.there, s32[1,6]{1,0:T(1,128)} %bitcast.31, bf16[4,256,256]{2,1,0:T(8,128)(2,1)} %rhs.7, bf16[4,256,256]{2,1,0:T(8,128)(2,1)} %dinv.7, bf16[32,32,256]{2,1,0:T(8,128)(2,1)} %all-to-all-done.2.known, ...), custom_call_target="tpu_custom_call" | custom-call | flops 100663296 | bytes 3145728 | tf_op jit(solution)/shard_map/level3/pallas_call | solution.py:47
  (1 shorter events, 0.0 us)
Async XLA Ops:
  6.5 40.0 %all-gather.7.cloned.1.call-start = ((), (), s32[]{:S(2)}) async-start(), calls=%async_computation.3 | async-start | bytes 3538944 | tf_op jit(solution)/shard_map/all_gather | solution.py:217
  9.3 69.9 %all-gather.9.cloned.1.call-start = ((), (), s32[]{:S(2)}) async-start(), calls=%async_computation.4 | async-start | bytes 1966080 | tf_op jit(solution)/shard_map/all_gather | solution.py:217
  10.1 28.6 %all-to-all-start = ((bf16[32,32,256]{2,1,0:T(8,128)(2,1)}), bf16[32,32,256]{2,1,0:T(8,128)(2,1)}, u32[]{:S(2)}, u32[]{:S(2)}) async-start(bf16[32,32,256]{2,1,0:T(8,128)(2,1)} %get-tuple-element.61), calls=%async_computation | async-start | bytes 1048576 | tf_op jit(solution)/shard_map/all_to_all | solution.py:215
  21.8 87.7 %all-gather.11.cloned.1.call-start = ((), (), s32[]{:S(2)}) async-start(), calls=%async_computation.5 | async-start | bytes 3538944 | tf_op jit(solution)/shard_map/all_gather | solution.py:217
  23.2 5.3 %collective-permute-start.2 = (s32[3,6]{1,0:T(4,128)S(1)}, s32[3,6]{1,0:T(4,128)S(1)}, u32[]{:S(2)}, u32[]{:S(2)}) collective-permute-start(s32[3,6]{1,0:T(4,128)S(1)} %bitcast.34), channel_id=1, source_target_pairs={{0,6},{1,7},{2,0},{3,1},{4,2},{5,3},{6,4},{7,5},{8,14},{9,15},{10,... | collective-permute-start | bytes 224 | tf_op jit(solution)/shard_map/ppermute | solution.py:214
  26.2 5.2 %collective-permute-start.1 = (s32[3,6]{1,0:T(4,128)S(1)}, s32[3,6]{1,0:T(4,128)S(1)}, u32[]{:S(2)}, u32[]{:S(2)}) collective-permute-start(s32[3,6]{1,0:T(4,128)S(1)} %bitcast.35), channel_id=1, source_target_pairs={{0,4},{1,5},{2,6},{3,7},{4,0},{5,1},{6,2},{7,3},{8,12},{9,13},{10,... | collective-permute-start | bytes 224 | tf_op jit(solution)/shard_map/ppermute | solution.py:214
  26.9 4.8 %collective-permute-start = (s32[3,6]{1,0:T(4,128)S(1)}, s32[3,6]{1,0:T(4,128)S(1)}, u32[]{:S(2)}, u32[]{:S(2)}) collective-permute-start(s32[3,6]{1,0:T(4,128)S(1)} %bitcast.36), channel_id=1, source_target_pairs={{0,2},{1,3},{2,4},{3,5},{4,6},{5,7},{6,0},{7,1},{8,10},{9,11},{10,... | collective-permute-start | bytes 224 | tf_op jit(solution)/shard_map/ppermute | solution.py:214
  31.7 0.6 copy-start
  32.3 1.3 %collective-permute-start.3 = (s32[4,3,6]{2,1,0:T(4,128)S(1)}, s32[4,3,6]{2,1,0:T(4,128)}, u32[]{:S(2)}, u32[]{:S(2)}) collective-permute-start(s32[4,3,6]{2,1,0:T(4,128)S(1)} %pad_add_fusion.here), channel_id=1, source_target_pairs={{0,1},{1,0},{2,3},{3,2},{4,5},{5,4},{6,7},{7,6},{8,9},{9,8},{10,11... | collective-permute-start | bytes 872 | tf_op jit(solution)/shard_map/ppermute | solution.py:214
  40.7 19.9 %collective-permute-start.7 = (bf16[6,3,256,256]{3,2,1,0:T(8,128)(2,1)}, bf16[6,3,256,256]{3,2,1,0:T(8,128)(2,1)}, u32[]{:S(2)}, u32[]{:S(2)}) collective-permute-start(bf16[6,3,256,256]{3,2,1,0:T(8,128)(2,1)} %bitcast.19), channel_id=1, source_target_pairs={{0,1},{1,0},{2,3},{3,2},{4,5},{5,4},{6,7},{7,6},{8,9},{9,8},{10,11... | collective-permute-start | bytes 7077896 | tf_op jit(solution)/shard_map/ppermute | solution.py:214
  40.7 10.6 %collective-permute-start.4 = (bf16[2,6,32,256]{3,2,1,0:T(8,128)(2,1)}, bf16[2,6,32,256]{3,2,1,0:T(8,128)(2,1)}, u32[]{:S(2)}, u32[]{:S(2)}) collective-permute-start(bf16[2,6,32,256]{3,2,1,0:T(8,128)(2,1)} %get-tuple-element.70), channel_id=1, source_target_pairs={{0,2},{1,3},{2,4},{3,5},{4,6},{5,7},{6,0},{7,1},{8,10},{9,11},{10,... | collective-permute-start | bytes 589832 | tf_op jit(solution)/shard_map/ppermute | solution.py:214
  42.2 12.8 %collective-permute-start.5 = (bf16[2,6,32,256]{3,2,1,0:T(8,128)(2,1)}, bf16[2,6,32,256]{3,2,1,0:T(8,128)(2,1)}, u32[]{:S(2)}, u32[]{:S(2)}) collective-permute-start(bf16[2,6,32,256]{3,2,1,0:T(8,128)(2,1)} %get-tuple-element.71), channel_id=1, source_target_pairs={{0,4},{1,5},{2,6},{3,7},{4,0},{5,1},{6,2},{7,3},{8,12},{9,13},{10,... | collective-permute-start | bytes 589832 | tf_op jit(solution)/shard_map/ppermute | solution.py:214
  45.2 9.8 %collective-permute-start.6 = (bf16[2,6,32,256]{3,2,1,0:T(8,128)(2,1)}, bf16[2,6,32,256]{3,2,1,0:T(8,128)(2,1)}, u32[]{:S(2)}, u32[]{:S(2)}) collective-permute-start(bf16[2,6,32,256]{3,2,1,0:T(8,128)(2,1)} %get-tuple-element.72), channel_id=1, source_target_pairs={{0,6},{1,7},{2,0},{3,1},{4,2},{5,3},{6,4},{7,5},{8,14},{9,15},{10,... | collective-permute-start | bytes 589832 | tf_op jit(solution)/shard_map/ppermute | solution.py:214
  55.0 22.4 %all-to-all-start.1 = ((bf16[32,32,256]{2,1,0:T(8,128)(2,1)}), bf16[32,32,256]{2,1,0:T(8,128)(2,1)}, u32[]{:S(2)}, u32[]{:S(2)}) async-start(bf16[32,32,256]{2,1,0:T(8,128)(2,1)} %get-tuple-element.73), calls=%async_computation.1 | async-start | bytes 1048576 | tf_op jit(solution)/shard_map/all_to_all | solution.py:215
  63.6 5.2 %collective-permute-start.8 = (f32[32,256]{1,0:T(8,128)}, f32[32,256]{1,0:T(8,128)}, u32[]{:S(2)}, u32[]{:S(2)}) collective-permute-start(f32[32,256]{1,0:T(8,128)} %get-tuple-element.80), channel_id=1, source_target_pairs={{0,6},{1,7},{2,0},{3,1},{4,2},{5,3},{6,4},{7,5},{8,14},{9,15},{10,... | collective-permute-start | bytes 98312 | tf_op jit(solution)/shard_map/ppermute | solution.py:214
  65.7 6.5 %collective-permute-start.9 = (f32[32,256]{1,0:T(8,128)}, f32[32,256]{1,0:T(8,128)}, u32[]{:S(2)}, u32[]{:S(2)}) collective-permute-start(f32[32,256]{1,0:T(8,128)} %get-tuple-element.81), channel_id=1, source_target_pairs={{0,4},{1,5},{2,6},{3,7},{4,0},{5,1},{6,2},{7,3},{8,12},{9,13},{10,... | collective-permute-start | bytes 98312 | tf_op jit(solution)/shard_map/ppermute | solution.py:214
  66.9 6.2 %collective-permute-start.10 = (f32[32,256]{1,0:T(8,128)}, f32[32,256]{1,0:T(8,128)}, u32[]{:S(2)}, u32[]{:S(2)}) collective-permute-start(f32[32,256]{1,0:T(8,128)} %get-tuple-element.82), channel_id=1, source_target_pairs={{0,2},{1,3},{2,4},{3,5},{4,6},{5,7},{6,0},{7,1},{8,10},{9,11},{10,... | collective-permute-start | bytes 98312 | tf_op jit(solution)/shard_map/ppermute | solution.py:214
  79.2 5.0 %collective-permute-start.11 = (bf16[4,768,256]{2,1,0:T(8,128)(2,1)}, bf16[4,768,256]{2,1,0:T(8,128)(2,1)}, u32[]{:S(2)}, u32[]{:S(2)}) collective-permute-start(bf16[4,768,256]{2,1,0:T(8,128)(2,1)} %bitcast.25), channel_id=1, source_target_pairs={{0,1},{1,0},{2,3},{3,2},{4,5},{5,4},{6,7},{7,6},{8,9},{9,8},{10,11... | collective-permute-start | bytes 4718600 | tf_op jit(solution)/shard_map/ppermute | solution.py:214
  79.2 9.8 %collective-permute-start.12 = (bf16[1,6,32,256]{3,2,1,0:T(8,128)(2,1)}, bf16[1,6,32,256]{3,2,1,0:T(8,128)(2,1)}, u32[]{:S(2)}, u32[]{:S(2)}) collective-permute-start(bf16[1,6,32,256]{3,2,1,0:T(8,128)(2,1)} %get-tuple-element.97), channel_id=1, source_target_pairs={{0,2},{1,3},{2,4},{3,5},{4,6},{5,7},{6,0},{7,1},{8,10},{9,11},{10,... | collective-permute-start | bytes 294920 | tf_op jit(solution)/shard_map/ppermute | solution.py:214
  80.0 9.1 %collective-permute-start.13 = (bf16[1,6,32,256]{3,2,1,0:T(8,128)(2,1)}, bf16[1,6,32,256]{3,2,1,0:T(8,128)(2,1)}, u32[]{:S(2)}, u32[]{:S(2)}) collective-permute-start(bf16[1,6,32,256]{3,2,1,0:T(8,128)(2,1)} %get-tuple-element.98), channel_id=1, source_target_pairs={{0,4},{1,5},{2,6},{3,7},{4,0},{5,1},{6,2},{7,3},{8,12},{9,13},{10,... | collective-permute-start | bytes 294920 | tf_op jit(solution)/shard_map/ppermute | solution.py:214
  83.1 5.9 %collective-permute-start.14 = (bf16[1,6,32,256]{3,2,1,0:T(8,128)(2,1)}, bf16[1,6,32,256]{3,2,1,0:T(8,128)(2,1)}, u32[]{:S(2)}, u32[]{:S(2)}) collective-permute-start(bf16[1,6,32,256]{3,2,1,0:T(8,128)(2,1)} %get-tuple-element.99), channel_id=1, source_target_pairs={{0,6},{1,7},{2,0},{3,1},{4,2},{5,3},{6,4},{7,5},{8,14},{9,15},{10,... | collective-permute-start | bytes 294920 | tf_op jit(solution)/shard_map/ppermute | solution.py:214
  89.1 23.0 %all-to-all-start.2 = ((bf16[32,32,256]{2,1,0:T(8,128)(2,1)}), bf16[32,32,256]{2,1,0:T(8,128)(2,1)}, u32[]{:S(2)}, u32[]{:S(2)}) async-start(bf16[32,32,256]{2,1,0:T(8,128)(2,1)} %get-tuple-element.100), calls=%async_computation.2 | async-start | bytes 1048576 | tf_op jit(solution)/shard_map/all_to_all | solution.py:215
  97.9 11.6 %collective-permute-start.15 = (f32[32,256]{1,0:T(8,128)}, f32[32,256]{1,0:T(8,128)}, u32[]{:S(2)}, u32[]{:S(2)}) collective-permute-start(f32[32,256]{1,0:T(8,128)} %get-tuple-element.111), channel_id=1, source_target_pairs={{0,6},{1,7},{2,0},{3,1},{4,2},{5,3},{6,4},{7,5},{8,14},{9,15},{10,... | collective-permute-start | bytes 98312 | tf_op jit(solution)/shard_map/ppermute | solution.py:214
  100.6 8.9 %collective-permute-start.16 = (f32[32,256]{1,0:T(8,128)}, f32[32,256]{1,0:T(8,128)}, u32[]{:S(2)}, u32[]{:S(2)}) collective-permute-start(f32[32,256]{1,0:T(8,128)} %get-tuple-element.112), channel_id=1, source_target_pairs={{0,4},{1,5},{2,6},{3,7},{4,0},{5,1},{6,2},{7,3},{8,12},{9,13},{10,... | collective-permute-start | bytes 98312 | tf_op jit(solution)/shard_map/ppermute | solution.py:214
  101.2 8.4 %collective-permute-start.17 = (f32[32,256]{1,0:T(8,128)}, f32[32,256]{1,0:T(8,128)}, u32[]{:S(2)}, u32[]{:S(2)}) collective-permute-start(f32[32,256]{1,0:T(8,128)} %get-tuple-element.113), channel_id=1, source_target_pairs={{0,2},{1,3},{2,4},{3,5},{4,6},{5,7},{6,0},{7,1},{8,10},{9,11},{10,... | collective-permute-start | bytes 98312 | tf_op jit(solution)/shard_map/ppermute | solution.py:214
Sparse Core Ops, SparseCore 0:
  9.5 35.6 all-gather.6
  47.0 28.7 all-gather.8
  77.7 31.8 all-gather.10

commit v14 on v13

--- a/solution.py
+++ b/solution.py
@@ -55,6 +55,24 @@
         compiler_params=pltpu.CompilerParams(vmem_limit_bytes=VMEM_BYTES),
         name=name,
     )(*args)
+
+
+def cut_kernel(tiles, cut):
+    for slot in range(SLOTS):
+        cut[slot * SIZE : (slot + 1) * SIZE] = tiles[0, slot]
+
+
+def cut_call(tiles, pair):
+    cut = (SLOTS * SIZE, SIZE)
+    return call(
+        cut_kernel,
+        "cut",
+        [(cut, BF16)],
+        [block_of((1, SLOTS, SIZE, SIZE), pair)],
+        [block_of(cut)],
+        (tiles,),
+        moved=2**20,
+    )[0]
 
 
 def first_kernel(place, rhs, dinv, *refs):
@@ -220,8 +238,11 @@
     own = cols.transpose(2, 1, 0).reshape(SLOTS, -1)
     here = jnp.stack([own] + [move(own, TURN[d]) for d in range(1, CHIPS)])
     there = move(here, SWAP)
-    answer0, spread0, *cuts = first_call(place, rhs, dinv, tiles, (0, 2, 5))
-    gathered0, gathered2, gathered5 = gather(cuts[0], COL), gather(cuts[1], "chip"), gather(cuts[2], COL)
+    cut0 = cut_call(tiles, 0)
+    gathered0 = gather(cut0, COL)
+    early, cut0 = lax.optimization_barrier((rhs, cut0))
+    answer0, spread0, cut2, cut5 = first_call(place, early, dinv, tiles, (2, 5))
+    gathered2, gathered5 = gather(cut2, "chip"), gather(cut5, COL)
 
     def send(picked):
         return [picked[0]] + [move(picked[d], TURN[d]) for d in range(1, CHIPS)]

time: 125 us -> 125 us (level)
  Pallas kernels: 26.3 us -> 27.9 us
    pallas_call x8 -> x9, Pallas kernels: 26.3 us -> 27.9 us  [call(): pl.pallas_call(kernel, grid=(1,), out_shape=tuple((jax.ShapeDtypeStruct(s...]
  transfers between devices with their start and end apart: 24 -> 24, of which waited for: 11 -> 11; matrix products, arithmetic and copies ran while one was open for 1% -> 1% of each run, Pallas kernels for 15% -> 17%
where the time goes in v14:
time: 125 us; the launch traced here: 124 us
  starting transfers between devices  45.9 us (37%)
  waiting for transfers between devices  34.6 us (28%)
  Pallas kernels  27.9 us (22%)
  between operations  13.2 us (11%)
  local copies, waits for them, and re-layouts  1.96 us (2%)
    pallas_call x9, Pallas kernels, call(): pl.pallas_call(kernel, grid=(1,), out_shape=tuple((jax.ShapeDtypeStruct(s...  27.9 us
    all_to_all x3, starting transfers between devices, local(): over_row = lambda array: lax.all_to_all(array, 'row', 0, 0, tiled=True)  23 us
    ppermute x18, starting transfers between devices, local(): move = lambda array, pairs: lax.ppermute(array, COL, pairs)  22.8 us
    ppermute x18, waiting for transfers between devices, local(): move = lambda array, pairs: lax.ppermute(array, COL, pairs)  13.5 us
    all_to_all x3, waiting for transfers between devices, local(): over_row = lambda array: lax.all_to_all(array, 'row', 0, 0, tiled=True)  12.5 us
    all_gather x3, waiting for transfers between devices, local(): lax.all_gather(array, axes, axis=0, tiled=False)  7.83 us
  transfers between devices with their start and end apart: 24, of which 11 were waited for; matrix products, arithmetic and copies ran while one was open for 1% of the time, Pallas kernels for 17%

profile of v14, /device:TPU:2, one launch (start us, length us, event | category | flops | bytes accessed | tf_op | source)
XLA Modules:
  0.0 123.6 jit_solution(15406844547014930851)
XLA Ops:
  6.5 0.0 all-gather.7.cloned.1.call-start
  6.5 1.8 %cut.1 = bf16[768,256]{1,0:T(8,128)(2,1)} custom-call(bf16[6,3,256,256]{3,2,1,0:T(8,128)(2,1)} %bitcast.16), custom_call_target="tpu_custom_call" | custom-call | bytes 1048576 | tf_op jit(solution)/shard_map/cut/pallas_call | solution.py:47
  8.3 0.0 all-gather.7.cloned.1.call-update
  8.3 0.0 all-gather.9.cloned.1.call-start
  8.4 2.6 %level0.1 = (f32[32,256]{1,0:T(8,128)}, bf16[32,32,256]{2,1,0:T(8,128)(2,1)}, bf16[768,256]{1,0:T(8,128)(2,1)}, bf16[768,256]{1,0:T(8,128)(2,1)}) custom-call(s32[1]{0:T(128)} %bitcast.place, bf16[4,256,256]{2,1,0:T(8,128)(2,1)} %rhs.6, bf16[4,256,256]{2,1,0:T(8,128)(2,1)} %dinv.7, bf16[6,3,256,256]{3,2,1,0:T(8,128)(2,1)} %bitcast.17, ...), custom_call_target="tpu_custom_call" | custom-call | bytes 4194304 | tf_op jit(solution)/shard_map/level0/pallas_call | solution.py:47
  11.0 0.0 all-gather.9.cloned.1.call-update
  11.0 11.7 %all-to-all-start = ((bf16[32,32,256]{2,1,0:T(8,128)(2,1)}), bf16[32,32,256]{2,1,0:T(8,128)(2,1)}, u32[]{:S(2)}, u32[]{:S(2)}) async-start(bf16[32,32,256]{2,1,0:T(8,128)(2,1)} %get-tuple-element.62), calls=%async_computation | async-start | bytes 1048576 | tf_op jit(solution)/shard_map/all_to_all | solution.py:233
  22.7 0.0 all-gather.11.cloned.1.call-start
  22.8 0.7 all-gather.11.cloned.1.call-update
  23.5 0.7 copy.9
  24.2 3.0 %collective-permute-start.2 = (s32[3,6]{1,0:T(4,128)S(1)}, s32[3,6]{1,0:T(4,128)S(1)}, u32[]{:S(2)}, u32[]{:S(2)}) collective-permute-start(s32[3,6]{1,0:T(4,128)S(1)} %bitcast.34), channel_id=1, source_target_pairs={{0,6},{1,7},{2,0},{3,1},{4,2},{5,3},{6,4},{7,5},{8,14},{9,15},{10,... | collective-permute-start | bytes 224 | tf_op jit(solution)/shard_map/ppermute | solution.py:232
  27.1 0.6 collective-permute-start.1
  27.8 1.0 collective-permute-start
  28.7 0.7 copy.6
  29.4 0.0 collective-permute-done.2
  29.4 2.9 %collective-permute-done.1 = s32[3,6]{1,0:T(4,128)S(1)} collective-permute-done((s32[3,6]{1,0:T(4,128)S(1)}, s32[3,6]{1,0:T(4,128)S(1)}, u32[]{:S(2)}, u32[]{:S(2)}) %collective-permute-start.1) | collective-permute-done | bytes 104 | tf_op jit(solution)/shard_map/ppermute | solution.py:232
  32.3 0.2 collective-permute-done
  32.6 0.0 copy-start
  32.6 0.6 copy-done
  33.2 0.0 collective-permute-start.3
  33.2 1.3 %collective-permute-done.3.there = s32[4,3,6]{2,1,0:T(4,128)} collective-permute-done((s32[4,3,6]{2,1,0:T(4,128)S(1)}, s32[4,3,6]{2,1,0:T(4,128)}, u32[]{:S(2)}, u32[]{:S(2)}) %collective-permute-start.3) | collective-permute-done | bytes 320 | tf_op jit(solution)/shard_map/ppermute | solution.py:232
  34.5 5.1 %all-to-all-done.known = bf16[32,32,256]{2,1,0:T(8,128)(2,1)} async-done(((bf16[32,32,256]{2,1,0:T(8,128)(2,1)}), bf16[32,32,256]{2,1,0:T(8,128)(2,1)}, u32[]{:S(2)}, u32[]{:S(2)}) %all-to-all-start) | async-done | bytes 524320 | tf_op jit(solution)/shard_map/all_to_all | solution.py:233
  39.6 2.1 %pick13.1 = (bf16[2,6,32,256]{3,2,1,0:T(8,128)(2,1)}, bf16[2,6,32,256]{3,2,1,0:T(8,128)(2,1)}, bf16[2,6,32,256]{3,2,1,0:T(8,128)(2,1)}, bf16[2,6,32,256]{3,2,1,0:T(8,128)(2,1)}) custom-call(s32[1]{0:T(128)} %bitcast.place, s32[4,3,6]{2,1,0:T(4,128)} %copy-done, s32[4,3,6]{2,1,0:T(4,128)} %collective-permute-done.3.there, bf16[32,32,256]{2,1,0:T(8,128)(2,1)} %all-to-all-done.known), custom_call_target="tpu_custom_call" | custom-call | bytes 2097152 | tf_op jit(solution)/shard_map/pick13/pallas_call | solution.py:47
  41.6 0.0 collective-permute-start.7
  41.6 1.6 %collective-permute-start.4 = (bf16[2,6,32,256]{3,2,1,0:T(8,128)(2,1)}, bf16[2,6,32,256]{3,2,1,0:T(8,128)(2,1)}, u32[]{:S(2)}, u32[]{:S(2)}) collective-permute-start(bf16[2,6,32,256]{3,2,1,0:T(8,128)(2,1)} %get-tuple-element.70), channel_id=1, source_target_pairs={{0,2},{1,3},{2,4},{3,5},{4,6},{5,7},{6,0},{7,1},{8,10},{9,11},{10,... | collective-permute-start | bytes 589832 | tf_op jit(solution)/shard_map/ppermute | solution.py:232
  43.2 2.9 %collective-permute-start.5 = (bf16[2,6,32,256]{3,2,1,0:T(8,128)(2,1)}, bf16[2,6,32,256]{3,2,1,0:T(8,128)(2,1)}, u32[]{:S(2)}, u32[]{:S(2)}) collective-permute-start(bf16[2,6,32,256]{3,2,1,0:T(8,128)(2,1)} %get-tuple-element.71), channel_id=1, source_target_pairs={{0,4},{1,5},{2,6},{3,7},{4,0},{5,1},{6,2},{7,3},{8,12},{9,13},{10,... | collective-permute-start | bytes 589832 | tf_op jit(solution)/shard_map/ppermute | solution.py:232
  46.1 1.3 %collective-permute-start.6 = (bf16[2,6,32,256]{3,2,1,0:T(8,128)(2,1)}, bf16[2,6,32,256]{3,2,1,0:T(8,128)(2,1)}, u32[]{:S(2)}, u32[]{:S(2)}) collective-permute-start(bf16[2,6,32,256]{3,2,1,0:T(8,128)(2,1)} %get-tuple-element.72), channel_id=1, source_target_pairs={{0,6},{1,7},{2,0},{3,1},{4,2},{5,3},{6,4},{7,5},{8,14},{9,15},{10,... | collective-permute-start | bytes 589832 | tf_op jit(solution)/shard_map/ppermute | solution.py:232
  47.4 0.0 all-gather.7.cloned.1.call-done
  47.4 4.8 %level1.1 = (f32[32,256]{1,0:T(8,128)}, bf16[32,32,256]{2,1,0:T(8,128)(2,1)}) custom-call(s32[1]{0:T(128)} %bitcast.place, s32[4,3,6]{2,1,0:T(4,128)} %copy-done, s32[4,3,6]{2,1,0:T(4,128)} %collective-permute-done.3.there, s32[1,6]{1,0:T(1,128)} %bitcast.27, bf16[4,256,256]{2,1,0:T(8,128)(2,1)} %rhs.6, bf16[4,256,256]{2,1,0:T(8,128)(2,1)} %dinv.7, ...), custom_call_target="tpu_custom_call" | custom-call | flops 100663296 | bytes 3145728 | tf_op jit(solution)/shard_map/level1/pallas_call | solution.py:47
  52.3 0.0 collective-permute-done.4.refs_1_
  52.3 3.7 %collective-permute-done.5.refs_2_ = bf16[2,6,32,256]{3,2,1,0:T(8,128)(2,1)} collective-permute-done((bf16[2,6,32,256]{3,2,1,0:T(8,128)(2,1)}, bf16[2,6,32,256]{3,2,1,0:T(8,128)(2,1)}, u32[]{:S(2)}, u32[]{:S(2)}) %collective-permute-start.5) | collective-permute-done | bytes 196640 | tf_op jit(solution)/shard_map/ppermute | solution.py:232
  55.9 0.0 collective-permute-done.6.refs_3_
  55.9 5.6 %all-to-all-start.1 = ((bf16[32,32,256]{2,1,0:T(8,128)(2,1)}), bf16[32,32,256]{2,1,0:T(8,128)(2,1)}, u32[]{:S(2)}, u32[]{:S(2)}) async-start(bf16[32,32,256]{2,1,0:T(8,128)(2,1)} %get-tuple-element.73), calls=%async_computation.1 | async-start | bytes 1048576 | tf_op jit(solution)/shard_map/all_to_all | solution.py:233
  61.5 0.0 collective-permute-done.7.refs_5_.refs_7_.refs_9_
  61.6 3.0 %partial13.1 = (f32[32,256]{1,0:T(8,128)}, f32[32,256]{1,0:T(8,128)}, f32[32,256]{1,0:T(8,128)}, f32[32,256]{1,0:T(8,128)}, f32[32,256]{1,0:T(8,128)}, /*index=5...) custom-call(s32[1]{0:T(128)} %bitcast.place, s32[1,6]{1,0:T(1,128)} %bitcast.28, ...), custom_call_target="tpu_custom_call" | custom-call | flops 201326592 | bytes 2097152 | tf_op jit(solution)/shard_map/partial13/pallas_call | solution.py:47
  64.5 2.2 %collective-permute-start.8 = (f32[32,256]{1,0:T(8,128)}, f32[32,256]{1,0:T(8,128)}, u32[]{:S(2)}, u32[]{:S(2)}) collective-permute-start(f32[32,256]{1,0:T(8,128)} %get-tuple-element.80), channel_id=1, source_target_pairs={{0,6},{1,7},{2,0},{3,1},{4,2},{5,3},{6,4},{7,5},{8,14},{9,15},{10,... | collective-permute-start | bytes 98312 | tf_op jit(solution)/shard_map/ppermute | solution.py:232
  66.7 1.1 collective-permute-start.9
  67.8 0.8 collective-permute-start.10
  68.6 1.1 collective-permute-done.8.refs_3_
  69.7 3.5 %collective-permute-done.9.refs_4_ = f32[32,256]{1,0:T(8,128)} collective-permute-done((f32[32,256]{1,0:T(8,128)}, f32[32,256]{1,0:T(8,128)}, u32[]{:S(2)}, u32[]{:S(2)}) %collective-permute-start.9) | collective-permute-done | bytes 32800 | tf_op jit(solution)/shard_map/ppermute | solution.py:232
  73.2 0.8 collective-permute-done.10.refs_5_
  74.0 4.4 %all-to-all-done.1.known = bf16[32,32,256]{2,1,0:T(8,128)(2,1)} async-done(((bf16[32,32,256]{2,1,0:T(8,128)(2,1)}), bf16[32,32,256]{2,1,0:T(8,128)(2,1)}, u32[]{:S(2)}, u32[]{:S(2)}) %all-to-all-start.1) | async-done | bytes 524320 | tf_op jit(solution)/shard_map/all_to_all | solution.py:233
  78.4 1.8 %pick4.1 = (bf16[1,6,32,256]{3,2,1,0:T(8,128)(2,1)}, bf16[1,6,32,256]{3,2,1,0:T(8,128)(2,1)}, bf16[1,6,32,256]{3,2,1,0:T(8,128)(2,1)}, bf16[1,6,32,256]{3,2,1,0:T(8,128)(2,1)}) custom-call(s32[1]{0:T(128)} %bitcast.place, s32[4,3,6]{2,1,0:T(4,128)} %copy-done, s32[4,3,6]{2,1,0:T(4,128)} %collective-permute-done.3.there, ...), custom_call_target="tpu_custom_call" | custom-call | bytes 2097152 | tf_op jit(solution)/shard_map/pick4/pallas_call | solution.py:47
  80.2 0.0 all-gather.9.cloned.1.call-done
  80.2 0.0 collective-permute-start.11
  80.2 0.7 collective-permute-start.12
  80.9 3.2 %collective-permute-start.13 = (bf16[1,6,32,256]{3,2,1,0:T(8,128)(2,1)}, bf16[1,6,32,256]{3,2,1,0:T(8,128)(2,1)}, u32[]{:S(2)}, u32[]{:S(2)}) collective-permute-start(bf16[1,6,32,256]{3,2,1,0:T(8,128)(2,1)} %get-tuple-element.98), channel_id=1, source_target_pairs={{0,4},{1,5},{2,6},{3,7},{4,0},{5,1},{6,2},{7,3},{8,12},{9,13},{10,... | collective-permute-start | bytes 294920 | tf_op jit(solution)/shard_map/ppermute | solution.py:232
  84.1 1.1 collective-permute-start.14
  85.1 0.0 collective-permute-done.11.refs_1_
  85.1 4.8 %level2.1 = (f32[32,256]{1,0:T(8,128)}, bf16[32,32,256]{2,1,0:T(8,128)(2,1)}) custom-call(s32[1]{0:T(128)} %bitcast.place, s32[4,3,6]{2,1,0:T(4,128)} %copy-done, s32[4,3,6]{2,1,0:T(4,128)} %collective-permute-done.3.there, s32[1,6]{1,0:T(1,128)} %bitcast.29, bf16[4,256,256]{2,1,0:T(8,128)(2,1)} %rhs.6, bf16[4,256,256]{2,1,0:T(8,128)(2,1)} %dinv.7, ...), custom_call_target="tpu_custom_call" | custom-call | flops 100663296 | bytes 3145728 | tf_op jit(solution)/shard_map/level2/pallas_call | solution.py:47
  90.0 0.0 collective-permute-done.12.refs_1_
  90.0 0.0 collective-permute-done.13.refs_2_
  90.0 0.0 collective-permute-done.14.refs_3_
  90.0 5.6 %all-to-all-start.2 = ((bf16[32,32,256]{2,1,0:T(8,128)(2,1)}), bf16[32,32,256]{2,1,0:T(8,128)(2,1)}, u32[]{:S(2)}, u32[]{:S(2)}) async-start(bf16[32,32,256]{2,1,0:T(8,128)(2,1)} %get-tuple-element.100), calls=%async_computation.2 | async-start | bytes 1048576 | tf_op jit(solution)/shard_map/all_to_all | solution.py:233
  95.7 2.4 %partial4.1 = (f32[32,256]{1,0:T(8,128)}, f32[32,256]{1,0:T(8,128)}, f32[32,256]{1,0:T(8,128)}, f32[32,256]{1,0:T(8,128)}) custom-call(s32[1]{0:T(128)} %bitcast.place, s32[1,6]{1,0:T(1,128)} %bitcast.30, bf16[1,6,32,256]{3,2,1,0:T(8,128)(2,1)} %get-tuple-element.102.refs_0_, bf16[1,6,32,256]{3,2,1,0:T(8,128)(2,1)} %collective-permute-done.12.refs_1_, ...), custom_call_target="tpu_custom_call" | custom-call | flops 201326592 | bytes 2097152 | tf_op jit(solution)/shard_map/partial4/pallas_call | solution.py:47
  98.1 2.5 %collective-permute-start.15 = (f32[32,256]{1,0:T(8,128)}, f32[32,256]{1,0:T(8,128)}, u32[]{:S(2)}, u32[]{:S(2)}) collective-permute-start(f32[32,256]{1,0:T(8,128)} %get-tuple-element.111), channel_id=1, source_target_pairs={{0,6},{1,7},{2,0},{3,1},{4,2},{5,3},{6,4},{7,5},{8,14},{9,15},{10,... | collective-permute-start | bytes 98312 | tf_op jit(solution)/shard_map/ppermute | solution.py:232
  100.6 0.9 collective-permute-start.16
  101.4 0.1 collective-permute-start.17
  101.5 7.8 %all-gather.11.cloned.1.call-done = bf16[6144,256]{1,0:T(8,128)(2,1)} async-done(((bf16[768,256]{1,0:T(8,128)(2,1)}), bf16[6144,256]{1,0:T(8,128)(2,1)}) %all-gather.11.cloned.1.call-update) | async-done | bytes 3145744 | tf_op jit(solution)/shard_map/all_gather | solution.py:235
  109.3 0.0 collective-permute-done.15.refs_2_
  109.3 0.0 collective-permute-done.16.refs_3_
  109.3 0.0 collective-permute-done.17.refs_4_
  109.3 3.1 %all-to-all-done.2.known = bf16[32,32,256]{2,1,0:T(8,128)(2,1)} async-done(((bf16[32,32,256]{2,1,0:T(8,128)(2,1)}), bf16[32,32,256]{2,1,0:T(8,128)(2,1)}, u32[]{:S(2)}, u32[]{:S(2)}) %all-to-all-start.2) | async-done | bytes 524320 | tf_op jit(solution)/shard_map/all_to_all | solution.py:233
  112.4 4.6 %level3.1 = f32[4,32,256]{2,1,0:T(8,128)} custom-call(s32[1]{0:T(128)} %bitcast.place, s32[4,3,6]{2,1,0:T(4,128)} %copy-done, s32[4,3,6]{2,1,0:T(4,128)} %collective-permute-done.3.there, s32[1,6]{1,0:T(1,128)} %bitcast.31, bf16[4,256,256]{2,1,0:T(8,128)(2,1)} %rhs.6, bf16[4,256,256]{2,1,0:T(8,128)(2,1)} %dinv.7, bf16[32,32,256]{2,1,0:T(8,128)(2,1)} %all-to-all-done.2.known, ...), custom_call_target="tpu_custom_call" | custom-call | flops 100663296 | bytes 3145728 | tf_op jit(solution)/shard_map/level3/pallas_call | solution.py:47
  (1 shorter events, 0.0 us)
Async XLA Ops:
  6.5 40.9 %all-gather.7.cloned.1.call-start = ((), (), s32[]{:S(2)}) async-start(), calls=%async_computation.3 | async-start | bytes 3538944 | tf_op jit(solution)/shard_map/all_gather | solution.py:235
  8.3 71.9 %all-gather.9.cloned.1.call-start = ((), (), s32[]{:S(2)}) async-start(), calls=%async_computation.4 | async-start | bytes 1966080 | tf_op jit(solution)/shard_map/all_gather | solution.py:235
  11.0 28.6 %all-to-all-start = ((bf16[32,32,256]{2,1,0:T(8,128)(2,1)}), bf16[32,32,256]{2,1,0:T(8,128)(2,1)}, u32[]{:S(2)}, u32[]{:S(2)}) async-start(bf16[32,32,256]{2,1,0:T(8,128)(2,1)} %get-tuple-element.62), calls=%async_computation | async-start | bytes 1048576 | tf_op jit(solution)/shard_map/all_to_all | solution.py:233
  22.7 86.6 %all-gather.11.cloned.1.call-start = ((), (), s32[]{:S(2)}) async-start(), calls=%async_computation.5 | async-start | bytes 3538944 | tf_op jit(solution)/shard_map/all_gather | solution.py:235
  24.2 5.3 %collective-permute-start.2 = (s32[3,6]{1,0:T(4,128)S(1)}, s32[3,6]{1,0:T(4,128)S(1)}, u32[]{:S(2)}, u32[]{:S(2)}) collective-permute-start(s32[3,6]{1,0:T(4,128)S(1)} %bitcast.34), channel_id=1, source_target_pairs={{0,6},{1,7},{2,0},{3,1},{4,2},{5,3},{6,4},{7,5},{8,14},{9,15},{10,... | collective-permute-start | bytes 224 | tf_op jit(solution)/shard_map/ppermute | solution.py:232
  27.1 5.2 %collective-permute-start.1 = (s32[3,6]{1,0:T(4,128)S(1)}, s32[3,6]{1,0:T(4,128)S(1)}, u32[]{:S(2)}, u32[]{:S(2)}) collective-permute-start(s32[3,6]{1,0:T(4,128)S(1)} %bitcast.35), channel_id=1, source_target_pairs={{0,4},{1,5},{2,6},{3,7},{4,0},{5,1},{6,2},{7,3},{8,12},{9,13},{10,... | collective-permute-start | bytes 224 | tf_op jit(solution)/shard_map/ppermute | solution.py:232
  27.8 4.8 %collective-permute-start = (s32[3,6]{1,0:T(4,128)S(1)}, s32[3,6]{1,0:T(4,128)S(1)}, u32[]{:S(2)}, u32[]{:S(2)}) collective-permute-start(s32[3,6]{1,0:T(4,128)S(1)} %bitcast.36), channel_id=1, source_target_pairs={{0,2},{1,3},{2,4},{3,5},{4,6},{5,7},{6,0},{7,1},{8,10},{9,11},{10,... | collective-permute-start | bytes 224 | tf_op jit(solution)/shard_map/ppermute | solution.py:232
  32.6 0.6 copy-start
  33.2 1.3 %collective-permute-start.3 = (s32[4,3,6]{2,1,0:T(4,128)S(1)}, s32[4,3,6]{2,1,0:T(4,128)}, u32[]{:S(2)}, u32[]{:S(2)}) collective-permute-start(s32[4,3,6]{2,1,0:T(4,128)S(1)} %pad_add_fusion.here), channel_id=1, source_target_pairs={{0,1},{1,0},{2,3},{3,2},{4,5},{5,4},{6,7},{7,6},{8,9},{9,8},{10,11... | collective-permute-start | bytes 872 | tf_op jit(solution)/shard_map/ppermute | solution.py:232
  41.6 19.9 %collective-permute-start.7 = (bf16[6,3,256,256]{3,2,1,0:T(8,128)(2,1)}, bf16[6,3,256,256]{3,2,1,0:T(8,128)(2,1)}, u32[]{:S(2)}, u32[]{:S(2)}) collective-permute-start(bf16[6,3,256,256]{3,2,1,0:T(8,128)(2,1)} %bitcast.19), channel_id=1, source_target_pairs={{0,1},{1,0},{2,3},{3,2},{4,5},{5,4},{6,7},{7,6},{8,9},{9,8},{10,11... | collective-permute-start | bytes 7077896 | tf_op jit(solution)/shard_map/ppermute | solution.py:232
  41.6 10.6 %collective-permute-start.4 = (bf16[2,6,32,256]{3,2,1,0:T(8,128)(2,1)}, bf16[2,6,32,256]{3,2,1,0:T(8,128)(2,1)}, u32[]{:S(2)}, u32[]{:S(2)}) collective-permute-start(bf16[2,6,32,256]{3,2,1,0:T(8,128)(2,1)} %get-tuple-element.70), channel_id=1, source_target_pairs={{0,2},{1,3},{2,4},{3,5},{4,6},{5,7},{6,0},{7,1},{8,10},{9,11},{10,... | collective-permute-start | bytes 589832 | tf_op jit(solution)/shard_map/ppermute | solution.py:232
  43.2 12.7 %collective-permute-start.5 = (bf16[2,6,32,256]{3,2,1,0:T(8,128)(2,1)}, bf16[2,6,32,256]{3,2,1,0:T(8,128)(2,1)}, u32[]{:S(2)}, u32[]{:S(2)}) collective-permute-start(bf16[2,6,32,256]{3,2,1,0:T(8,128)(2,1)} %get-tuple-element.71), channel_id=1, source_target_pairs={{0,4},{1,5},{2,6},{3,7},{4,0},{5,1},{6,2},{7,3},{8,12},{9,13},{10,... | collective-permute-start | bytes 589832 | tf_op jit(solution)/shard_map/ppermute | solution.py:232
  46.1 9.8 %collective-permute-start.6 = (bf16[2,6,32,256]{3,2,1,0:T(8,128)(2,1)}, bf16[2,6,32,256]{3,2,1,0:T(8,128)(2,1)}, u32[]{:S(2)}, u32[]{:S(2)}) collective-permute-start(bf16[2,6,32,256]{3,2,1,0:T(8,128)(2,1)} %get-tuple-element.72), channel_id=1, source_target_pairs={{0,6},{1,7},{2,0},{3,1},{4,2},{5,3},{6,4},{7,5},{8,14},{9,15},{10,... | collective-permute-start | bytes 589832 | tf_op jit(solution)/shard_map/ppermute | solution.py:232
  55.9 22.4 %all-to-all-start.1 = ((bf16[32,32,256]{2,1,0:T(8,128)(2,1)}), bf16[32,32,256]{2,1,0:T(8,128)(2,1)}, u32[]{:S(2)}, u32[]{:S(2)}) async-start(bf16[32,32,256]{2,1,0:T(8,128)(2,1)} %get-tuple-element.73), calls=%async_computation.1 | async-start | bytes 1048576 | tf_op jit(solution)/shard_map/all_to_all | solution.py:233
  64.5 5.2 %collective-permute-start.8 = (f32[32,256]{1,0:T(8,128)}, f32[32,256]{1,0:T(8,128)}, u32[]{:S(2)}, u32[]{:S(2)}) collective-permute-start(f32[32,256]{1,0:T(8,128)} %get-tuple-element.80), channel_id=1, source_target_pairs={{0,6},{1,7},{2,0},{3,1},{4,2},{5,3},{6,4},{7,5},{8,14},{9,15},{10,... | collective-permute-start | bytes 98312 | tf_op jit(solution)/shard_map/ppermute | solution.py:232
  66.7 6.5 %collective-permute-start.9 = (f32[32,256]{1,0:T(8,128)}, f32[32,256]{1,0:T(8,128)}, u32[]{:S(2)}, u32[]{:S(2)}) collective-permute-start(f32[32,256]{1,0:T(8,128)} %get-tuple-element.81), channel_id=1, source_target_pairs={{0,4},{1,5},{2,6},{3,7},{4,0},{5,1},{6,2},{7,3},{8,12},{9,13},{10,... | collective-permute-start | bytes 98312 | tf_op jit(solution)/shard_map/ppermute | solution.py:232
  67.8 6.2 %collective-permute-start.10 = (f32[32,256]{1,0:T(8,128)}, f32[32,256]{1,0:T(8,128)}, u32[]{:S(2)}, u32[]{:S(2)}) collective-permute-start(f32[32,256]{1,0:T(8,128)} %get-tuple-element.82), channel_id=1, source_target_pairs={{0,2},{1,3},{2,4},{3,5},{4,6},{5,7},{6,0},{7,1},{8,10},{9,11},{10,... | collective-permute-start | bytes 98312 | tf_op jit(solution)/shard_map/ppermute | solution.py:232
  80.2 5.0 %collective-permute-start.11 = (bf16[4,768,256]{2,1,0:T(8,128)(2,1)}, bf16[4,768,256]{2,1,0:T(8,128)(2,1)}, u32[]{:S(2)}, u32[]{:S(2)}) collective-permute-start(bf16[4,768,256]{2,1,0:T(8,128)(2,1)} %bitcast.25), channel_id=1, source_target_pairs={{0,1},{1,0},{2,3},{3,2},{4,5},{5,4},{6,7},{7,6},{8,9},{9,8},{10,11... | collective-permute-start | bytes 4718600 | tf_op jit(solution)/shard_map/ppermute | solution.py:232
  80.2 9.8 %collective-permute-start.12 = (bf16[1,6,32,256]{3,2,1,0:T(8,128)(2,1)}, bf16[1,6,32,256]{3,2,1,0:T(8,128)(2,1)}, u32[]{:S(2)}, u32[]{:S(2)}) collective-permute-start(bf16[1,6,32,256]{3,2,1,0:T(8,128)(2,1)} %get-tuple-element.97), channel_id=1, source_target_pairs={{0,2},{1,3},{2,4},{3,5},{4,6},{5,7},{6,0},{7,1},{8,10},{9,11},{10,... | collective-permute-start | bytes 294920 | tf_op jit(solution)/shard_map/ppermute | solution.py:232
  80.9 9.1 %collective-permute-start.13 = (bf16[1,6,32,256]{3,2,1,0:T(8,128)(2,1)}, bf16[1,6,32,256]{3,2,1,0:T(8,128)(2,1)}, u32[]{:S(2)}, u32[]{:S(2)}) collective-permute-start(bf16[1,6,32,256]{3,2,1,0:T(8,128)(2,1)} %get-tuple-element.98), channel_id=1, source_target_pairs={{0,4},{1,5},{2,6},{3,7},{4,0},{5,1},{6,2},{7,3},{8,12},{9,13},{10,... | collective-permute-start | bytes 294920 | tf_op jit(solution)/shard_map/ppermute | solution.py:232
  84.1 5.9 %collective-permute-start.14 = (bf16[1,6,32,256]{3,2,1,0:T(8,128)(2,1)}, bf16[1,6,32,256]{3,2,1,0:T(8,128)(2,1)}, u32[]{:S(2)}, u32[]{:S(2)}) collective-permute-start(bf16[1,6,32,256]{3,2,1,0:T(8,128)(2,1)} %get-tuple-element.99), channel_id=1, source_target_pairs={{0,6},{1,7},{2,0},{3,1},{4,2},{5,3},{6,4},{7,5},{8,14},{9,15},{10,... | collective-permute-start | bytes 294920 | tf_op jit(solution)/shard_map/ppermute | solution.py:232
  90.0 22.4 %all-to-all-start.2 = ((bf16[32,32,256]{2,1,0:T(8,128)(2,1)}), bf16[32,32,256]{2,1,0:T(8,128)(2,1)}, u32[]{:S(2)}, u32[]{:S(2)}) async-start(bf16[32,32,256]{2,1,0:T(8,128)(2,1)} %get-tuple-element.100), calls=%async_computation.2 | async-start | bytes 1048576 | tf_op jit(solution)/shard_map/all_to_all | solution.py:233
  98.1 11.2 %collective-permute-start.15 = (f32[32,256]{1,0:T(8,128)}, f32[32,256]{1,0:T(8,128)}, u32[]{:S(2)}, u32[]{:S(2)}) collective-permute-start(f32[32,256]{1,0:T(8,128)} %get-tuple-element.111), channel_id=1, source_target_pairs={{0,6},{1,7},{2,0},{3,1},{4,2},{5,3},{6,4},{7,5},{8,14},{9,15},{10,... | collective-permute-start | bytes 98312 | tf_op jit(solution)/shard_map/ppermute | solution.py:232
  100.6 8.8 %collective-permute-start.16 = (f32[32,256]{1,0:T(8,128)}, f32[32,256]{1,0:T(8,128)}, u32[]{:S(2)}, u32[]{:S(2)}) collective-permute-start(f32[32,256]{1,0:T(8,128)} %get-tuple-element.112), channel_id=1, source_target_pairs={{0,4},{1,5},{2,6},{3,7},{4,0},{5,1},{6,2},{7,3},{8,12},{9,13},{10,... | collective-permute-start | bytes 98312 | tf_op jit(solution)/shard_map/ppermute | solution.py:232
  101.4 7.9 %collective-permute-start.17 = (f32[32,256]{1,0:T(8,128)}, f32[32,256]{1,0:T(8,128)}, u32[]{:S(2)}, u32[]{:S(2)}) collective-permute-start(f32[32,256]{1,0:T(8,128)} %get-tuple-element.113), channel_id=1, source_target_pairs={{0,2},{1,3},{2,4},{3,5},{4,6},{5,7},{6,0},{7,1},{8,10},{9,11},{10,... | collective-permute-start | bytes 98312 | tf_op jit(solution)/shard_map/ppermute | solution.py:232
Sparse Core Ops, SparseCore 0:
  9.2 33.4 all-gather.6
  44.4 31.2 all-gather.8
  77.6 31.6 all-gather.10

commit v15 on v12

--- a/solution.py
+++ b/solution.py
@@ -221,7 +221,7 @@
     here = jnp.stack([own] + [move(own, TURN[d]) for d in range(1, CHIPS)])
     there = move(here, SWAP)
     answer0, spread0, *cuts = first_call(place, rhs, dinv, tiles, (0, 2, 5))
-    gathered0, gathered2, gathered5 = gather(cuts[0], "chip"), gather(cuts[1], COL), gather(cuts[2], COL)
+    gathered0, gathered2, gathered5 = gather(cuts[0], "chip"), gather(cuts[1], "chip"), gather(cuts[2], COL)
 
     def send(picked):
         return [picked[0]] + [move(picked[d], TURN[d]) for d in range(1, CHIPS)]
@@ -248,7 +248,9 @@
     picked = pick_call("pick4", (4,), place, here, there, known1)
     known1, *picked = lax.optimization_barrier((known1, *picked))
     got = send(picked)
-    answer2, spread2 = level_call(2, 2, place, here, there, live, rhs, dinv, known1, [gathered2], back2, [])
+    gathered2, _ = lax.optimization_barrier((gathered2, picked[0]))
+    gathered2 = [gathered2, move(gathered2, SWAP)]
+    answer2, spread2 = level_call(2, 2, place, here, there, live, rhs, dinv, known1, gathered2, back2, [])
     spread2, *got = lax.optimization_barrier((spread2, *got))
     known2 = over_row(spread2)
 

time: 127 us -> 132 us (1.039)
  waiting for transfers between devices: 32 us -> 39.3 us
  local copies, waits for them, and re-layouts: 1.96 us -> 0.6 us
    ppermute x18 -> x19, waiting for transfers between devices: 14.1 us -> 18.3 us  [local(): move = lambda array, pairs: lax.ppermute(array, COL, pairs)]
    all_to_all x3, waiting for transfers between devices: 14.9 us -> 18.7 us  [local(): over_row = lambda array: lax.all_to_all(array, 'row', 0, 0, tiled=True)]
    ppermute x18 -> x19, starting transfers between devices: 25.1 us -> 24.3 us  [local(): move = lambda array, pairs: lax.ppermute(array, COL, pairs)]
  transfers between devices with their start and end apart: 24 -> 25, of which waited for: 15 -> 17; matrix products, arithmetic and copies ran while one was open for 1% -> 0% of each run, Pallas kernels for 15% -> 14%
where the time goes in v15:
time: 132 us; the launch traced here: 131 us
  starting transfers between devices  51.9 us (39%)
  waiting for transfers between devices  39.3 us (30%)
  Pallas kernels  26.2 us (20%)
  between operations  13.2 us (10%)
    all_to_all x3, starting transfers between devices, local(): over_row = lambda array: lax.all_to_all(array, 'row', 0, 0, tiled=True)  27.6 us
    pallas_call x8, Pallas kernels, call(): pl.pallas_call(kernel, grid=(1,), out_shape=tuple((jax.ShapeDtypeStruct(s...  26.2 us
    ppermute x19, starting transfers between devices, local(): move = lambda array, pairs: lax.ppermute(array, COL, pairs)  24.3 us
    all_to_all x3, waiting for transfers between devices, local(): over_row = lambda array: lax.all_to_all(array, 'row', 0, 0, tiled=True)  18.7 us
    ppermute x19, waiting for transfers between devices, local(): move = lambda array, pairs: lax.ppermute(array, COL, pairs)  18.3 us
  transfers between devices with their start and end apart: 25, of which 17 were waited for; matrix products, arithmetic and copies ran while one was open for 0% of the time, Pallas kernels for 14%

profile of v15, /device:TPU:2, one launch (start us, length us, event | category | flops | bytes accessed | tf_op | source)
XLA Modules:
  0.0 131.3 jit_solution(6214422686222745878)
XLA Ops:
  6.5 0.0 all-gather.7.cloned.1.call-start
  6.5 2.7 %level0.1 = (f32[32,256]{1,0:T(8,128)}, bf16[32,32,256]{2,1,0:T(8,128)(2,1)}, bf16[768,256]{1,0:T(8,128)(2,1)}, bf16[768,256]{1,0:T(8,128)(2,1)}, bf16[768,256]{1,0:T(8,128)(2,1)}) custom-call(s32[1]{0:T(128)} %bitcast.place, bf16[4,256,256]{2,1,0:T(8,128)(2,1)} %rhs.7, bf16[4,256,256]{2,1,0:T(8,128)(2,1)} %dinv.7, bf16[6,3,256,256]{3,2,1,0:T(8,128)(2,1)} %bitcast.16, ...), custom_call_target="tpu_custom_call" | custom-call | bytes 4194304 | tf_op jit(solution)/shard_map/level0/pallas_call | solution.py:47
  9.3 0.0 copy-start.1
  9.3 0.0 all-gather.7.cloned.1.call-update
  9.3 0.0 all-gather.9.cloned.1.call-start
  9.4 0.7 all-gather.9.cloned.1.call-update
  10.1 11.7 %all-to-all-start = ((bf16[32,32,256]{2,1,0:T(8,128)(2,1)}), bf16[32,32,256]{2,1,0:T(8,128)(2,1)}, u32[]{:S(2)}, u32[]{:S(2)}) async-start(bf16[32,32,256]{2,1,0:T(8,128)(2,1)} %get-tuple-element.64), calls=%async_computation | async-start | bytes 1048576 | tf_op jit(solution)/shard_map/all_to_all | solution.py:215
  21.7 0.0 all-gather.11.cloned.1.call-start
  21.8 0.7 all-gather.11.cloned.1.call-update
  22.5 0.0 copy-done.1
  22.5 1.7 %collective-permute-start = (s32[3,6]{1,0:T(4,128)S(1)}, s32[3,6]{1,0:T(4,128)S(1)}, u32[]{:S(2)}, u32[]{:S(2)}) collective-permute-start(s32[3,6]{1,0:T(4,128)S(1)} %bitcast.35), channel_id=1, source_target_pairs={{0,2},{1,3},{2,4},{3,5},{4,6},{5,7},{6,0},{7,1},{8,10},{9,11},{10,... | collective-permute-start | bytes 224 | tf_op jit(solution)/shard_map/ppermute | solution.py:214
  24.2 2.9 %collective-permute-start.1 = (s32[3,6]{1,0:T(4,128)S(1)}, s32[3,6]{1,0:T(4,128)S(1)}, u32[]{:S(2)}, u32[]{:S(2)}) collective-permute-start(s32[3,6]{1,0:T(4,128)S(1)} %bitcast.36), channel_id=1, source_target_pairs={{0,4},{1,5},{2,6},{3,7},{4,0},{5,1},{6,2},{7,3},{8,12},{9,13},{10,... | collective-permute-start | bytes 224 | tf_op jit(solution)/shard_map/ppermute | solution.py:214
  27.1 1.3 %collective-permute-start.2 = (s32[3,6]{1,0:T(4,128)S(1)}, s32[3,6]{1,0:T(4,128)S(1)}, u32[]{:S(2)}, u32[]{:S(2)}) collective-permute-start(s32[3,6]{1,0:T(4,128)S(1)} %bitcast.37), channel_id=1, source_target_pairs={{0,6},{1,7},{2,0},{3,1},{4,2},{5,3},{6,4},{7,5},{8,14},{9,15},{10,... | collective-permute-start | bytes 224 | tf_op jit(solution)/shard_map/ppermute | solution.py:214
  28.4 0.0 collective-permute-done
  28.4 0.9 collective-permute-done.1
  29.4 1.3 collective-permute-done.2
  30.7 0.0 copy-start
  30.7 0.6 copy-done
  31.3 0.0 collective-permute-start.3
  31.3 1.3 collective-permute-done.3.there
  32.6 6.1 %all-to-all-done.known = bf16[32,32,256]{2,1,0:T(8,128)(2,1)} async-done(((bf16[32,32,256]{2,1,0:T(8,128)(2,1)}), bf16[32,32,256]{2,1,0:T(8,128)(2,1)}, u32[]{:S(2)}, u32[]{:S(2)}) %all-to-all-start) | async-done | bytes 524320 | tf_op jit(solution)/shard_map/all_to_all | solution.py:215
  38.6 2.0 %pick13.1 = (bf16[2,6,32,256]{3,2,1,0:T(8,128)(2,1)}, bf16[2,6,32,256]{3,2,1,0:T(8,128)(2,1)}, bf16[2,6,32,256]{3,2,1,0:T(8,128)(2,1)}, bf16[2,6,32,256]{3,2,1,0:T(8,128)(2,1)}) custom-call(s32[1]{0:T(128)} %bitcast.place, s32[4,3,6]{2,1,0:T(4,128)} %copy-done, s32[4,3,6]{2,1,0:T(4,128)} %collective-permute-done.3.there, bf16[32,32,256]{2,1,0:T(8,128)(2,1)} %all-to-all-done.known), custom_call_target="tpu_custom_call" | custom-call | bytes 2097152 | tf_op jit(solution)/shard_map/pick13/pallas_call | solution.py:47
  40.6 0.9 all-gather.7.cloned.1.call-done
  41.5 0.0 collective-permute-start.4
  41.5 0.5 collective-permute-start.8
  42.0 0.7 collective-permute-start.5
  42.7 2.9 %collective-permute-start.6 = (bf16[2,6,32,256]{3,2,1,0:T(8,128)(2,1)}, bf16[2,6,32,256]{3,2,1,0:T(8,128)(2,1)}, u32[]{:S(2)}, u32[]{:S(2)}) collective-permute-start(bf16[2,6,32,256]{3,2,1,0:T(8,128)(2,1)} %get-tuple-element.75), channel_id=1, source_target_pairs={{0,4},{1,5},{2,6},{3,7},{4,0},{5,1},{6,2},{7,3},{8,12},{9,13},{10,... | collective-permute-start | bytes 589832 | tf_op jit(solution)/shard_map/ppermute | solution.py:214
  45.6 1.3 %collective-permute-start.7 = (bf16[2,6,32,256]{3,2,1,0:T(8,128)(2,1)}, bf16[2,6,32,256]{3,2,1,0:T(8,128)(2,1)}, u32[]{:S(2)}, u32[]{:S(2)}) collective-permute-start(bf16[2,6,32,256]{3,2,1,0:T(8,128)(2,1)} %get-tuple-element.76), channel_id=1, source_target_pairs={{0,6},{1,7},{2,0},{3,1},{4,2},{5,3},{6,4},{7,5},{8,14},{9,15},{10,... | collective-permute-start | bytes 589832 | tf_op jit(solution)/shard_map/ppermute | solution.py:214
  47.0 0.0 collective-permute-done.4.refs_1_
  47.0 4.8 %level1.1 = (f32[32,256]{1,0:T(8,128)}, bf16[32,32,256]{2,1,0:T(8,128)(2,1)}) custom-call(s32[1]{0:T(128)} %bitcast.place, s32[4,3,6]{2,1,0:T(4,128)} %copy-done, s32[4,3,6]{2,1,0:T(4,128)} %collective-permute-done.3.there, s32[1,6]{1,0:T(1,128)} %bitcast.28, bf16[4,256,256]{2,1,0:T(8,128)(2,1)} %rhs.7, bf16[4,256,256]{2,1,0:T(8,128)(2,1)} %dinv.7, ...), custom_call_target="tpu_custom_call" | custom-call | flops 100663296 | bytes 3145728 | tf_op jit(solution)/shard_map/level1/pallas_call | solution.py:47
  51.7 0.0 collective-permute-done.5.refs_1_
  51.7 3.3 %collective-permute-done.6.refs_2_ = bf16[2,6,32,256]{3,2,1,0:T(8,128)(2,1)} collective-permute-done((bf16[2,6,32,256]{3,2,1,0:T(8,128)(2,1)}, bf16[2,6,32,256]{3,2,1,0:T(8,128)(2,1)}, u32[]{:S(2)}, u32[]{:S(2)}) %collective-permute-start.6) | collective-permute-done | bytes 196640 | tf_op jit(solution)/shard_map/ppermute | solution.py:214
  55.0 0.2 collective-permute-done.7.refs_3_
  55.2 10.2 %all-to-all-start.1 = ((bf16[32,32,256]{2,1,0:T(8,128)(2,1)}), bf16[32,32,256]{2,1,0:T(8,128)(2,1)}, u32[]{:S(2)}, u32[]{:S(2)}) async-start(bf16[32,32,256]{2,1,0:T(8,128)(2,1)} %get-tuple-element.77), calls=%async_computation.1 | async-start | bytes 1048576 | tf_op jit(solution)/shard_map/all_to_all | solution.py:215
  65.4 0.0 collective-permute-done.8.refs_5_.refs_7_.refs_9_
  65.4 3.0 %partial13.1 = (f32[32,256]{1,0:T(8,128)}, f32[32,256]{1,0:T(8,128)}, f32[32,256]{1,0:T(8,128)}, f32[32,256]{1,0:T(8,128)}, f32[32,256]{1,0:T(8,128)}, /*index=5...) custom-call(s32[1]{0:T(128)} %bitcast.place, s32[1,6]{1,0:T(1,128)} %bitcast.29, ...), custom_call_target="tpu_custom_call" | custom-call | flops 201326592 | bytes 2097152 | tf_op jit(solution)/shard_map/partial13/pallas_call | solution.py:47
  68.4 1.8 %collective-permute-start.10 = (f32[32,256]{1,0:T(8,128)}, f32[32,256]{1,0:T(8,128)}, u32[]{:S(2)}, u32[]{:S(2)}) collective-permute-start(f32[32,256]{1,0:T(8,128)} %get-tuple-element.85), channel_id=1, source_target_pairs={{0,4},{1,5},{2,6},{3,7},{4,0},{5,1},{6,2},{7,3},{8,12},{9,13},{10,... | collective-permute-start | bytes 98312 | tf_op jit(solution)/shard_map/ppermute | solution.py:214
  70.3 1.7 %collective-permute-start.11 = (f32[32,256]{1,0:T(8,128)}, f32[32,256]{1,0:T(8,128)}, u32[]{:S(2)}, u32[]{:S(2)}) collective-permute-start(f32[32,256]{1,0:T(8,128)} %get-tuple-element.86), channel_id=1, source_target_pairs={{0,2},{1,3},{2,4},{3,5},{4,6},{5,7},{6,0},{7,1},{8,10},{9,11},{10,... | collective-permute-start | bytes 98312 | tf_op jit(solution)/shard_map/ppermute | solution.py:214
  72.0 1.5 %collective-permute-start.9 = (f32[32,256]{1,0:T(8,128)}, f32[32,256]{1,0:T(8,128)}, u32[]{:S(2)}, u32[]{:S(2)}) collective-permute-start(f32[32,256]{1,0:T(8,128)} %get-tuple-element.84), channel_id=1, source_target_pairs={{0,6},{1,7},{2,0},{3,1},{4,2},{5,3},{6,4},{7,5},{8,14},{9,15},{10,... | collective-permute-start | bytes 98312 | tf_op jit(solution)/shard_map/ppermute | solution.py:214
  73.5 1.0 collective-permute-done.10.refs_4_
  74.5 1.2 collective-permute-done.11.refs_5_
  75.7 0.5 collective-permute-done.9.refs_3_
  76.2 5.2 %all-to-all-done.1.known = bf16[32,32,256]{2,1,0:T(8,128)(2,1)} async-done(((bf16[32,32,256]{2,1,0:T(8,128)(2,1)}), bf16[32,32,256]{2,1,0:T(8,128)(2,1)}, u32[]{:S(2)}, u32[]{:S(2)}) %all-to-all-start.1) | async-done | bytes 524320 | tf_op jit(solution)/shard_map/all_to_all | solution.py:215
  81.4 1.8 %pick4.1 = (bf16[1,6,32,256]{3,2,1,0:T(8,128)(2,1)}, bf16[1,6,32,256]{3,2,1,0:T(8,128)(2,1)}, bf16[1,6,32,256]{3,2,1,0:T(8,128)(2,1)}, bf16[1,6,32,256]{3,2,1,0:T(8,128)(2,1)}) custom-call(s32[1]{0:T(128)} %bitcast.place, s32[4,3,6]{2,1,0:T(4,128)} %copy-done, s32[4,3,6]{2,1,0:T(4,128)} %collective-permute-done.3.there, ...), custom_call_target="tpu_custom_call" | custom-call | bytes 2097152 | tf_op jit(solution)/shard_map/pick4/pallas_call | solution.py:47
  83.3 0.0 all-gather.9.cloned.1.call-done
  83.3 0.0 collective-permute-start.12
  83.3 2.3 %collective-permute-start.13 = (bf16[1,6,32,256]{3,2,1,0:T(8,128)(2,1)}, bf16[1,6,32,256]{3,2,1,0:T(8,128)(2,1)}, u32[]{:S(2)}, u32[]{:S(2)}) collective-permute-start(bf16[1,6,32,256]{3,2,1,0:T(8,128)(2,1)} %get-tuple-element.101), channel_id=1, source_target_pairs={{0,2},{1,3},{2,4},{3,5},{4,6},{5,7},{6,0},{7,1},{8,10},{9,11},{10,... | collective-permute-start | bytes 294920 | tf_op jit(solution)/shard_map/ppermute | solution.py:214
  85.5 3.0 %collective-permute-start.14 = (bf16[1,6,32,256]{3,2,1,0:T(8,128)(2,1)}, bf16[1,6,32,256]{3,2,1,0:T(8,128)(2,1)}, u32[]{:S(2)}, u32[]{:S(2)}) collective-permute-start(bf16[1,6,32,256]{3,2,1,0:T(8,128)(2,1)} %get-tuple-element.102), channel_id=1, source_target_pairs={{0,4},{1,5},{2,6},{3,7},{4,0},{5,1},{6,2},{7,3},{8,12},{9,13},{10,... | collective-permute-start | bytes 294920 | tf_op jit(solution)/shard_map/ppermute | solution.py:214
  88.5 0.0 collective-permute-start.15
  88.5 0.0 collective-permute-done.12.refs_1_
  88.5 4.8 %level2.1 = (f32[32,256]{1,0:T(8,128)}, bf16[32,32,256]{2,1,0:T(8,128)(2,1)}) custom-call(s32[1]{0:T(128)} %bitcast.place, s32[4,3,6]{2,1,0:T(4,128)} %copy-done, s32[4,3,6]{2,1,0:T(4,128)} %collective-permute-done.3.there, s32[1,6]{1,0:T(1,128)} %bitcast.30, bf16[4,256,256]{2,1,0:T(8,128)(2,1)} %rhs.7, bf16[4,256,256]{2,1,0:T(8,128)(2,1)} %dinv.7, ...), custom_call_target="tpu_custom_call" | custom-call | flops 100663296 | bytes 3145728 | tf_op jit(solution)/shard_map/level2/pallas_call | solution.py:47
  93.3 0.0 collective-permute-done.13.refs_1_
  93.3 4.0 %collective-permute-done.14.refs_2_ = bf16[1,6,32,256]{3,2,1,0:T(8,128)(2,1)} collective-permute-done((bf16[1,6,32,256]{3,2,1,0:T(8,128)(2,1)}, bf16[1,6,32,256]{3,2,1,0:T(8,128)(2,1)}, u32[]{:S(2)}, u32[]{:S(2)}) %collective-permute-start.14) | collective-permute-done | bytes 98336 | tf_op jit(solution)/shard_map/ppermute | solution.py:214
  97.2 0.4 collective-permute-done.15.refs_3_
  97.6 5.7 %all-to-all-start.2 = ((bf16[32,32,256]{2,1,0:T(8,128)(2,1)}), bf16[32,32,256]{2,1,0:T(8,128)(2,1)}, u32[]{:S(2)}, u32[]{:S(2)}) async-start(bf16[32,32,256]{2,1,0:T(8,128)(2,1)} %get-tuple-element.104), calls=%async_computation.2 | async-start | bytes 1048576 | tf_op jit(solution)/shard_map/all_to_all | solution.py:215
  103.3 2.4 %partial4.1 = (f32[32,256]{1,0:T(8,128)}, f32[32,256]{1,0:T(8,128)}, f32[32,256]{1,0:T(8,128)}, f32[32,256]{1,0:T(8,128)}) custom-call(s32[1]{0:T(128)} %bitcast.place, s32[1,6]{1,0:T(1,128)} %bitcast.31, bf16[1,6,32,256]{3,2,1,0:T(8,128)(2,1)} %get-tuple-element.106.refs_0_, bf16[1,6,32,256]{3,2,1,0:T(8,128)(2,1)} %collective-permute-done.13.refs_1_, ...), custom_call_target="tpu_custom_call" | custom-call | flops 201326592 | bytes 2097152 | tf_op jit(solution)/shard_map/partial4/pallas_call | solution.py:47
  105.7 0.8 collective-permute-start.16
  106.6 0.5 collective-permute-start.17
  107.1 1.3 collective-permute-start.18
  108.4 1.6 %collective-permute-done.16.refs_2_ = f32[32,256]{1,0:T(8,128)} collective-permute-done((f32[32,256]{1,0:T(8,128)}, f32[32,256]{1,0:T(8,128)}, u32[]{:S(2)}, u32[]{:S(2)}) %collective-permute-start.16) | collective-permute-done | bytes 32800 | tf_op jit(solution)/shard_map/ppermute | solution.py:214
  110.0 2.3 %collective-permute-done.17.refs_3_ = f32[32,256]{1,0:T(8,128)} collective-permute-done((f32[32,256]{1,0:T(8,128)}, f32[32,256]{1,0:T(8,128)}, u32[]{:S(2)}, u32[]{:S(2)}) %collective-permute-start.17) | collective-permute-done | bytes 32800 | tf_op jit(solution)/shard_map/ppermute | solution.py:214
  112.3 0.4 collective-permute-done.18.refs_4_
  112.7 7.4 %all-to-all-done.2.known = bf16[32,32,256]{2,1,0:T(8,128)(2,1)} async-done(((bf16[32,32,256]{2,1,0:T(8,128)(2,1)}), bf16[32,32,256]{2,1,0:T(8,128)(2,1)}, u32[]{:S(2)}, u32[]{:S(2)}) %all-to-all-start.2) | async-done | bytes 524320 | tf_op jit(solution)/shard_map/all_to_all | solution.py:215
  120.1 4.6 %level3.1 = f32[4,32,256]{2,1,0:T(8,128)} custom-call(s32[1]{0:T(128)} %bitcast.place, s32[4,3,6]{2,1,0:T(4,128)} %copy-done, s32[4,3,6]{2,1,0:T(4,128)} %collective-permute-done.3.there, s32[1,6]{1,0:T(1,128)} %bitcast.32, bf16[4,256,256]{2,1,0:T(8,128)(2,1)} %rhs.7, bf16[4,256,256]{2,1,0:T(8,128)(2,1)} %dinv.7, bf16[32,32,256]{2,1,0:T(8,128)(2,1)} %all-to-all-done.2.known, ...), custom_call_target="tpu_custom_call" | custom-call | flops 100663296 | bytes 3145728 | tf_op jit(solution)/shard_map/level3/pallas_call | solution.py:47
  (4 shorter events, 0.0 us)
Async XLA Ops:
  6.5 35.0 %all-gather.7.cloned.1.call-start = ((), (), s32[]{:S(2)}) async-start(), calls=%async_computation.3 | async-start | bytes 1966080 | tf_op jit(solution)/shard_map/all_gather | solution.py:217
  9.3 13.2 %copy-start.1 = (s32[6,1,3]{0,1,2:T(1,128)S(1)}, s32[6,1,3]{0,1,2:T(1,128)}, u32[]{:S(2)}) copy-start(s32[6,1,3]{0,1,2:T(1,128)} %param.8) | copy-start | bytes 220
  9.3 74.0 %all-gather.9.cloned.1.call-start = ((), (), s32[]{:S(2)}) async-start(), calls=%async_computation.4 | async-start | bytes 1966080 | tf_op jit(solution)/shard_map/all_gather | solution.py:217
  10.1 28.6 %all-to-all-start = ((bf16[32,32,256]{2,1,0:T(8,128)(2,1)}), bf16[32,32,256]{2,1,0:T(8,128)(2,1)}, u32[]{:S(2)}, u32[]{:S(2)}) async-start(bf16[32,32,256]{2,1,0:T(8,128)(2,1)} %get-tuple-element.64), calls=%async_computation | async-start | bytes 1048576 | tf_op jit(solution)/shard_map/all_to_all | solution.py:215
  21.7 86.7 %all-gather.11.cloned.1.call-start = ((), (), s32[]{:S(2)}) async-start(), calls=%async_computation.5 | async-start | bytes 3538944 | tf_op jit(solution)/shard_map/all_gather | solution.py:217
  22.5 5.9 %collective-permute-start = (s32[3,6]{1,0:T(4,128)S(1)}, s32[3,6]{1,0:T(4,128)S(1)}, u32[]{:S(2)}, u32[]{:S(2)}) collective-permute-start(s32[3,6]{1,0:T(4,128)S(1)} %bitcast.35), channel_id=1, source_target_pairs={{0,2},{1,3},{2,4},{3,5},{4,6},{5,7},{6,0},{7,1},{8,10},{9,11},{10,... | collective-permute-start | bytes 224 | tf_op jit(solution)/shard_map/ppermute | solution.py:214
  24.2 5.2 %collective-permute-start.1 = (s32[3,6]{1,0:T(4,128)S(1)}, s32[3,6]{1,0:T(4,128)S(1)}, u32[]{:S(2)}, u32[]{:S(2)}) collective-permute-start(s32[3,6]{1,0:T(4,128)S(1)} %bitcast.36), channel_id=1, source_target_pairs={{0,4},{1,5},{2,6},{3,7},{4,0},{5,1},{6,2},{7,3},{8,12},{9,13},{10,... | collective-permute-start | bytes 224 | tf_op jit(solution)/shard_map/ppermute | solution.py:214
  27.1 3.6 %collective-permute-start.2 = (s32[3,6]{1,0:T(4,128)S(1)}, s32[3,6]{1,0:T(4,128)S(1)}, u32[]{:S(2)}, u32[]{:S(2)}) collective-permute-start(s32[3,6]{1,0:T(4,128)S(1)} %bitcast.37), channel_id=1, source_target_pairs={{0,6},{1,7},{2,0},{3,1},{4,2},{5,3},{6,4},{7,5},{8,14},{9,15},{10,... | collective-permute-start | bytes 224 | tf_op jit(solution)/shard_map/ppermute | solution.py:214
  30.7 0.6 copy-start
  31.3 1.3 collective-permute-start.3
  41.5 5.4 %collective-permute-start.4 = (bf16[4,768,256]{2,1,0:T(8,128)(2,1)}, bf16[4,768,256]{2,1,0:T(8,128)(2,1)}, u32[]{:S(2)}, u32[]{:S(2)}) collective-permute-start(bf16[4,768,256]{2,1,0:T(8,128)(2,1)} %bitcast.26), channel_id=1, source_target_pairs={{0,1},{1,0},{2,3},{3,2},{4,5},{5,4},{6,7},{7,6},{8,9},{9,8},{10,11... | collective-permute-start | bytes 4718600 | tf_op jit(solution)/shard_map/ppermute | solution.py:214
  41.5 23.9 %collective-permute-start.8 = (bf16[6,3,256,256]{3,2,1,0:T(8,128)(2,1)}, bf16[6,3,256,256]{3,2,1,0:T(8,128)(2,1)}, u32[]{:S(2)}, u32[]{:S(2)}) collective-permute-start(bf16[6,3,256,256]{3,2,1,0:T(8,128)(2,1)} %bitcast.19), channel_id=1, source_target_pairs={{0,1},{1,0},{2,3},{3,2},{4,5},{5,4},{6,7},{7,6},{8,9},{9,8},{10,11... | collective-permute-start | bytes 7077896 | tf_op jit(solution)/shard_map/ppermute | solution.py:214
  42.0 9.7 %collective-permute-start.5 = (bf16[2,6,32,256]{3,2,1,0:T(8,128)(2,1)}, bf16[2,6,32,256]{3,2,1,0:T(8,128)(2,1)}, u32[]{:S(2)}, u32[]{:S(2)}) collective-permute-start(bf16[2,6,32,256]{3,2,1,0:T(8,128)(2,1)} %get-tuple-element.74), channel_id=1, source_target_pairs={{0,2},{1,3},{2,4},{3,5},{4,6},{5,7},{6,0},{7,1},{8,10},{9,11},{10,... | collective-permute-start | bytes 589832 | tf_op jit(solution)/shard_map/ppermute | solution.py:214
  42.7 12.3 %collective-permute-start.6 = (bf16[2,6,32,256]{3,2,1,0:T(8,128)(2,1)}, bf16[2,6,32,256]{3,2,1,0:T(8,128)(2,1)}, u32[]{:S(2)}, u32[]{:S(2)}) collective-permute-start(bf16[2,6,32,256]{3,2,1,0:T(8,128)(2,1)} %get-tuple-element.75), channel_id=1, source_target_pairs={{0,4},{1,5},{2,6},{3,7},{4,0},{5,1},{6,2},{7,3},{8,12},{9,13},{10,... | collective-permute-start | bytes 589832 | tf_op jit(solution)/shard_map/ppermute | solution.py:214
  45.6 9.6 %collective-permute-start.7 = (bf16[2,6,32,256]{3,2,1,0:T(8,128)(2,1)}, bf16[2,6,32,256]{3,2,1,0:T(8,128)(2,1)}, u32[]{:S(2)}, u32[]{:S(2)}) collective-permute-start(bf16[2,6,32,256]{3,2,1,0:T(8,128)(2,1)} %get-tuple-element.76), channel_id=1, source_target_pairs={{0,6},{1,7},{2,0},{3,1},{4,2},{5,3},{6,4},{7,5},{8,14},{9,15},{10,... | collective-permute-start | bytes 589832 | tf_op jit(solution)/shard_map/ppermute | solution.py:214
  55.2 26.2 %all-to-all-start.1 = ((bf16[32,32,256]{2,1,0:T(8,128)(2,1)}), bf16[32,32,256]{2,1,0:T(8,128)(2,1)}, u32[]{:S(2)}, u32[]{:S(2)}) async-start(bf16[32,32,256]{2,1,0:T(8,128)(2,1)} %get-tuple-element.77), calls=%async_computation.1 | async-start | bytes 1048576 | tf_op jit(solution)/shard_map/all_to_all | solution.py:215
  68.4 6.1 %collective-permute-start.10 = (f32[32,256]{1,0:T(8,128)}, f32[32,256]{1,0:T(8,128)}, u32[]{:S(2)}, u32[]{:S(2)}) collective-permute-start(f32[32,256]{1,0:T(8,128)} %get-tuple-element.85), channel_id=1, source_target_pairs={{0,4},{1,5},{2,6},{3,7},{4,0},{5,1},{6,2},{7,3},{8,12},{9,13},{10,... | collective-permute-start | bytes 98312 | tf_op jit(solution)/shard_map/ppermute | solution.py:214
  70.3 5.4 %collective-permute-start.11 = (f32[32,256]{1,0:T(8,128)}, f32[32,256]{1,0:T(8,128)}, u32[]{:S(2)}, u32[]{:S(2)}) collective-permute-start(f32[32,256]{1,0:T(8,128)} %get-tuple-element.86), channel_id=1, source_target_pairs={{0,2},{1,3},{2,4},{3,5},{4,6},{5,7},{6,0},{7,1},{8,10},{9,11},{10,... | collective-permute-start | bytes 98312 | tf_op jit(solution)/shard_map/ppermute | solution.py:214
  72.0 4.2 %collective-permute-start.9 = (f32[32,256]{1,0:T(8,128)}, f32[32,256]{1,0:T(8,128)}, u32[]{:S(2)}, u32[]{:S(2)}) collective-permute-start(f32[32,256]{1,0:T(8,128)} %get-tuple-element.84), channel_id=1, source_target_pairs={{0,6},{1,7},{2,0},{3,1},{4,2},{5,3},{6,4},{7,5},{8,14},{9,15},{10,... | collective-permute-start | bytes 98312 | tf_op jit(solution)/shard_map/ppermute | solution.py:214
  83.3 5.2 %collective-permute-start.12 = (bf16[4,768,256]{2,1,0:T(8,128)(2,1)}, bf16[4,768,256]{2,1,0:T(8,128)(2,1)}, u32[]{:S(2)}, u32[]{:S(2)}) collective-permute-start(bf16[4,768,256]{2,1,0:T(8,128)(2,1)} %bitcast.24), channel_id=1, source_target_pairs={{0,1},{1,0},{2,3},{3,2},{4,5},{5,4},{6,7},{7,6},{8,9},{9,8},{10,11... | collective-permute-start | bytes 4718600 | tf_op jit(solution)/shard_map/ppermute | solution.py:214
  83.3 10.0 %collective-permute-start.13 = (bf16[1,6,32,256]{3,2,1,0:T(8,128)(2,1)}, bf16[1,6,32,256]{3,2,1,0:T(8,128)(2,1)}, u32[]{:S(2)}, u32[]{:S(2)}) collective-permute-start(bf16[1,6,32,256]{3,2,1,0:T(8,128)(2,1)} %get-tuple-element.101), channel_id=1, source_target_pairs={{0,2},{1,3},{2,4},{3,5},{4,6},{5,7},{6,0},{7,1},{8,10},{9,11},{10,... | collective-permute-start | bytes 294920 | tf_op jit(solution)/shard_map/ppermute | solution.py:214
  85.5 11.7 %collective-permute-start.14 = (bf16[1,6,32,256]{3,2,1,0:T(8,128)(2,1)}, bf16[1,6,32,256]{3,2,1,0:T(8,128)(2,1)}, u32[]{:S(2)}, u32[]{:S(2)}) collective-permute-start(bf16[1,6,32,256]{3,2,1,0:T(8,128)(2,1)} %get-tuple-element.102), channel_id=1, source_target_pairs={{0,4},{1,5},{2,6},{3,7},{4,0},{5,1},{6,2},{7,3},{8,12},{9,13},{10,... | collective-permute-start | bytes 294920 | tf_op jit(solution)/shard_map/ppermute | solution.py:214
  88.5 9.1 %collective-permute-start.15 = (bf16[1,6,32,256]{3,2,1,0:T(8,128)(2,1)}, bf16[1,6,32,256]{3,2,1,0:T(8,128)(2,1)}, u32[]{:S(2)}, u32[]{:S(2)}) collective-permute-start(bf16[1,6,32,256]{3,2,1,0:T(8,128)(2,1)} %get-tuple-element.103), channel_id=1, source_target_pairs={{0,6},{1,7},{2,0},{3,1},{4,2},{5,3},{6,4},{7,5},{8,14},{9,15},{10,... | collective-permute-start | bytes 294920 | tf_op jit(solution)/shard_map/ppermute | solution.py:214
  97.6 22.5 %all-to-all-start.2 = ((bf16[32,32,256]{2,1,0:T(8,128)(2,1)}), bf16[32,32,256]{2,1,0:T(8,128)(2,1)}, u32[]{:S(2)}, u32[]{:S(2)}) async-start(bf16[32,32,256]{2,1,0:T(8,128)(2,1)} %get-tuple-element.104), calls=%async_computation.2 | async-start | bytes 1048576 | tf_op jit(solution)/shard_map/all_to_all | solution.py:215
  105.7 4.2 %collective-permute-start.16 = (f32[32,256]{1,0:T(8,128)}, f32[32,256]{1,0:T(8,128)}, u32[]{:S(2)}, u32[]{:S(2)}) collective-permute-start(f32[32,256]{1,0:T(8,128)} %get-tuple-element.115), channel_id=1, source_target_pairs={{0,6},{1,7},{2,0},{3,1},{4,2},{5,3},{6,4},{7,5},{8,14},{9,15},{10,... | collective-permute-start | bytes 98312 | tf_op jit(solution)/shard_map/ppermute | solution.py:214
  106.6 5.7 %collective-permute-start.17 = (f32[32,256]{1,0:T(8,128)}, f32[32,256]{1,0:T(8,128)}, u32[]{:S(2)}, u32[]{:S(2)}) collective-permute-start(f32[32,256]{1,0:T(8,128)} %get-tuple-element.116), channel_id=1, source_target_pairs={{0,4},{1,5},{2,6},{3,7},{4,0},{5,1},{6,2},{7,3},{8,12},{9,13},{10,... | collective-permute-start | bytes 98312 | tf_op jit(solution)/shard_map/ppermute | solution.py:214
  107.1 5.5 %collective-permute-start.18 = (f32[32,256]{1,0:T(8,128)}, f32[32,256]{1,0:T(8,128)}, u32[]{:S(2)}, u32[]{:S(2)}) collective-permute-start(f32[32,256]{1,0:T(8,128)} %get-tuple-element.117), channel_id=1, source_target_pairs={{0,2},{1,3},{2,4},{3,5},{4,6},{5,7},{6,0},{7,1},{8,10},{9,11},{10,... | collective-permute-start | bytes 98312 | tf_op jit(solution)/shard_map/ppermute | solution.py:214
Sparse Core Ops, SparseCore 0:
  9.4 32.0 all-gather.6
  43.3 29.5 all-gather.8
  74.7 32.7 all-gather.10

commit v16 on v14

--- a/solution.py
+++ b/solution.py
@@ -242,7 +242,7 @@
     gathered0 = gather(cut0, COL)
     early, cut0 = lax.optimization_barrier((rhs, cut0))
     answer0, spread0, cut2, cut5 = first_call(place, early, dinv, tiles, (2, 5))
-    gathered2, gathered5 = gather(cut2, "chip"), gather(cut5, COL)
+    gathered2, gathered5 = gather(cut2, COL), gather(cut5, COL)
 
     def send(picked):
         return [picked[0]] + [move(picked[d], TURN[d]) for d in range(1, CHIPS)]
@@ -266,9 +266,7 @@
     picked = pick_call("pick4", (4,), place, here, there, known1)
     known1, *picked = lax.optimization_barrier((known1, *picked))
     got = send(picked)
-    gathered2, _ = lax.optimization_barrier((gathered2, picked[0]))
-    gathered2 = [gathered2, move(gathered2, SWAP)]
-    answer2, spread2 = level_call(2, 2, place, here, there, live, rhs, dinv, known1, gathered2, back2, [])
+    answer2, spread2 = level_call(2, 2, place, here, there, live, rhs, dinv, known1, [gathered2], back2, [])
     spread2, *got = lax.optimization_barrier((spread2, *got))
     known2 = over_row(spread2)
 

time: 125 us -> 124 us (level)
    all_to_all x3, waiting for transfers between devices: 12.5 us -> 10.3 us  [local(): over_row = lambda array: lax.all_to_all(array, 'row', 0, 0, tiled=True)]
    all_gather x3, waiting for transfers between devices: 7.83 us -> 9.51 us  [local(): lax.all_gather(array, axes, axis=0, tiled=False)]
    ppermute x18 -> x17, starting transfers between devices: 22.8 us -> 22.4 us  [local(): move = lambda array, pairs: lax.ppermute(array, COL, pairs)]
    ppermute x18 -> x17, waiting for transfers between devices: 13.5 us -> 13.6 us  [local(): move = lambda array, pairs: lax.ppermute(array, COL, pairs)]
  transfers between devices with their start and end apart: 24 -> 23, of which waited for: 11 -> 11; matrix products, arithmetic and copies ran while one was open for 1% -> 1% of each run, Pallas kernels for 17% -> 17%
where the time goes in v16:
time: 124 us; the launch traced here: 122 us
  starting transfers between devices  45.5 us (37%)
  waiting for transfers between devices  34.1 us (28%)
  Pallas kernels  27.7 us (22%)
  between operations  13.2 us (11%)
  local copies, waits for them, and re-layouts  1.96 us (2%)
    pallas_call x9, Pallas kernels, call(): pl.pallas_call(kernel, grid=(1,), out_shape=tuple((jax.ShapeDtypeStruct(s...  27.7 us
    all_to_all x3, starting transfers between devices, local(): over_row = lambda array: lax.all_to_all(array, 'row', 0, 0, tiled=True)  23 us
    ppermute x17, starting transfers between devices, local(): move = lambda array, pairs: lax.ppermute(array, COL, pairs)  22.4 us
    ppermute x17, waiting for transfers between devices, local(): move = lambda array, pairs: lax.ppermute(array, COL, pairs)  13.6 us
    all_to_all x3, waiting for transfers between devices, local(): over_row = lambda array: lax.all_to_all(array, 'row', 0, 0, tiled=True)  10.3 us
    all_gather x3, waiting for transfers between devices, local(): lax.all_gather(array, axes, axis=0, tiled=False)  9.51 us
  transfers between devices with their start and end apart: 23, of which 11 were waited for; matrix products, arithmetic and copies ran while one was open for 1% of the time, Pallas kernels for 17%

profile of v16, /device:TPU:2, one launch (start us, length us, event | category | flops | bytes accessed | tf_op | source)
XLA Modules:
  0.0 122.4 jit_solution(7358970589823294876)
XLA Ops:
  6.5 0.0 all-gather.7.cloned.1.call-start
  6.5 1.8 %cut.1 = bf16[768,256]{1,0:T(8,128)(2,1)} custom-call(bf16[6,3,256,256]{3,2,1,0:T(8,128)(2,1)} %bitcast.16), custom_call_target="tpu_custom_call" | custom-call | bytes 1048576 | tf_op jit(solution)/shard_map/cut/pallas_call | solution.py:47
  8.3 0.0 all-gather.7.cloned.1.call-update
  8.3 0.0 all-gather.9.cloned.1.call-start
  8.4 2.5 %level0.1 = (f32[32,256]{1,0:T(8,128)}, bf16[32,32,256]{2,1,0:T(8,128)(2,1)}, bf16[768,256]{1,0:T(8,128)(2,1)}, bf16[768,256]{1,0:T(8,128)(2,1)}) custom-call(s32[1]{0:T(128)} %bitcast.place, bf16[4,256,256]{2,1,0:T(8,128)(2,1)} %rhs.6, bf16[4,256,256]{2,1,0:T(8,128)(2,1)} %dinv.7, bf16[6,3,256,256]{3,2,1,0:T(8,128)(2,1)} %bitcast.17, ...), custom_call_target="tpu_custom_call" | custom-call | bytes 4194304 | tf_op jit(solution)/shard_map/level0/pallas_call | solution.py:47
  10.9 0.0 all-gather.9.cloned.1.call-update
  10.9 0.0 all-gather.11.cloned.1.call-start
  11.0 0.7 all-gather.11.cloned.1.call-update
  11.7 11.7 %all-to-all-start = ((bf16[32,32,256]{2,1,0:T(8,128)(2,1)}), bf16[32,32,256]{2,1,0:T(8,128)(2,1)}, u32[]{:S(2)}, u32[]{:S(2)}) async-start(bf16[32,32,256]{2,1,0:T(8,128)(2,1)} %get-tuple-element.61), calls=%async_computation | async-start | bytes 1048576 | tf_op jit(solution)/shard_map/all_to_all | solution.py:233
  23.4 0.7 copy.9
  24.1 3.0 %collective-permute-start.2 = (s32[3,6]{1,0:T(4,128)S(1)}, s32[3,6]{1,0:T(4,128)S(1)}, u32[]{:S(2)}, u32[]{:S(2)}) collective-permute-start(s32[3,6]{1,0:T(4,128)S(1)} %bitcast.33), channel_id=1, source_target_pairs={{0,6},{1,7},{2,0},{3,1},{4,2},{5,3},{6,4},{7,5},{8,14},{9,15},{10,... | collective-permute-start | bytes 224 | tf_op jit(solution)/shard_map/ppermute | solution.py:232
  27.1 0.6 collective-permute-start.1
  27.7 1.0 collective-permute-start
  28.7 0.7 copy.6
  29.4 0.0 collective-permute-done.2
  29.4 2.9 %collective-permute-done.1 = s32[3,6]{1,0:T(4,128)S(1)} collective-permute-done((s32[3,6]{1,0:T(4,128)S(1)}, s32[3,6]{1,0:T(4,128)S(1)}, u32[]{:S(2)}, u32[]{:S(2)}) %collective-permute-start.1) | collective-permute-done | bytes 104 | tf_op jit(solution)/shard_map/ppermute | solution.py:232
  32.3 0.2 collective-permute-done
  32.5 0.0 copy-start
  32.5 0.6 copy-done
  33.1 0.0 collective-permute-start.3
  33.1 1.3 %collective-permute-done.3.there = s32[4,3,6]{2,1,0:T(4,128)} collective-permute-done((s32[4,3,6]{2,1,0:T(4,128)S(1)}, s32[4,3,6]{2,1,0:T(4,128)}, u32[]{:S(2)}, u32[]{:S(2)}) %collective-permute-start.3) | collective-permute-done | bytes 320 | tf_op jit(solution)/shard_map/ppermute | solution.py:232
  34.4 5.8 %all-to-all-done.known = bf16[32,32,256]{2,1,0:T(8,128)(2,1)} async-done(((bf16[32,32,256]{2,1,0:T(8,128)(2,1)}), bf16[32,32,256]{2,1,0:T(8,128)(2,1)}, u32[]{:S(2)}, u32[]{:S(2)}) %all-to-all-start) | async-done | bytes 524320 | tf_op jit(solution)/shard_map/all_to_all | solution.py:233
  40.3 2.0 %pick13.1 = (bf16[2,6,32,256]{3,2,1,0:T(8,128)(2,1)}, bf16[2,6,32,256]{3,2,1,0:T(8,128)(2,1)}, bf16[2,6,32,256]{3,2,1,0:T(8,128)(2,1)}, bf16[2,6,32,256]{3,2,1,0:T(8,128)(2,1)}) custom-call(s32[1]{0:T(128)} %bitcast.place, s32[4,3,6]{2,1,0:T(4,128)} %copy-done, s32[4,3,6]{2,1,0:T(4,128)} %collective-permute-done.3.there, bf16[32,32,256]{2,1,0:T(8,128)(2,1)} %all-to-all-done.known), custom_call_target="tpu_custom_call" | custom-call | bytes 2097152 | tf_op jit(solution)/shard_map/pick13/pallas_call | solution.py:47
  42.3 0.0 collective-permute-start.7
  42.3 1.6 %collective-permute-start.4 = (bf16[2,6,32,256]{3,2,1,0:T(8,128)(2,1)}, bf16[2,6,32,256]{3,2,1,0:T(8,128)(2,1)}, u32[]{:S(2)}, u32[]{:S(2)}) collective-permute-start(bf16[2,6,32,256]{3,2,1,0:T(8,128)(2,1)} %get-tuple-element.69), channel_id=1, source_target_pairs={{0,2},{1,3},{2,4},{3,5},{4,6},{5,7},{6,0},{7,1},{8,10},{9,11},{10,... | collective-permute-start | bytes 589832 | tf_op jit(solution)/shard_map/ppermute | solution.py:232
  43.9 2.9 %collective-permute-start.5 = (bf16[2,6,32,256]{3,2,1,0:T(8,128)(2,1)}, bf16[2,6,32,256]{3,2,1,0:T(8,128)(2,1)}, u32[]{:S(2)}, u32[]{:S(2)}) collective-permute-start(bf16[2,6,32,256]{3,2,1,0:T(8,128)(2,1)} %get-tuple-element.70), channel_id=1, source_target_pairs={{0,4},{1,5},{2,6},{3,7},{4,0},{5,1},{6,2},{7,3},{8,12},{9,13},{10,... | collective-permute-start | bytes 589832 | tf_op jit(solution)/shard_map/ppermute | solution.py:232
  46.7 1.3 %collective-permute-start.6 = (bf16[2,6,32,256]{3,2,1,0:T(8,128)(2,1)}, bf16[2,6,32,256]{3,2,1,0:T(8,128)(2,1)}, u32[]{:S(2)}, u32[]{:S(2)}) collective-permute-start(bf16[2,6,32,256]{3,2,1,0:T(8,128)(2,1)} %get-tuple-element.71), channel_id=1, source_target_pairs={{0,6},{1,7},{2,0},{3,1},{4,2},{5,3},{6,4},{7,5},{8,14},{9,15},{10,... | collective-permute-start | bytes 589832 | tf_op jit(solution)/shard_map/ppermute | solution.py:232
  48.1 0.0 all-gather.7.cloned.1.call-done
  48.1 4.8 %level1.1 = (f32[32,256]{1,0:T(8,128)}, bf16[32,32,256]{2,1,0:T(8,128)(2,1)}) custom-call(s32[1]{0:T(128)} %bitcast.place, s32[4,3,6]{2,1,0:T(4,128)} %copy-done, s32[4,3,6]{2,1,0:T(4,128)} %collective-permute-done.3.there, s32[1,6]{1,0:T(1,128)} %bitcast.26, bf16[4,256,256]{2,1,0:T(8,128)(2,1)} %rhs.6, bf16[4,256,256]{2,1,0:T(8,128)(2,1)} %dinv.7, ...), custom_call_target="tpu_custom_call" | custom-call | flops 100663296 | bytes 3145728 | tf_op jit(solution)/shard_map/level1/pallas_call | solution.py:47
  52.9 0.0 collective-permute-done.4.refs_1_
  52.9 3.7 %collective-permute-done.5.refs_2_ = bf16[2,6,32,256]{3,2,1,0:T(8,128)(2,1)} collective-permute-done((bf16[2,6,32,256]{3,2,1,0:T(8,128)(2,1)}, bf16[2,6,32,256]{3,2,1,0:T(8,128)(2,1)}, u32[]{:S(2)}, u32[]{:S(2)}) %collective-permute-start.5) | collective-permute-done | bytes 196640 | tf_op jit(solution)/shard_map/ppermute | solution.py:232
  56.6 0.0 collective-permute-done.6.refs_3_
  56.6 5.6 %all-to-all-start.1 = ((bf16[32,32,256]{2,1,0:T(8,128)(2,1)}), bf16[32,32,256]{2,1,0:T(8,128)(2,1)}, u32[]{:S(2)}, u32[]{:S(2)}) async-start(bf16[32,32,256]{2,1,0:T(8,128)(2,1)} %get-tuple-element.72), calls=%async_computation.1 | async-start | bytes 1048576 | tf_op jit(solution)/shard_map/all_to_all | solution.py:233
  62.2 0.0 collective-permute-done.7.refs_5_.refs_7_.refs_9_
  62.2 3.0 %partial13.1 = (f32[32,256]{1,0:T(8,128)}, f32[32,256]{1,0:T(8,128)}, f32[32,256]{1,0:T(8,128)}, f32[32,256]{1,0:T(8,128)}, f32[32,256]{1,0:T(8,128)}, /*index=5...) custom-call(s32[1]{0:T(128)} %bitcast.place, s32[1,6]{1,0:T(1,128)} %bitcast.27, ...), custom_call_target="tpu_custom_call" | custom-call | flops 201326592 | bytes 2097152 | tf_op jit(solution)/shard_map/partial13/pallas_call | solution.py:47
  65.2 2.2 %collective-permute-start.8 = (f32[32,256]{1,0:T(8,128)}, f32[32,256]{1,0:T(8,128)}, u32[]{:S(2)}, u32[]{:S(2)}) collective-permute-start(f32[32,256]{1,0:T(8,128)} %get-tuple-element.79), channel_id=1, source_target_pairs={{0,6},{1,7},{2,0},{3,1},{4,2},{5,3},{6,4},{7,5},{8,14},{9,15},{10,... | collective-permute-start | bytes 98312 | tf_op jit(solution)/shard_map/ppermute | solution.py:232
  67.4 1.1 collective-permute-start.9
  68.5 0.8 collective-permute-start.10
  69.3 1.1 collective-permute-done.8.refs_2_
  70.4 3.5 %collective-permute-done.9.refs_3_ = f32[32,256]{1,0:T(8,128)} collective-permute-done((f32[32,256]{1,0:T(8,128)}, f32[32,256]{1,0:T(8,128)}, u32[]{:S(2)}, u32[]{:S(2)}) %collective-permute-start.9) | collective-permute-done | bytes 32800 | tf_op jit(solution)/shard_map/ppermute | solution.py:232
  73.9 0.8 collective-permute-done.10.refs_4_
  74.7 4.3 %all-to-all-done.1.known = bf16[32,32,256]{2,1,0:T(8,128)(2,1)} async-done(((bf16[32,32,256]{2,1,0:T(8,128)(2,1)}), bf16[32,32,256]{2,1,0:T(8,128)(2,1)}, u32[]{:S(2)}, u32[]{:S(2)}) %all-to-all-start.1) | async-done | bytes 524320 | tf_op jit(solution)/shard_map/all_to_all | solution.py:233
  79.0 1.8 %pick4.1 = (bf16[1,6,32,256]{3,2,1,0:T(8,128)(2,1)}, bf16[1,6,32,256]{3,2,1,0:T(8,128)(2,1)}, bf16[1,6,32,256]{3,2,1,0:T(8,128)(2,1)}, bf16[1,6,32,256]{3,2,1,0:T(8,128)(2,1)}) custom-call(s32[1]{0:T(128)} %bitcast.place, s32[4,3,6]{2,1,0:T(4,128)} %copy-done, s32[4,3,6]{2,1,0:T(4,128)} %collective-permute-done.3.there, ...), custom_call_target="tpu_custom_call" | custom-call | bytes 2097152 | tf_op jit(solution)/shard_map/pick4/pallas_call | solution.py:47
  80.8 0.6 collective-permute-start.11
  81.5 3.2 %collective-permute-start.12 = (bf16[1,6,32,256]{3,2,1,0:T(8,128)(2,1)}, bf16[1,6,32,256]{3,2,1,0:T(8,128)(2,1)}, u32[]{:S(2)}, u32[]{:S(2)}) collective-permute-start(bf16[1,6,32,256]{3,2,1,0:T(8,128)(2,1)} %get-tuple-element.96), channel_id=1, source_target_pairs={{0,4},{1,5},{2,6},{3,7},{4,0},{5,1},{6,2},{7,3},{8,12},{9,13},{10,... | collective-permute-start | bytes 294920 | tf_op jit(solution)/shard_map/ppermute | solution.py:232
  84.7 1.1 collective-permute-start.13
  85.7 0.0 all-gather.9.cloned.1.call-done
  85.7 4.8 %level2.1 = (f32[32,256]{1,0:T(8,128)}, bf16[32,32,256]{2,1,0:T(8,128)(2,1)}) custom-call(s32[1]{0:T(128)} %bitcast.place, s32[4,3,6]{2,1,0:T(4,128)} %copy-done, s32[4,3,6]{2,1,0:T(4,128)} %collective-permute-done.3.there, s32[1,6]{1,0:T(1,128)} %bitcast.28, bf16[4,256,256]{2,1,0:T(8,128)(2,1)} %rhs.6, bf16[4,256,256]{2,1,0:T(8,128)(2,1)} %dinv.7, ...), custom_call_target="tpu_custom_call" | custom-call | flops 100663296 | bytes 3145728 | tf_op jit(solution)/shard_map/level2/pallas_call | solution.py:47
  90.5 0.0 collective-permute-done.11.refs_1_
  90.5 0.0 collective-permute-done.12.refs_2_
  90.6 0.0 collective-permute-done.13.refs_3_
  90.6 5.6 %all-to-all-start.2 = ((bf16[32,32,256]{2,1,0:T(8,128)(2,1)}), bf16[32,32,256]{2,1,0:T(8,128)(2,1)}, u32[]{:S(2)}, u32[]{:S(2)}) async-start(bf16[32,32,256]{2,1,0:T(8,128)(2,1)} %get-tuple-element.98), calls=%async_computation.2 | async-start | bytes 1048576 | tf_op jit(solution)/shard_map/all_to_all | solution.py:233
  96.2 2.4 %partial4.1 = (f32[32,256]{1,0:T(8,128)}, f32[32,256]{1,0:T(8,128)}, f32[32,256]{1,0:T(8,128)}, f32[32,256]{1,0:T(8,128)}) custom-call(s32[1]{0:T(128)} %bitcast.place, s32[1,6]{1,0:T(1,128)} %bitcast.29, bf16[1,6,32,256]{3,2,1,0:T(8,128)(2,1)} %get-tuple-element.100.refs_0_, bf16[1,6,32,256]{3,2,1,0:T(8,128)(2,1)} %collective-permute-done.11.refs_1_, ...), custom_call_target="tpu_custom_call" | custom-call | flops 201326592 | bytes 2097152 | tf_op jit(solution)/shard_map/partial4/pallas_call | solution.py:47
  98.6 1.3 %collective-permute-start.14 = (f32[32,256]{1,0:T(8,128)}, f32[32,256]{1,0:T(8,128)}, u32[]{:S(2)}, u32[]{:S(2)}) collective-permute-start(f32[32,256]{1,0:T(8,128)} %get-tuple-element.109), channel_id=1, source_target_pairs={{0,6},{1,7},{2,0},{3,1},{4,2},{5,3},{6,4},{7,5},{8,14},{9,15},{10,... | collective-permute-start | bytes 98312 | tf_op jit(solution)/shard_map/ppermute | solution.py:232
  99.9 1.7 %collective-permute-start.15 = (f32[32,256]{1,0:T(8,128)}, f32[32,256]{1,0:T(8,128)}, u32[]{:S(2)}, u32[]{:S(2)}) collective-permute-start(f32[32,256]{1,0:T(8,128)} %get-tuple-element.110), channel_id=1, source_target_pairs={{0,4},{1,5},{2,6},{3,7},{4,0},{5,1},{6,2},{7,3},{8,12},{9,13},{10,... | collective-permute-start | bytes 98312 | tf_op jit(solution)/shard_map/ppermute | solution.py:232
  101.6 0.0 collective-permute-start.16
  101.6 9.5 %all-gather.11.cloned.1.call-done = bf16[6144,256]{1,0:T(8,128)(2,1)} async-done(((bf16[768,256]{1,0:T(8,128)(2,1)}), bf16[6144,256]{1,0:T(8,128)(2,1)}) %all-gather.11.cloned.1.call-update) | async-done | bytes 3145744 | tf_op jit(solution)/shard_map/all_gather | solution.py:235
  111.2 0.0 collective-permute-done.14.refs_2_
  111.2 0.0 collective-permute-done.15.refs_3_
  111.2 0.0 collective-permute-done.16.refs_4_
  111.2 0.1 all-to-all-done.2.known
  111.3 4.6 %level3.1 = f32[4,32,256]{2,1,0:T(8,128)} custom-call(s32[1]{0:T(128)} %bitcast.place, s32[4,3,6]{2,1,0:T(4,128)} %copy-done, s32[4,3,6]{2,1,0:T(4,128)} %collective-permute-done.3.there, s32[1,6]{1,0:T(1,128)} %bitcast.30, bf16[4,256,256]{2,1,0:T(8,128)(2,1)} %rhs.6, bf16[4,256,256]{2,1,0:T(8,128)(2,1)} %dinv.7, bf16[32,32,256]{2,1,0:T(8,128)(2,1)} %all-to-all-done.2.known, ...), custom_call_target="tpu_custom_call" | custom-call | flops 100663296 | bytes 3145728 | tf_op jit(solution)/shard_map/level3/pallas_call | solution.py:47
  (1 shorter events, 0.0 us)
Async XLA Ops:
  6.5 41.6 %all-gather.7.cloned.1.call-start = ((), (), s32[]{:S(2)}) async-start(), calls=%async_computation.3 | async-start | bytes 3538944 | tf_op jit(solution)/shard_map/all_gather | solution.py:235
  8.3 77.4 %all-gather.9.cloned.1.call-start = ((), (), s32[]{:S(2)}) async-start(), calls=%async_computation.4 | async-start | bytes 3538944 | tf_op jit(solution)/shard_map/all_gather | solution.py:235
  10.9 100.2 %all-gather.11.cloned.1.call-start = ((), (), s32[]{:S(2)}) async-start(), calls=%async_computation.5 | async-start | bytes 3538944 | tf_op jit(solution)/shard_map/all_gather | solution.py:235
  11.7 28.6 %all-to-all-start = ((bf16[32,32,256]{2,1,0:T(8,128)(2,1)}), bf16[32,32,256]{2,1,0:T(8,128)(2,1)}, u32[]{:S(2)}, u32[]{:S(2)}) async-start(bf16[32,32,256]{2,1,0:T(8,128)(2,1)} %get-tuple-element.61), calls=%async_computation | async-start | bytes 1048576 | tf_op jit(solution)/shard_map/all_to_all | solution.py:233
  24.1 5.3 %collective-permute-start.2 = (s32[3,6]{1,0:T(4,128)S(1)}, s32[3,6]{1,0:T(4,128)S(1)}, u32[]{:S(2)}, u32[]{:S(2)}) collective-permute-start(s32[3,6]{1,0:T(4,128)S(1)} %bitcast.33), channel_id=1, source_target_pairs={{0,6},{1,7},{2,0},{3,1},{4,2},{5,3},{6,4},{7,5},{8,14},{9,15},{10,... | collective-permute-start | bytes 224 | tf_op jit(solution)/shard_map/ppermute | solution.py:232
  27.1 5.2 %collective-permute-start.1 = (s32[3,6]{1,0:T(4,128)S(1)}, s32[3,6]{1,0:T(4,128)S(1)}, u32[]{:S(2)}, u32[]{:S(2)}) collective-permute-start(s32[3,6]{1,0:T(4,128)S(1)} %bitcast.34), channel_id=1, source_target_pairs={{0,4},{1,5},{2,6},{3,7},{4,0},{5,1},{6,2},{7,3},{8,12},{9,13},{10,... | collective-permute-start | bytes 224 | tf_op jit(solution)/shard_map/ppermute | solution.py:232
  27.7 4.8 %collective-permute-start = (s32[3,6]{1,0:T(4,128)S(1)}, s32[3,6]{1,0:T(4,128)S(1)}, u32[]{:S(2)}, u32[]{:S(2)}) collective-permute-start(s32[3,6]{1,0:T(4,128)S(1)} %bitcast.35), channel_id=1, source_target_pairs={{0,2},{1,3},{2,4},{3,5},{4,6},{5,7},{6,0},{7,1},{8,10},{9,11},{10,... | collective-permute-start | bytes 224 | tf_op jit(solution)/shard_map/ppermute | solution.py:232
  32.5 0.6 copy-start
  33.1 1.3 %collective-permute-start.3 = (s32[4,3,6]{2,1,0:T(4,128)S(1)}, s32[4,3,6]{2,1,0:T(4,128)}, u32[]{:S(2)}, u32[]{:S(2)}) collective-permute-start(s32[4,3,6]{2,1,0:T(4,128)S(1)} %pad_add_fusion.here), channel_id=1, source_target_pairs={{0,1},{1,0},{2,3},{3,2},{4,5},{5,4},{6,7},{7,6},{8,9},{9,8},{10,11... | collective-permute-start | bytes 872 | tf_op jit(solution)/shard_map/ppermute | solution.py:232
  42.3 19.9 %collective-permute-start.7 = (bf16[6,3,256,256]{3,2,1,0:T(8,128)(2,1)}, bf16[6,3,256,256]{3,2,1,0:T(8,128)(2,1)}, u32[]{:S(2)}, u32[]{:S(2)}) collective-permute-start(bf16[6,3,256,256]{3,2,1,0:T(8,128)(2,1)} %bitcast.19), channel_id=1, source_target_pairs={{0,1},{1,0},{2,3},{3,2},{4,5},{5,4},{6,7},{7,6},{8,9},{9,8},{10,11... | collective-permute-start | bytes 7077896 | tf_op jit(solution)/shard_map/ppermute | solution.py:232
  42.3 10.6 %collective-permute-start.4 = (bf16[2,6,32,256]{3,2,1,0:T(8,128)(2,1)}, bf16[2,6,32,256]{3,2,1,0:T(8,128)(2,1)}, u32[]{:S(2)}, u32[]{:S(2)}) collective-permute-start(bf16[2,6,32,256]{3,2,1,0:T(8,128)(2,1)} %get-tuple-element.69), channel_id=1, source_target_pairs={{0,2},{1,3},{2,4},{3,5},{4,6},{5,7},{6,0},{7,1},{8,10},{9,11},{10,... | collective-permute-start | bytes 589832 | tf_op jit(solution)/shard_map/ppermute | solution.py:232
  43.9 12.7 %collective-permute-start.5 = (bf16[2,6,32,256]{3,2,1,0:T(8,128)(2,1)}, bf16[2,6,32,256]{3,2,1,0:T(8,128)(2,1)}, u32[]{:S(2)}, u32[]{:S(2)}) collective-permute-start(bf16[2,6,32,256]{3,2,1,0:T(8,128)(2,1)} %get-tuple-element.70), channel_id=1, source_target_pairs={{0,4},{1,5},{2,6},{3,7},{4,0},{5,1},{6,2},{7,3},{8,12},{9,13},{10,... | collective-permute-start | bytes 589832 | tf_op jit(solution)/shard_map/ppermute | solution.py:232
  46.7 9.8 %collective-permute-start.6 = (bf16[2,6,32,256]{3,2,1,0:T(8,128)(2,1)}, bf16[2,6,32,256]{3,2,1,0:T(8,128)(2,1)}, u32[]{:S(2)}, u32[]{:S(2)}) collective-permute-start(bf16[2,6,32,256]{3,2,1,0:T(8,128)(2,1)} %get-tuple-element.71), channel_id=1, source_target_pairs={{0,6},{1,7},{2,0},{3,1},{4,2},{5,3},{6,4},{7,5},{8,14},{9,15},{10,... | collective-permute-start | bytes 589832 | tf_op jit(solution)/shard_map/ppermute | solution.py:232
  56.6 22.5 %all-to-all-start.1 = ((bf16[32,32,256]{2,1,0:T(8,128)(2,1)}), bf16[32,32,256]{2,1,0:T(8,128)(2,1)}, u32[]{:S(2)}, u32[]{:S(2)}) async-start(bf16[32,32,256]{2,1,0:T(8,128)(2,1)} %get-tuple-element.72), calls=%async_computation.1 | async-start | bytes 1048576 | tf_op jit(solution)/shard_map/all_to_all | solution.py:233
  65.2 5.2 %collective-permute-start.8 = (f32[32,256]{1,0:T(8,128)}, f32[32,256]{1,0:T(8,128)}, u32[]{:S(2)}, u32[]{:S(2)}) collective-permute-start(f32[32,256]{1,0:T(8,128)} %get-tuple-element.79), channel_id=1, source_target_pairs={{0,6},{1,7},{2,0},{3,1},{4,2},{5,3},{6,4},{7,5},{8,14},{9,15},{10,... | collective-permute-start | bytes 98312 | tf_op jit(solution)/shard_map/ppermute | solution.py:232
  67.4 6.5 %collective-permute-start.9 = (f32[32,256]{1,0:T(8,128)}, f32[32,256]{1,0:T(8,128)}, u32[]{:S(2)}, u32[]{:S(2)}) collective-permute-start(f32[32,256]{1,0:T(8,128)} %get-tuple-element.80), channel_id=1, source_target_pairs={{0,4},{1,5},{2,6},{3,7},{4,0},{5,1},{6,2},{7,3},{8,12},{9,13},{10,... | collective-permute-start | bytes 98312 | tf_op jit(solution)/shard_map/ppermute | solution.py:232
  68.5 6.2 %collective-permute-start.10 = (f32[32,256]{1,0:T(8,128)}, f32[32,256]{1,0:T(8,128)}, u32[]{:S(2)}, u32[]{:S(2)}) collective-permute-start(f32[32,256]{1,0:T(8,128)} %get-tuple-element.81), channel_id=1, source_target_pairs={{0,2},{1,3},{2,4},{3,5},{4,6},{5,7},{6,0},{7,1},{8,10},{9,11},{10,... | collective-permute-start | bytes 98312 | tf_op jit(solution)/shard_map/ppermute | solution.py:232
  80.8 9.7 %collective-permute-start.11 = (bf16[1,6,32,256]{3,2,1,0:T(8,128)(2,1)}, bf16[1,6,32,256]{3,2,1,0:T(8,128)(2,1)}, u32[]{:S(2)}, u32[]{:S(2)}) collective-permute-start(bf16[1,6,32,256]{3,2,1,0:T(8,128)(2,1)} %get-tuple-element.95), channel_id=1, source_target_pairs={{0,2},{1,3},{2,4},{3,5},{4,6},{5,7},{6,0},{7,1},{8,10},{9,11},{10,... | collective-permute-start | bytes 294920 | tf_op jit(solution)/shard_map/ppermute | solution.py:232
  81.5 9.0 %collective-permute-start.12 = (bf16[1,6,32,256]{3,2,1,0:T(8,128)(2,1)}, bf16[1,6,32,256]{3,2,1,0:T(8,128)(2,1)}, u32[]{:S(2)}, u32[]{:S(2)}) collective-permute-start(bf16[1,6,32,256]{3,2,1,0:T(8,128)(2,1)} %get-tuple-element.96), channel_id=1, source_target_pairs={{0,4},{1,5},{2,6},{3,7},{4,0},{5,1},{6,2},{7,3},{8,12},{9,13},{10,... | collective-permute-start | bytes 294920 | tf_op jit(solution)/shard_map/ppermute | solution.py:232
  84.7 5.9 %collective-permute-start.13 = (bf16[1,6,32,256]{3,2,1,0:T(8,128)(2,1)}, bf16[1,6,32,256]{3,2,1,0:T(8,128)(2,1)}, u32[]{:S(2)}, u32[]{:S(2)}) collective-permute-start(bf16[1,6,32,256]{3,2,1,0:T(8,128)(2,1)} %get-tuple-element.97), channel_id=1, source_target_pairs={{0,6},{1,7},{2,0},{3,1},{4,2},{5,3},{6,4},{7,5},{8,14},{9,15},{10,... | collective-permute-start | bytes 294920 | tf_op jit(solution)/shard_map/ppermute | solution.py:232
  90.6 20.7 %all-to-all-start.2 = ((bf16[32,32,256]{2,1,0:T(8,128)(2,1)}), bf16[32,32,256]{2,1,0:T(8,128)(2,1)}, u32[]{:S(2)}, u32[]{:S(2)}) async-start(bf16[32,32,256]{2,1,0:T(8,128)(2,1)} %get-tuple-element.98), calls=%async_computation.2 | async-start | bytes 1048576 | tf_op jit(solution)/shard_map/all_to_all | solution.py:233
  98.6 12.5 %collective-permute-start.14 = (f32[32,256]{1,0:T(8,128)}, f32[32,256]{1,0:T(8,128)}, u32[]{:S(2)}, u32[]{:S(2)}) collective-permute-start(f32[32,256]{1,0:T(8,128)} %get-tuple-element.109), channel_id=1, source_target_pairs={{0,6},{1,7},{2,0},{3,1},{4,2},{5,3},{6,4},{7,5},{8,14},{9,15},{10,... | collective-permute-start | bytes 98312 | tf_op jit(solution)/shard_map/ppermute | solution.py:232
  99.9 11.2 %collective-permute-start.15 = (f32[32,256]{1,0:T(8,128)}, f32[32,256]{1,0:T(8,128)}, u32[]{:S(2)}, u32[]{:S(2)}) collective-permute-start(f32[32,256]{1,0:T(8,128)} %get-tuple-element.110), channel_id=1, source_target_pairs={{0,4},{1,5},{2,6},{3,7},{4,0},{5,1},{6,2},{7,3},{8,12},{9,13},{10,... | collective-permute-start | bytes 98312 | tf_op jit(solution)/shard_map/ppermute | solution.py:232
  101.6 9.5 %collective-permute-start.16 = (f32[32,256]{1,0:T(8,128)}, f32[32,256]{1,0:T(8,128)}, u32[]{:S(2)}, u32[]{:S(2)}) collective-permute-start(f32[32,256]{1,0:T(8,128)} %get-tuple-element.111), channel_id=1, source_target_pairs={{0,2},{1,3},{2,4},{3,5},{4,6},{5,7},{6,0},{7,1},{8,10},{9,11},{10,... | collective-permute-start | bytes 98312 | tf_op jit(solution)/shard_map/ppermute | solution.py:232
Sparse Core Ops, SparseCore 0:
  9.2 33.3 all-gather.6
  44.5 33.1 all-gather.8
  79.5 31.6 all-gather.10
